TPU v7x, 32 devices: a whole 2x2x4 slice. The times are simulated.
32 devices in a mesh: seq: 8 (over z, y), head: 4 (over x, core).
Axes of the slice: x: 2, y: 2, z: 4, core: 2. Of those that a mesh axis runs over, the one named last changes fastest.
Arguments:
- hidden_in: bfloat16 [6144, 2048], P('seq'), may hold values from -6 to 6
- lengths: int32 [3], replicated, may hold values from 1 to 6016, as said below
- attn_gain: float32 [2048], replicated, may hold values from 0.5 to 1.5
- w_query: bfloat16 [2048, 2048], P(None, 'head'), may hold values from -0.125 to 0.125
- w_key: bfloat16 [2048, 2048], P(None, 'head'), may hold values from -0.125 to 0.125
- w_value: bfloat16 [2048, 4096], P(None, 'head'), may hold values from -0.125 to 0.125
- w_gate: bfloat16 [2048, 4096], P(None, 'head'), may hold values from -0.125 to 0.125
- w_alpha: bfloat16 [2048, 16], P(None, 'head'), may hold values from -0.125 to 0.125
- w_beta: bfloat16 [2048, 16], P(None, 'head'), may hold values from -0.125 to 0.125
- conv_query: float32 [4, 2048], P(None, 'head'), may hold values from -3 to 3
- conv_key: float32 [4, 2048], P(None, 'head'), may hold values from -3 to 3
- conv_value: float32 [4, 4096], P(None, 'head'), may hold values from -3 to 3
- decay_log: float32 [16], replicated, may hold values from -3 to 2.7
- decay_bias: float32 [16], replicated, may hold values from -9 to -3
- out_gain: float32 [256], replicated, may hold values from 0.5 to 1.5
- w_out: bfloat16 [4096, 2048], P('head'), may hold values from -0.1875 to 0.1875
- ffn_gain: float32 [2048], replicated, may hold values from 0.5 to 1.5
- w_ffn_gate: bfloat16 [2048, 5504], P(None, 'head'), may hold values from -0.125 to 0.125
- w_ffn_up: bfloat16 [2048, 5504], P(None, 'head'), may hold values from -0.125 to 0.125
- w_ffn_down: bfloat16 [5504, 2048], P('head'), may hold values from -0.15625 to 0.15625
- grad_out: bfloat16 [6144, 2048], P('seq', 'head'), may hold values from -6 to 6
Outputs:
- hidden_out: bfloat16 [6144, 2048], P('seq', 'head')
- grad_in: float32 [6144, 2048], P('seq', 'head')
- grad_attn_gain: float32 [2048], P('seq')
- grad_w_query: float32 [2048, 2048], P('seq', 'head')
- grad_w_key: float32 [2048, 2048], P('seq', 'head')
- grad_w_value: float32 [2048, 4096], P('seq', 'head')
- grad_w_gate: float32 [2048, 4096], P('seq', 'head')
- grad_w_alpha: float32 [2048, 16], P('seq', 'head')
- grad_w_beta: float32 [2048, 16], P('seq', 'head')
- grad_conv_query: float32 [4, 2048], P(None, ('head', 'seq'))
- grad_conv_key: float32 [4, 2048], P(None, ('head', 'seq'))
- grad_conv_value: float32 [4, 4096], P(None, ('head', 'seq'))
- grad_decay_log: float32 [16], replicated
- grad_decay_bias: float32 [16], replicated
- grad_out_gain: float32 [256], replicated
- grad_w_out: float32 [4096, 2048], P('head', 'seq')
- grad_ffn_gain: float32 [2048], P('seq')
- grad_w_ffn_gate: float32 [2048, 5504], P('seq', 'head')
- grad_w_ffn_up: float32 [2048, 5504], P('seq', 'head')
- grad_w_ffn_down: float32 [5504, 2048], P('head', 'seq')
Inputs may be any that keep to these rules, and one draw needn't show every extreme that they name: `lengths`: three sequences in order; each is padded to a multiple of 64 positions, the padded sequences fill all 6144 positions, and the first and the last padded sequence each take fewer than 768 positions.
All inputs are finite; a program needn't handle non-finite values.
Results may differ from a plain program's by a relative error of at most 0.025.
Values may be sent and summed in bfloat16 or wider, within the bound.
A program may use at most 320 MiB of HBM per device.

v0:
```python
import jax
import jax.numpy as jnp
from jax import lax
from jax.sharding import PartitionSpec as P

DK = 128
DV = 256
GROUP = 64
CONV = 4


highest = lax.Precision.HIGHEST
epsilon_norm = 1e-06
epsilon_gate = 1e-05


def shifted(block, axis, distance):
    devices = range(lax.axis_size(axis))
    route = [(i - distance, i) for i in devices if i - distance in devices]
    return lax.ppermute(block, axis, route)


def prefix(shard, axis, combine, identity, reverse):
    devices, place = (lax.axis_size(axis), lax.axis_index(axis))
    everything = jax.tree.map(
        lambda part, kind: lax.all_gather(part.astype(kind), axis),
        shard,
        (jnp.bfloat16, jnp.bfloat16),
    )
    start = jax.tree.map(
        lambda part, zero: jnp.broadcast_to(jnp.asarray(zero, part.dtype), part.shape),
        shard,
        identity,
    )

    def turn(k, before):
        at = devices - 1 - k if reverse else k
        reached = at > place if reverse else at < place
        new = combine(
            before, jax.tree.map(lambda part, own: part[at].astype(own.dtype), everything, shard)
        )
        return jax.tree.map(lambda a, b: jnp.where(reached, a, b), new, before)

    return lax.fori_loop(0, devices, turn, start)


def batch_dot(spec, left, right):
    return jnp.einsum(spec, left, right, precision=highest, preferred_element_type=jnp.float32)


def rounded(values):
    return lax.optimization_barrier(values.astype(jnp.bfloat16)).astype(jnp.float32)


def layout(lengths, positions):
    padded = (lengths + (GROUP - 1)) // GROUP * GROUP
    seq_ends = jnp.cumsum(padded)
    begins = seq_ends - padded
    offset = positions[:, None] - begins[None, :]
    inside = (offset >= 0) & (positions[:, None] < seq_ends[None, :])
    valid_mask = jnp.any(inside & (offset < lengths[None, :]), axis=1).astype(jnp.float32)
    starts = jnp.any(offset == 0, axis=1).astype(jnp.float32)
    return (valid_mask, starts)


def delayed(values, shift_by):
    if shift_by == 0:
        return values
    return jnp.concatenate([jnp.zeros((shift_by,), values.dtype), values[:-shift_by]])


def convolve(extended, weight, starts):
    token_rows = starts.shape[0]
    running = extended[CONV - 1 :] * weight[0]
    alive = jnp.ones_like(starts)
    for tap_index in range(1, CONV):
        alive = alive * (1.0 - delayed(starts, tap_index - 1))
        begin_row = CONV - 1 - tap_index
        running = (
            running
            + extended[begin_row : begin_row + token_rows] * weight[tap_index] * alive[:, None]
        )
    return jax.nn.silu(running)


def unit_rows(values):
    return values * lax.rsqrt(jnp.sum(values * values, axis=-1, keepdims=True) + epsilon_norm)


def make_features(starts, valid_mask, head_count):

    def features(
        ext_query,
        ext_key,
        ext_value,
        conv_query,
        conv_key,
        conv_value,
        alpha_pre,
        beta_pre,
        decay_log,
        decay_bias,
    ):
        token_rows = starts.shape[0]
        query_act = convolve(ext_query, conv_query, starts).reshape(token_rows, head_count, DK)
        key_act = convolve(ext_key, conv_key, starts).reshape(token_rows, head_count, DK)
        value_act = convolve(ext_value, conv_value, starts).reshape(token_rows, head_count, DV)
        query = unit_rows(query_act) * DK ** (-0.5)
        key_rows = unit_rows(key_act) * valid_mask[:, None, None]
        value = value_act * valid_mask[:, None, None]
        decay = -jnp.exp(decay_log) * jax.nn.softplus(alpha_pre + decay_bias) * valid_mask[:, None]
        beta = jax.nn.sigmoid(beta_pre)
        return (query, key_rows, value, decay, beta)

    return features


def unit_inverse(strict):
    group_len = strict.shape[-1]
    identity_c = jnp.eye(group_len, dtype=jnp.float32)
    result = identity_c - strict
    power_term = batch_dot("...ij,...jk->...ik", strict, strict)
    degree = 2
    while degree < group_len:
        result = batch_dot("...ij,...jk->...ik", result, identity_c + power_term)
        power_term = batch_dot("...ij,...jk->...ik", power_term, power_term)
        degree = degree * 2
    return result


def prepare(query, key_rows, value, decay, beta):
    group_len = query.shape[-2]
    cumulative = jnp.cumsum(decay, axis=-1)
    lower_mask = jnp.tril(jnp.ones((group_len, group_len), dtype=bool))
    strict_mask = jnp.tril(jnp.ones((group_len, group_len), dtype=bool), -1)
    log_gap = cumulative[..., :, None] - cumulative[..., None, :]
    decay_ratio = jnp.where(lower_mask, jnp.exp(jnp.where(lower_mask, log_gap, 0.0)), 0.0)
    similar = batch_dot("...ik,...jk->...ij", key_rows, key_rows)
    coupling = jnp.where(strict_mask, beta[..., :, None] * decay_ratio * similar, 0.0)
    inverse = unit_inverse(coupling)
    growth = jnp.exp(cumulative)[..., None]
    weights_w = batch_dot("...ij,...jk->...ik", inverse, beta[..., None] * growth * key_rows)
    values_u = batch_dot("...ij,...jk->...ik", inverse, beta[..., None] * value)
    mixing = decay_ratio * batch_dot("...ik,...jk->...ij", query, key_rows)
    closing = cumulative[..., -1:]
    key_decayed = jnp.exp(closing - cumulative)[..., None] * key_rows
    return (growth * query, mixing, weights_w, values_u, key_decayed, jnp.exp(closing[..., 0]))


def group_output(state, parts):
    query_d, mixing, weights_w, values_u, key_decayed, fading = parts
    fresh = values_u - batch_dot("...ck,...kv->...cv", weights_w, state)
    block_out = batch_dot("...ck,...kv->...cv", query_d, state) + batch_dot(
        "...cd,...dv->...cv", mixing, fresh
    )
    after = fading[..., None, None] * state + batch_dot("...ck,...cv->...kv", key_decayed, fresh)
    return (block_out, after)


def to_blocks(values, group_count):
    shaped = values.reshape((group_count, values.shape[0] // group_count) + values.shape[1:])
    return jnp.swapaxes(shaped, 1, 2)


def from_blocks(blocks):
    merged = jnp.swapaxes(blocks, 1, 2)
    return merged.reshape((merged.shape[0] * merged.shape[1],) + merged.shape[2:])


def gated_norm(delta_out, gate_heads, out_gain):
    scale_row = lax.rsqrt(jnp.mean(delta_out * delta_out, axis=-1, keepdims=True) + epsilon_gate)
    return delta_out * scale_row * out_gain * jax.nn.silu(gate_heads)


def affine(earlier, later):
    return (
        batch_dot("hij,hjk->hik", later[0], earlier[0]),
        batch_dot("hij,hjk->hik", later[0], earlier[1]) + later[1],
    )


def with_rim(values, rim_rows):
    return jnp.concatenate(
        [values[: values.shape[0] - (CONV - 1)], values[values.shape[0] - (CONV - 1) :] + rim_rows]
    )


def dense(left, right):
    return jnp.dot(left, right, preferred_element_type=jnp.float32)


def shards(
    hidden_in,
    lengths,
    attn_gain,
    w_query,
    w_key,
    w_value,
    w_gate,
    w_alpha,
    w_beta,
    conv_query,
    conv_key,
    conv_value,
    decay_log,
    decay_bias,
    out_gain,
    w_out,
    ffn_gain,
    w_ffn_gate,
    w_ffn_up,
    w_ffn_down,
    grad_out,
):
    token_rows = hidden_in.shape[0]
    head_count = w_alpha.shape[1]
    col_width = grad_out.shape[1]
    group_count = token_rows // GROUP
    positions = lax.axis_index("seq") * token_rows + jnp.arange(token_rows, dtype=jnp.int32)
    valid_mask, starts = layout(lengths, positions)
    keep_flags = 1.0 - starts[::GROUP]
    head_first = lax.axis_index("head") * head_count
    col_first = lax.axis_index("head") * col_width
    local_log = lax.dynamic_slice_in_dim(decay_log, head_first, head_count)
    local_bias = lax.dynamic_slice_in_dim(decay_bias, head_first, head_count)
    inputs32 = hidden_in.astype(jnp.float32)
    attn_scale = lax.rsqrt(jnp.mean(inputs32 * inputs32, axis=-1, keepdims=True) + epsilon_norm)
    attn_hat = inputs32 * attn_scale
    normed = (attn_hat * attn_gain).astype(jnp.bfloat16)
    query_pre = dense(normed, w_query).astype(jnp.bfloat16)
    key_pre = dense(normed, w_key).astype(jnp.bfloat16)
    value_pre = dense(normed, w_value).astype(jnp.bfloat16)
    gate_pre = dense(normed, w_gate)
    alpha_pre = dense(normed, w_alpha)
    beta_pre = dense(normed, w_beta)
    tail_first = token_rows - (CONV - 1)
    rim_query, rim_key, rim_value = shifted(
        (query_pre[tail_first:], key_pre[tail_first:], value_pre[tail_first:]), "seq", 1
    )
    ext_query = jnp.concatenate([rim_query, query_pre]).astype(jnp.float32)
    ext_key = jnp.concatenate([rim_key, key_pre]).astype(jnp.float32)
    ext_value = jnp.concatenate([rim_value, value_pre]).astype(jnp.float32)
    features = make_features(starts, valid_mask, head_count)
    made, feature_pull = jax.vjp(
        features,
        ext_query,
        ext_key,
        ext_value,
        conv_query,
        conv_key,
        conv_value,
        alpha_pre,
        beta_pre,
        local_log,
        local_bias,
    )
    query_f, key_f, value_f, decay, beta = made
    blocks_query = to_blocks(rounded(query_f), group_count)
    blocks_key = to_blocks(rounded(key_f), group_count)
    blocks_value = to_blocks(rounded(value_f), group_count)
    blocks_decay = to_blocks(decay, group_count)
    blocks_beta = to_blocks(beta, group_count)
    query_d, mixing, weights_w, values_u, key_decayed, fading = prepare(
        blocks_query, blocks_key, blocks_value, blocks_decay, blocks_beta
    )
    identity_k = jnp.eye(DK, dtype=jnp.float32)
    group_linear = fading[..., None, None] * identity_k - batch_dot(
        "...ck,...cj->...kj", key_decayed, weights_w
    )
    group_offset = batch_dot("...ck,...cv->...kv", key_decayed, values_u)
    start_linear = jnp.broadcast_to(identity_k, (head_count, DK, DK))
    start_offset = jnp.zeros((head_count, DK, DV), jnp.float32)

    def compose(carry, block):
        linear_part, offset_part = carry
        block_linear, block_offset, keep_flag = block
        linear_part = batch_dot("hij,hjk->hik", block_linear, keep_flag * linear_part)
        offset_part = (
            batch_dot("hij,hjk->hik", block_linear, keep_flag * offset_part) + block_offset
        )
        return ((linear_part, offset_part), None)

    (device_linear, device_offset), _ = lax.scan(
        compose, (start_linear, start_offset), (group_linear, group_offset, keep_flags)
    )
    _, entry_state = prefix(
        (device_linear, device_offset), "seq", affine, (start_linear, start_offset), False
    )

    def advance(state, block):
        block_linear, block_offset, keep_flag = block
        used = keep_flag * state
        return (batch_dot("hij,hjk->hik", block_linear, used) + block_offset, used)

    _, used_states = lax.scan(advance, entry_state, (group_linear, group_offset, keep_flags))
    fresh = values_u - batch_dot("nhck,nhkv->nhcv", weights_w, used_states)
    block_out = batch_dot("nhck,nhkv->nhcv", query_d, used_states) + batch_dot(
        "nhcd,nhdv->nhcv", mixing, fresh
    )
    delta_out = from_blocks(block_out) * valid_mask[:, None, None]
    gate_heads = gate_pre.reshape(token_rows, head_count, DV)
    gated_f, gated_pull = jax.vjp(gated_norm, delta_out, gate_heads, out_gain)
    gated = gated_f.astype(jnp.bfloat16).reshape(token_rows, head_count * DV)
    mixed = lax.psum_scatter(
        dense(gated, w_out).astype(jnp.bfloat16), "head", scatter_dimension=1, tiled=True
    ).astype(jnp.float32)
    middle = lax.dynamic_slice_in_dim(inputs32, col_first, col_width, 1) + mixed
    sent = lax.all_gather(middle.astype(jnp.bfloat16), "head", axis=1, tiled=True).astype(
        jnp.float32
    )
    ffn_scale = lax.rsqrt(jnp.mean(sent * sent, axis=-1, keepdims=True) + epsilon_norm)
    ffn_hat = sent * ffn_scale
    normed_ffn = (ffn_hat * ffn_gain).astype(jnp.bfloat16)
    ffn_gate_pre = dense(normed_ffn, w_ffn_gate)
    ffn_up_pre = dense(normed_ffn, w_ffn_up)
    sigmoid_gate = jax.nn.sigmoid(ffn_gate_pre)
    silu_gate = ffn_gate_pre * sigmoid_gate
    inner_act = (silu_gate * ffn_up_pre).astype(jnp.bfloat16)
    ffn_out = lax.psum_scatter(
        dense(inner_act, w_ffn_down).astype(jnp.bfloat16), "head", scatter_dimension=1, tiled=True
    ).astype(jnp.float32)
    hidden_out = (middle + ffn_out).astype(jnp.bfloat16)
    grad_rows = lax.all_gather(grad_out, "head", axis=1, tiled=True)
    d_inner = dense(grad_rows, w_ffn_down.T)
    grad_w_ffn_down = dense(inner_act.T, grad_rows)
    d_ffn_gate = (
        d_inner * ffn_up_pre * sigmoid_gate * (1.0 + ffn_gate_pre * (1.0 - sigmoid_gate))
    ).astype(jnp.bfloat16)
    d_ffn_up = (d_inner * silu_gate).astype(jnp.bfloat16)
    grad_w_ffn_gate = dense(normed_ffn.T, d_ffn_gate)
    grad_w_ffn_up = dense(normed_ffn.T, d_ffn_up)
    d_normed_ffn = dense(d_ffn_gate, w_ffn_gate.T) + dense(d_ffn_up, w_ffn_up.T)
    d_normed_ffn = lax.psum(d_normed_ffn.astype(jnp.bfloat16), "head").astype(jnp.float32)
    grad_ffn_gain = jnp.sum(d_normed_ffn * ffn_hat, axis=0)
    scaled_ffn = ffn_gain * d_normed_ffn
    d_sent = ffn_scale * (
        scaled_ffn - ffn_hat * jnp.mean(ffn_hat * scaled_ffn, axis=-1, keepdims=True)
    )
    d_sent_cols = lax.dynamic_slice_in_dim(d_sent, col_first, col_width, 1)
    d_middle = grad_out.astype(jnp.float32) + d_sent_cols
    d_mixed = lax.all_gather(d_middle.astype(jnp.bfloat16), "head", axis=1, tiled=True)
    grad_w_out = dense(gated.T, d_mixed)
    d_gated = dense(d_mixed, w_out.T).reshape(token_rows, head_count, DV)
    d_delta, d_gate_heads, grad_gain_part = gated_pull(d_gated)
    d_delta = d_delta * valid_mask[:, None, None]
    d_gate_pre = d_gate_heads.reshape(token_rows, head_count * DV).astype(jnp.bfloat16)
    d_blocks = to_blocks(d_delta, group_count)
    local_grad = batch_dot("nhck,nhcv->nhkv", query_d, d_blocks) - batch_dot(
        "nhck,nhcv->nhkv", weights_w, batch_dot("nhcd,nhcv->nhdv", mixing, d_blocks)
    )

    def collect_back(carry, block):
        block_linear, block_grad, keep_flag = block
        return (keep_flag * (block_grad + batch_dot("hji,hjk->hik", block_linear, carry)), None)

    entry_grad, _ = lax.scan(
        collect_back, start_offset, (group_linear, local_grad, keep_flags), reverse=True
    )
    _, exit_grad = prefix(
        (jnp.swapaxes(device_linear, 1, 2), entry_grad),
        "seq",
        affine,
        (start_linear, start_offset),
        True,
    )

    def group_back(carry, block):
        query_c, key_c, value_c, decay_c, beta_c, used, keep_flag, d_out_c = block

        def group_fn(query_c, key_c, value_c, decay_c, beta_c, used):
            return group_output(used, prepare(query_c, key_c, value_c, decay_c, beta_c))

        _, pullback = jax.vjp(group_fn, query_c, key_c, value_c, decay_c, beta_c, used)
        d_query_c, d_key_c, d_value_c, d_decay_c, d_beta_c, d_used = pullback((d_out_c, carry))
        return (keep_flag * d_used, (d_query_c, d_key_c, d_value_c, d_decay_c, d_beta_c))

    _, block_grads = lax.scan(
        group_back,
        exit_grad,
        (
            blocks_query,
            blocks_key,
            blocks_value,
            blocks_decay,
            blocks_beta,
            used_states,
            keep_flags,
            d_blocks,
        ),
        reverse=True,
    )
    d_query, d_key, d_value, d_decay, d_beta = [from_blocks(piece) for piece in block_grads]
    (
        d_ext_query,
        d_ext_key,
        d_ext_value,
        grad_conv_query,
        grad_conv_key,
        grad_conv_value,
        d_alpha,
        d_beta_pre,
        grad_log_local,
        grad_bias_local,
    ) = feature_pull((d_query, d_key, d_value, d_decay, d_beta))
    back_query, back_key, back_value = shifted(
        (d_ext_query[: CONV - 1], d_ext_key[: CONV - 1], d_ext_value[: CONV - 1]), "seq", -1
    )
    d_query_pre = with_rim(d_ext_query[CONV - 1 :], back_query).astype(jnp.bfloat16)
    d_key_pre = with_rim(d_ext_key[CONV - 1 :], back_key).astype(jnp.bfloat16)
    d_value_pre = with_rim(d_ext_value[CONV - 1 :], back_value).astype(jnp.bfloat16)
    d_alpha = d_alpha.astype(jnp.bfloat16)
    d_beta_pre = d_beta_pre.astype(jnp.bfloat16)
    grad_w_query = dense(normed.T, d_query_pre)
    grad_w_key = dense(normed.T, d_key_pre)
    grad_w_value = dense(normed.T, d_value_pre)
    grad_w_gate = dense(normed.T, d_gate_pre)
    grad_w_alpha = dense(normed.T, d_alpha)
    grad_w_beta = dense(normed.T, d_beta_pre)
    d_normed = (
        dense(d_query_pre, w_query.T)
        + dense(d_key_pre, w_key.T)
        + dense(d_value_pre, w_value.T)
        + dense(d_gate_pre, w_gate.T)
        + dense(d_alpha, w_alpha.T)
        + dense(d_beta_pre, w_beta.T)
    )
    d_normed = lax.psum(d_normed.astype(jnp.bfloat16), "head").astype(jnp.float32)
    grad_attn_gain = jnp.sum(d_normed * attn_hat, axis=0)
    scaled_attn = attn_gain * d_normed
    d_inputs = attn_scale * (
        scaled_attn - attn_hat * jnp.mean(attn_hat * scaled_attn, axis=-1, keepdims=True)
    )
    d_input_cols = lax.dynamic_slice_in_dim(d_inputs, col_first, col_width, 1)
    grad_in = d_middle + d_input_cols
    full_log = lax.dynamic_update_slice_in_dim(
        jnp.zeros(decay_log.shape, jnp.float32), grad_log_local, head_first, 0
    )
    full_bias = lax.dynamic_update_slice_in_dim(
        jnp.zeros(decay_bias.shape, jnp.float32), grad_bias_local, head_first, 0
    )
    grad_decay_log, grad_decay_bias, grad_out_gain = lax.psum(
        (full_log, full_bias, grad_gain_part), ("seq", "head")
    )
    (
        s_attn_gain,
        s_query,
        s_key,
        s_value,
        s_gate,
        s_alpha,
        s_beta,
        s_conv_query,
        s_conv_key,
        s_conv_value,
        s_out,
        s_ffn_gate,
        s_ffn_up,
        s_ffn_down,
        s_ffn_gain,
    ) = (
        lax.psum_scatter(
            grad_attn_gain.astype(jnp.bfloat16), "seq", scatter_dimension=0, tiled=True
        ).astype(jnp.float32),
        lax.psum_scatter(
            grad_w_query.astype(jnp.bfloat16), "seq", scatter_dimension=0, tiled=True
        ).astype(jnp.float32),
        lax.psum_scatter(
            grad_w_key.astype(jnp.bfloat16), "seq", scatter_dimension=0, tiled=True
        ).astype(jnp.float32),
        lax.psum_scatter(
            grad_w_value.astype(jnp.bfloat16), "seq", scatter_dimension=0, tiled=True
        ).astype(jnp.float32),
        lax.psum_scatter(
            grad_w_gate.astype(jnp.bfloat16), "seq", scatter_dimension=0, tiled=True
        ).astype(jnp.float32),
        lax.psum_scatter(
            grad_w_alpha.astype(jnp.bfloat16), "seq", scatter_dimension=0, tiled=True
        ).astype(jnp.float32),
        lax.psum_scatter(
            grad_w_beta.astype(jnp.bfloat16), "seq", scatter_dimension=0, tiled=True
        ).astype(jnp.float32),
        lax.psum_scatter(
            grad_conv_query.astype(jnp.bfloat16), "seq", scatter_dimension=1, tiled=True
        ).astype(jnp.float32),
        lax.psum_scatter(
            grad_conv_key.astype(jnp.bfloat16), "seq", scatter_dimension=1, tiled=True
        ).astype(jnp.float32),
        lax.psum_scatter(
            grad_conv_value.astype(jnp.bfloat16), "seq", scatter_dimension=1, tiled=True
        ).astype(jnp.float32),
        lax.psum_scatter(
            grad_w_out.astype(jnp.bfloat16), "seq", scatter_dimension=1, tiled=True
        ).astype(jnp.float32),
        lax.psum_scatter(
            grad_w_ffn_gate.astype(jnp.bfloat16), "seq", scatter_dimension=0, tiled=True
        ).astype(jnp.float32),
        lax.psum_scatter(
            grad_w_ffn_up.astype(jnp.bfloat16), "seq", scatter_dimension=0, tiled=True
        ).astype(jnp.float32),
        lax.psum_scatter(
            grad_w_ffn_down.astype(jnp.bfloat16), "seq", scatter_dimension=1, tiled=True
        ).astype(jnp.float32),
        lax.psum_scatter(
            grad_ffn_gain.astype(jnp.bfloat16), "seq", scatter_dimension=0, tiled=True
        ).astype(jnp.float32),
    )
    return (
        hidden_out,
        grad_in,
        s_attn_gain,
        s_query,
        s_key,
        s_value,
        s_gate,
        s_alpha,
        s_beta,
        s_conv_query,
        s_conv_key,
        s_conv_value,
        grad_decay_log,
        grad_decay_bias,
        grad_out_gain,
        s_out,
        s_ffn_gain,
        s_ffn_gate,
        s_ffn_up,
        s_ffn_down,
    )


def solution(mesh):
    return jax.shard_map(
        shards,
        mesh=mesh,
        in_specs=(
            P("seq", None),
            P(),
            P(),
            P(None, "head"),
            P(None, "head"),
            P(None, "head"),
            P(None, "head"),
            P(None, "head"),
            P(None, "head"),
            P(None, "head"),
            P(None, "head"),
            P(None, "head"),
            P(),
            P(),
            P(),
            P("head", None),
            P(),
            P(None, "head"),
            P(None, "head"),
            P("head", None),
            P("seq", "head"),
        ),
        out_specs=(
            P("seq", "head"),
            P("seq", "head"),
            P("seq"),
            P("seq", "head"),
            P("seq", "head"),
            P("seq", "head"),
            P("seq", "head"),
            P("seq", "head"),
            P("seq", "head"),
            P(None, ("head", "seq")),
            P(None, ("head", "seq")),
            P(None, ("head", "seq")),
            P(),
            P(),
            P(),
            P("head", "seq"),
            P("seq"),
            P("seq", "head"),
            P("seq", "head"),
            P("head", "seq"),
        ),
        check_vma=False,
    )
```

profile of v0, /device:TPU:0, one launch (start us, length us, event | category | flops | bytes accessed | tf_op | source)
XLA Modules:
  0.0 2598.6 jit_solution(6685574418341192960)
XLA Ops:
  106.0 60.8 %while.96 = (s32[]{:T(128)}, f32[4,128,128]{2,1,0:T(8,128)S(1)}, f32[4,128,256]{2,1,0:T(8,128)S(1)}, f32[12,4,128,128]{3,2,1,0:T(8,128)}, f32[12]{0:T(128)S(1)},...) while((s32[]{:T(128)}, f32[4,128,128]{2,1,0:T(8,128)S(1)}, f32[4,128,256]{2,1,0:T(8,128)S(1)}, ...), condition=%wide.region_8.9_spmd.clone, body=%wide.region_7.8_spmd.clone.sunk | while | flops 302448640 | bytes 4196982 | solution.py:283
  179.6 27.5 %all-gather.18.cloned.1.call-done = bf16[32,128,128]{2,1,0:T(8,128)(2,1)} async-done(((bf16[4,128,128]{2,1,0:T(8,128)(2,1)}), bf16[32,128,128]{2,1,0:T(8,128)(2,1)}) %all-gather.18.cloned.1.call-update) | async-done | bytes 1048592 | tf_op jit(solution)/shard_map/all_gather | solution.py:26
  207.1 50.8 %all-gather.20.cloned.1.call-done = bf16[32,128,256]{2,1,0:T(8,128)(2,1)} async-done(((bf16[4,128,256]{2,1,0:T(8,128)(2,1)}), bf16[32,128,256]{2,1,0:T(8,128)(2,1)}) %all-gather.20.cloned.1.call-update) | async-done | bytes 2097168 | tf_op jit(solution)/shard_map/all_gather | solution.py:26
  257.9 12.5 while.97
  270.5 54.3 %while.94 = (s32[]{:T(128)}, f32[4,128,256]{2,1,0:T(8,128)S(1)}, f32[12,4,128,256]{3,2,1,0:T(8,128)}, f32[12,4,128,128]{3,2,1,0:T(8,128)}, f32[12]{0:T(128)S(1)}, /*index=5*/f32[12,4,128,256]{3,2,1,0:T(8,128)}, s32[]{:T(128)}) while((s32[]{:T(128)}, f32[4,128,256]{2,1,0:T(8,128)S(1)}, f32[12,4,128,256]{3,2,1,0:T(8,128)}, ...), condition=%wide.region_12.13_spmd, body=%wide.region_11.12_spmd.sunk | while | flops 201719808 | bytes 3934309 | solution.py:295
  366.9 31.1 %reduce-scatter.26.cloned.1.call-done = bf16[768,512]{1,0:T(8,128)(2,1)} async-done(((bf16[768,2048]{1,0:T(8,128)(2,1)}), bf16[768,512]{1,0:T(8,128)(2,1)}) %reduce-scatter.26.cloned.1.call-update) | async-done | bytes 786448 | tf_op jit(solution)/shard_map/reduce_scatter | solution.py:304
  401.6 27.8 %all-gather.12.cloned.1.call-done = bf16[768,2048]{1,0:T(8,128)(2,1)} async-done(((bf16[768,512]{1,0:T(8,128)(2,1)}), bf16[768,2048]{1,0:T(8,128)(2,1)}) %all-gather.12.cloned.1.call-update) | async-done | bytes 3145744 | tf_op jit(solution)/shard_map/all_gather | solution.py:308
  459.5 14.0 multiply_convert_fusion.2
  491.6 68.5 %all-reduce.33.cloned.1.call-done = bf16[768,2048]{1,0:T(8,128)(2,1)} async-done(((bf16[768,2048]{1,0:T(8,128)(2,1)}), bf16[768,2048]{1,0:T(8,128)(2,1)}) %all-reduce.33.cloned.1.call-update) | async-done | bytes 3145744 | tf_op jit(solution)/shard_map/psum | solution.py:333
  576.8 22.7 all-gather.16.cloned.1.call-done
  637.8 36.6 %while.98 = (s32[]{:T(128)}, f32[4,128,256]{2,1,0:T(8,128)S(1)}, f32[12]{0:T(128)S(1)}, f32[12,4,128,256]{3,2,1,0:T(8,128)}, f32[12,4,128,128]{3,2,1,0:T(8,128)}, /*index=5*/s32[]{:T(128)}, s32[]{:T(128)}, s32[]{:T(128)}) while((s32[]{:T(128)}, f32[4,128,256]{2,1,0:T(8,128)S(1)}, f32[12]{0:T(128)S(1)}, ...), condition=%wide.region_21.22_spmd.clone, body=%wide.region_20.21_spmd.clone.sunk | while | flops 201719808 | bytes 2885758 | solution.py:356
  694.1 30.5 %all-gather.24.cloned.1.call-done = bf16[32,128,256]{2,1,0:T(8,128)(2,1)} async-done(((bf16[4,128,256]{2,1,0:T(8,128)(2,1)}), bf16[32,128,256]{2,1,0:T(8,128)(2,1)}) %all-gather.24.cloned.1.call-update) | async-done | bytes 2097168 | tf_op jit(solution)/shard_map/all_gather | solution.py:26
  724.6 12.8 while.99
  742.1 666.5 %while.95 = (s32[]{:T(128)}, f32[4,128,256]{2,1,0:T(8,128)S(1)}, f32[12,4,64,128]{3,2,1,0:T(8,128)}, f32[12,4,64,128]{3,2,1,0:T(8,128)}, f32[12,4,64,256]{3,2,1,...) while((s32[]{:T(128)}, f32[4,128,256]{2,1,0:T(8,128)S(1)}, ...), condition=%wide.region_36.37_spmd, body=%wide.region_24.36_spmd.sunk | while | flops 1563772928 | bytes 30003264 | solution.py:377
  1439.7 11.3 multiply_reduce_fusion.9
  1458.1 9.6 convolution_convert_fusion.1
  1467.8 9.6 convolution_convert_fusion
  1477.8 9.5 convolution_convert_fusion.2
  1530.7 17.6 add_convert_fusion
  1589.4 43.9 %all-reduce.28 = (f32[16]{0:T(128)}, f32[16]{0:T(128)}, f32[256]{0:T(256)}) all-reduce(f32[16]{0:T(128)S(1)} %multiply_dynamic-update-slice_fusion, f32[16]{0:T(128)S(1)} %dynamic_update_slice.59, f32[256]{0:T(256)S(1)} %copy-done.141), channel_id=1, replica_groups=mesh['seq'=8,'head'=4] {'seq','head'}, use_global_device_ids=true, to_apply=%region_65.66 | all-reduce | flops 288 | bytes 2304 | tf_op jit(solution)/shard_map/psum | solution.py:441
  1639.7 63.4 %reduce-scatter.46.cloned.1.call-done = bf16[256,4]{1,0:T(8,128)(2,1)} async-done(((bf16[2048,4]{1,0:T(8,128)(2,1)}), bf16[256,4]{1,0:T(8,128)(2,1)}) %reduce-scatter.46.cloned.1.call-update) | async-done | bytes 2064
  1704.6 63.5 %reduce-scatter.48.cloned.1.call-done = bf16[256,4]{1,0:T(8,128)(2,1)} async-done(((bf16[2048,4]{1,0:T(8,128)(2,1)}), bf16[256,4]{1,0:T(8,128)(2,1)}) %reduce-scatter.48.cloned.1.call-update) | async-done | bytes 2064
  1769.7 109.5 %reduce-scatter.40.cloned.1.call-done = bf16[256,1376]{0,1:T(8,128)(2,1)} async-done(((bf16[2048,1376]{0,1:T(8,128)(2,1)}), bf16[256,1376]{0,1:T(8,128)(2,1)}) %reduce-scatter.40.cloned.1.call-update) | async-done | bytes 704528 | tf_op jit(solution)/shard_map/reduce_scatter | solution.py:494
  1881.5 109.5 %reduce-scatter.42.cloned.1.call-done = bf16[256,1376]{0,1:T(8,128)(2,1)} async-done(((bf16[2048,1376]{0,1:T(8,128)(2,1)}), bf16[256,1376]{0,1:T(8,128)(2,1)}) %reduce-scatter.42.cloned.1.call-update) | async-done | bytes 704528 | tf_op jit(solution)/shard_map/reduce_scatter | solution.py:497
  1993.3 109.5 %reduce-scatter.44.cloned.1.call-done = bf16[1376,256]{1,0:T(8,128)(2,1)} async-done(((bf16[1376,2048]{1,0:T(8,128)(2,1)}), bf16[1376,256]{1,0:T(8,128)(2,1)}) %reduce-scatter.44.cloned.1.call-update) | async-done | bytes 704528 | tf_op jit(solution)/shard_map/reduce_scatter | solution.py:500
  2105.1 68.3 %all-reduce.35.cloned.1.call-done = bf16[768,2048]{1,0:T(8,128)(2,1)} async-done(((bf16[768,2048]{1,0:T(8,128)(2,1)}), bf16[768,2048]{1,0:T(8,128)(2,1)}) %all-reduce.35.cloned.1.call-update) | async-done | bytes 3145744 | tf_op jit(solution)/shard_map/psum | solution.py:427
  2180.9 21.7 all-reduce.29
  2208.5 36.1 %reduce-scatter.30.cloned.1.call-done = bf16[256,512]{1,0:T(8,128)(2,1)} async-done(((bf16[2048,512]{1,0:T(8,128)(2,1)}), bf16[256,512]{1,0:T(8,128)(2,1)}) %reduce-scatter.30.cloned.1.call-update) | async-done | bytes 262160 | tf_op jit(solution)/shard_map/reduce_scatter | solution.py:464
  2246.3 68.8 %reduce-scatter.32.cloned.1.call-done = bf16[256,512]{1,0:T(8,128)(2,1)} async-done(((bf16[2048,512]{1,0:T(8,128)(2,1)}), bf16[256,512]{1,0:T(8,128)(2,1)}) %reduce-scatter.32.cloned.1.call-update) | async-done | bytes 262160 | tf_op jit(solution)/shard_map/reduce_scatter | solution.py:467
  2317.0 89.3 %reduce-scatter.38.cloned.1.call-done = bf16[1024,256]{1,0:T(8,128)(2,1)} async-done(((bf16[1024,2048]{1,0:T(8,128)(2,1)}), bf16[1024,256]{1,0:T(8,128)(2,1)}) %reduce-scatter.38.cloned.1.call-update) | async-done | bytes 524304 | tf_op jit(solution)/shard_map/reduce_scatter | solution.py:491
  2408.4 89.7 %reduce-scatter.36.cloned.1.call-done = bf16[256,1024]{1,0:T(8,128)(2,1)} async-done(((bf16[2048,1024]{1,0:T(8,128)(2,1)}), bf16[256,1024]{1,0:T(8,128)(2,1)}) %reduce-scatter.36.cloned.1.call-update) | async-done | bytes 524304 | tf_op jit(solution)/shard_map/reduce_scatter | solution.py:473
  2500.2 89.0 %reduce-scatter.34.cloned.1.call-done = bf16[256,1024]{1,0:T(8,128)(2,1)} async-done(((bf16[2048,1024]{1,0:T(8,128)(2,1)}), bf16[256,1024]{1,0:T(8,128)(2,1)}) %reduce-scatter.34.cloned.1.call-update) | async-done | bytes 524304 | tf_op jit(solution)/shard_map/reduce_scatter | solution.py:470
  (2092 shorter events, 1278.4 us)
Async XLA Ops:
  7.2 199.9 %all-gather.18.cloned.1.call-start = ((), (), s32[]{:S(2)}) async-start(), calls=%async_computation.30 | async-start | bytes 1179648 | tf_op jit(solution)/shard_map/all_gather | solution.py:26
  10.7 337.5 %copy-start.97 = (f32[768]{0:T(1024)}, f32[768]{0:T(1024)S(1)}, u32[]{:S(2)}) copy-start(f32[768]{0:T(1024)S(1)} %add_rsqrt_fusion.3) | copy-start | bytes 9220
  13.4 28.8 %collective-permute-start = (bf16[3,512]{1,0:T(4,128)(2,1)S(1)}, bf16[3,512]{1,0:T(4,128)(2,1)S(1)}, u32[]{:S(2)}, u32[]{:S(2)}) collective-permute-start(bf16[3,512]{1,0:T(4,128)(2,1)S(1)} %slice.185), channel_id=1, source_target_pairs={{0,4},{4,8},{8,12},{12,16},{16,20},{20,24},{24,28},{1,5},{5,9},{9,... | collective-permute-start | bytes 9224 | tf_op jit(solution)/shard_map/ppermute | solution.py:20
  21.3 22.3 collective-permute-start.1
  29.5 60.0 %collective-permute-start.2 = (bf16[3,1024]{1,0:T(4,128)(2,1)S(1)}, bf16[3,1024]{1,0:T(4,128)(2,1)S(1)}, u32[]{:S(2)}, u32[]{:S(2)}) collective-permute-start(bf16[3,1024]{1,0:T(4,128)(2,1)S(1)} %slice.196), channel_id=1, source_target_pairs={{0,4},{4,8},{8,12},{12,16},{16,20},{20,24},{24,28},{1,5},{5,9},{9,... | collective-permute-start | bytes 18440 | tf_op jit(solution)/shard_map/ppermute | solution.py:20
  33.3 314.9 %copy-start.79 = (f32[768]{0:T(1024)}, f32[768]{0:T(1024)S(1)}, u32[]{:S(2)}) copy-start(f32[768]{0:T(1024)S(1)} %convert_element_type.313) | copy-start | bytes 9220
  167.5 90.4 %all-gather.20.cloned.1.call-start = ((), (), s32[]{:S(2)}) async-start(), calls=%async_computation.31 | async-start | bytes 2359296 | tf_op jit(solution)/shard_map/all_gather | solution.py:26
  168.3 229.6 %reduce-scatter.26.cloned.1.call-start = ((), (), s32[]{:S(2)}) async-start(), calls=%async_computation.15 | async-start | bytes 3932160 | tf_op jit(solution)/shard_map/reduce_scatter | solution.py:304
  361.4 68.1 %all-gather.12.cloned.1.call-start = ((), (), s32[]{:S(2)}) async-start(), calls=%async_computation.16 | async-start | bytes 3932160 | tf_op jit(solution)/shard_map/all_gather | solution.py:308
  400.8 58.7 %all-gather.14.cloned.1.call-start = ((), (), s32[]{:S(2)}) async-start(), calls=%async_computation.18 | async-start | bytes 3932160 | tf_op jit(solution)/shard_map/all_gather | solution.py:323
  401.4 158.8 %all-reduce.33.cloned.1.call-start = ((), (), s32[]{:S(2)}) async-start(), calls=%async_computation.19 | async-start | bytes 6291456 | tf_op jit(solution)/shard_map/psum | solution.py:333
  491.6 107.9 %all-gather.16.cloned.1.call-start = ((), (), s32[]{:S(2)}) async-start(), calls=%async_computation.20 | async-start | bytes 3932160 | tf_op jit(solution)/shard_map/all_gather | solution.py:341
  570.7 123.3 %all-gather.22.cloned.1.call-start = ((), (), s32[]{:S(2)}) async-start(), calls=%async_computation.32 | async-start | bytes 1179648 | tf_op jit(solution)/shard_map/all_gather | solution.py:26
  571.6 153.0 %all-gather.24.cloned.1.call-start = ((), (), s32[]{:S(2)}) async-start(), calls=%async_computation.33 | async-start | bytes 2359296 | tf_op jit(solution)/shard_map/all_gather | solution.py:26
  675.1 911.0 %reduce-scatter.28.cloned.1.call-start = ((), (), s32[]{:S(2)}) async-start(), calls=%async_computation.17 | async-start | bytes 3932160 | tf_op jit(solution)/shard_map/reduce_scatter | solution.py:319
  694.0 939.3 %reduce-scatter.50.cloned.1.call-start = ((), (), s32[]{:S(2)}) async-start(), calls=%async_computation.36 | async-start | bytes 147456
  1451.0 183.7 %reduce-scatter.52.cloned.1.call-start = ((), (), s32[]{:S(2)}) async-start(), calls=%async_computation.37 | async-start | bytes 147456
  1451.9 186.5 %reduce-scatter.54.cloned.1.call-start = ((), (), s32[]{:S(2)}) async-start(), calls=%async_computation.38 | async-start | bytes 294912
  1452.9 250.2 %reduce-scatter.46.cloned.1.call-start = ((), (), s32[]{:S(2)}) async-start(), calls=%async_computation.34 | async-start | bytes 589824
  1454.1 314.1 %reduce-scatter.48.cloned.1.call-start = ((), (), s32[]{:S(2)}) async-start(), calls=%async_computation.35 | async-start | bytes 589824
  1458.0 421.2 %reduce-scatter.40.cloned.1.call-start = ((), (), s32[]{:S(2)}) async-start(), calls=%async_computation.27 | async-start | bytes 6340608 | tf_op jit(solution)/shard_map/reduce_scatter | solution.py:494
  1467.7 523.3 %reduce-scatter.42.cloned.1.call-start = ((), (), s32[]{:S(2)}) async-start(), calls=%async_computation.28 | async-start | bytes 6340608 | tf_op jit(solution)/shard_map/reduce_scatter | solution.py:497
  1477.4 625.4 %reduce-scatter.44.cloned.1.call-start = ((), (), s32[]{:S(2)}) async-start(), calls=%async_computation.29 | async-start | bytes 6340608 | tf_op jit(solution)/shard_map/reduce_scatter | solution.py:500
  1487.5 685.9 %all-reduce.35.cloned.1.call-start = ((), (), s32[]{:S(2)}) async-start(), calls=%async_computation.21 | async-start | bytes 6291456 | tf_op jit(solution)/shard_map/psum | solution.py:427
  1491.4 28.8 %collective-permute-start.3 = (f32[3,512]{1,0:T(4,128)}, f32[3,512]{1,0:T(4,128)}, u32[]{:S(2)}, u32[]{:S(2)}) collective-permute-start(f32[3,512]{1,0:T(4,128)} %pad_add_fusion.5), channel_id=1, source_target_pairs={{4,0},{8,4},{12,8},{16,12},{20,16},{24,20},{28,24},{5,1},{9,5},{13... | collective-permute-start | bytes 18440 | tf_op jit(solution)/shard_map/ppermute | solution.py:20
  1515.4 6.2 collective-permute-start.4
  1517.3 13.4 collective-permute-start.5
  1548.4 696.2 %reduce-scatter.30.cloned.1.call-start = ((), (), s32[]{:S(2)}) async-start(), calls=%async_computation.22 | async-start | bytes 2359296 | tf_op jit(solution)/shard_map/reduce_scatter | solution.py:464
  1554.5 760.6 %reduce-scatter.32.cloned.1.call-start = ((), (), s32[]{:S(2)}) async-start(), calls=%async_computation.23 | async-start | bytes 2359296 | tf_op jit(solution)/shard_map/reduce_scatter | solution.py:467
  1559.8 846.4 %reduce-scatter.38.cloned.1.call-start = ((), (), s32[]{:S(2)}) async-start(), calls=%async_computation.26 | async-start | bytes 4718592 | tf_op jit(solution)/shard_map/reduce_scatter | solution.py:491
  1568.1 930.0 %reduce-scatter.36.cloned.1.call-start = ((), (), s32[]{:S(2)}) async-start(), calls=%async_computation.25 | async-start | bytes 4718592 | tf_op jit(solution)/shard_map/reduce_scatter | solution.py:473
  1576.2 1013.0 %reduce-scatter.34.cloned.1.call-start = ((), (), s32[]{:S(2)}) async-start(), calls=%async_computation.24 | async-start | bytes 4718592 | tf_op jit(solution)/shard_map/reduce_scatter | solution.py:470
  (366 other events, 3441.6 us)
Sparse Core Ops, SparseCore 0:
  167.7 39.4 all-gather.17
  209.8 48.0 all-gather.19
  361.5 36.4 reduce-scatter.25
  400.9 28.5 all-gather.11
  430.9 28.5 all-gather.13
  491.7 68.4 all-reduce.32
  570.9 28.6 all-gather.15
  602.4 40.1 all-gather.21
  675.3 49.3 all-gather.23
  727.2 36.4 reduce-scatter.27
  1451.1 59.3 reduce-scatter.49
  1514.3 59.8 reduce-scatter.51
  1578.1 60.2 reduce-scatter.53
  1642.1 60.9 reduce-scatter.45
  1707.2 60.8 reduce-scatter.47
  1771.7 107.4 reduce-scatter.39
  1882.7 108.2 reduce-scatter.41
  1994.5 108.2 reduce-scatter.43
  2105.1 68.1 all-reduce.34
  2176.7 67.7 reduce-scatter.29
  2248.1 67.0 reduce-scatter.31
  2318.8 87.4 reduce-scatter.37
  2410.3 87.6 reduce-scatter.35
  2501.5 87.6 reduce-scatter.33
where the time goes:
time: 2620 us; the launch traced here: 2600 us
  waiting for transfers between devices  1170 us (45%)
  matrix products  965 us (37%)
  other arithmetic  198 us (8%)
  local copies, waits for them, and re-layouts  157 us (6%)
  blocking collectives  65.6 us (3%)
    dot_general x698, matrix products, batch_dot(): jnp.einsum(spec, left, right, precision=highest, preferred_element_type=j...  764 us
    dot_general x30, matrix products, dense(): return jnp.dot(left, right, preferred_element_type=jnp.float32)  201 us
    unnamed x29, waiting for transfers between devices  130 us
    reduce_scatter x1, waiting for transfers between devices, shards(): lax.psum_scatter(grad_w_ffn_gate.astype(jnp.bfloat16), 'seq', scatter_dim...  109 us
    reduce_scatter x1, waiting for transfers between devices, shards(): lax.psum_scatter(grad_w_ffn_down.astype(jnp.bfloat16), 'seq', scatter_dim...  109 us
    reduce_scatter x1, waiting for transfers between devices, shards(): lax.psum_scatter(grad_w_ffn_up.astype(jnp.bfloat16), 'seq', scatter_dimen...  109 us
    all_gather x4, waiting for transfers between devices, prefix(): lax.all_gather(part.astype(kind), axis)  109 us
    reduce_scatter x1, waiting for transfers between devices, shards(): lax.psum_scatter(grad_w_gate.astype(jnp.bfloat16), 'seq', scatter_dimensi...  89.7 us
  transfers between devices with their start and end apart: 30, of which 21 were waited for; matrix products, arithmetic and copies ran while one was open for 41% of the time, Pallas kernels for 0%

commit v1 on v0

--- a/solution.py
+++ b/solution.py
@@ -20,28 +20,105 @@
     return lax.ppermute(block, axis, route)
 
 
-def prefix(shard, axis, combine, identity, reverse):
-    devices, place = (lax.axis_size(axis), lax.axis_index(axis))
-    everything = jax.tree.map(
-        lambda part, kind: lax.all_gather(part.astype(kind), axis),
-        shard,
-        (jnp.bfloat16, jnp.bfloat16),
-    )
-    start = jax.tree.map(
-        lambda part, zero: jnp.broadcast_to(jnp.asarray(zero, part.dtype), part.shape),
-        shard,
-        identity,
-    )
-
-    def turn(k, before):
-        at = devices - 1 - k if reverse else k
-        reached = at > place if reverse else at < place
-        new = combine(
-            before, jax.tree.map(lambda part, own: part[at].astype(own.dtype), everything, shard)
+def exchanged(block, axis, bit):
+    route = [(i, i ^ bit) for i in range(lax.axis_size(axis))]
+    return lax.ppermute(block, axis, route)
+
+
+def half(block, axis, at, count):
+    width = block.shape[axis] // count
+    return lax.dynamic_slice_in_dim(block, at * width, width, axis)
+
+
+def head_scattered(partial):
+    place = lax.axis_index("head")
+    core, chip = (place % 2, place // 2)
+    rows, cols = partial.shape
+    parts = partial.reshape(rows, 2, 2, cols // 4)
+    low = jnp.concatenate([parts[:, 0, 0], parts[:, 1, 0]], axis=1)
+    high = jnp.concatenate([parts[:, 0, 1], parts[:, 1, 1]], axis=1)
+    mine = jnp.where(core == 0, low, high)
+    other = jnp.where(core == 0, high, low).astype(jnp.bfloat16)
+    mine = mine.astype(jnp.float32) + exchanged(other, "head", 1).astype(jnp.float32)
+    kept = half(mine, 1, chip, 2)
+    sent = half(mine, 1, 1 - chip, 2).astype(jnp.bfloat16)
+    return kept + exchanged(sent, "head", 2).astype(jnp.float32)
+
+
+def head_gathered(block):
+    place = lax.axis_index("head")
+    core, chip = (place % 2, place // 2)
+    across = exchanged(block, "head", 2)
+    beside = exchanged(block, "head", 1)
+    corner = exchanged(across, "head", 1)
+    low = jnp.where(core == 0, block, beside)
+    high = jnp.where(core == 0, beside, block)
+    far_low = jnp.where(core == 0, across, corner)
+    far_high = jnp.where(core == 0, corner, across)
+    near = jnp.concatenate([low, high], axis=1)
+    far = jnp.concatenate([far_low, far_high], axis=1)
+    return jnp.where(
+        chip == 0,
+        jnp.concatenate([near, far], axis=1),
+        jnp.concatenate([far, near], axis=1),
+    )
+
+
+def head_summed(values):
+    bit = 1
+    while bit < lax.axis_size("head"):
+        values = values + exchanged(values, "head", bit)
+        bit = bit * 2
+    return values
+
+
+def all_summed(values):
+    values = head_summed(values)
+    bit = 1
+    while bit < lax.axis_size("seq"):
+        values = values + exchanged(values, "seq", bit)
+        bit = bit * 2
+    return values
+
+
+def seq_scattered(partial):
+    devices, place = (lax.axis_size("seq"), lax.axis_index("seq"))
+    rows, cols = partial.shape
+    parts = partial.astype(jnp.bfloat16).reshape(devices // 2, 2, rows // devices, cols)
+    odd = place % 2
+    mine = jnp.where(odd == 0, parts[:, 0], parts[:, 1])
+    other = jnp.where(odd == 0, parts[:, 1], parts[:, 0])
+    got = exchanged(other, "seq", 1)
+    mine = (mine.astype(jnp.float32) + got.astype(jnp.float32)).astype(jnp.bfloat16)
+    groups = [list(range(first, devices, 2)) for first in range(2)]
+    return lax.psum_scatter(
+        mine.reshape(rows // 2, cols),
+        "seq",
+        scatter_dimension=0,
+        axis_index_groups=groups,
+        tiled=True,
+    ).astype(jnp.float32)
+
+
+def prefix(linear, offset, direction):
+    linear, offset = shifted(
+        (linear.astype(jnp.bfloat16), offset.astype(jnp.bfloat16)), "seq", direction
+    )
+    offset = offset.astype(jnp.float32)
+    distance = 1
+    while True:
+        last = distance * 2 >= lax.axis_size("seq") - 1
+        sent = (linear, offset.astype(jnp.bfloat16))
+        before_linear, before_offset = shifted(sent, "seq", direction * distance)
+        offset = offset + jnp.einsum(
+            "hij,hjk->hik", linear, before_offset, preferred_element_type=jnp.float32
         )
-        return jax.tree.map(lambda a, b: jnp.where(reached, a, b), new, before)
-
-    return lax.fori_loop(0, devices, turn, start)
+        if last:
+            return offset
+        linear = jnp.einsum(
+            "hij,hjk->hik", linear, before_linear, preferred_element_type=jnp.float32
+        ).astype(jnp.bfloat16)
+        distance = distance * 2
 
 
 def batch_dot(spec, left, right):
@@ -170,13 +247,6 @@
 def gated_norm(delta_out, gate_heads, out_gain):
     scale_row = lax.rsqrt(jnp.mean(delta_out * delta_out, axis=-1, keepdims=True) + epsilon_gate)
     return delta_out * scale_row * out_gain * jax.nn.silu(gate_heads)
-
-
-def affine(earlier, later):
-    return (
-        batch_dot("hij,hjk->hik", later[0], earlier[0]),
-        batch_dot("hij,hjk->hik", later[0], earlier[1]) + later[1],
-    )
 
 
 def with_rim(values, rim_rows):
@@ -234,9 +304,16 @@
     alpha_pre = dense(normed, w_alpha)
     beta_pre = dense(normed, w_beta)
     tail_first = token_rows - (CONV - 1)
-    rim_query, rim_key, rim_value = shifted(
-        (query_pre[tail_first:], key_pre[tail_first:], value_pre[tail_first:]), "seq", 1
-    )
+    key_first = query_pre.shape[1]
+    value_first = key_first + key_pre.shape[1]
+    rims = shifted(
+        jnp.concatenate([query_pre[tail_first:], key_pre[tail_first:], value_pre[tail_first:]], 1),
+        "seq",
+        1,
+    )
+    rim_query = rims[:, :key_first]
+    rim_key = rims[:, key_first:value_first]
+    rim_value = rims[:, value_first:]
     ext_query = jnp.concatenate([rim_query, query_pre]).astype(jnp.float32)
     ext_key = jnp.concatenate([rim_key, key_pre]).astype(jnp.float32)
     ext_value = jnp.concatenate([rim_value, value_pre]).astype(jnp.float32)
@@ -283,9 +360,7 @@
     (device_linear, device_offset), _ = lax.scan(
         compose, (start_linear, start_offset), (group_linear, group_offset, keep_flags)
     )
-    _, entry_state = prefix(
-        (device_linear, device_offset), "seq", affine, (start_linear, start_offset), False
-    )
+    entry_state = prefix(device_linear, device_offset, 1)
 
     def advance(state, block):
         block_linear, block_offset, keep_flag = block
@@ -301,13 +376,9 @@
     gate_heads = gate_pre.reshape(token_rows, head_count, DV)
     gated_f, gated_pull = jax.vjp(gated_norm, delta_out, gate_heads, out_gain)
     gated = gated_f.astype(jnp.bfloat16).reshape(token_rows, head_count * DV)
-    mixed = lax.psum_scatter(
-        dense(gated, w_out).astype(jnp.bfloat16), "head", scatter_dimension=1, tiled=True
-    ).astype(jnp.float32)
+    mixed = head_scattered(dense(gated, w_out))
     middle = lax.dynamic_slice_in_dim(inputs32, col_first, col_width, 1) + mixed
-    sent = lax.all_gather(middle.astype(jnp.bfloat16), "head", axis=1, tiled=True).astype(
-        jnp.float32
-    )
+    sent = head_gathered(middle.astype(jnp.bfloat16)).astype(jnp.float32)
     ffn_scale = lax.rsqrt(jnp.mean(sent * sent, axis=-1, keepdims=True) + epsilon_norm)
     ffn_hat = sent * ffn_scale
     normed_ffn = (ffn_hat * ffn_gain).astype(jnp.bfloat16)
@@ -316,30 +387,28 @@
     sigmoid_gate = jax.nn.sigmoid(ffn_gate_pre)
     silu_gate = ffn_gate_pre * sigmoid_gate
     inner_act = (silu_gate * ffn_up_pre).astype(jnp.bfloat16)
-    ffn_out = lax.psum_scatter(
-        dense(inner_act, w_ffn_down).astype(jnp.bfloat16), "head", scatter_dimension=1, tiled=True
-    ).astype(jnp.float32)
+    ffn_out = head_scattered(dense(inner_act, w_ffn_down))
     hidden_out = (middle + ffn_out).astype(jnp.bfloat16)
-    grad_rows = lax.all_gather(grad_out, "head", axis=1, tiled=True)
+    grad_rows = head_gathered(grad_out)
     d_inner = dense(grad_rows, w_ffn_down.T)
-    grad_w_ffn_down = dense(inner_act.T, grad_rows)
+    grad_w_ffn_down = seq_scattered(dense(grad_rows.T, inner_act))
     d_ffn_gate = (
         d_inner * ffn_up_pre * sigmoid_gate * (1.0 + ffn_gate_pre * (1.0 - sigmoid_gate))
     ).astype(jnp.bfloat16)
     d_ffn_up = (d_inner * silu_gate).astype(jnp.bfloat16)
-    grad_w_ffn_gate = dense(normed_ffn.T, d_ffn_gate)
-    grad_w_ffn_up = dense(normed_ffn.T, d_ffn_up)
+    grad_w_ffn_gate = seq_scattered(dense(normed_ffn.T, d_ffn_gate))
+    grad_w_ffn_up = seq_scattered(dense(normed_ffn.T, d_ffn_up))
     d_normed_ffn = dense(d_ffn_gate, w_ffn_gate.T) + dense(d_ffn_up, w_ffn_up.T)
-    d_normed_ffn = lax.psum(d_normed_ffn.astype(jnp.bfloat16), "head").astype(jnp.float32)
-    grad_ffn_gain = jnp.sum(d_normed_ffn * ffn_hat, axis=0)
-    scaled_ffn = ffn_gain * d_normed_ffn
-    d_sent = ffn_scale * (
-        scaled_ffn - ffn_hat * jnp.mean(ffn_hat * scaled_ffn, axis=-1, keepdims=True)
-    )
-    d_sent_cols = lax.dynamic_slice_in_dim(d_sent, col_first, col_width, 1)
+    weighted_ffn = d_normed_ffn * ffn_hat
+    grad_ffn_gain = jnp.sum(weighted_ffn, axis=0)
+    ffn_dots = head_summed(jnp.mean(weighted_ffn * ffn_gain, axis=-1))[:, None]
+    cols = lambda rows: lax.dynamic_slice_in_dim(rows, col_first, col_width, rows.ndim - 1)
+    d_sent_cols = ffn_scale * (
+        cols(ffn_gain) * head_scattered(d_normed_ffn) - cols(ffn_hat) * ffn_dots
+    )
     d_middle = grad_out.astype(jnp.float32) + d_sent_cols
-    d_mixed = lax.all_gather(d_middle.astype(jnp.bfloat16), "head", axis=1, tiled=True)
-    grad_w_out = dense(gated.T, d_mixed)
+    d_mixed = head_gathered(d_middle.astype(jnp.bfloat16))
+    grad_w_out = seq_scattered(dense(d_mixed.T, gated))
     d_gated = dense(d_mixed, w_out.T).reshape(token_rows, head_count, DV)
     d_delta, d_gate_heads, grad_gain_part = gated_pull(d_gated)
     d_delta = d_delta * valid_mask[:, None, None]
@@ -351,44 +420,23 @@
 
     def collect_back(carry, block):
         block_linear, block_grad, keep_flag = block
-        return (keep_flag * (block_grad + batch_dot("hji,hjk->hik", block_linear, carry)), None)
+        return (keep_flag * (block_grad + batch_dot("hji,hjk->hik", block_linear, carry)), carry)
 
     entry_grad, _ = lax.scan(
         collect_back, start_offset, (group_linear, local_grad, keep_flags), reverse=True
     )
-    _, exit_grad = prefix(
-        (jnp.swapaxes(device_linear, 1, 2), entry_grad),
-        "seq",
-        affine,
-        (start_linear, start_offset),
-        True,
-    )
-
-    def group_back(carry, block):
-        query_c, key_c, value_c, decay_c, beta_c, used, keep_flag, d_out_c = block
-
-        def group_fn(query_c, key_c, value_c, decay_c, beta_c, used):
-            return group_output(used, prepare(query_c, key_c, value_c, decay_c, beta_c))
-
-        _, pullback = jax.vjp(group_fn, query_c, key_c, value_c, decay_c, beta_c, used)
-        d_query_c, d_key_c, d_value_c, d_decay_c, d_beta_c, d_used = pullback((d_out_c, carry))
-        return (keep_flag * d_used, (d_query_c, d_key_c, d_value_c, d_decay_c, d_beta_c))
-
-    _, block_grads = lax.scan(
-        group_back,
-        exit_grad,
-        (
-            blocks_query,
-            blocks_key,
-            blocks_value,
-            blocks_decay,
-            blocks_beta,
-            used_states,
-            keep_flags,
-            d_blocks,
-        ),
-        reverse=True,
-    )
+    exit_grad = prefix(jnp.swapaxes(device_linear, 1, 2), entry_grad, -1)
+    _, after_grads = lax.scan(
+        collect_back, exit_grad, (group_linear, local_grad, keep_flags), reverse=True
+    )
+
+    def group_fn(query_c, key_c, value_c, decay_c, beta_c):
+        return group_output(used_states, prepare(query_c, key_c, value_c, decay_c, beta_c))
+
+    _, pullback = jax.vjp(
+        group_fn, blocks_query, blocks_key, blocks_value, blocks_decay, blocks_beta
+    )
+    block_grads = pullback((d_blocks, after_grads))
     d_query, d_key, d_value, d_decay, d_beta = [from_blocks(piece) for piece in block_grads]
     (
         d_ext_query,
@@ -402,20 +450,48 @@
         grad_log_local,
         grad_bias_local,
     ) = feature_pull((d_query, d_key, d_value, d_decay, d_beta))
-    back_query, back_key, back_value = shifted(
-        (d_ext_query[: CONV - 1], d_ext_key[: CONV - 1], d_ext_value[: CONV - 1]), "seq", -1
-    )
+    backs = shifted(
+        jnp.concatenate(
+            [d_ext_query[: CONV - 1], d_ext_key[: CONV - 1], d_ext_value[: CONV - 1]], 1
+        ),
+        "seq",
+        -1,
+    )
+    back_query = backs[:, :key_first]
+    back_key = backs[:, key_first:value_first]
+    back_value = backs[:, value_first:]
     d_query_pre = with_rim(d_ext_query[CONV - 1 :], back_query).astype(jnp.bfloat16)
     d_key_pre = with_rim(d_ext_key[CONV - 1 :], back_key).astype(jnp.bfloat16)
     d_value_pre = with_rim(d_ext_value[CONV - 1 :], back_value).astype(jnp.bfloat16)
     d_alpha = d_alpha.astype(jnp.bfloat16)
     d_beta_pre = d_beta_pre.astype(jnp.bfloat16)
-    grad_w_query = dense(normed.T, d_query_pre)
-    grad_w_key = dense(normed.T, d_key_pre)
-    grad_w_value = dense(normed.T, d_value_pre)
-    grad_w_gate = dense(normed.T, d_gate_pre)
+    grad_w_gate = seq_scattered(dense(normed.T, d_gate_pre))
+    grad_w_query = seq_scattered(dense(normed.T, d_query_pre))
+    grad_w_key = seq_scattered(dense(normed.T, d_key_pre))
+    grad_w_value = seq_scattered(dense(normed.T, d_value_pre))
     grad_w_alpha = dense(normed.T, d_alpha)
     grad_w_beta = dense(normed.T, d_beta_pre)
+    devices = lax.axis_size("seq")
+    small = jnp.concatenate(
+        [grad_w_alpha.reshape(devices, -1), grad_w_beta.reshape(devices, -1)]
+        + [
+            jnp.swapaxes(piece.reshape(CONV, devices, -1), 0, 1).reshape(devices, -1)
+            for piece in (grad_conv_query, grad_conv_key, grad_conv_value)
+        ],
+        axis=1,
+    )
+    small_width = small.shape[1]
+    small = seq_scattered(small.reshape(devices * small_width // 128, 128)).reshape(small_width)
+    small_pieces = []
+    for rows, width in [
+        (normed.shape[1] // devices, head_count),
+        (normed.shape[1] // devices, head_count),
+        (CONV, grad_conv_query.shape[1] // devices),
+        (CONV, grad_conv_key.shape[1] // devices),
+        (CONV, grad_conv_value.shape[1] // devices),
+    ]:
+        small_pieces.append(small[: rows * width].reshape(rows, width))
+        small = small[rows * width :]
     d_normed = (
         dense(d_query_pre, w_query.T)
         + dense(d_key_pre, w_key.T)
@@ -424,13 +500,12 @@
         + dense(d_alpha, w_alpha.T)
         + dense(d_beta_pre, w_beta.T)
     )
-    d_normed = lax.psum(d_normed.astype(jnp.bfloat16), "head").astype(jnp.float32)
-    grad_attn_gain = jnp.sum(d_normed * attn_hat, axis=0)
-    scaled_attn = attn_gain * d_normed
-    d_inputs = attn_scale * (
-        scaled_attn - attn_hat * jnp.mean(attn_hat * scaled_attn, axis=-1, keepdims=True)
-    )
-    d_input_cols = lax.dynamic_slice_in_dim(d_inputs, col_first, col_width, 1)
+    weighted_attn = d_normed * attn_hat
+    grad_attn_gain = jnp.sum(weighted_attn, axis=0)
+    attn_dots = head_summed(jnp.mean(weighted_attn * attn_gain, axis=-1))[:, None]
+    d_input_cols = attn_scale * (
+        cols(attn_gain) * head_scattered(d_normed) - cols(attn_hat) * attn_dots
+    )
     grad_in = d_middle + d_input_cols
     full_log = lax.dynamic_update_slice_in_dim(
         jnp.zeros(decay_log.shape, jnp.float32), grad_log_local, head_first, 0
@@ -438,93 +513,31 @@
     full_bias = lax.dynamic_update_slice_in_dim(
         jnp.zeros(decay_bias.shape, jnp.float32), grad_bias_local, head_first, 0
     )
-    grad_decay_log, grad_decay_bias, grad_out_gain = lax.psum(
-        (full_log, full_bias, grad_gain_part), ("seq", "head")
-    )
-    (
-        s_attn_gain,
-        s_query,
-        s_key,
-        s_value,
-        s_gate,
-        s_alpha,
-        s_beta,
-        s_conv_query,
-        s_conv_key,
-        s_conv_value,
-        s_out,
-        s_ffn_gate,
-        s_ffn_up,
-        s_ffn_down,
-        s_ffn_gain,
-    ) = (
-        lax.psum_scatter(
-            grad_attn_gain.astype(jnp.bfloat16), "seq", scatter_dimension=0, tiled=True
-        ).astype(jnp.float32),
-        lax.psum_scatter(
-            grad_w_query.astype(jnp.bfloat16), "seq", scatter_dimension=0, tiled=True
-        ).astype(jnp.float32),
-        lax.psum_scatter(
-            grad_w_key.astype(jnp.bfloat16), "seq", scatter_dimension=0, tiled=True
-        ).astype(jnp.float32),
-        lax.psum_scatter(
-            grad_w_value.astype(jnp.bfloat16), "seq", scatter_dimension=0, tiled=True
-        ).astype(jnp.float32),
-        lax.psum_scatter(
-            grad_w_gate.astype(jnp.bfloat16), "seq", scatter_dimension=0, tiled=True
-        ).astype(jnp.float32),
-        lax.psum_scatter(
-            grad_w_alpha.astype(jnp.bfloat16), "seq", scatter_dimension=0, tiled=True
-        ).astype(jnp.float32),
-        lax.psum_scatter(
-            grad_w_beta.astype(jnp.bfloat16), "seq", scatter_dimension=0, tiled=True
-        ).astype(jnp.float32),
-        lax.psum_scatter(
-            grad_conv_query.astype(jnp.bfloat16), "seq", scatter_dimension=1, tiled=True
-        ).astype(jnp.float32),
-        lax.psum_scatter(
-            grad_conv_key.astype(jnp.bfloat16), "seq", scatter_dimension=1, tiled=True
-        ).astype(jnp.float32),
-        lax.psum_scatter(
-            grad_conv_value.astype(jnp.bfloat16), "seq", scatter_dimension=1, tiled=True
-        ).astype(jnp.float32),
-        lax.psum_scatter(
-            grad_w_out.astype(jnp.bfloat16), "seq", scatter_dimension=1, tiled=True
-        ).astype(jnp.float32),
-        lax.psum_scatter(
-            grad_w_ffn_gate.astype(jnp.bfloat16), "seq", scatter_dimension=0, tiled=True
-        ).astype(jnp.float32),
-        lax.psum_scatter(
-            grad_w_ffn_up.astype(jnp.bfloat16), "seq", scatter_dimension=0, tiled=True
-        ).astype(jnp.float32),
-        lax.psum_scatter(
-            grad_w_ffn_down.astype(jnp.bfloat16), "seq", scatter_dimension=1, tiled=True
-        ).astype(jnp.float32),
-        lax.psum_scatter(
-            grad_ffn_gain.astype(jnp.bfloat16), "seq", scatter_dimension=0, tiled=True
-        ).astype(jnp.float32),
-    )
+    sums = all_summed(
+        jnp.concatenate([grad_gain_part, grad_ffn_gain, grad_attn_gain, full_log, full_bias])
+    )
+    gain_first = out_gain.shape[0]
+    attn_first = gain_first + ffn_gain.shape[0]
+    log_first = attn_first + attn_gain.shape[0]
+    bias_first = log_first + decay_log.shape[0]
+    rows_of = lambda whole: half(whole, 0, lax.axis_index("seq"), devices)
     return (
         hidden_out,
         grad_in,
-        s_attn_gain,
-        s_query,
-        s_key,
-        s_value,
-        s_gate,
-        s_alpha,
-        s_beta,
-        s_conv_query,
-        s_conv_key,
-        s_conv_value,
-        grad_decay_log,
-        grad_decay_bias,
-        grad_out_gain,
-        s_out,
-        s_ffn_gain,
-        s_ffn_gate,
-        s_ffn_up,
-        s_ffn_down,
+        rows_of(sums[attn_first:log_first]),
+        grad_w_query,
+        grad_w_key,
+        grad_w_value,
+        grad_w_gate,
+        *small_pieces,
+        sums[log_first:bias_first],
+        sums[bias_first:],
+        sums[:gain_first],
+        grad_w_out.T,
+        rows_of(sums[gain_first:attn_first]),
+        grad_w_ffn_gate,
+        grad_w_ffn_up,
+        grad_w_ffn_down.T,
     )
 
 

time: 2620 us -> 1550 us (0.59)
  waiting for transfers between devices: 1170 us -> 375 us
  matrix products: 965 us -> 553 us
  local copies, waits for them, and re-layouts: 157 us -> 311 us
  blocking collectives: 65.6 us -> 0 us
  starting transfers between devices: 18.4 us -> 70.3 us
    reduce_scatter x10 -> x8, waiting for transfers between devices: 732 us -> 0.01 us  [seq_scattered(): lax.psum_scatter(mine.reshape(rows // 2, cols), 'seq', scatter_dimension=...]
    dot_general x698 -> x115, matrix products: 764 us -> 370 us  [batch_dot(): jnp.einsum(spec, left, right, precision=highest, preferred_element_type=j...]
    ppermute x0 -> x35, waiting for transfers between devices: none -> 340 us  [exchanged(): return lax.ppermute(block, axis, route)]
    all_gather x7 -> x0, waiting for transfers between devices: 168 us -> none  [the longest x4 109 us: prefix(): lax.all_gather(part.astype(kind), axis)]
    psum x2 -> x0, waiting for transfers between devices: 137 us -> none  [the longest x1 68.5 us: shards(): lax.psum(d_normed_ffn.astype(jnp.bfloat16), 'head').astype(jnp.float32)]
    unnamed x29 -> x10, waiting for transfers between devices: 130 us -> 0.15 us
    reshape x0 -> x14, local copies, waits for them, and re-layouts: none -> 48.6 us  [the longest x3 41.1 us: seq_scattered(): partial.astype(jnp.bfloat16).reshape(devices // 2, 2, rows // devices, cols)]
    psum x1 -> x0, blocking collectives: 43.9 us -> none  [shards(): lax.psum((full_log, full_bias, grad_gain_part), ('seq', 'head'))]
  transfers between devices with their start and end apart: 30 -> 60, of which waited for: 21 -> 25; matrix products, arithmetic and copies ran while one was open for 41% -> 30% of each run, Pallas kernels for 0% -> 0%
where the time goes in v1:
time: 1550 us; the launch traced here: 1530 us
  matrix products  553 us (36%)
  waiting for transfers between devices  375 us (24%)
  local copies, waits for them, and re-layouts  311 us (20%)
  other arithmetic  205 us (13%)
  starting transfers between devices  70.3 us (5%)
  between operations  18.2 us (1%)
    dot_general x115, matrix products, batch_dot(): jnp.einsum(spec, left, right, precision=highest, preferred_element_type=j...  370 us
    ppermute x35, waiting for transfers between devices, exchanged(): return lax.ppermute(block, axis, route)  340 us
    dot_general x30, matrix products, dense(): return jnp.dot(left, right, preferred_element_type=jnp.float32)  175 us
    unnamed x579, local copies, waits for them, and re-layouts  75.2 us
    reshape x3, local copies, waits for them, and re-layouts, seq_scattered(): partial.astype(jnp.bfloat16).reshape(devices // 2, 2, rows // devices, cols)  41.1 us
    ppermute x16, starting transfers between devices, shifted(): return lax.ppermute(block, axis, route)  40 us
    convert_element_type x9, other arithmetic, seq_scattered(): (mine.astype(jnp.float32) + got.astype(jnp.float32)).astype(jnp.bfloat16)  36.3 us
    slice x3, local copies, waits for them, and re-layouts, seq_scattered(): mine = jnp.where(odd == 0, parts[:, 0], parts[:, 1])  36.2 us
  transfers between devices with their start and end apart: 60, of which 25 were waited for; matrix products, arithmetic and copies ran while one was open for 30% of the time, Pallas kernels for 0%

profile of v1, /device:TPU:0, one launch (start us, length us, event | category | flops | bytes accessed | tf_op | source)
XLA Modules:
  0.0 1534.2 jit_solution(6992093921617511982)
XLA Ops:
  146.7 69.4 %while.58 = (s32[]{:T(128)}, f32[4,128,128]{2,1,0:T(8,128)}, f32[4,128,256]{2,1,0:T(8,128)S(1)}, f32[12,4,128,128]{3,2,1,0:T(8,128)}, f32[12]{0:T(128)S(1)}, /*i...) while((s32[]{:T(128)}, f32[4,128,128]{2,1,0:T(8,128)}, f32[4,128,256]{2,1,0:T(8,128)S(1)}, ...), condition=%wide.region_8.9_spmd.clone, body=%wide.region_7.8_spmd.clone.sunk | while | flops 302448640 | bytes 5245575 | solution.py:360
  269.7 54.4 %while.56 = (s32[]{:T(128)}, f32[4,128,256]{2,1,0:T(8,128)S(1)}, f32[12,4,128,256]{3,2,1,0:T(8,128)}, f32[12,4,128,128]{3,2,1,0:T(8,128)}, f32[12]{0:T(128)S(1)}, /*index=5*/f32[12,4,128,256]{3,2,1,0:T(8,128)}, s32[]{:T(128)}) while((s32[]{:T(128)}, f32[4,128,256]{2,1,0:T(8,128)S(1)}, f32[12,4,128,256]{3,2,1,0:T(8,128)}, ...), condition=%wide.region_10.11_spmd, body=%wide.region_9.10_spmd.sunk | while | flops 201719808 | bytes 3934809 | solution.py:370
  385.9 12.2 collective-permute-done.9
  402.9 12.1 collective-permute-done.16
  415.5 15.5 %collective-permute-done.11 = bf16[768,512]{0,1:T(8,128)(2,1)} collective-permute-done((bf16[768,512]{0,1:T(8,128)(2,1)}, bf16[768,512]{0,1:T(8,128)(2,1)}, u32[]{:S(2)}, u32[]{:S(2)}) %collective-permute-start.11) | collective-permute-done | bytes 786464 | tf_op jit(solution)/shard_map/ppermute | solution.py:25
  452.6 11.3 multiply_convert_fusion.2
  463.8 12.2 fusion.283
  476.0 11.1 multiply_reduce_fusion.12
  495.7 16.6 %collective-permute-done.21 = f32[768]{0:T(1024)S(1)} collective-permute-done((f32[768]{0:T(1024)S(1)}, f32[768]{0:T(1024)S(1)}, u32[]{:S(2)}, u32[]{:S(2)}) %collective-permute-start.21) | collective-permute-done | bytes 3104 | tf_op jit(solution)/shard_map/ppermute | solution.py:25
  538.9 10.4 convolution_convert_fusion
  549.3 13.7 reshape.648
  603.3 36.4 %while.59 = (s32[]{:T(128)}, f32[4,128,256]{2,1,0:T(8,128)S(1)}, f32[12]{0:T(128)S(1)}, f32[12,4,128,256]{3,2,1,0:T(8,128)}, f32[12,4,128,128]{2,3,1,0:T(8,128)}, /*index=5*/s32[]{:T(128)}, s32[]{:T(128)}, s32[]{:T(128)}) while((s32[]{:T(128)}, f32[4,128,256]{2,1,0:T(8,128)S(1)}, f32[12]{0:T(128)S(1)}, ...), condition=%wide.region_17.18_spmd.clone, body=%wide.region_16.17_spmd.clone.sunk | while | flops 201719808 | bytes 2885750 | solution.py:425
  641.0 12.7 fusion.262
  655.2 9.8 fusion.65
  685.6 12.0 collective-permute-done.31
  703.3 46.2 %while.57 = (s32[]{:T(128)}, f32[4,128,256]{2,1,0:T(8,128)S(1)}, f32[12,4,128,256]{3,2,1,0:T(8,128)}, f32[12]{0:T(128)S(1)}, f32[12,4,128,256]{3,2,1,0:T(8,128)}...) while((s32[]{:T(128)}, f32[4,128,256]{2,1,0:T(8,128)S(1)}, f32[12,4,128,256]{3,2,1,0:T(8,128)}, ...), condition=%wide.region_19.20_spmd, body=%wide.region_18.19_spmd.sunk | while | flops 201588736 | bytes 3933809 | solution.py:429
  755.8 9.3 fusion.47
  843.7 11.9 fusion.70
  962.1 19.5 %collective-permute-done.46 = bf16[4,24,128]{2,1,0:T(8,128)(2,1)S(1)} collective-permute-done((bf16[4,24,128]{2,1,0:T(8,128)(2,1)S(1)}, bf16[4,24,128]{2,1,0:T(8,128)(2,1)S(1)}, u32[]{:S(2)}, u32[]{:S(2)}) %collective-permute-start.46) | collective-permute-done | bytes 24608 | tf_op jit(solution)/shard_map/ppermute | solution.py:25
  993.5 68.1 %collective-permute-done.42 = bf16[4,256,512]{2,1,0:T(8,128)(2,1)S(1)} collective-permute-done((bf16[4,256,512]{2,1,0:T(8,128)(2,1)S(1)}, bf16[4,256,512]{2,1,0:T(8,128)(2,1)S(1)}, u32[]{:S(2)}, u32[]{:S(2)}) %collective-permute-start.42) | collective-permute-done | bytes 1048608 | tf_op jit(solution)/shard_map/ppermute | solution.py:25
  1063.3 9.6 convolution_convert_fusion.1
  1072.9 13.7 reshape.646
  1100.5 11.9 fusion.263
  1127.1 13.7 reshape.644
  1140.8 38.4 %collective-permute-done.49 = bf16[4,256,1376]{1,2,0:T(8,128)(2,1)} collective-permute-done((bf16[4,256,1376]{1,2,0:T(8,128)(2,1)}, bf16[4,256,1376]{1,2,0:T(8,128)(2,1)}, u32[]{:S(2)}, u32[]{:S(2)}) %collective-permute-start.49) | collective-permute-done | bytes 2818080 | tf_op jit(solution)/shard_map/ppermute | solution.py:25
  1192.7 11.6 fusion.264
  1207.5 57.8 %collective-permute-done.48 = bf16[4,256,1376]{1,2,0:T(8,128)(2,1)S(1)} collective-permute-done((bf16[4,256,1376]{1,2,0:T(8,128)(2,1)S(1)}, bf16[4,256,1376]{1,2,0:T(8,128)(2,1)S(1)}, u32[]{:S(2)}, u32[]{:S(2)}) %collective-permute-start.48) | collective-permute-done | bytes 2818080 | tf_op jit(solution)/shard_map/ppermute | solution.py:25
  1281.9 41.7 %collective-permute-done.47 = bf16[4,256,1024]{2,1,0:T(8,128)(2,1)S(1)} collective-permute-done((bf16[4,256,1024]{2,1,0:T(8,128)(2,1)S(1)}, bf16[4,256,1024]{2,1,0:T(8,128)(2,1)S(1)}, u32[]{:S(2)}, u32[]{:S(2)}) %collective-permute-start.47) | collective-permute-done | bytes 2097184 | tf_op jit(solution)/shard_map/ppermute | solution.py:25
  1367.7 21.3 %collective-permute-done.45 = bf16[4,256,1024]{2,1,0:T(8,128)(2,1)S(1)} collective-permute-done((bf16[4,256,1024]{2,1,0:T(8,128)(2,1)S(1)}, bf16[4,256,1024]{2,1,0:T(8,128)(2,1)S(1)}, u32[]{:S(2)}, u32[]{:S(2)}) %collective-permute-start.45) | collective-permute-done | bytes 2097184 | tf_op jit(solution)/shard_map/ppermute | solution.py:25
  1411.1 16.7 %multiply_reduce_fusion.11 = (f32[2048]{0:T(1024)S(1)}, f32[768]{0:T(1024)S(1)}, f32[768,2048]{0,1:T(8,128)}, f32[768,2048]{0,1:T(8,128)}) fusion(f32[768]{0:T(1024)S(1)} %copy-done.200, bf16[768,2048]{0,1:T(8,128)(2,1)S(1)} %copy-done.16, f32[2048]{0:T(1024)S(1)} %copy-done.209, bf16[768,4]{0,1:T(4,128)(2,1)S(1)} %copy-done.206, ...), kind=kOutput, calls=%fused_computation.140 | convolution fusion | flops 29881600 | bytes 47230976 | tf_op jit(solution)/shard_map/dot_general | solution.py:259
  1456.0 14.9 collective-permute-done.38
  1493.7 9.2 collective-permute-done.34
  (1245 shorter events, 995.5 us)
Async XLA Ops:
  7.2 1478.4 %reduce-scatter.28.cloned.1.call-start = ((), (), s32[]{:S(2)}) async-start(), calls=%async_computation.17 | async-start | bytes 30720
  25.9 24.8 %collective-permute-start = (bf16[3,2048]{1,0:T(4,128)(2,1)}, bf16[3,2048]{1,0:T(4,128)(2,1)}, u32[]{:S(2)}, u32[]{:S(2)}) collective-permute-start(bf16[3,2048]{1,0:T(4,128)(2,1)} %pad_maximum_fusion.18), channel_id=1, source_target_pairs={{0,4},{4,8},{8,12},{12,16},{16,20},{20,24},{24,28},{1,5},{5,9},{9,... | collective-permute-start | bytes 36872 | tf_op jit(solution)/shard_map/ppermute | solution.py:20
  377.4 20.7 %collective-permute-start.9 = (bf16[768,512]{0,1:T(8,128)(2,1)}, bf16[768,512]{0,1:T(8,128)(2,1)}, u32[]{:S(2)}, u32[]{:S(2)}) collective-permute-start(bf16[768,512]{0,1:T(8,128)(2,1)} %dynamic-slice_convert_fusion.3), channel_id=1, source_target_pairs={{0,2},{1,3},{2,0},{3,1},{4,6},{5,7},{6,4},{7,5},{8,10},{9,11},{10,... | collective-permute-start | bytes 2359304 | tf_op jit(solution)/shard_map/ppermute | solution.py:25
  380.3 34.7 %collective-permute-start.16 = (bf16[768,512]{0,1:T(8,128)(2,1)S(1)}, bf16[768,512]{0,1:T(8,128)(2,1)}, u32[]{:S(2)}, u32[]{:S(2)}) collective-permute-start(bf16[768,512]{0,1:T(8,128)(2,1)S(1)} %copy.894), channel_id=1, source_target_pairs={{0,2},{1,3},{2,0},{3,1},{4,6},{5,7},{6,4},{7,5},{8,10},{9,11},{10,... | collective-permute-start | bytes 2359304 | tf_op jit(solution)/shard_map/ppermute | solution.py:25
  401.4 29.7 %collective-permute-start.11 = (bf16[768,512]{0,1:T(8,128)(2,1)}, bf16[768,512]{0,1:T(8,128)(2,1)}, u32[]{:S(2)}, u32[]{:S(2)}) collective-permute-start(bf16[768,512]{0,1:T(8,128)(2,1)} %fusion.199), channel_id=1, source_target_pairs={{0,2},{1,3},{2,0},{3,1},{4,6},{5,7},{6,4},{7,5},{8,10},{9,11},{10,... | collective-permute-start | bytes 2359304 | tf_op jit(solution)/shard_map/ppermute | solution.py:25
  402.9 28.2 %collective-permute-start.15 = (bf16[768,512]{0,1:T(8,128)(2,1)S(1)}, bf16[768,512]{0,1:T(8,128)(2,1)}, u32[]{:S(2)}, u32[]{:S(2)}) collective-permute-start(bf16[768,512]{0,1:T(8,128)(2,1)S(1)} %copy.894), channel_id=1, source_target_pairs={{0,1},{1,0},{2,3},{3,2},{4,5},{5,4},{6,7},{7,6},{8,9},{9,8},{10,11... | collective-permute-start | bytes 2359304 | tf_op jit(solution)/shard_map/ppermute | solution.py:25
  492.3 20.0 %collective-permute-start.19 = (bf16[768,512]{0,1:T(8,128)(2,1)S(1)}, bf16[768,512]{0,1:T(8,128)(2,1)S(1)}, u32[]{:S(2)}, u32[]{:S(2)}) collective-permute-start(bf16[768,512]{0,1:T(8,128)(2,1)S(1)} %dynamic-slice_convert_fusion.1), channel_id=1, source_target_pairs={{0,2},{1,3},{2,0},{3,1},{4,6},{5,7},{6,4},{7,5},{8,10},{9,11},{10,... | collective-permute-start | bytes 2359304 | tf_op jit(solution)/shard_map/ppermute | solution.py:25
  514.3 24.1 %collective-permute-start.23 = (bf16[768,512]{0,1:T(8,128)(2,1)}, bf16[768,512]{0,1:T(8,128)(2,1)}, u32[]{:S(2)}, u32[]{:S(2)}) collective-permute-start(bf16[768,512]{0,1:T(8,128)(2,1)} %get-tuple-element.651), channel_id=1, source_target_pairs={{0,2},{1,3},{2,0},{3,1},{4,6},{5,7},{6,4},{7,5},{8,10},{9,11},{10,... | collective-permute-start | bytes 2359304 | tf_op jit(solution)/shard_map/ppermute | solution.py:25
  531.7 153.9 %collective-permute-start.30 = (bf16[4,128,128]{2,1,0:T(8,128)(2,1)}, bf16[4,128,128]{2,1,0:T(8,128)(2,1)}, u32[]{:S(2)}, u32[]{:S(2)}) collective-permute-start(bf16[4,128,128]{2,1,0:T(8,128)(2,1)} %convolution_convert_fusion.14), channel_id=1, source_target_pairs={{8,0},{12,4},{16,8},{20,12},{24,16},{28,20},{9,1},{13,5},{17,9},{2... | collective-permute-start | bytes 393224 | tf_op jit(solution)/shard_map/ppermute | solution.py:20
  538.4 24.6 %collective-permute-start.22 = (bf16[768,512]{0,1:T(8,128)(2,1)}, bf16[768,512]{0,1:T(8,128)(2,1)}, u32[]{:S(2)}, u32[]{:S(2)}) collective-permute-start(bf16[768,512]{0,1:T(8,128)(2,1)} %get-tuple-element.651), channel_id=1, source_target_pairs={{0,1},{1,0},{2,3},{3,2},{4,5},{5,4},{6,7},{7,6},{8,9},{9,8},{10,11... | collective-permute-start | bytes 2359304 | tf_op jit(solution)/shard_map/ppermute | solution.py:25
  538.4 26.2 %collective-permute-start.24 = (bf16[768,512]{0,1:T(8,128)(2,1)}, bf16[768,512]{0,1:T(8,128)(2,1)}, u32[]{:S(2)}, u32[]{:S(2)}) collective-permute-start(bf16[768,512]{0,1:T(8,128)(2,1)} %collective-permute-done.23), channel_id=1, source_target_pairs={{0,1},{1,0},{2,3},{3,2},{4,5},{5,4},{6,7},{7,6},{8,9},{9,8},{10,11... | collective-permute-start | bytes 2359304 | tf_op jit(solution)/shard_map/ppermute | solution.py:25
  954.5 27.8 %collective-permute-start.43 = (bf16[4,256,512]{2,1,0:T(8,128)(2,1)}, bf16[4,256,512]{2,1,0:T(8,128)(2,1)S(1)}, u32[]{:S(2)}, u32[]{:S(2)}) collective-permute-start(bf16[4,256,512]{2,1,0:T(8,128)(2,1)} %select_bitcast_fusion.5), channel_id=1, source_target_pairs={{0,4},{4,0},{8,12},{12,8},{16,20},{20,16},{24,28},{28,24},{1,5},{5... | collective-permute-start | bytes 3145736 | tf_op jit(solution)/shard_map/ppermute | solution.py:25
  956.8 24.8 %collective-permute-start.46 = (bf16[4,24,128]{2,1,0:T(8,128)(2,1)S(1)}, bf16[4,24,128]{2,1,0:T(8,128)(2,1)S(1)}, u32[]{:S(2)}, u32[]{:S(2)}) collective-permute-start(bf16[4,24,128]{2,1,0:T(8,128)(2,1)S(1)} %fusion.197), channel_id=1, source_target_pairs={{0,4},{4,0},{8,12},{12,8},{16,20},{20,16},{24,28},{28,24},{1,5},{5... | collective-permute-start | bytes 73736 | tf_op jit(solution)/shard_map/ppermute | solution.py:25
  960.2 126.4 %collective-permute-start.50 = (bf16[4,256,1376]{1,2,0:T(8,128)(2,1)}, bf16[4,256,1376]{1,2,0:T(8,128)(2,1)}, u32[]{:S(2)}, u32[]{:S(2)}) collective-permute-start(bf16[4,256,1376]{1,2,0:T(8,128)(2,1)} %select_bitcast_fusion), channel_id=1, source_target_pairs={{0,4},{4,0},{8,12},{12,8},{16,20},{20,16},{24,28},{28,24},{1,5},{5... | collective-permute-start | bytes 8454152 | tf_op jit(solution)/shard_map/ppermute | solution.py:25
  982.3 527.6 %reduce-scatter.14.cloned.1.call-start = ((), (), s32[]{:S(2)}) async-start(), calls=%async_computation.10 | async-start | bytes 1310720 | tf_op jit(solution)/shard_map/reduce_scatter | solution.py:94
  985.3 526.4 %reduce-scatter.12.cloned.1.call-start = ((), (), s32[]{:S(2)}) async-start(), calls=%async_computation.9 | async-start | bytes 1310720 | tf_op jit(solution)/shard_map/reduce_scatter | solution.py:94
  991.4 70.2 %collective-permute-start.42 = (bf16[4,256,512]{2,1,0:T(8,128)(2,1)S(1)}, bf16[4,256,512]{2,1,0:T(8,128)(2,1)S(1)}, u32[]{:S(2)}, u32[]{:S(2)}) collective-permute-start(bf16[4,256,512]{2,1,0:T(8,128)(2,1)S(1)} %fusion.118), channel_id=1, source_target_pairs={{0,4},{4,0},{8,12},{12,8},{16,20},{20,16},{24,28},{28,24},{1,5},{5... | collective-permute-start | bytes 3145736 | tf_op jit(solution)/shard_map/ppermute | solution.py:25
  1063.0 450.6 %reduce-scatter.26.cloned.1.call-start = ((), (), s32[]{:S(2)}) async-start(), calls=%async_computation.16 | async-start | bytes 3604480 | tf_op jit(solution)/shard_map/reduce_scatter | solution.py:94
  1100.0 416.3 %reduce-scatter.24.cloned.1.call-start = ((), (), s32[]{:S(2)}) async-start(), calls=%async_computation.15 | async-start | bytes 3604480 | tf_op jit(solution)/shard_map/reduce_scatter | solution.py:94
  1118.7 60.5 %collective-permute-start.49 = (bf16[4,256,1376]{1,2,0:T(8,128)(2,1)}, bf16[4,256,1376]{1,2,0:T(8,128)(2,1)}, u32[]{:S(2)}, u32[]{:S(2)}) collective-permute-start(bf16[4,256,1376]{1,2,0:T(8,128)(2,1)} %select_bitcast_fusion.1), channel_id=1, source_target_pairs={{0,4},{4,0},{8,12},{12,8},{16,20},{20,16},{24,28},{28,24},{1,5},{5... | collective-permute-start | bytes 8454152 | tf_op jit(solution)/shard_map/ppermute | solution.py:25
  1192.5 326.3 %reduce-scatter.22.cloned.1.call-start = ((), (), s32[]{:S(2)}) async-start(), calls=%async_computation.14 | async-start | bytes 3604480 | tf_op jit(solution)/shard_map/reduce_scatter | solution.py:94
  1206.0 59.3 %collective-permute-start.48 = (bf16[4,256,1376]{1,2,0:T(8,128)(2,1)S(1)}, bf16[4,256,1376]{1,2,0:T(8,128)(2,1)S(1)}, u32[]{:S(2)}, u32[]{:S(2)}) collective-permute-start(bf16[4,256,1376]{1,2,0:T(8,128)(2,1)S(1)} %select_bitcast_fusion.2), channel_id=1, source_target_pairs={{0,4},{4,0},{8,12},{12,8},{16,20},{20,16},{24,28},{28,24},{1,5},{5... | collective-permute-start | bytes 8454152 | tf_op jit(solution)/shard_map/ppermute | solution.py:25
  1273.6 247.6 %reduce-scatter.20.cloned.1.call-start = ((), (), s32[]{:S(2)}) async-start(), calls=%async_computation.13 | async-start | bytes 2621440 | tf_op jit(solution)/shard_map/reduce_scatter | solution.py:94
  1280.6 42.9 %collective-permute-start.47 = (bf16[4,256,1024]{2,1,0:T(8,128)(2,1)S(1)}, bf16[4,256,1024]{2,1,0:T(8,128)(2,1)S(1)}, u32[]{:S(2)}, u32[]{:S(2)}) collective-permute-start(bf16[4,256,1024]{2,1,0:T(8,128)(2,1)S(1)} %select_bitcast_fusion.3), channel_id=1, source_target_pairs={{0,4},{4,0},{8,12},{12,8},{16,20},{20,16},{24,28},{28,24},{1,5},{5... | collective-permute-start | bytes 6291464 | tf_op jit(solution)/shard_map/ppermute | solution.py:25
  1330.4 192.9 %reduce-scatter.18.cloned.1.call-start = ((), (), s32[]{:S(2)}) async-start(), calls=%async_computation.12 | async-start | bytes 2621440 | tf_op jit(solution)/shard_map/reduce_scatter | solution.py:94
  1346.8 42.2 %collective-permute-start.45 = (bf16[4,256,1024]{2,1,0:T(8,128)(2,1)S(1)}, bf16[4,256,1024]{2,1,0:T(8,128)(2,1)S(1)}, u32[]{:S(2)}, u32[]{:S(2)}) collective-permute-start(bf16[4,256,1024]{2,1,0:T(8,128)(2,1)S(1)} %select_bitcast_fusion.4), channel_id=1, source_target_pairs={{0,4},{4,0},{8,12},{12,8},{16,20},{20,16},{24,28},{28,24},{1,5},{5... | collective-permute-start | bytes 6291464 | tf_op jit(solution)/shard_map/ppermute | solution.py:25
  1349.3 97.3 %collective-permute-start.13 = (bf16[768,1024]{0,1:T(8,128)(2,1)}, bf16[768,1024]{0,1:T(8,128)(2,1)}, u32[]{:S(2)}, u32[]{:S(2)}) collective-permute-start(bf16[768,1024]{0,1:T(8,128)(2,1)} %select_convert_fusion.2), channel_id=1, source_target_pairs={{0,1},{1,0},{2,3},{3,2},{4,5},{5,4},{6,7},{7,6},{8,9},{9,8},{10,11... | collective-permute-start | bytes 4718600 | tf_op jit(solution)/shard_map/ppermute | solution.py:25
  1391.9 133.6 %reduce-scatter.16.cloned.1.call-start = ((), (), s32[]{:S(2)}) async-start(), calls=%async_computation.11 | async-start | bytes 2621440 | tf_op jit(solution)/shard_map/reduce_scatter | solution.py:94
  1396.1 41.5 %collective-permute-start.44 = (bf16[4,256,1024]{2,1,0:T(8,128)(2,1)}, bf16[4,256,1024]{2,1,0:T(8,128)(2,1)}, u32[]{:S(2)}, u32[]{:S(2)}) collective-permute-start(bf16[4,256,1024]{2,1,0:T(8,128)(2,1)} %fusion.57), channel_id=1, source_target_pairs={{0,4},{4,0},{8,12},{12,8},{16,20},{20,16},{24,28},{28,24},{1,5},{5... | collective-permute-start | bytes 6291464 | tf_op jit(solution)/shard_map/ppermute | solution.py:25
  1446.6 32.1 %collective-permute-start.33 = (bf16[768,1024]{0,1:T(8,128)(2,1)}, bf16[768,1024]{0,1:T(8,128)(2,1)}, u32[]{:S(2)}, u32[]{:S(2)}) collective-permute-start(bf16[768,1024]{0,1:T(8,128)(2,1)} %select_convert_fusion), channel_id=1, source_target_pairs={{0,1},{1,0},{2,3},{3,2},{4,5},{5,4},{6,7},{7,6},{8,9},{9,8},{10,11... | collective-permute-start | bytes 4718600 | tf_op jit(solution)/shard_map/ppermute | solution.py:25
  1451.2 20.1 %collective-permute-start.14 = (bf16[768,512]{0,1:T(8,128)(2,1)S(1)}, bf16[768,512]{0,1:T(8,128)(2,1)}, u32[]{:S(2)}, u32[]{:S(2)}) collective-permute-start(bf16[768,512]{0,1:T(8,128)(2,1)S(1)} %dynamic-slice_convert_fusion.2), channel_id=1, source_target_pairs={{0,2},{1,3},{2,0},{3,1},{4,6},{5,7},{6,4},{7,5},{8,10},{9,11},{10,... | collective-permute-start | bytes 2359304 | tf_op jit(solution)/shard_map/ppermute | solution.py:25
  1455.4 20.2 %collective-permute-start.36 = (f32[768]{0:T(1024)S(1)}, f32[768]{0:T(1024)S(1)}, u32[]{:S(2)}, u32[]{:S(2)}) collective-permute-start(f32[768]{0:T(1024)S(1)} %fusion.234), channel_id=1, source_target_pairs={{0,2},{1,3},{2,0},{3,1},{4,6},{5,7},{6,4},{7,5},{8,10},{9,11},{10,... | collective-permute-start | bytes 9224 | tf_op jit(solution)/shard_map/ppermute | solution.py:25
  (320 other events, 3835.7 us)
Sparse Core Ops, SparseCore 0:
  982.4 17.0 reduce-scatter.27
  1002.5 25.3 reduce-scatter.13
  1063.1 25.3 reduce-scatter.11
  1100.1 54.3 reduce-scatter.25
  1192.6 54.1 reduce-scatter.23
  1273.7 54.2 reduce-scatter.21
  1330.5 43.5 reduce-scatter.19
  1392.0 42.1 reduce-scatter.17
  1442.2 42.7 reduce-scatter.15

commit v2 on v1

v2 whole, which is shorter than its diff:
```python
import functools

import jax
import jax.numpy as jnp
from jax import lax
from jax.experimental import pallas as pl
from jax.experimental.pallas import tpu as pltpu
from jax.sharding import PartitionSpec as P

DK = 128
DV = 256
GROUP = 64
CONV = 4
HALO = 16
WIDE = DK + DV

epsilon_norm = 1e-06
epsilon_gate = 1e-05

f32 = jnp.float32
bf16 = jnp.bfloat16


def contract(left, right, left_dim=1, right_dim=0):
    return lax.dot_general(
        left, right, (((left_dim,), (right_dim,)), ((), ())), preferred_element_type=f32
    )


def lane_heads(heads):
    return lax.broadcasted_iota(jnp.int32, (1, heads * GROUP), 1) // GROUP


def packed(full, heads):
    owner = lane_heads(heads)
    result = full[:GROUP]
    for head in range(1, heads):
        result = jnp.where(owner == head, full[head * GROUP : (head + 1) * GROUP], result)
    return result


def diagonal(values, heads):
    owner = lane_heads(heads)
    low = values.astype(bf16)
    return jnp.concatenate(
        [low * jnp.where(owner == head, 1.0, 0.0).astype(bf16) for head in range(heads)], axis=0
    )


def spread(columns, heads):
    owner = lane_heads(heads)
    result = jnp.broadcast_to(columns[0], (GROUP, heads * GROUP))
    for head in range(1, heads):
        result = jnp.where(owner == head, columns[head], result)
    return result


def halves(values):
    high = values.astype(bf16)
    return high, (values - high.astype(f32)).astype(bf16)


def product3(left, right, heads):
    left_high, left_low = halves(left)
    right_high, right_low = halves(right)
    rows = left.shape[0]
    first = contract(jnp.concatenate([left_high, left_low], axis=0), diagonal(right_high, heads))
    return first[:rows] + first[rows:] + contract(left_high, diagonal(right_low, heads))


def packed_inverse(coupling, heads):
    row = lax.broadcasted_iota(jnp.int32, coupling.shape, 0)
    lane = lax.broadcasted_iota(jnp.int32, coupling.shape, 1) % GROUP
    power = -coupling
    result = jnp.where(row == lane, 1.0, 0.0) + power
    power = product3(power, power, heads)
    degree = 2
    while degree * 2 < GROUP:
        both = product3(jnp.concatenate([result, power], axis=0), power, heads)
        result = result + both[:GROUP]
        power = both[GROUP:]
        degree = degree * 2
    return result + product3(result, power, heads)


def stacked(block, heads):
    width = block.shape[1] // heads
    return jnp.concatenate([block[:, h * width : (h + 1) * width] for h in range(heads)], axis=0)


def unstacked(block, heads):
    return jnp.concatenate([block[h * GROUP : (h + 1) * GROUP] for h in range(heads)], axis=1)


def fill(ext_ref, now_ref, before_ref, rim_ref, first, keep):
    before = jnp.where(first, rim_ref[...].astype(f32), before_ref[...].astype(f32))
    ext_ref[:HALO, :] = before * keep
    ext_ref[HALO:, :] = now_ref[...].astype(f32)


def tap_sum(ext_ref, conv_ref, low, width):
    total = ext_ref[pl.ds(HALO, GROUP), pl.ds(low, width)] * conv_ref[0:1, pl.ds(low, width)]
    for tap in range(1, CONV):
        total = total + (
            ext_ref[pl.ds(HALO - tap, GROUP), pl.ds(low, width)]
            * conv_ref[tap : tap + 1, pl.ds(low, width)]
        )
    return total


def decay_terms(scal, grow, heads):
    growth = [scal[:, h : h + 1] for h in range(heads)]
    betas = [scal[:, heads + h : heads + h + 1] for h in range(heads)]
    row = lax.broadcasted_iota(jnp.int32, (GROUP, heads * GROUP), 0)
    lane = lax.broadcasted_iota(jnp.int32, (GROUP, heads * GROUP), 1) % GROUP
    lower, strict = (row >= lane, row > lane)
    gap = spread(growth, heads) - grow
    ratio = jnp.where(lower, jnp.exp(jnp.where(lower, gap, 0.0)), 0.0)
    return ratio, spread(betas, heads), strict


def column_stack(scal, kind, heads):
    return jnp.concatenate(
        [scal[:, kind * heads + h : kind * heads + h + 1] for h in range(heads)], axis=0
    )


def forward_kernel(
    heads,
    groups,
    keep_ref,
    fade_ref,
    query_ref,
    key_ref,
    value_ref,
    query_before,
    key_before,
    value_before,
    query_rim,
    key_rim,
    value_rim,
    conv_query,
    conv_key,
    conv_value,
    scal_ref,
    grow_ref,
    query_out,
    key_out,
    value_out,
    wu_out,
    inverse_out,
    state_out,
    linear_out,
    local_out,
    device_out,
    state,
    ext_query,
    ext_key,
    ext_value,
):
    group = pl.program_id(0)
    first = group == 0

    @pl.when(first)
    def _():
        row = lax.broadcasted_iota(jnp.int32, (DK, WIDE), 0)
        lane = lax.broadcasted_iota(jnp.int32, (DK, WIDE), 1)
        unit = jnp.where(row == lane, 1.0, 0.0)
        for h in range(heads):
            state[pl.ds(h * DK, DK), :] = unit

    keep = keep_ref[group]
    fill(ext_query, query_ref, query_before, query_rim, first, keep)
    fill(ext_key, key_ref, key_before, key_rim, first, keep)
    fill(ext_value, value_ref, value_before, value_rim, first, keep)
    scal = scal_ref[...]
    valid = scal[:, 4 * heads : 4 * heads + 1]
    queries, keys, values = ([], [], [])
    for h in range(heads):
        act = jax.nn.silu(tap_sum(ext_query, conv_query, h * DK, DK))
        scale = lax.rsqrt(jnp.sum(act * act, axis=1, keepdims=True) + epsilon_norm)
        queries.append((act * scale * DK ** (-0.5)).astype(bf16))
        act = jax.nn.silu(tap_sum(ext_key, conv_key, h * DK, DK))
        scale = lax.rsqrt(jnp.sum(act * act, axis=1, keepdims=True) + epsilon_norm)
        keys.append((act * scale * valid).astype(bf16))
        act = jax.nn.silu(tap_sum(ext_value, conv_value, h * DV, DV))
        values.append((act * valid).astype(bf16))
    query_out[...] = jnp.concatenate(queries, axis=1)
    key_out[...] = jnp.concatenate(keys, axis=1)
    value_out[...] = jnp.concatenate(values, axis=1)
    query = jnp.concatenate(queries, axis=0)
    key = jnp.concatenate(keys, axis=0)
    value = jnp.concatenate(values, axis=0)
    scores = contract(jnp.concatenate([query, key], axis=0), key, 1, 1)
    mix = packed(scores[: heads * GROUP], heads)
    similar = packed(scores[heads * GROUP :], heads)
    ratio, betas, strict = decay_terms(scal, grow_ref[0], heads)
    mixing = diagonal(ratio * mix, heads)
    inverse = packed_inverse(jnp.where(strict, betas * ratio * similar, 0.0), heads).astype(bf16)
    inverse_out[...] = inverse
    beta = column_stack(scal, 1, heads)
    growth = column_stack(scal, 2, heads)
    closing = column_stack(scal, 3, heads)
    key_wide = key.astype(f32)
    right = jnp.concatenate([beta * growth * key_wide, beta * value.astype(f32)], axis=1)
    wu = contract(diagonal(inverse, heads), right.astype(bf16))
    wu_low = wu.astype(bf16)
    wu_out[0] = wu_low
    grown = (growth * query.astype(f32)).astype(bf16)
    fading = (closing * key_wide).astype(bf16)
    lane = lax.broadcasted_iota(jnp.int32, (1, WIDE), 1)
    fresh, seen = ([], [])
    for h in range(heads):
        rows = slice(h * GROUP, (h + 1) * GROUP)
        used = state[pl.ds(h * DK, DK), :] * keep
        used_low = used.astype(bf16)
        state_out[0, pl.ds(h * DK, DK), :] = used_low
        part = jnp.where(lane >= DK, wu[rows], 0.0) - contract(wu_low[rows, :DK], used_low)
        part = part.astype(bf16)
        after = fade_ref[group * heads + h] * used + contract(fading[rows], part, 0, 0)
        state[pl.ds(h * DK, DK), :] = after
        fresh.append(part)
        seen.append(contract(grown[rows], used_low))
    both = jnp.concatenate(seen, axis=0) + contract(mixing, jnp.concatenate(fresh, axis=0))
    for h in range(heads):
        rows = slice(h * GROUP, (h + 1) * GROUP)
        linear_out[:, pl.ds(h * DK, DK)] = (both[rows, :DK] * valid).astype(bf16)
        local_out[:, pl.ds(h * DV, DV)] = both[rows, DK:] * valid

    @pl.when(group == groups - 1)
    def _():
        device_out[...] = state[...]


def token_block(width, back=None):
    if back is None:
        return pl.BlockSpec((GROUP, width), lambda g: (g, 0))
    return pl.BlockSpec((GROUP, width), lambda g: (back - 1 - g, 0))


def before_block(width, back=None):
    ratio = GROUP // HALO
    if back is None:
        return pl.BlockSpec((HALO, width), lambda g: (jnp.maximum(g * ratio - 1, 0), 0))
    return pl.BlockSpec((HALO, width), lambda g: (jnp.maximum((back - 1 - g) * ratio - 1, 0), 0))


def whole(shape):
    return pl.BlockSpec(shape, lambda g: (0,) * len(shape))


def scalars(decay, beta, valid):
    tokens, heads = decay.shape
    groups = tokens // GROUP
    ones = jnp.tril(jnp.ones((GROUP, GROUP), f32))
    sums = jnp.einsum(
        "ij,gjh->gih", ones, decay.reshape(groups, GROUP, heads), precision=lax.Precision.HIGHEST
    )
    last = sums[:, -1:, :]
    flat = lambda part: part.reshape(tokens, heads)
    scal = jnp.concatenate(
        [flat(sums), beta, flat(jnp.exp(sums)), flat(jnp.exp(last - sums)), valid[:, None]], axis=1
    )
    grow = jnp.swapaxes(sums, 1, 2).reshape(groups, 1, heads * GROUP)
    return scal, grow, jnp.exp(last[:, 0, :])


def delta_forward(pres, rims, convs, scal, grow, fade, keep):
    tokens = scal.shape[0]
    heads, groups = (fade.shape[1], tokens // GROUP)
    widths = [pre.shape[1] for pre in pres]
    smem = pl.BlockSpec(memory_space=pltpu.SMEM)
    return pl.pallas_call(
        functools.partial(forward_kernel, heads, groups),
        grid=(groups,),
        in_specs=[smem, smem]
        + [token_block(w) for w in widths]
        + [before_block(w) for w in widths]
        + [whole((HALO, w)) for w in widths]
        + [whole((CONV, w)) for w in widths]
        + [token_block(scal.shape[1]), pl.BlockSpec((1, 1, heads * GROUP), lambda g: (g, 0, 0))],
        out_specs=[token_block(w) for w in widths]
        + [
            pl.BlockSpec((1, heads * GROUP, WIDE), lambda g: (g, 0, 0)),
            token_block(heads * GROUP),
            pl.BlockSpec((1, heads * DK, WIDE), lambda g: (g, 0, 0)),
            token_block(heads * DK),
            token_block(heads * DV),
            whole((heads * DK, WIDE)),
        ],
        out_shape=[jax.ShapeDtypeStruct((tokens, w), bf16) for w in widths]
        + [
            jax.ShapeDtypeStruct((groups, heads * GROUP, WIDE), bf16),
            jax.ShapeDtypeStruct((tokens, heads * GROUP), bf16),
            jax.ShapeDtypeStruct((groups, heads * DK, WIDE), bf16),
            jax.ShapeDtypeStruct((tokens, heads * DK), bf16),
            jax.ShapeDtypeStruct((tokens, heads * DV), f32),
            jax.ShapeDtypeStruct((heads * DK, WIDE), f32),
        ],
        scratch_shapes=[pltpu.VMEM((heads * DK, WIDE), f32)]
        + [pltpu.VMEM((HALO + GROUP, w), f32) for w in widths],
        compiler_params=pltpu.CompilerParams(vmem_limit_bytes=40 * 2**20),
        cost_estimate=pl.CostEstimate(flops=4 * 10**9, bytes_accessed=2 * 10**7, transcendentals=0),
        name="delta_forward",
    )(keep, fade.reshape(-1), *pres, *pres, *rims, *convs, scal, grow)


def backward_kernel(
    heads,
    groups,
    keep_ref,
    fade_ref,
    query_pre,
    key_pre,
    value_pre,
    query_before,
    key_before,
    value_before,
    query_rim,
    key_rim,
    value_rim,
    conv_query,
    conv_key,
    conv_value,
    scal_ref,
    grow_ref,
    query_ref,
    key_ref,
    value_ref,
    wu_ref,
    inverse_ref,
    state_ref,
    entry_ref,
    exit_ref,
    grad_ref,
    query_out,
    key_out,
    value_out,
    query_conv_out,
    key_conv_out,
    value_conv_out,
    query_back_out,
    key_back_out,
    value_back_out,
    query_tail_out,
    key_tail_out,
    value_tail_out,
    scal_out,
    row_out,
    carry,
    ext_query,
    ext_key,
    ext_value,
    dy_query,
    dy_key,
    dy_value,
):
    step = pl.program_id(0)
    group = groups - 1 - step
    keep = keep_ref[group]

    @pl.when(step == 0)
    def _():
        carry[...] = exit_ref[...]
        for ref in (dy_query, dy_key, dy_value):
            ref[...] = jnp.zeros_like(ref)
        for ref in (query_conv_out, key_conv_out, value_conv_out):
            ref[...] = jnp.zeros_like(ref)

    scal = scal_ref[...]
    valid = scal[:, 4 * heads : 4 * heads + 1]
    beta = column_stack(scal, 1, heads)
    growth = column_stack(scal, 2, heads)
    closing = column_stack(scal, 3, heads)
    query = stacked(query_ref[...], heads)
    key = stacked(key_ref[...], heads)
    value = stacked(value_ref[...], heads)
    grad = stacked(grad_ref[...], heads)
    query_wide, key_wide = (query.astype(f32), key.astype(f32))
    scores = contract(jnp.concatenate([query, key], axis=0), key, 1, 1)
    mix = packed(scores[: heads * GROUP], heads)
    similar = packed(scores[heads * GROUP :], heads)
    ratio, betas, strict = decay_terms(scal, grow_ref[0], heads)
    mixing = ratio * mix
    wu = wu_ref[0]
    grown_wide = growth * query_wide
    fading_wide = closing * key_wide
    grown = grown_wide.astype(bf16)
    fading = fading_wide.astype(bf16)
    mixed_back = contract(diagonal(mixing, heads), grad, 0, 0)
    fresh, d_fresh, d_grown, d_fading, d_weights = ([], [], [], [], [])
    for h in range(heads):
        rows = slice(h * GROUP, (h + 1) * GROUP)
        states = pl.ds(h * DK, DK)
        pair = state_ref[0, states, :]
        used = pair[:, DK:].astype(f32) + contract(pair[:, :DK], entry_ref[states, :])
        used_low = used.astype(bf16)
        weights = wu[rows, :DK]
        part = (wu[rows, DK:].astype(f32) - contract(weights, used_low)).astype(bf16)
        after = carry[states, :]
        after_low = after.astype(bf16)
        d_part = mixed_back[rows] + contract(fading[rows], after_low)
        d_part_low = d_part.astype(bf16)
        stack = jnp.concatenate([grad[rows], d_part_low], axis=0)
        seen = contract(stack, used_low, 1, 1)
        d_grown.append(seen[:GROUP])
        d_weights.append(-seen[GROUP:])
        d_fading.append(contract(part, after_low, 1, 1))
        fade = fade_ref[group * heads + h]
        carry[states, :] = keep * (
            fade * after
            + contract(jnp.concatenate([grown[rows], -weights], axis=0), stack, 0, 0)
        )
        row_out[0, heads + h : heads + h + 1, :] = fade * jnp.sum(
            after * used, axis=0, keepdims=True
        )
        fresh.append(part)
        d_fresh.append(d_part_low)
    d_grown = jnp.concatenate(d_grown, axis=0)
    d_fading = jnp.concatenate(d_fading, axis=0)
    d_weights = jnp.concatenate(d_weights, axis=0).astype(bf16)
    d_fresh = jnp.concatenate(d_fresh, axis=0)
    d_mixing = packed(contract(grad, jnp.concatenate(fresh, axis=0), 1, 1), heads)
    d_right = contract(
        diagonal(inverse_ref[...], heads), jnp.concatenate([d_weights, d_fresh], axis=1), 0, 0
    )
    d_coupling = -packed(contract(d_right.astype(bf16), wu, 1, 1), heads)
    d_coupling = jnp.where(strict, d_coupling, 0.0)
    ratio_grad = ratio * d_coupling
    from_similar = diagonal(betas * ratio_grad, heads)
    from_mix = diagonal(ratio * d_mixing, heads)
    plain = contract(jnp.concatenate([from_mix, from_similar], axis=0), key)
    turned = contract(
        jnp.concatenate([from_similar, from_mix], axis=0),
        jnp.concatenate([key, query], axis=0),
        0,
        0,
    )
    count = heads * GROUP
    d_scaled = d_right[:, :DK]
    d_query = growth * d_grown + plain[:count]
    d_key = beta * growth * d_scaled + closing * d_fading + plain[count:] + turned
    d_value = beta * d_right[:, DK:]
    grown_key = growth * key_wide
    ratio_similar = ratio_grad * similar
    flows = betas * ratio_similar + mixing * d_mixing
    fading_flow = d_fading * fading_wide
    sum_growth = jnp.sum(
        d_grown * grown_wide + d_scaled * (beta * grown_key) - fading_flow, axis=1, keepdims=True
    )
    sum_fading = jnp.sum(fading_flow, axis=1, keepdims=True)
    value_flow = d_right[:, DK:] * value.astype(f32)
    sum_beta = jnp.sum(
        d_scaled * grown_key + value_flow[:, :DK] + value_flow[:, DK:], axis=1, keepdims=True
    )
    row_out[0, 0:1, :] = jnp.sum(flows, axis=0, keepdims=True)
    owner = lane_heads(heads)
    lane = lax.broadcasted_iota(jnp.int32, (GROUP, scal_out.shape[1]), 1)
    columns = jnp.zeros((GROUP, scal_out.shape[1]), f32)
    for h in range(heads):
        rows = slice(h * GROUP, (h + 1) * GROUP)
        flow = jnp.sum(jnp.where(owner == h, flows, 0.0), axis=1, keepdims=True)
        more = jnp.sum(jnp.where(owner == h, ratio_similar, 0.0), axis=1, keepdims=True)
        columns = jnp.where(lane == h, sum_growth[rows] + flow, columns)
        columns = jnp.where(lane == heads + h, sum_beta[rows] + more, columns)
        columns = jnp.where(lane == 2 * heads + h, sum_fading[rows], columns)
    scal_out[...] = columns

    first = group == 0
    after_keep = jnp.where(step == 0, 0.0, keep_ref[jnp.minimum(group + 1, groups - 1)])
    sections = (
        (query_pre, query_before, query_rim, conv_query, ext_query, dy_query, DK, d_query),
        (key_pre, key_before, key_rim, conv_key, ext_key, dy_key, DK, d_key),
        (value_pre, value_before, value_rim, conv_value, ext_value, dy_value, DV, d_value),
    )
    outs = (
        (query_out, query_conv_out, query_back_out, query_tail_out),
        (key_out, key_conv_out, key_back_out, key_tail_out),
        (value_out, value_conv_out, value_back_out, value_tail_out),
    )
    for kind, (section, out) in enumerate(zip(sections, outs)):
        now_ref, before_ref, rim_ref, conv_ref, ext_ref, dy_ref, width, cotangent = section
        pre_out, conv_out, back_out, tail_out = out
        fill(ext_ref, now_ref, before_ref, rim_ref, first, keep)
        dy_ref[8 + GROUP :, :] = dy_ref[8:16, :] * after_keep
        for h in range(heads):
            lanes = pl.ds(h * width, width)
            rows = slice(h * GROUP, (h + 1) * GROUP)
            total = tap_sum(ext_ref, conv_ref, h * width, width)
            sigmoid = jax.nn.sigmoid(total)
            act = total * sigmoid
            d_act = cotangent[rows]
            if kind > 0:
                d_act = d_act * valid
            if kind < 2:
                scale = lax.rsqrt(jnp.sum(act * act, axis=1, keepdims=True) + epsilon_norm)
                inner = jnp.sum(act * d_act, axis=1, keepdims=True)
                d_act = scale * (d_act - act * (scale * scale * inner))
            if kind == 0:
                d_act = d_act * DK ** (-0.5)
            d_total = d_act * (sigmoid * (1.0 + total * (1.0 - sigmoid)))
            dy_ref[pl.ds(8, GROUP), lanes] = d_total
            for tap in range(CONV):
                product = d_total * ext_ref[pl.ds(HALO - tap, GROUP), lanes]
                conv_out[pl.ds(tap * 8, 8), lanes] += jnp.sum(
                    product.reshape(GROUP // 8, 8, width), axis=0
                )
            d_pre = d_total * conv_ref[0:1, lanes]
            for tap in range(1, CONV):
                d_pre = d_pre + dy_ref[pl.ds(8 + tap, GROUP), lanes] * conv_ref[tap : tap + 1, lanes]
            pre_out[:, lanes] = d_pre.astype(bf16)

            @pl.when(step == 0)
            def _():
                tail_out[:, lanes] = d_pre[GROUP - 8 :]

            @pl.when(first)
            def _():
                d_back = dy_ref[pl.ds(1, 8), lanes] * conv_ref[1:2, lanes]
                for tap in range(2, CONV):
                    d_back = d_back + dy_ref[pl.ds(tap, 8), lanes] * conv_ref[tap : tap + 1, lanes]
                back_out[:, lanes] = d_back * keep


def delta_backward(pres, rims, convs, scal, grow, fade, keep, made, entry, exit_grad, grad):
    tokens = scal.shape[0]
    heads, groups = (fade.shape[1], tokens // GROUP)
    widths = [pre.shape[1] for pre in pres]
    smem = pl.BlockSpec(memory_space=pltpu.SMEM)
    turn = lambda *shape: pl.BlockSpec(shape, lambda g: (groups - 1 - g, 0, 0))
    columns = 3 * heads
    return pl.pallas_call(
        functools.partial(backward_kernel, heads, groups),
        grid=(groups,),
        in_specs=[smem, smem]
        + [token_block(w, groups) for w in widths]
        + [before_block(w, groups) for w in widths]
        + [whole((HALO, w)) for w in widths]
        + [whole((CONV, w)) for w in widths]
        + [token_block(scal.shape[1], groups), turn(1, 1, heads * GROUP)]
        + [token_block(w, groups) for w in widths]
        + [
            turn(1, heads * GROUP, WIDE),
            token_block(heads * GROUP, groups),
            turn(1, heads * DK, WIDE),
            whole((heads * DK, DV)),
            whole((heads * DK, DV)),
            token_block(heads * DV, groups),
        ],
        out_specs=[token_block(w, groups) for w in widths]
        + [whole((CONV * 8, w)) for w in widths]
        + [whole((8, w)) for w in widths]
        + [whole((8, w)) for w in widths]
        + [token_block(columns, groups), turn(1, 2 * heads, heads * GROUP)],
        out_shape=[jax.ShapeDtypeStruct((tokens, w), bf16) for w in widths]
        + [jax.ShapeDtypeStruct((CONV * 8, w), f32) for w in widths]
        + [jax.ShapeDtypeStruct((8, w), f32) for w in widths]
        + [jax.ShapeDtypeStruct((8, w), f32) for w in widths]
        + [
            jax.ShapeDtypeStruct((tokens, columns), f32),
            jax.ShapeDtypeStruct((groups, 2 * heads, heads * GROUP), f32),
        ],
        scratch_shapes=[pltpu.VMEM((heads * DK, DV), f32)]
        + [pltpu.VMEM((HALO + GROUP, w), f32) for w in widths]
        + [pltpu.VMEM((16 + GROUP, w), f32) for w in widths],
        compiler_params=pltpu.CompilerParams(vmem_limit_bytes=40 * 2**20),
        cost_estimate=pl.CostEstimate(flops=9 * 10**9, bytes_accessed=3 * 10**7, transcendentals=0),
        name="delta_backward",
    )(keep, fade.reshape(-1), *pres, *pres, *rims, *convs, scal, grow, *made, entry, exit_grad, grad)


def scalar_grads(columns, rows):
    groups, heads = (rows.shape[0], columns.shape[1] // 3)
    parts = columns.reshape(groups, GROUP, 3, heads)
    turned = jnp.swapaxes(rows[:, 0, :].reshape(groups, heads, GROUP), 1, 2)
    sums = parts[:, :, 0] - turned
    last = jnp.sum(parts[:, :, 2], axis=1) + jnp.sum(rows[:, heads:], axis=2)
    ones = jnp.triu(jnp.ones((GROUP, GROUP), f32))
    d_decay = jnp.einsum("ij,gjh->gih", ones, sums, precision=lax.Precision.HIGHEST)
    d_decay = d_decay + last[:, None, :]
    tokens = columns.shape[0]
    return d_decay.reshape(tokens, heads), parts[:, :, 1].reshape(tokens, heads)


def gated_forward_kernel(heads, linear_ref, local_ref, gate_ref, entry_ref, gain_ref, gated_out):
    for h in range(heads):
        wide = pl.ds(h * DV, DV)
        out = local_ref[:, wide] + contract(
            linear_ref[:, pl.ds(h * DK, DK)], entry_ref[pl.ds(h * DK, DK), :]
        )
        scale = lax.rsqrt(jnp.mean(out * out, axis=1, keepdims=True) + epsilon_gate)
        gate = gate_ref[:, wide]
        gated_out[:, wide] = (out * scale * gain_ref[...] * jax.nn.silu(gate)).astype(bf16)


def row_block(rows, width):
    return pl.BlockSpec((rows, width), lambda g: (g, 0))


def gated_forward(linear, local, gate, entry, gain):
    tokens, heads = (local.shape[0], local.shape[1] // DV)
    rows = 2 * GROUP
    return pl.pallas_call(
        functools.partial(gated_forward_kernel, heads),
        grid=(tokens // rows,),
        in_specs=[
            row_block(rows, heads * DK),
            row_block(rows, heads * DV),
            row_block(rows, heads * DV),
            whole((heads * DK, DV)),
            whole((1, DV)),
        ],
        out_specs=row_block(rows, heads * DV),
        out_shape=jax.ShapeDtypeStruct((tokens, heads * DV), bf16),
        compiler_params=pltpu.CompilerParams(vmem_limit_bytes=24 * 2**20),
        cost_estimate=pl.CostEstimate(flops=10**9, bytes_accessed=10**7, transcendentals=0),
        name="gated_forward",
    )(linear, local, gate, entry, gain[None, :])


def gated_backward_kernel(
    heads,
    linear_ref,
    local_ref,
    gate_ref,
    entry_ref,
    gain_ref,
    grad_ref,
    valid_ref,
    delta_out,
    gate_out,
    gain_out,
    entry_out,
):
    @pl.when(pl.program_id(0) == 0)
    def _():
        gain_out[...] = jnp.zeros_like(gain_out)
        entry_out[...] = jnp.zeros_like(entry_out)

    rows = local_ref.shape[0]
    for h in range(heads):
        wide = pl.ds(h * DV, DV)
        linear = linear_ref[:, pl.ds(h * DK, DK)]
        out = local_ref[:, wide] + contract(linear, entry_ref[pl.ds(h * DK, DK), :])
        scale = lax.rsqrt(jnp.mean(out * out, axis=1, keepdims=True) + epsilon_gate)
        unit = out * scale
        gate = gate_ref[:, wide]
        sigmoid = jax.nn.sigmoid(gate)
        grad = grad_ref[:, wide]
        silu = gate * sigmoid
        product = grad * unit
        gain_out[...] += jnp.sum((product * silu).reshape(rows // 8, 8, DV), axis=0)
        gate_out[:, wide] = (
            product * gain_ref[...] * (sigmoid * (1.0 + gate * (1.0 - sigmoid)))
        ).astype(bf16)
        d_unit = grad * gain_ref[...] * silu
        inner = jnp.mean(d_unit * unit, axis=1, keepdims=True)
        delta = (scale * (d_unit - unit * inner) * valid_ref[...]).astype(bf16)
        delta_out[:, wide] = delta
        entry_out[pl.ds(h * DK, DK), :] += contract(linear, delta, 0, 0)


def gated_backward(linear, local, gate, entry, gain, grad, valid):
    tokens, heads = (local.shape[0], local.shape[1] // DV)
    rows = 2 * GROUP
    return pl.pallas_call(
        functools.partial(gated_backward_kernel, heads),
        grid=(tokens // rows,),
        in_specs=[
            row_block(rows, heads * DK),
            row_block(rows, heads * DV),
            row_block(rows, heads * DV),
            whole((heads * DK, DV)),
            whole((1, DV)),
            row_block(rows, heads * DV),
            row_block(rows, 1),
        ],
        out_specs=[
            row_block(rows, heads * DV),
            row_block(rows, heads * DV),
            whole((8, DV)),
            whole((heads * DK, DV)),
        ],
        out_shape=[
            jax.ShapeDtypeStruct((tokens, heads * DV), bf16),
            jax.ShapeDtypeStruct((tokens, heads * DV), bf16),
            jax.ShapeDtypeStruct((8, DV), f32),
            jax.ShapeDtypeStruct((heads * DK, DV), f32),
        ],
        compiler_params=pltpu.CompilerParams(vmem_limit_bytes=24 * 2**20),
        cost_estimate=pl.CostEstimate(flops=2 * 10**9, bytes_accessed=2 * 10**7, transcendentals=0),
        name="gated_backward",
    )(linear, local, gate, entry, gain[None, :], grad, valid[:, None])


def column_place(tile, tiles, place):
    block, inner = (tile // (tiles // 4), tile % (tiles // 4))
    core = jnp.where(block < 2, 1 - place % 2, place % 2)
    chip = jnp.where(block % 2 == 0, 1 - place // 2, place // 2)
    return (chip * 2 + core) * (tiles // 4) + inner


def plain_dense_kernel(place_ref, left_ref, right_ref, out_ref):
    out_ref[...] = contract(left_ref[...], right_ref[...]).astype(bf16)


def plain_dense(left, right, place, tile=256):
    rows, cols = (left.shape[0], right.shape[1])
    tiles = cols // tile
    return pl.pallas_call(
        plain_dense_kernel,
        grid_spec=pltpu.PrefetchScalarGridSpec(
            num_scalar_prefetch=1,
            grid=(tiles,),
            in_specs=[
                pl.BlockSpec(left.shape, lambda i, place: (0, 0)),
                pl.BlockSpec(
                    (right.shape[0], tile), lambda i, place: (0, column_place(i, tiles, place[0]))
                ),
            ],
            out_specs=pl.BlockSpec((rows, tile), lambda i, place: (0, i)),
        ),
        out_shape=jax.ShapeDtypeStruct((rows, cols), bf16),
        compiler_params=pltpu.CompilerParams(vmem_limit_bytes=24 * 2**20),
        cost_estimate=pl.CostEstimate(
            flops=2 * rows * cols * left.shape[1], bytes_accessed=10**7, transcendentals=0
        ),
        name="plain_dense",
    )(place, left, right)


def norm_dense_kernel(count, place_ref, *refs):
    lefts, rights = (refs[:count], refs[count : 2 * count])
    rows_ref, scale_ref, gain_ref, out_ref, gain_out, dots_out = refs[2 * count :]
    total = contract(lefts[0][...], rights[0][...], 1, 1)
    for left, right in zip(lefts[1:], rights[1:]):
        total = total + contract(left[...], right[...], 1, 1)
    out_ref[...] = total.astype(bf16)
    weighted = total * (rows_ref[...].astype(f32) * scale_ref[...])
    gain_out[...] = jnp.sum(weighted, axis=0, keepdims=True)
    dots = jnp.sum(weighted * gain_ref[...], axis=1, keepdims=True)

    @pl.when(pl.program_id(0) == 0)
    def _():
        dots_out[...] = dots

    @pl.when(pl.program_id(0) > 0)
    def _():
        dots_out[...] += dots


def norm_dense(pairs, rows, scale, gain, place, tile=256):
    tokens, cols = rows.shape
    tiles = cols // tile
    lefts, rights = ([left for left, _ in pairs], [right for _, right in pairs])
    placed = lambda i, place: (0, column_place(i, tiles, place[0]))
    return pl.pallas_call(
        functools.partial(norm_dense_kernel, len(pairs)),
        grid_spec=pltpu.PrefetchScalarGridSpec(
            num_scalar_prefetch=1,
            grid=(tiles,),
            in_specs=[pl.BlockSpec(left.shape, lambda i, place: (0, 0)) for left in lefts]
            + [
                pl.BlockSpec(
                    (tile, right.shape[1]),
                    lambda i, place: (column_place(i, tiles, place[0]), 0),
                )
                for right in rights
            ]
            + [
                pl.BlockSpec((tokens, tile), placed),
                pl.BlockSpec((tokens, 1), lambda i, place: (0, 0)),
                pl.BlockSpec((1, tile), placed),
            ],
            out_specs=[
                pl.BlockSpec((tokens, tile), lambda i, place: (0, i)),
                pl.BlockSpec((1, tile), placed),
                pl.BlockSpec((tokens, 1), lambda i, place: (0, 0)),
            ],
        ),
        out_shape=[
            jax.ShapeDtypeStruct((tokens, cols), bf16),
            jax.ShapeDtypeStruct((1, cols), f32),
            jax.ShapeDtypeStruct((tokens, 1), f32),
        ],
        compiler_params=pltpu.CompilerParams(vmem_limit_bytes=32 * 2**20),
        cost_estimate=pl.CostEstimate(
            flops=2 * tokens * cols * sum(right.shape[1] for right in rights),
            bytes_accessed=2 * 10**7,
            transcendentals=0,
        ),
        name="norm_dense",
    )(place, *lefts, *rights, rows, scale, gain[None, :])


def shifted(block, axis, distance):
    devices = range(lax.axis_size(axis))
    route = [(i - distance, i) for i in devices if i - distance in devices]
    return lax.ppermute(block, axis, route)


def exchanged(block, axis, bit):
    route = [(i, i ^ bit) for i in range(lax.axis_size(axis))]
    return lax.ppermute(block, axis, route)


def half(block, axis, at, count):
    width = block.shape[axis] // count
    return lax.dynamic_slice_in_dim(block, at * width, width, axis)


def head_scattered(partial):
    width = partial.shape[1] // 2
    mine = partial[:, width:].astype(f32) + exchanged(partial[:, :width], "head", 1).astype(f32)
    width = width // 2
    return mine[:, width:] + exchanged(mine[:, :width].astype(bf16), "head", 2).astype(f32)


def head_gathered(block):
    place = lax.axis_index("head")
    core, chip = (place % 2, place // 2)
    across = exchanged(block, "head", 2)
    beside = exchanged(block, "head", 1)
    corner = exchanged(across, "head", 1)
    low = jnp.where(core == 0, block, beside)
    high = jnp.where(core == 0, beside, block)
    far_low = jnp.where(core == 0, across, corner)
    far_high = jnp.where(core == 0, corner, across)
    near = jnp.concatenate([low, high], axis=1)
    far = jnp.concatenate([far_low, far_high], axis=1)
    return jnp.where(
        chip == 0,
        jnp.concatenate([near, far], axis=1),
        jnp.concatenate([far, near], axis=1),
    )


def head_summed(values):
    bit = 1
    while bit < lax.axis_size("head"):
        values = values + exchanged(values, "head", bit)
        bit = bit * 2
    return values


def all_summed(values):
    values = head_summed(values)
    bit = 1
    while bit < lax.axis_size("seq"):
        values = values + exchanged(values, "seq", bit)
        bit = bit * 2
    return values


def own_half(rows, odd):
    tokens, width = rows.shape
    devices = lax.axis_size("seq")
    parts = rows.reshape(tokens, devices // 2, 2, width // devices)
    return lax.dynamic_index_in_dim(parts, odd, 2, False).reshape(tokens, width // 2)


def halves_of(rows):
    odd = lax.axis_index("seq") % 2
    return own_half(rows, odd), own_half(rows, 1 - odd)


def seq_scattered(mine):
    devices = lax.axis_size("seq")
    groups = [list(range(first, devices, 2)) for first in range(2)]
    return lax.psum_scatter(
        mine.astype(bf16), "seq", scatter_dimension=0, axis_index_groups=groups, tiled=True
    ).astype(f32)


def weight_grad(rows, cols):
    own, other = rows
    got = exchanged(dense(other.T, cols).astype(bf16), "seq", 1)
    return seq_scattered(dense(own.T, cols) + got.astype(f32))


def prefix(pair, direction):
    pair = shifted(pair.astype(bf16), "seq", direction)
    offset = pair[:, :, DK:].astype(f32)
    distance = 1
    while True:
        last = distance * 2 >= lax.axis_size("seq") - 1
        sent = pair[:, :, DK:] if last else pair
        before = shifted(sent, "seq", direction * distance)
        moved = jnp.einsum("hij,hjk->hik", pair[:, :, :DK], before, preferred_element_type=f32)
        if last:
            return offset + moved
        offset = offset + moved[:, :, DK:]
        pair = jnp.concatenate([moved[:, :, :DK], offset], axis=2).astype(bf16)
        distance = distance * 2


def layout(lengths, positions):
    padded = (lengths + (GROUP - 1)) // GROUP * GROUP
    seq_ends = jnp.cumsum(padded)
    begins = seq_ends - padded
    offset = positions[:, None] - begins[None, :]
    inside = (offset >= 0) & (positions[:, None] < seq_ends[None, :])
    valid_mask = jnp.any(inside & (offset < lengths[None, :]), axis=1).astype(jnp.float32)
    starts = jnp.any(offset == 0, axis=1).astype(jnp.float32)
    return (valid_mask, starts)


def dense(left, right):
    return jnp.dot(left, right, preferred_element_type=jnp.float32)


def shards(
    hidden_in,
    lengths,
    attn_gain,
    w_query,
    w_key,
    w_value,
    w_gate,
    w_alpha,
    w_beta,
    conv_query,
    conv_key,
    conv_value,
    decay_log,
    decay_bias,
    out_gain,
    w_out,
    ffn_gain,
    w_ffn_gate,
    w_ffn_up,
    w_ffn_down,
    grad_out,
):
    token_rows = hidden_in.shape[0]
    head_count = w_alpha.shape[1]
    col_width = grad_out.shape[1]
    devices = lax.axis_size("seq")
    positions = lax.axis_index("seq") * token_rows + jnp.arange(token_rows, dtype=jnp.int32)
    valid_mask, starts = layout(lengths, positions)
    keep_flags = 1.0 - starts[::GROUP]
    head_place = lax.axis_index("head")
    place = head_place[None].astype(jnp.int32)
    head_first = head_place * head_count
    col_first = head_place * col_width
    cols = lambda rows: lax.dynamic_slice_in_dim(rows, col_first, col_width, rows.ndim - 1)
    local_log = lax.dynamic_slice_in_dim(decay_log, head_first, head_count)
    local_bias = lax.dynamic_slice_in_dim(decay_bias, head_first, head_count)

    inputs32 = hidden_in.astype(f32)
    attn_scale = lax.rsqrt(jnp.mean(inputs32 * inputs32, axis=-1, keepdims=True) + epsilon_norm)
    normed = (inputs32 * attn_scale * attn_gain).astype(bf16)
    pres = [dense(normed, weight).astype(bf16) for weight in (w_query, w_key, w_value)]
    widths = [pre.shape[1] for pre in pres]
    edges = [0, widths[0], widths[0] + widths[1], sum(widths)]
    split = lambda rows: [rows[:, a:b] for a, b in zip(edges[:-1], edges[1:])]
    tail_first = token_rows - (CONV - 1)
    rims = shifted(jnp.concatenate([pre[tail_first:] for pre in pres], 1), "seq", 1)
    rims = split(jnp.pad(rims, ((HALO - (CONV - 1), 0), (0, 0))))
    alpha_pre = dense(normed, w_alpha)
    beta_pre = dense(normed, w_beta)

    def decays(alpha_pre, decay_log, decay_bias):
        rate = jnp.exp(decay_log) * jax.nn.softplus(alpha_pre + decay_bias)
        return -rate * valid_mask[:, None]

    decay, decay_pull = jax.vjp(decays, alpha_pre, local_log, local_bias)
    beta = jax.nn.sigmoid(beta_pre)
    scal, grow, fade = scalars(decay, beta, valid_mask)
    convs = [conv_query, conv_key, conv_value]
    *made, linear, local, device_pair = delta_forward(
        pres, rims, convs, scal, grow, fade, keep_flags
    )
    device_pair = device_pair.reshape(head_count, DK, WIDE)
    entry = prefix(device_pair, 1).astype(bf16).reshape(head_count * DK, DV)
    gate_pre = dense(normed, w_gate)
    gated = gated_forward(linear, local, gate_pre, entry, out_gain)
    mixed = head_scattered(plain_dense(gated, w_out, place))
    middle = cols(hidden_in).astype(f32) + mixed
    sent = head_gathered(middle.astype(bf16))
    sent32 = sent.astype(f32)
    ffn_scale = lax.rsqrt(jnp.mean(sent32 * sent32, axis=-1, keepdims=True) + epsilon_norm)
    normed_ffn = (sent32 * ffn_scale * ffn_gain).astype(bf16)
    ffn_gate_pre = dense(normed_ffn, w_ffn_gate)
    ffn_up_pre = dense(normed_ffn, w_ffn_up)
    sigmoid_gate = jax.nn.sigmoid(ffn_gate_pre)
    silu_gate = ffn_gate_pre * sigmoid_gate
    inner_act = (silu_gate * ffn_up_pre).astype(bf16)
    ffn_out = head_scattered(plain_dense(inner_act, w_ffn_down, place))
    hidden_out = (middle + ffn_out).astype(bf16)
    grad_rows = head_gathered(grad_out)
    d_inner = dense(grad_rows, w_ffn_down.T)
    grad_w_ffn_down = weight_grad(halves_of(grad_rows), inner_act)
    d_ffn_gate = (
        d_inner * ffn_up_pre * sigmoid_gate * (1.0 + ffn_gate_pre * (1.0 - sigmoid_gate))
    ).astype(bf16)
    d_ffn_up = (d_inner * silu_gate).astype(bf16)
    ffn_halves = halves_of(normed_ffn)
    grad_w_ffn_gate = weight_grad(ffn_halves, d_ffn_gate)
    grad_w_ffn_up = weight_grad(ffn_halves, d_ffn_up)
    d_normed_ffn, grad_ffn_gain, ffn_dots = norm_dense(
        [(d_ffn_gate, w_ffn_gate), (d_ffn_up, w_ffn_up)], sent, ffn_scale, ffn_gain, place
    )
    ffn_dots = head_summed(ffn_dots[:, 0])[:, None] / sent.shape[1]
    d_sent_cols = ffn_scale * (
        cols(ffn_gain) * head_scattered(d_normed_ffn) - cols(sent32) * ffn_scale * ffn_dots
    )
    d_middle = grad_out.astype(f32) + d_sent_cols
    d_mixed = head_gathered(d_middle.astype(bf16))
    d_gated = dense(d_mixed, w_out.T)
    d_delta, d_gate_pre, gain_part, entry_grad = gated_backward(
        linear, local, gate_pre, entry, out_gain, d_gated, valid_mask
    )
    grad_w_out = weight_grad(halves_of(d_mixed), gated)
    back_pair = jnp.concatenate(
        [
            jnp.swapaxes(device_pair[:, :, :DK], 1, 2),
            entry_grad.reshape(head_count, DK, DV),
        ],
        axis=2,
    )
    exit_grad = prefix(back_pair, -1).reshape(head_count * DK, DV)
    results = delta_backward(
        pres, rims, convs, scal, grow, fade, keep_flags, made, entry, exit_grad, d_delta
    )
    d_pres, conv_parts, backs, tails = (results[i : i + 3] for i in range(0, 12, 3))
    d_decay, d_beta = scalar_grads(*results[12:])
    d_alpha, grad_log_local, grad_bias_local = decay_pull(d_decay)
    d_alpha = d_alpha.astype(bf16)
    d_beta_pre = (d_beta * beta * (1.0 - beta)).astype(bf16)
    backs = shifted(jnp.concatenate(backs, 1)[8 - (CONV - 1) :], "seq", -1)
    tails = split(jnp.concatenate(tails, 1) + jnp.pad(backs, ((8 - (CONV - 1), 0), (0, 0))))
    d_query_pre, d_key_pre, d_value_pre = [
        lax.dynamic_update_slice(d_pre, tail.astype(bf16), (token_rows - 8, 0))
        for d_pre, tail in zip(d_pres, tails)
    ]
    normed_halves = halves_of(normed)
    grad_w_gate = weight_grad(normed_halves, d_gate_pre)
    grad_w_query = weight_grad(normed_halves, d_query_pre)
    grad_w_key = weight_grad(normed_halves, d_key_pre)
    grad_w_value = weight_grad(normed_halves, d_value_pre)
    small = [dense(normed.T, d_alpha).reshape(devices, -1), dense(normed.T, d_beta_pre).reshape(devices, -1)]
    for part in conv_parts:
        part = jnp.sum(part.reshape(CONV, 8, -1), axis=1).reshape(CONV, devices, -1)
        small.append(jnp.swapaxes(part, 0, 1).reshape(devices, -1))
    small = jnp.concatenate(small, axis=1)
    small_width = small.shape[1]
    odd = lax.axis_index("seq") % 2
    small = small.astype(bf16).reshape(devices // 2, 2, small_width // 128, 128)
    got = exchanged(lax.dynamic_index_in_dim(small, 1 - odd, 1, False), "seq", 1)
    small = lax.dynamic_index_in_dim(small, odd, 1, False).astype(f32) + got.astype(f32)
    small = seq_scattered(small.reshape(devices * small_width // 256, 128)).reshape(small_width)
    small_pieces = []
    for rows, width in [(normed.shape[1] // devices, head_count)] * 2 + [
        (CONV, width // devices) for width in widths
    ]:
        small_pieces.append(small[: rows * width].reshape(rows, width))
        small = small[rows * width :]
    d_normed, grad_attn_gain, attn_dots = norm_dense(
        [
            (d_query_pre, w_query),
            (d_key_pre, w_key),
            (d_value_pre, w_value),
            (d_gate_pre, w_gate),
            (d_alpha, w_alpha),
            (d_beta_pre, w_beta),
        ],
        hidden_in,
        attn_scale,
        attn_gain,
        place,
    )
    attn_dots = head_summed(attn_dots[:, 0])[:, None] / hidden_in.shape[1]
    grad_in = d_middle + attn_scale * (
        cols(attn_gain) * head_scattered(d_normed)
        - cols(hidden_in).astype(f32) * attn_scale * attn_dots
    )
    full_log = lax.dynamic_update_slice_in_dim(
        jnp.zeros(decay_log.shape, f32), grad_log_local, head_first, 0
    )
    full_bias = lax.dynamic_update_slice_in_dim(
        jnp.zeros(decay_bias.shape, f32), grad_bias_local, head_first, 0
    )
    sums = all_summed(
        jnp.concatenate(
            [jnp.sum(gain_part, 0), grad_ffn_gain[0], grad_attn_gain[0], full_log, full_bias]
        )
    )
    gain_first = out_gain.shape[0]
    attn_first = gain_first + ffn_gain.shape[0]
    log_first = attn_first + attn_gain.shape[0]
    bias_first = log_first + decay_log.shape[0]
    rows_of = lambda whole: half(whole, 0, lax.axis_index("seq"), devices)
    return (
        hidden_out,
        grad_in,
        rows_of(sums[attn_first:log_first]),
        grad_w_query,
        grad_w_key,
        grad_w_value,
        grad_w_gate,
        *small_pieces,
        sums[log_first:bias_first],
        sums[bias_first:],
        sums[:gain_first],
        grad_w_out.T,
        rows_of(sums[gain_first:attn_first]),
        grad_w_ffn_gate,
        grad_w_ffn_up,
        grad_w_ffn_down.T,
    )


def solution(mesh):
    return jax.shard_map(
        shards,
        mesh=mesh,
        in_specs=(
            P("seq", None),
            P(),
            P(),
            P(None, "head"),
            P(None, "head"),
            P(None, "head"),
            P(None, "head"),
            P(None, "head"),
            P(None, "head"),
            P(None, "head"),
            P(None, "head"),
            P(None, "head"),
            P(),
            P(),
            P(),
            P("head", None),
            P(),
            P(None, "head"),
            P(None, "head"),
            P("head", None),
            P("seq", "head"),
        ),
        out_specs=(
            P("seq", "head"),
            P("seq", "head"),
            P("seq"),
            P("seq", "head"),
            P("seq", "head"),
            P("seq", "head"),
            P("seq", "head"),
            P("seq", "head"),
            P("seq", "head"),
            P(None, ("head", "seq")),
            P(None, ("head", "seq")),
            P(None, ("head", "seq")),
            P(),
            P(),
            P(),
            P("head", "seq"),
            P("seq"),
            P("seq", "head"),
            P("seq", "head"),
            P("head", "seq"),
        ),
        check_vma=False,
    )
```

time: 1550 us -> 951 us (0.61)
  matrix products: 553 us -> 116 us
  local copies, waits for them, and re-layouts: 311 us -> 143 us
  Pallas kernels: 0 us -> 140 us
  other arithmetic: 205 us -> 72.5 us
    dot_general x123 -> x8, matrix products: 379 us -> 3.64 us  [the longest x6 2.45 us: prefix(): jnp.einsum('hij,hjk->hik', pair[:, :, :DK], before, preferred_element_typ...]
    pallas_call x0 -> x8, Pallas kernels: none -> 140 us  [the longest x1 49.5 us: delta_backward(): pl.pallas_call(functools.partial(backward_kernel, heads, groups), grid=(g...]
    dot_general x30 -> x28, matrix products: 175 us -> 112 us  [dense(): return jnp.dot(left, right, preferred_element_type=jnp.float32)]
    reshape x19 -> x12, local copies, waits for them, and re-layouts: 63.5 us -> 8.08 us  [the longest x3 4.47 us: scalars(): flat = lambda part: part.reshape(tokens, heads)]
    convert_element_type x35 -> x14, other arithmetic: 73.9 us -> 29.3 us  [the longest x6 12.5 us: seq_scattered(): return lax.psum_scatter(mine.astype(bf16), 'seq', scatter_dimension=0, ax...]
    slice x17, local copies, waits for them, and re-layouts: 42.4 us -> 9.75 us  [the longest x4 4.38 us: head_scattered(): mine[:, :width].astype(bf16)]
    reduce_sum x13 -> x6, other arithmetic: 34 us -> 2.85 us  [the longest x1 1.96 us: decays(): rate = jnp.exp(decay_log) * jax.nn.softplus(alpha_pre + decay_bias)]
    concatenate x2 -> x15, local copies, waits for them, and re-layouts: 0.08 us -> 24.9 us  [the longest x12 23.4 us: head_gathered(): jnp.concatenate([near, far], axis=1)]
  transfers between devices with their start and end apart: 60 -> 54, of which waited for: 25 -> 27; matrix products, arithmetic and copies ran while one was open for 30% -> 22% of each run, Pallas kernels for 0% -> 8%
where the time goes in v2:
time: 951 us; the launch traced here: 942 us
  waiting for transfers between devices  386 us (41%)
  local copies, waits for them, and re-layouts  143 us (15%)
  Pallas kernels  140 us (15%)
  matrix products  116 us (12%)
  other arithmetic  72.5 us (8%)
  starting transfers between devices  67.7 us (7%)
  between operations  16.5 us (2%)
    ppermute x35, waiting for transfers between devices, exchanged(): return lax.ppermute(block, axis, route)  327 us
    dot_general x28, matrix products, dense(): return jnp.dot(left, right, preferred_element_type=jnp.float32)  112 us
    unnamed x325, local copies, waits for them, and re-layouts  77.8 us
    ppermute x10, waiting for transfers between devices, shifted(): return lax.ppermute(block, axis, route)  58.8 us
    pallas_call x1, Pallas kernels, delta_backward(): pl.pallas_call(functools.partial(backward_kernel, heads, groups), grid=(g...  49.5 us
    pallas_call x1, Pallas kernels, delta_forward(): pl.pallas_call(functools.partial(forward_kernel, heads, groups), grid=(gr...  38.8 us
    ppermute x35, starting transfers between devices, exchanged(): return lax.ppermute(block, axis, route)  34.2 us
    ppermute x10, starting transfers between devices, shifted(): return lax.ppermute(block, axis, route)  32.2 us
  transfers between devices with their start and end apart: 54, of which 27 were waited for; matrix products, arithmetic and copies ran while one was open for 22% of the time, Pallas kernels for 8%

profile of v2, /device:TPU:0, one launch (start us, length us, event | category | flops | bytes accessed | tf_op | source)
XLA Modules:
  0.0 941.6 jit_solution(10165196746343509340)
XLA Ops:
  24.3 5.9 collective-permute-start
  57.5 38.8 %delta_forward.1 = (bf16[768,512]{1,0:T(8,128)(2,1)S(1)}, bf16[768,512]{1,0:T(8,128)(2,1)S(1)}, bf16[768,1024]{1,0:T(8,128)(2,1)S(1)}, bf16[12,256,384]{2,1,0:T(...) custom-call(f32[12]{0:T(128)S(1)} %copy-done.77, ...), custom_call_target="tpu_custom_call" | custom-call | flops 4000000000 | bytes 20000000 | tf_op jit(solution)/shard_map/delta_forward/pallas_call | solution.py:273
  99.7 8.1 collective-permute-done.1
  112.1 7.1 collective-permute-done.2
  119.7 6.3 collective-permute-start.3
  126.0 6.2 collective-permute-done.3
  159.7 18.7 %collective-permute-done.6 = bf16[768,512]{1,0:T(8,128)(2,1)} collective-permute-done((bf16[768,512]{1,0:T(8,128)(2,1)}, bf16[768,512]{1,0:T(8,128)(2,1)}, u32[]{:S(2)}, u32[]{:S(2)}) %collective-permute-start.6) | collective-permute-done | bytes 786464 | tf_op jit(solution)/shard_map/ppermute | solution.py:804
  183.0 12.3 %collective-permute-done.13 = bf16[768,512]{1,0:T(8,128)(2,1)} collective-permute-done((bf16[768,512]{1,0:T(8,128)(2,1)}, bf16[768,512]{1,0:T(8,128)(2,1)}, u32[]{:S(2)}, u32[]{:S(2)}) %collective-permute-start.13) | collective-permute-done | bytes 786464 | tf_op jit(solution)/shard_map/ppermute | solution.py:804
  195.8 8.3 copy.454.refs_2_
  204.1 8.3 copy.455.refs_3_
  225.4 6.8 fusion.50
  232.2 6.8 fusion.51
  239.2 12.9 %multiply_convert_fusion.2 = (bf16[768,1376]{1,0:T(8,128)(2,1)}, bf16[768,1376]{1,0:T(8,128)(2,1)}, bf16[768,1376]{1,0:T(8,128)(2,1)}) fusion(f32[768,1376]{1,0:T(8,128)} %fusion.51, f32[768,1376]{1,0:T(8,128)} %fusion.50, bf16[1376,2048]{1,0:T(8,128)(2,1)} %right_ref.3, bf16[768,512]{1,0:T(8,128)(2,1)} %get-tuple-element.274, ...), kind=kOutput, calls=%fused_computation.11 | convolution fusion | flops 4371111936 | bytes 23576576 | tf_op jit(solution)/shard_map/dot_general | solution.py:909
  262.5 13.9 %norm_dense.2 = (bf16[768,2048]{1,0:T(8,128)(2,1)S(1)}, f32[1,2048]{1,0:T(1,128)S(1)}, f32[768,1]{1,0:T(8,128)S(1)}) custom-call(s32[1]{0:T(128)} %bitcast.place_ref, bf16[768,1376]{1,0:T(8,128)(2,1)S(1)} %copy-done.84, bf16[768,1376]{1,0:T(8,128)(2,1)S(1)} %copy-done.86, bf16[2048,1376]{1,0:T(8,128)(2,1)S(1)} %copy-done.5, ...), custom_call_target="tpu_custom_call" | custom-call | flops 8657043456 | bytes 20000000 | tf_op jit(solution)/shard_map/norm_dense/pallas_call | solution.py:757
  289.4 13.5 %collective-permute-done.18 = f32[768]{0:T(1024)S(1)} collective-permute-done((f32[768]{0:T(1024)S(1)}, f32[768]{0:T(1024)S(1)}, u32[]{:S(2)}, u32[]{:S(2)}) %collective-permute-start.18) | collective-permute-done | bytes 3104 | tf_op jit(solution)/shard_map/ppermute | solution.py:804
  308.8 17.8 %collective-permute-done.20 = bf16[768,512]{1,0:T(8,128)(2,1)} collective-permute-done((bf16[768,512]{1,0:T(8,128)(2,1)}, bf16[768,512]{1,0:T(8,128)(2,1)}, u32[]{:S(2)}, u32[]{:S(2)}) %collective-permute-start.20) | collective-permute-done | bytes 786464 | tf_op jit(solution)/shard_map/ppermute | solution.py:804
  348.2 12.1 %collective-permute-done.22 = bf16[4,128,384]{2,1,0:T(8,128)(2,1)S(1)} collective-permute-done((bf16[4,128,384]{2,1,0:T(8,128)(2,1)S(1)}, bf16[4,128,384]{2,1,0:T(8,128)(2,1)S(1)}, u32[]{:S(2)}, u32[]{:S(2)}) %collective-permute-start.22) | collective-permute-done | bytes 393248 | tf_op jit(solution)/shard_map/ppermute | solution.py:799
  368.3 8.3 collective-permute-done.23
  382.3 8.1 collective-permute-done.24
  399.0 6.9 collective-permute-done.25
  406.3 49.5 %delta_backward.1 = (bf16[768,512]{1,0:T(8,128)(2,1)S(1)}, bf16[768,512]{1,0:T(8,128)(2,1)S(1)}, bf16[768,1024]{1,0:T(8,128)(2,1)S(1)}, f32[32,512]{1,0:T(8,128)...) custom-call(f32[12]{0:T(128)S(1)} %copy-done.78, ...), custom_call_target="tpu_custom_call" | custom-call | flops 8999999488 | bytes 30000000 | tf_op jit(solution)/shard_map/delta_backward/pallas_call | solution.py:532
  475.3 6.9 add_convert_fusion.1
  489.0 58.2 %collective-permute-done.42 = bf16[1024,1376]{0,1:T(8,128)(2,1)S(1)} collective-permute-done((bf16[1024,1376]{0,1:T(8,128)(2,1)S(1)}, bf16[1024,1376]{0,1:T(8,128)(2,1)S(1)}, u32[]{:S(2)}, u32[]{:S(2)}) %collective-permute-start.42) | collective-permute-done | bytes 2818080 | tf_op jit(solution)/shard_map/ppermute | solution.py:804
  570.5 57.5 %collective-permute-done.44 = bf16[1024,1376]{0,1:T(8,128)(2,1)S(1)} collective-permute-done((bf16[1024,1376]{0,1:T(8,128)(2,1)S(1)}, bf16[1024,1376]{0,1:T(8,128)(2,1)S(1)}, u32[]{:S(2)}, u32[]{:S(2)}) %collective-permute-start.44) | collective-permute-done | bytes 2818080 | tf_op jit(solution)/shard_map/ppermute | solution.py:804
  652.2 8.3 collective-permute-done.37
  675.1 18.1 %collective-permute-done.36 = bf16[1024,512]{1,0:T(8,128)(2,1)S(1)} collective-permute-done((bf16[1024,512]{1,0:T(8,128)(2,1)S(1)}, bf16[1024,512]{1,0:T(8,128)(2,1)S(1)}, u32[]{:S(2)}, u32[]{:S(2)}) %collective-permute-start.36) | collective-permute-done | bytes 1048608 | tf_op jit(solution)/shard_map/ppermute | solution.py:804
  695.3 35.2 %collective-permute-done.41 = bf16[1024,1024]{1,0:T(8,128)(2,1)} collective-permute-done((bf16[1024,1024]{1,0:T(8,128)(2,1)}, bf16[1024,1024]{1,0:T(8,128)(2,1)}, u32[]{:S(2)}, u32[]{:S(2)}) %collective-permute-start.41) | collective-permute-done | bytes 2097184 | tf_op jit(solution)/shard_map/ppermute | solution.py:804
  741.1 38.4 %collective-permute-done.39 = bf16[1024,1024]{1,0:T(8,128)(2,1)S(1)} collective-permute-done((bf16[1024,1024]{1,0:T(8,128)(2,1)S(1)}, bf16[1024,1024]{1,0:T(8,128)(2,1)S(1)}, u32[]{:S(2)}, u32[]{:S(2)}) %collective-permute-start.39) | collective-permute-done | bytes 2097184 | tf_op jit(solution)/shard_map/ppermute | solution.py:804
  795.7 7.7 plain_dense.3
  806.4 21.6 %collective-permute-done.38 = bf16[1024,1024]{1,0:T(8,128)(2,1)} collective-permute-done((bf16[1024,1024]{1,0:T(8,128)(2,1)}, bf16[1024,1024]{1,0:T(8,128)(2,1)}, u32[]{:S(2)}, u32[]{:S(2)}) %collective-permute-start.38) | collective-permute-done | bytes 2097184 | tf_op jit(solution)/shard_map/ppermute | solution.py:804
  846.7 16.2 %norm_dense.3 = (bf16[768,2048]{1,0:T(8,128)(2,1)S(1)}, f32[1,2048]{1,0:T(1,128)S(1)}, f32[768,1]{1,0:T(8,128)S(1)}) custom-call(s32[1]{0:T(128)} %bitcast.place_ref, bf16[768,512]{1,0:T(8,128)(2,1)S(1)} %copy-done.68, bf16[768,512]{1,0:T(8,128)(2,1)S(1)} %copy-done.70, bf16[768,1024]{1,0:T(8,128)(2,1)S(1)} %copy-done.64, bf16[768,1024]{1,0:T(8,128)(2,1)S(1)} %copy-done.61, ...), custom_call_target="tpu_custom_call" | custom-call | flops 9688842240 | bytes 20000000 | tf_op jit(solution)/shard_map/norm_dense/pallas_call | solution.py:757
  897.5 14.1 %collective-permute-done.28 = bf16[768,512]{1,0:T(8,128)(2,1)} collective-permute-done((bf16[768,512]{1,0:T(8,128)(2,1)}, bf16[768,512]{1,0:T(8,128)(2,1)}, u32[]{:S(2)}, u32[]{:S(2)}) %collective-permute-start.28) | collective-permute-done | bytes 786464 | tf_op jit(solution)/shard_map/ppermute | solution.py:804
  (618 shorter events, 366.2 us)
Async XLA Ops:
  7.2 880.4 %reduce-scatter.28.cloned.1.call-start = ((), (), s32[]{:S(2)}) async-start(), calls=%async_computation.17 | async-start | bytes 30720
  24.3 22.9 %collective-permute-start = (bf16[3,2048]{1,0:T(4,128)(2,1)}, bf16[3,2048]{1,0:T(4,128)(2,1)}, u32[]{:S(2)}, u32[]{:S(2)}) collective-permute-start(bf16[3,2048]{1,0:T(4,128)(2,1)} %pad_maximum_fusion.7), channel_id=1, source_target_pairs={{0,4},{4,8},{8,12},{12,16},{16,20},{20,24},{24,28},{1,5},{5,9},{9,... | collective-permute-start | bytes 36872 | tf_op jit(solution)/shard_map/ppermute | solution.py:799
  157.7 20.7 %collective-permute-start.6 = (bf16[768,512]{1,0:T(8,128)(2,1)}, bf16[768,512]{1,0:T(8,128)(2,1)}, u32[]{:S(2)}, u32[]{:S(2)}) collective-permute-start(bf16[768,512]{1,0:T(8,128)(2,1)} %slice.414), channel_id=1, source_target_pairs={{0,2},{1,3},{2,0},{3,1},{4,6},{5,7},{6,4},{7,5},{8,10},{9,11},{10,... | collective-permute-start | bytes 2359304 | tf_op jit(solution)/shard_map/ppermute | solution.py:804
  159.2 36.0 %collective-permute-start.13 = (bf16[768,512]{1,0:T(8,128)(2,1)}, bf16[768,512]{1,0:T(8,128)(2,1)}, u32[]{:S(2)}, u32[]{:S(2)}) collective-permute-start(bf16[768,512]{1,0:T(8,128)(2,1)} %param.41), channel_id=1, source_target_pairs={{0,2},{1,3},{2,0},{3,1},{4,6},{5,7},{6,4},{7,5},{8,10},{9,11},{10,... | collective-permute-start | bytes 2359304 | tf_op jit(solution)/shard_map/ppermute | solution.py:804
  181.5 31.0 %collective-permute-start.8 = (bf16[768,512]{1,0:T(8,128)(2,1)}, bf16[768,512]{1,0:T(8,128)(2,1)}, u32[]{:S(2)}, u32[]{:S(2)}) collective-permute-start(bf16[768,512]{1,0:T(8,128)(2,1)} %fusion.52), channel_id=1, source_target_pairs={{0,2},{1,3},{2,0},{3,1},{4,6},{5,7},{6,4},{7,5},{8,10},{9,11},{10,... | collective-permute-start | bytes 2359304 | tf_op jit(solution)/shard_map/ppermute | solution.py:804
  183.0 29.5 %collective-permute-start.12 = (bf16[768,512]{1,0:T(8,128)(2,1)}, bf16[768,512]{1,0:T(8,128)(2,1)}, u32[]{:S(2)}, u32[]{:S(2)}) collective-permute-start(bf16[768,512]{1,0:T(8,128)(2,1)} %param.41), channel_id=1, source_target_pairs={{0,1},{1,0},{2,3},{3,2},{4,5},{5,4},{6,7},{7,6},{8,9},{9,8},{10,11... | collective-permute-start | bytes 2359304 | tf_op jit(solution)/shard_map/ppermute | solution.py:804
  195.3 19.5 %collective-permute-start.14 = (bf16[768,512]{1,0:T(8,128)(2,1)}, bf16[768,512]{1,0:T(8,128)(2,1)}, u32[]{:S(2)}, u32[]{:S(2)}) collective-permute-start(bf16[768,512]{1,0:T(8,128)(2,1)} %collective-permute-done.13), channel_id=1, source_target_pairs={{0,1},{1,0},{2,3},{3,2},{4,5},{5,4},{6,7},{7,6},{8,9},{9,8},{10,11... | collective-permute-start | bytes 2359304 | tf_op jit(solution)/shard_map/ppermute | solution.py:804
  195.3 22.4 %collective-permute-start.7 = (bf16[768,512]{1,0:T(8,128)(2,1)}, bf16[768,512]{1,0:T(8,128)(2,1)}, u32[]{:S(2)}, u32[]{:S(2)}) collective-permute-start(bf16[768,512]{1,0:T(8,128)(2,1)} %fusion.52), channel_id=1, source_target_pairs={{0,1},{1,0},{2,3},{3,2},{4,5},{5,4},{6,7},{7,6},{8,9},{9,8},{10,11... | collective-permute-start | bytes 2359304 | tf_op jit(solution)/shard_map/ppermute | solution.py:804
  282.8 20.2 %collective-permute-start.16 = (bf16[768,512]{1,0:T(8,128)(2,1)}, bf16[768,512]{1,0:T(8,128)(2,1)}, u32[]{:S(2)}, u32[]{:S(2)}) collective-permute-start(bf16[768,512]{1,0:T(8,128)(2,1)} %slice.412), channel_id=1, source_target_pairs={{0,2},{1,3},{2,0},{3,1},{4,6},{5,7},{6,4},{7,5},{8,10},{9,11},{10,... | collective-permute-start | bytes 2359304 | tf_op jit(solution)/shard_map/ppermute | solution.py:804
  307.2 19.4 %collective-permute-start.20 = (bf16[768,512]{1,0:T(8,128)(2,1)}, bf16[768,512]{1,0:T(8,128)(2,1)}, u32[]{:S(2)}, u32[]{:S(2)}) collective-permute-start(bf16[768,512]{1,0:T(8,128)(2,1)} %get-tuple-element.250), channel_id=1, source_target_pairs={{0,2},{1,3},{2,0},{3,1},{4,6},{5,7},{6,4},{7,5},{8,10},{9,11},{10,... | collective-permute-start | bytes 2359304 | tf_op jit(solution)/shard_map/ppermute | solution.py:804
  308.8 21.0 %collective-permute-start.19 = (bf16[768,512]{1,0:T(8,128)(2,1)}, bf16[768,512]{1,0:T(8,128)(2,1)}, u32[]{:S(2)}, u32[]{:S(2)}) collective-permute-start(bf16[768,512]{1,0:T(8,128)(2,1)} %get-tuple-element.250), channel_id=1, source_target_pairs={{0,1},{1,0},{2,3},{3,2},{4,5},{5,4},{6,7},{7,6},{8,9},{9,8},{10,11... | collective-permute-start | bytes 2359304 | tf_op jit(solution)/shard_map/ppermute | solution.py:804
  360.3 16.3 %collective-permute-start.23 = (bf16[4,128,384]{2,1,0:T(8,128)(2,1)S(1)}, bf16[4,128,384]{2,1,0:T(8,128)(2,1)}, u32[]{:S(2)}, u32[]{:S(2)}) collective-permute-start(bf16[4,128,384]{2,1,0:T(8,128)(2,1)S(1)} %collective-permute-done.22), channel_id=1, source_target_pairs={{4,0},{8,4},{12,8},{16,12},{20,16},{24,20},{28,24},{5,1},{9,5},{13... | collective-permute-start | bytes 1179656 | tf_op jit(solution)/shard_map/ppermute | solution.py:799
  396.7 78.7 %collective-permute-start.43 = (bf16[1024,1376]{0,1:T(8,128)(2,1)}, bf16[1024,1376]{0,1:T(8,128)(2,1)}, u32[]{:S(2)}, u32[]{:S(2)}) collective-permute-start(bf16[1024,1376]{0,1:T(8,128)(2,1)} %convolution_convert_fusion.1), channel_id=1, source_target_pairs={{0,4},{4,0},{8,12},{12,8},{16,20},{20,16},{24,28},{28,24},{1,5},{5... | collective-permute-start | bytes 8454152 | tf_op jit(solution)/shard_map/ppermute | solution.py:804
  475.1 442.2 %reduce-scatter.24.cloned.1.call-start = ((), (), s32[]{:S(2)}) async-start(), calls=%async_computation.15 | async-start | bytes 3522560 | tf_op jit(solution)/shard_map/reduce_scatter | solution.py:870
  482.3 437.3 %reduce-scatter.22.cloned.1.call-start = ((), (), s32[]{:S(2)}) async-start(), calls=%async_computation.14 | async-start | bytes 3522560 | tf_op jit(solution)/shard_map/reduce_scatter | solution.py:870
  487.0 60.3 %collective-permute-start.42 = (bf16[1024,1376]{0,1:T(8,128)(2,1)S(1)}, bf16[1024,1376]{0,1:T(8,128)(2,1)S(1)}, u32[]{:S(2)}, u32[]{:S(2)}) collective-permute-start(bf16[1024,1376]{0,1:T(8,128)(2,1)S(1)} %convolution_convert_fusion.2), channel_id=1, source_target_pairs={{0,4},{4,0},{8,12},{12,8},{16,20},{20,16},{24,28},{28,24},{1,5},{5... | collective-permute-start | bytes 8454152 | tf_op jit(solution)/shard_map/ppermute | solution.py:804
  551.5 370.4 %reduce-scatter.26.cloned.1.call-start = ((), (), s32[]{:S(2)}) async-start(), calls=%async_computation.16 | async-start | bytes 3522560 | tf_op jit(solution)/shard_map/reduce_scatter | solution.py:870
  568.7 59.3 %collective-permute-start.44 = (bf16[1024,1376]{0,1:T(8,128)(2,1)S(1)}, bf16[1024,1376]{0,1:T(8,128)(2,1)S(1)}, u32[]{:S(2)}, u32[]{:S(2)}) collective-permute-start(bf16[1024,1376]{0,1:T(8,128)(2,1)S(1)} %convolution_convert_fusion), channel_id=1, source_target_pairs={{0,4},{4,0},{8,12},{12,8},{16,20},{20,16},{24,28},{28,24},{1,5},{5... | collective-permute-start | bytes 8454152 | tf_op jit(solution)/shard_map/ppermute | solution.py:804
  632.1 292.1 %reduce-scatter.14.cloned.1.call-start = ((), (), s32[]{:S(2)}) async-start(), calls=%async_computation.10 | async-start | bytes 1310720 | tf_op jit(solution)/shard_map/reduce_scatter | solution.py:870
  640.3 20.1 %collective-permute-start.37 = (bf16[1024,512]{1,0:T(8,128)(2,1)}, bf16[1024,512]{1,0:T(8,128)(2,1)}, u32[]{:S(2)}, u32[]{:S(2)}) collective-permute-start(bf16[1024,512]{1,0:T(8,128)(2,1)} %convolution_convert_fusion.9), channel_id=1, source_target_pairs={{0,4},{4,0},{8,12},{12,8},{16,20},{20,16},{24,28},{28,24},{1,5},{5... | collective-permute-start | bytes 3145736 | tf_op jit(solution)/shard_map/ppermute | solution.py:804
  664.2 261.8 %reduce-scatter.12.cloned.1.call-start = ((), (), s32[]{:S(2)}) async-start(), calls=%async_computation.9 | async-start | bytes 1310720 | tf_op jit(solution)/shard_map/reduce_scatter | solution.py:870
  667.0 26.2 %collective-permute-start.36 = (bf16[1024,512]{1,0:T(8,128)(2,1)S(1)}, bf16[1024,512]{1,0:T(8,128)(2,1)S(1)}, u32[]{:S(2)}, u32[]{:S(2)}) collective-permute-start(bf16[1024,512]{1,0:T(8,128)(2,1)S(1)} %convolution_convert_fusion.10), channel_id=1, source_target_pairs={{0,4},{4,0},{8,12},{12,8},{16,20},{20,16},{24,28},{28,24},{1,5},{5... | collective-permute-start | bytes 3145736 | tf_op jit(solution)/shard_map/ppermute | solution.py:804
  674.8 55.6 %collective-permute-start.41 = (bf16[1024,1024]{1,0:T(8,128)(2,1)}, bf16[1024,1024]{1,0:T(8,128)(2,1)}, u32[]{:S(2)}, u32[]{:S(2)}) collective-permute-start(bf16[1024,1024]{1,0:T(8,128)(2,1)} %convolution_convert_fusion.5), channel_id=1, source_target_pairs={{0,4},{4,0},{8,12},{12,8},{16,20},{20,16},{24,28},{28,24},{1,5},{5... | collective-permute-start | bytes 6291464 | tf_op jit(solution)/shard_map/ppermute | solution.py:804
  695.2 232.6 %reduce-scatter.20.cloned.1.call-start = ((), (), s32[]{:S(2)}) async-start(), calls=%async_computation.13 | async-start | bytes 2621440 | tf_op jit(solution)/shard_map/reduce_scatter | solution.py:870
  735.7 194.6 %reduce-scatter.18.cloned.1.call-start = ((), (), s32[]{:S(2)}) async-start(), calls=%async_computation.12 | async-start | bytes 2621440 | tf_op jit(solution)/shard_map/reduce_scatter | solution.py:870
  739.6 39.9 %collective-permute-start.39 = (bf16[1024,1024]{1,0:T(8,128)(2,1)S(1)}, bf16[1024,1024]{1,0:T(8,128)(2,1)S(1)}, u32[]{:S(2)}, u32[]{:S(2)}) collective-permute-start(bf16[1024,1024]{1,0:T(8,128)(2,1)S(1)} %convolution_convert_fusion.6), channel_id=1, source_target_pairs={{0,4},{4,0},{8,12},{12,8},{16,20},{20,16},{24,28},{28,24},{1,5},{5... | collective-permute-start | bytes 6291464 | tf_op jit(solution)/shard_map/ppermute | solution.py:804
  782.6 149.8 %reduce-scatter.16.cloned.1.call-start = ((), (), s32[]{:S(2)}) async-start(), calls=%async_computation.11 | async-start | bytes 2621440 | tf_op jit(solution)/shard_map/reduce_scatter | solution.py:870
  788.7 39.3 %collective-permute-start.38 = (bf16[1024,1024]{1,0:T(8,128)(2,1)}, bf16[1024,1024]{1,0:T(8,128)(2,1)}, u32[]{:S(2)}, u32[]{:S(2)}) collective-permute-start(bf16[1024,1024]{1,0:T(8,128)(2,1)} %convolution_convert_fusion.7), channel_id=1, source_target_pairs={{0,4},{4,0},{8,12},{12,8},{16,20},{20,16},{24,28},{28,24},{1,5},{5... | collective-permute-start | bytes 6291464 | tf_op jit(solution)/shard_map/ppermute | solution.py:804
  806.4 65.1 %collective-permute-start.10 = (bf16[768,1024]{1,0:T(8,128)(2,1)}, bf16[768,1024]{1,0:T(8,128)(2,1)}, u32[]{:S(2)}, u32[]{:S(2)}) collective-permute-start(bf16[768,1024]{1,0:T(8,128)(2,1)} %slice.284), channel_id=1, source_target_pairs={{0,1},{1,0},{2,3},{3,2},{4,5},{5,4},{6,7},{7,6},{8,9},{9,8},{10,11... | collective-permute-start | bytes 4718600 | tf_op jit(solution)/shard_map/ppermute | solution.py:804
  865.9 16.9 %collective-permute-start.27 = (bf16[768,1024]{1,0:T(8,128)(2,1)}, bf16[768,1024]{1,0:T(8,128)(2,1)}, u32[]{:S(2)}, u32[]{:S(2)}) collective-permute-start(bf16[768,1024]{1,0:T(8,128)(2,1)} %slice.256), channel_id=1, source_target_pairs={{0,1},{1,0},{2,3},{3,2},{4,5},{5,4},{6,7},{7,6},{8,9},{9,8},{10,11... | collective-permute-start | bytes 4718600 | tf_op jit(solution)/shard_map/ppermute | solution.py:804
  875.3 22.1 %collective-permute-start.11 = (bf16[768,512]{1,0:T(8,128)(2,1)}, bf16[768,512]{1,0:T(8,128)(2,1)}, u32[]{:S(2)}, u32[]{:S(2)}) collective-permute-start(bf16[768,512]{1,0:T(8,128)(2,1)} %slice.413), channel_id=1, source_target_pairs={{0,2},{1,3},{2,0},{3,1},{4,6},{5,7},{6,4},{7,5},{8,10},{9,11},{10,... | collective-permute-start | bytes 2359304 | tf_op jit(solution)/shard_map/ppermute | solution.py:804
  886.9 24.7 %collective-permute-start.28 = (bf16[768,512]{1,0:T(8,128)(2,1)}, bf16[768,512]{1,0:T(8,128)(2,1)}, u32[]{:S(2)}, u32[]{:S(2)}) collective-permute-start(bf16[768,512]{1,0:T(8,128)(2,1)} %slice.411), channel_id=1, source_target_pairs={{0,2},{1,3},{2,0},{3,1},{4,6},{5,7},{6,4},{7,5},{8,10},{9,11},{10,... | collective-permute-start | bytes 2359304 | tf_op jit(solution)/shard_map/ppermute | solution.py:804
  (178 other events, 1905.0 us)
Sparse Core Ops, SparseCore 0:
  475.2 17.3 reduce-scatter.27
  495.1 53.3 reduce-scatter.23
  551.6 54.1 reduce-scatter.21
  632.3 53.4 reduce-scatter.25
  688.4 26.9 reduce-scatter.13
  718.2 25.7 reduce-scatter.11
  746.3 42.4 reduce-scatter.19
  791.3 43.1 reduce-scatter.17
  836.7 43.2 reduce-scatter.15

commit v3 on v2

--- a/solution.py
+++ b/solution.py
@@ -13,6 +13,8 @@
 CONV = 4
 HALO = 16
 WIDE = DK + DV
+VMEM = 60 * 2**20
+SMALL = 30 * 2**20
 
 epsilon_norm = 1e-06
 epsilon_gate = 1e-05
@@ -108,20 +110,53 @@
     return total
 
 
-def decay_terms(scal, grow, heads):
-    growth = [scal[:, h : h + 1] for h in range(heads)]
-    betas = [scal[:, heads + h : heads + h + 1] for h in range(heads)]
+def summed_rows(mask, values, pieces=3):
+    parts = []
+    for _ in range(pieces):
+        parts.append(values.astype(bf16))
+        values = values - parts[-1].astype(f32)
+    width = values.shape[1]
+    sums = contract(mask.astype(bf16), jnp.concatenate(parts, axis=1))
+    return sum(sums[:, i * width : (i + 1) * width] for i in range(pieces))
+
+
+def token_terms(scal_ref, rate_ref, heads):
+    scal = scal_ref[...]
+    rate = rate_ref[...]
+    shifted_alpha = scal[:, :heads] + rate[1:2]
+    valid = scal[:, 2 * heads : 2 * heads + 1]
+    decay = -rate[0:1] * jax.nn.softplus(shifted_alpha) * valid
+    beta = jax.nn.sigmoid(scal[:, heads : 2 * heads])
     row = lax.broadcasted_iota(jnp.int32, (GROUP, heads * GROUP), 0)
     lane = lax.broadcasted_iota(jnp.int32, (GROUP, heads * GROUP), 1) % GROUP
+    wide = spread([decay[:, h : h + 1] for h in range(heads)], heads)
+    square_row = lax.broadcasted_iota(jnp.int32, (GROUP, GROUP), 0)
+    square_lane = lax.broadcasted_iota(jnp.int32, (GROUP, GROUP), 1)
+    sums = summed_rows(jnp.where(square_row >= square_lane, 1.0, 0.0), wide)
+    across = jnp.sum(jnp.where(row <= lane, wide, 0.0), axis=0, keepdims=True)
     lower, strict = (row >= lane, row > lane)
-    gap = spread(growth, heads) - grow
-    ratio = jnp.where(lower, jnp.exp(jnp.where(lower, gap, 0.0)), 0.0)
-    return ratio, spread(betas, heads), strict
-
-
-def column_stack(scal, kind, heads):
-    return jnp.concatenate(
-        [scal[:, kind * heads + h : kind * heads + h + 1] for h in range(heads)], axis=0
+    ratio = jnp.where(lower, jnp.exp(jnp.where(lower, sums - across, 0.0)), 0.0)
+    betas = [beta[:, h : h + 1] for h in range(heads)]
+    last = sums[GROUP - 1 :]
+    grown, closing = (jnp.exp(sums), jnp.exp(last - sums))
+    column = lambda values: jnp.concatenate(
+        [values[:, h * GROUP : h * GROUP + 1] for h in range(heads)], axis=0
+    )
+    fade = jnp.exp(last)
+    fades = [fade[:, h * GROUP : h * GROUP + 1] for h in range(heads)]
+    return dict(
+        alpha=shifted_alpha,
+        rate=rate[0:1],
+        valid=valid,
+        decay=decay,
+        beta=beta,
+        ratio=ratio,
+        strict=strict,
+        betas=spread(betas, heads),
+        beta_column=jnp.concatenate(betas, axis=0),
+        growth=column(grown),
+        closing=column(closing),
+        fades=fades,
     )
 
 
@@ -129,7 +164,6 @@
     heads,
     groups,
     keep_ref,
-    fade_ref,
     query_ref,
     key_ref,
     value_ref,
@@ -143,7 +177,7 @@
     conv_key,
     conv_value,
     scal_ref,
-    grow_ref,
+    rate_ref,
     query_out,
     key_out,
     value_out,
@@ -173,8 +207,8 @@
     fill(ext_query, query_ref, query_before, query_rim, first, keep)
     fill(ext_key, key_ref, key_before, key_rim, first, keep)
     fill(ext_value, value_ref, value_before, value_rim, first, keep)
-    scal = scal_ref[...]
-    valid = scal[:, 4 * heads : 4 * heads + 1]
+    terms = token_terms(scal_ref, rate_ref, heads)
+    valid = terms["valid"]
     queries, keys, values = ([], [], [])
     for h in range(heads):
         act = jax.nn.silu(tap_sum(ext_query, conv_query, h * DK, DK))
@@ -194,13 +228,11 @@
     scores = contract(jnp.concatenate([query, key], axis=0), key, 1, 1)
     mix = packed(scores[: heads * GROUP], heads)
     similar = packed(scores[heads * GROUP :], heads)
-    ratio, betas, strict = decay_terms(scal, grow_ref[0], heads)
+    ratio, betas, strict = (terms["ratio"], terms["betas"], terms["strict"])
     mixing = diagonal(ratio * mix, heads)
     inverse = packed_inverse(jnp.where(strict, betas * ratio * similar, 0.0), heads).astype(bf16)
     inverse_out[...] = inverse
-    beta = column_stack(scal, 1, heads)
-    growth = column_stack(scal, 2, heads)
-    closing = column_stack(scal, 3, heads)
+    beta, growth, closing = (terms["beta_column"], terms["growth"], terms["closing"])
     key_wide = key.astype(f32)
     right = jnp.concatenate([beta * growth * key_wide, beta * value.astype(f32)], axis=1)
     wu = contract(diagonal(inverse, heads), right.astype(bf16))
@@ -217,7 +249,7 @@
         state_out[0, pl.ds(h * DK, DK), :] = used_low
         part = jnp.where(lane >= DK, wu[rows], 0.0) - contract(wu_low[rows, :DK], used_low)
         part = part.astype(bf16)
-        after = fade_ref[group * heads + h] * used + contract(fading[rows], part, 0, 0)
+        after = terms["fades"][h] * used + contract(fading[rows], part, 0, 0)
         state[pl.ds(h * DK, DK), :] = after
         fresh.append(part)
         seen.append(contract(grown[rows], used_low))
@@ -249,36 +281,20 @@
     return pl.BlockSpec(shape, lambda g: (0,) * len(shape))
 
 
-def scalars(decay, beta, valid):
-    tokens, heads = decay.shape
-    groups = tokens // GROUP
-    ones = jnp.tril(jnp.ones((GROUP, GROUP), f32))
-    sums = jnp.einsum(
-        "ij,gjh->gih", ones, decay.reshape(groups, GROUP, heads), precision=lax.Precision.HIGHEST
-    )
-    last = sums[:, -1:, :]
-    flat = lambda part: part.reshape(tokens, heads)
-    scal = jnp.concatenate(
-        [flat(sums), beta, flat(jnp.exp(sums)), flat(jnp.exp(last - sums)), valid[:, None]], axis=1
-    )
-    grow = jnp.swapaxes(sums, 1, 2).reshape(groups, 1, heads * GROUP)
-    return scal, grow, jnp.exp(last[:, 0, :])
-
-
-def delta_forward(pres, rims, convs, scal, grow, fade, keep):
+def delta_forward(pres, rims, convs, scal, rate, keep):
     tokens = scal.shape[0]
-    heads, groups = (fade.shape[1], tokens // GROUP)
+    heads, groups = (rate.shape[1], tokens // GROUP)
     widths = [pre.shape[1] for pre in pres]
     smem = pl.BlockSpec(memory_space=pltpu.SMEM)
     return pl.pallas_call(
         functools.partial(forward_kernel, heads, groups),
         grid=(groups,),
-        in_specs=[smem, smem]
+        in_specs=[smem]
         + [token_block(w) for w in widths]
         + [before_block(w) for w in widths]
         + [whole((HALO, w)) for w in widths]
         + [whole((CONV, w)) for w in widths]
-        + [token_block(scal.shape[1]), pl.BlockSpec((1, 1, heads * GROUP), lambda g: (g, 0, 0))],
+        + [token_block(scal.shape[1]), whole(rate.shape)],
         out_specs=[token_block(w) for w in widths]
         + [
             pl.BlockSpec((1, heads * GROUP, WIDE), lambda g: (g, 0, 0)),
@@ -299,17 +315,16 @@
         ],
         scratch_shapes=[pltpu.VMEM((heads * DK, WIDE), f32)]
         + [pltpu.VMEM((HALO + GROUP, w), f32) for w in widths],
-        compiler_params=pltpu.CompilerParams(vmem_limit_bytes=40 * 2**20),
-        cost_estimate=pl.CostEstimate(flops=4 * 10**9, bytes_accessed=2 * 10**7, transcendentals=0),
+        compiler_params=pltpu.CompilerParams(vmem_limit_bytes=VMEM),
+        cost_estimate=pl.CostEstimate(flops=10**6, bytes_accessed=10**4, transcendentals=0),
         name="delta_forward",
-    )(keep, fade.reshape(-1), *pres, *pres, *rims, *convs, scal, grow)
+    )(keep, *pres, *pres, *rims, *convs, scal, rate)
 
 
 def backward_kernel(
     heads,
     groups,
     keep_ref,
-    fade_ref,
     query_pre,
     key_pre,
     value_pre,
@@ -323,7 +338,7 @@
     conv_key,
     conv_value,
     scal_ref,
-    grow_ref,
+    rate_ref,
     query_ref,
     key_ref,
     value_ref,
@@ -346,7 +361,7 @@
     key_tail_out,
     value_tail_out,
     scal_out,
-    row_out,
+    rate_out,
     carry,
     ext_query,
     ext_key,
@@ -364,14 +379,12 @@
         carry[...] = exit_ref[...]
         for ref in (dy_query, dy_key, dy_value):
             ref[...] = jnp.zeros_like(ref)
-        for ref in (query_conv_out, key_conv_out, value_conv_out):
+        for ref in (query_conv_out, key_conv_out, value_conv_out, rate_out):
             ref[...] = jnp.zeros_like(ref)
 
-    scal = scal_ref[...]
-    valid = scal[:, 4 * heads : 4 * heads + 1]
-    beta = column_stack(scal, 1, heads)
-    growth = column_stack(scal, 2, heads)
-    closing = column_stack(scal, 3, heads)
+    terms = token_terms(scal_ref, rate_ref, heads)
+    valid = terms["valid"]
+    beta, growth, closing = (terms["beta_column"], terms["growth"], terms["closing"])
     query = stacked(query_ref[...], heads)
     key = stacked(key_ref[...], heads)
     value = stacked(value_ref[...], heads)
@@ -380,7 +393,7 @@
     scores = contract(jnp.concatenate([query, key], axis=0), key, 1, 1)
     mix = packed(scores[: heads * GROUP], heads)
     similar = packed(scores[heads * GROUP :], heads)
-    ratio, betas, strict = decay_terms(scal, grow_ref[0], heads)
+    ratio, betas, strict = (terms["ratio"], terms["betas"], terms["strict"])
     mixing = ratio * mix
     wu = wu_ref[0]
     grown_wide = growth * query_wide
@@ -388,7 +401,7 @@
     grown = grown_wide.astype(bf16)
     fading = fading_wide.astype(bf16)
     mixed_back = contract(diagonal(mixing, heads), grad, 0, 0)
-    fresh, d_fresh, d_grown, d_fading, d_weights = ([], [], [], [], [])
+    fresh, d_fresh, d_grown, d_fading, d_weights, d_fades = ([], [], [], [], [], [])
     for h in range(heads):
         rows = slice(h * GROUP, (h + 1) * GROUP)
         states = pl.ds(h * DK, DK)
@@ -406,14 +419,13 @@
         d_grown.append(seen[:GROUP])
         d_weights.append(-seen[GROUP:])
         d_fading.append(contract(part, after_low, 1, 1))
-        fade = fade_ref[group * heads + h]
+        fade = terms["fades"][h]
         carry[states, :] = keep * (
             fade * after
             + contract(jnp.concatenate([grown[rows], -weights], axis=0), stack, 0, 0)
         )
-        row_out[0, heads + h : heads + h + 1, :] = fade * jnp.sum(
-            after * used, axis=0, keepdims=True
-        )
+        d_fade = jnp.sum(after * used, axis=0, keepdims=True)
+        d_fades.append(fade * jnp.sum(d_fade, axis=1, keepdims=True))
         fresh.append(part)
         d_fresh.append(d_part_low)
     d_grown = jnp.concatenate(d_grown, axis=0)
@@ -453,18 +465,37 @@
     sum_beta = jnp.sum(
         d_scaled * grown_key + value_flow[:, :DK] + value_flow[:, DK:], axis=1, keepdims=True
     )
-    row_out[0, 0:1, :] = jnp.sum(flows, axis=0, keepdims=True)
+    flow_high, flow_low = halves(flows)
+    ones = jnp.full((GROUP, 128), 1.0, bf16)
+    turned_flow = contract(
+        jnp.concatenate([flow_high, flow_low], axis=0),
+        jnp.concatenate([ones, ones], axis=0),
+        0,
+        0,
+    )[:, :1]
     owner = lane_heads(heads)
-    lane = lax.broadcasted_iota(jnp.int32, (GROUP, scal_out.shape[1]), 1)
-    columns = jnp.zeros((GROUP, scal_out.shape[1]), f32)
+    lane = lax.broadcasted_iota(jnp.int32, (GROUP, 128), 1)
+    d_sums = jnp.zeros((GROUP, 128), f32)
+    d_beta = jnp.zeros((GROUP, 128), f32)
+    d_last = jnp.zeros((1, 128), f32)
     for h in range(heads):
         rows = slice(h * GROUP, (h + 1) * GROUP)
         flow = jnp.sum(jnp.where(owner == h, flows, 0.0), axis=1, keepdims=True)
         more = jnp.sum(jnp.where(owner == h, ratio_similar, 0.0), axis=1, keepdims=True)
-        columns = jnp.where(lane == h, sum_growth[rows] + flow, columns)
-        columns = jnp.where(lane == heads + h, sum_beta[rows] + more, columns)
-        columns = jnp.where(lane == 2 * heads + h, sum_fading[rows], columns)
-    scal_out[...] = columns
+        d_sums = jnp.where(lane == h, sum_growth[rows] + flow - turned_flow[rows], d_sums)
+        d_beta = jnp.where(lane == h, sum_beta[rows] + more, d_beta)
+        total = jnp.sum(sum_fading[rows], axis=0, keepdims=True) + d_fades[h]
+        d_last = jnp.where(lane[:1] == h, total, d_last)
+    square_row = lax.broadcasted_iota(jnp.int32, (GROUP, GROUP), 0)
+    square_lane = lax.broadcasted_iota(jnp.int32, (GROUP, GROUP), 1)
+    later = jnp.where(square_row <= square_lane, 1.0, 0.0)
+    d_decay = (summed_rows(later, d_sums) + d_last)[:, :heads]
+    d_beta = d_beta[:, :heads]
+    d_alpha = -d_decay * terms["rate"] * jax.nn.sigmoid(terms["alpha"]) * valid
+    d_beta = d_beta * terms["beta"] * (1.0 - terms["beta"])
+    scal_out[...] = jnp.concatenate([d_alpha, d_beta], axis=1).astype(bf16)
+    rate_out[0:1, :] += jnp.sum(d_decay * terms["decay"], axis=0, keepdims=True)
+    rate_out[1:2, :] += jnp.sum(d_alpha, axis=0, keepdims=True)
 
     first = group == 0
     after_keep = jnp.where(step == 0, 0.0, keep_ref[jnp.minimum(group + 1, groups - 1)])
@@ -522,22 +553,22 @@
                 back_out[:, lanes] = d_back * keep
 
 
-def delta_backward(pres, rims, convs, scal, grow, fade, keep, made, entry, exit_grad, grad):
+def delta_backward(pres, rims, convs, scal, rate, keep, made, entry, exit_grad, grad):
     tokens = scal.shape[0]
-    heads, groups = (fade.shape[1], tokens // GROUP)
+    heads, groups = (rate.shape[1], tokens // GROUP)
     widths = [pre.shape[1] for pre in pres]
     smem = pl.BlockSpec(memory_space=pltpu.SMEM)
     turn = lambda *shape: pl.BlockSpec(shape, lambda g: (groups - 1 - g, 0, 0))
-    columns = 3 * heads
+    columns = 2 * heads
     return pl.pallas_call(
         functools.partial(backward_kernel, heads, groups),
         grid=(groups,),
-        in_specs=[smem, smem]
+        in_specs=[smem]
         + [token_block(w, groups) for w in widths]
         + [before_block(w, groups) for w in widths]
         + [whole((HALO, w)) for w in widths]
         + [whole((CONV, w)) for w in widths]
-        + [token_block(scal.shape[1], groups), turn(1, 1, heads * GROUP)]
+        + [token_block(scal.shape[1], groups), whole(rate.shape)]
         + [token_block(w, groups) for w in widths]
         + [
             turn(1, heads * GROUP, WIDE),
@@ -551,35 +582,22 @@
         + [whole((CONV * 8, w)) for w in widths]
         + [whole((8, w)) for w in widths]
         + [whole((8, w)) for w in widths]
-        + [token_block(columns, groups), turn(1, 2 * heads, heads * GROUP)],
+        + [token_block(columns, groups), whole((8, heads))],
         out_shape=[jax.ShapeDtypeStruct((tokens, w), bf16) for w in widths]
         + [jax.ShapeDtypeStruct((CONV * 8, w), f32) for w in widths]
         + [jax.ShapeDtypeStruct((8, w), f32) for w in widths]
         + [jax.ShapeDtypeStruct((8, w), f32) for w in widths]
         + [
-            jax.ShapeDtypeStruct((tokens, columns), f32),
-            jax.ShapeDtypeStruct((groups, 2 * heads, heads * GROUP), f32),
+            jax.ShapeDtypeStruct((tokens, columns), bf16),
+            jax.ShapeDtypeStruct((8, heads), f32),
         ],
         scratch_shapes=[pltpu.VMEM((heads * DK, DV), f32)]
         + [pltpu.VMEM((HALO + GROUP, w), f32) for w in widths]
         + [pltpu.VMEM((16 + GROUP, w), f32) for w in widths],
-        compiler_params=pltpu.CompilerParams(vmem_limit_bytes=40 * 2**20),
-        cost_estimate=pl.CostEstimate(flops=9 * 10**9, bytes_accessed=3 * 10**7, transcendentals=0),
+        compiler_params=pltpu.CompilerParams(vmem_limit_bytes=VMEM),
+        cost_estimate=pl.CostEstimate(flops=10**6, bytes_accessed=10**4, transcendentals=0),
         name="delta_backward",
-    )(keep, fade.reshape(-1), *pres, *pres, *rims, *convs, scal, grow, *made, entry, exit_grad, grad)
-
-
-def scalar_grads(columns, rows):
-    groups, heads = (rows.shape[0], columns.shape[1] // 3)
-    parts = columns.reshape(groups, GROUP, 3, heads)
-    turned = jnp.swapaxes(rows[:, 0, :].reshape(groups, heads, GROUP), 1, 2)
-    sums = parts[:, :, 0] - turned
-    last = jnp.sum(parts[:, :, 2], axis=1) + jnp.sum(rows[:, heads:], axis=2)
-    ones = jnp.triu(jnp.ones((GROUP, GROUP), f32))
-    d_decay = jnp.einsum("ij,gjh->gih", ones, sums, precision=lax.Precision.HIGHEST)
-    d_decay = d_decay + last[:, None, :]
-    tokens = columns.shape[0]
-    return d_decay.reshape(tokens, heads), parts[:, :, 1].reshape(tokens, heads)
+    )(keep, *pres, *pres, *rims, *convs, scal, rate, *made, entry, exit_grad, grad)
 
 
 def gated_forward_kernel(heads, linear_ref, local_ref, gate_ref, entry_ref, gain_ref, gated_out):
@@ -612,7 +630,7 @@
         ],
         out_specs=row_block(rows, heads * DV),
         out_shape=jax.ShapeDtypeStruct((tokens, heads * DV), bf16),
-        compiler_params=pltpu.CompilerParams(vmem_limit_bytes=24 * 2**20),
+        compiler_params=pltpu.CompilerParams(vmem_limit_bytes=SMALL),
         cost_estimate=pl.CostEstimate(flops=10**9, bytes_accessed=10**7, transcendentals=0),
         name="gated_forward",
     )(linear, local, gate, entry, gain[None, :])
@@ -687,8 +705,8 @@
             jax.ShapeDtypeStruct((8, DV), f32),
             jax.ShapeDtypeStruct((heads * DK, DV), f32),
         ],
-        compiler_params=pltpu.CompilerParams(vmem_limit_bytes=24 * 2**20),
-        cost_estimate=pl.CostEstimate(flops=2 * 10**9, bytes_accessed=2 * 10**7, transcendentals=0),
+        compiler_params=pltpu.CompilerParams(vmem_limit_bytes=SMALL),
+        cost_estimate=pl.CostEstimate(flops=10**6, bytes_accessed=10**4, transcendentals=0),
         name="gated_backward",
     )(linear, local, gate, entry, gain[None, :], grad, valid[:, None])
 
@@ -701,7 +719,8 @@
 
 
 def plain_dense_kernel(place_ref, left_ref, right_ref, out_ref):
-    out_ref[...] = contract(left_ref[...], right_ref[...]).astype(bf16)
+    left = left_ref[:, : right_ref.shape[0]]
+    out_ref[...] = contract(left, right_ref[...]).astype(bf16)
 
 
 def plain_dense(left, right, place, tile=256):
@@ -721,7 +740,7 @@
             out_specs=pl.BlockSpec((rows, tile), lambda i, place: (0, i)),
         ),
         out_shape=jax.ShapeDtypeStruct((rows, cols), bf16),
-        compiler_params=pltpu.CompilerParams(vmem_limit_bytes=24 * 2**20),
+        compiler_params=pltpu.CompilerParams(vmem_limit_bytes=SMALL),
         cost_estimate=pl.CostEstimate(
             flops=2 * rows * cols * left.shape[1], bytes_accessed=10**7, transcendentals=0
         ),
@@ -729,12 +748,13 @@
     )(place, left, right)
 
 
-def norm_dense_kernel(count, place_ref, *refs):
+def norm_dense_kernel(sides, place_ref, *refs):
+    count = len(sides)
     lefts, rights = (refs[:count], refs[count : 2 * count])
     rows_ref, scale_ref, gain_ref, out_ref, gain_out, dots_out = refs[2 * count :]
-    total = contract(lefts[0][...], rights[0][...], 1, 1)
-    for left, right in zip(lefts[1:], rights[1:]):
-        total = total + contract(left[...], right[...], 1, 1)
+    total = 0.0
+    for left, right, side in zip(lefts, rights, sides):
+        total = total + contract(left[:, : right.shape[side]], right[...], 1, side)
     out_ref[...] = total.astype(bf16)
     weighted = total * (rows_ref[...].astype(f32) * scale_ref[...])
     gain_out[...] = jnp.sum(weighted, axis=0, keepdims=True)
@@ -754,18 +774,19 @@
     tiles = cols // tile
     lefts, rights = ([left for left, _ in pairs], [right for _, right in pairs])
     placed = lambda i, place: (0, column_place(i, tiles, place[0]))
+    upright = lambda i, place: (column_place(i, tiles, place[0]), 0)
+    sides = [1 if right.shape[0] == cols else 0 for right in rights]
     return pl.pallas_call(
-        functools.partial(norm_dense_kernel, len(pairs)),
+        functools.partial(norm_dense_kernel, sides),
         grid_spec=pltpu.PrefetchScalarGridSpec(
             num_scalar_prefetch=1,
             grid=(tiles,),
             in_specs=[pl.BlockSpec(left.shape, lambda i, place: (0, 0)) for left in lefts]
             + [
-                pl.BlockSpec(
-                    (tile, right.shape[1]),
-                    lambda i, place: (column_place(i, tiles, place[0]), 0),
-                )
-                for right in rights
+                pl.BlockSpec((tile, right.shape[1]), upright)
+                if side
+                else pl.BlockSpec((right.shape[0], tile), placed)
+                for right, side in zip(rights, sides)
             ]
             + [
                 pl.BlockSpec((tokens, tile), placed),
@@ -783,9 +804,9 @@
             jax.ShapeDtypeStruct((1, cols), f32),
             jax.ShapeDtypeStruct((tokens, 1), f32),
         ],
-        compiler_params=pltpu.CompilerParams(vmem_limit_bytes=32 * 2**20),
+        compiler_params=pltpu.CompilerParams(vmem_limit_bytes=VMEM),
         cost_estimate=pl.CostEstimate(
-            flops=2 * tokens * cols * sum(right.shape[1] for right in rights),
+            flops=2 * tokens * cols * sum(left.shape[1] for left in lefts),
             bytes_accessed=2 * 10**7,
             transcendentals=0,
         ),
@@ -809,30 +830,180 @@
     return lax.dynamic_slice_in_dim(block, at * width, width, axis)
 
 
+def weight_grad_kernel(turned, place_ref, rows_ref, got_rows_ref, cols_ref, got_cols_ref, out_ref):
+    if turned:
+        total = contract(cols_ref[...], rows_ref[...], 0, 0)
+        total = total + contract(got_cols_ref[...], got_rows_ref[...], 0, 0)
+        total = total[: out_ref.shape[0]]
+    else:
+        total = contract(rows_ref[...], cols_ref[...], 0, 0)
+        total = total + contract(got_rows_ref[...], got_cols_ref[...], 0, 0)
+    out_ref[...] = total.astype(bf16)
+
+
+def pair_grad(rows, got_rows, cols, got_cols, turned, kept=None):
+    odd = lax.axis_index("seq").astype(jnp.int32) % 2
+    devices = lax.axis_size("seq")
+    tokens, padded = cols.shape
+    count = padded if kept is None else kept
+    width = rows.shape[1] // devices
+    if width % 128:
+        part = jnp.concatenate([own_half(rows, odd, width), got_rows], axis=0)
+        cols = jnp.concatenate([cols, got_cols], axis=0)[:, :count]
+        if turned:
+            part = part.reshape(2 * tokens, devices // 2, width)
+            total = jnp.einsum("tn,tcw->cnw", cols, part, preferred_element_type=f32)
+            return total.reshape(devices // 2 * count, width).astype(bf16)
+        return dense(part.T, cols).astype(bf16)
+    block = (count, width) if turned else (width, count)
+    still = pl.BlockSpec((tokens, padded), lambda i, place: (0, 0))
+    return pl.pallas_call(
+        functools.partial(weight_grad_kernel, turned),
+        grid_spec=pltpu.PrefetchScalarGridSpec(
+            num_scalar_prefetch=1,
+            grid=(devices // 2,),
+            in_specs=[
+                pl.BlockSpec((tokens, width), lambda i, place: (0, 2 * i + place[0])),
+                pl.BlockSpec((tokens, width), lambda i, place: (0, i)),
+                still,
+                still,
+            ],
+            out_specs=pl.BlockSpec(block, lambda i, place: (i, 0)),
+        ),
+        out_shape=jax.ShapeDtypeStruct((devices // 2 * block[0], block[1]), bf16),
+        compiler_params=pltpu.CompilerParams(vmem_limit_bytes=SMALL),
+        cost_estimate=pl.CostEstimate(
+            flops=2 * tokens * count * rows.shape[1], bytes_accessed=10**7, transcendentals=0
+        ),
+        name="weight_grad",
+    )(odd[None], rows, got_rows, cols, got_cols)
+
+
+def partner_rows(block):
+    width = block.shape[1] * 4 // lax.axis_size("seq")
+    odd = lax.axis_index("seq") % 2
+    if block.shape[1] == 2 * width:
+        part = half(block, 1, 1 - odd, 2)
+    else:
+        part = own_half(block, 1 - odd, width)
+    return exchanged(part, "seq", 1)
+
+
+def gather_kernel(norm, place_ref, *refs):
+    blocks = [ref[...] for ref in refs[:4]]
+    width = blocks[0].shape[1]
+    place = place_ref[0]
+    out_ref = refs[5] if norm else refs[4]
+    spots = [pl.ds(pl.multiple_of((place ^ at) * width, 128), width) for at in range(4)]
+    for block, spot in zip(blocks, spots):
+        out_ref[:, spot] = block
+    if norm:
+        gain_ref, normed_out, scale_out = (refs[4], refs[6], refs[7])
+        wides = [block.astype(f32) for block in blocks]
+        total = sum(jnp.sum(wide * wide, axis=1, keepdims=True) for wide in wides)
+        scale = lax.rsqrt(total / (4 * width) + epsilon_norm)
+        scale_out[...] = scale
+        for wide, spot in zip(wides, spots):
+            normed_out[:, spot] = (wide * scale * gain_ref[:, spot]).astype(bf16)
+
+
+def head_gathered(block, gain=None):
+    place = lax.axis_index("head").astype(jnp.int32)
+    tokens, width = block.shape
+    across = exchanged(block, "head", 2)
+    beside = exchanged(block, "head", 1)
+    corner = exchanged(across, "head", 1)
+    rows = 4 * GROUP
+    norm = gain is not None
+    spec = lambda cols: pl.BlockSpec((rows, cols), lambda i, place: (i, 0))
+    whole_shape = jax.ShapeDtypeStruct((tokens, 4 * width), bf16)
+    out_specs, out_shape = (spec(4 * width), whole_shape)
+    if norm:
+        out_specs = [out_specs, spec(4 * width), spec(1)]
+        out_shape = [whole_shape, whole_shape, jax.ShapeDtypeStruct((tokens, 1), f32)]
+    gain_spec = pl.BlockSpec((1, 4 * width), lambda i, place: (0, 0))
+    return pl.pallas_call(
+        functools.partial(gather_kernel, norm),
+        grid_spec=pltpu.PrefetchScalarGridSpec(
+            num_scalar_prefetch=1,
+            grid=(tokens // rows,),
+            in_specs=[spec(width)] * 4 + ([gain_spec] if norm else []),
+            out_specs=out_specs,
+        ),
+        out_shape=out_shape,
+        compiler_params=pltpu.CompilerParams(vmem_limit_bytes=SMALL),
+        cost_estimate=pl.CostEstimate(flops=10**6, bytes_accessed=6 * 10**6, transcendentals=0),
+        name="gather",
+    )(place[None], block, beside, across, corner, *([gain[None, :]] if norm else []))
+
+
+def rows_dense_kernel(left_ref, right_ref, out_ref):
+    out_ref[...] = contract(left_ref[...], right_ref[...], 1, 1)
+
+
+def rows_dense(left, right):
+    tokens, rows = (left.shape[0], 4 * GROUP)
+    return pl.pallas_call(
+        rows_dense_kernel,
+        grid=(tokens // rows,),
+        in_specs=[row_block(rows, left.shape[1]), whole(right.shape)],
+        out_specs=row_block(rows, right.shape[0]),
+        out_shape=jax.ShapeDtypeStruct((tokens, right.shape[0]), f32),
+        compiler_params=pltpu.CompilerParams(vmem_limit_bytes=SMALL),
+        cost_estimate=pl.CostEstimate(
+            flops=2 * left.size * right.shape[0], bytes_accessed=10**7, transcendentals=0
+        ),
+        name="rows_dense",
+    )(left, right)
+
+
+def ffn_kernel(normed_ref, gate_ref, up_ref, grad_ref, inner_out, d_gate_out, d_up_out):
+    normed = normed_ref[...]
+    gate = contract(normed, gate_ref[...], 1, 1)
+    up = contract(normed, up_ref[...], 1, 1)
+    sigmoid = jax.nn.sigmoid(gate)
+    silu = gate * sigmoid
+    grad = grad_ref[...]
+    padding = inner_out.shape[1] - gate.shape[1]
+    for ref, values in (
+        (inner_out, silu * up),
+        (d_gate_out, grad * up * (sigmoid * (1.0 + gate * (1.0 - sigmoid)))),
+        (d_up_out, grad * silu),
+    ):
+        values = values.astype(bf16)
+        if padding:
+            values = jnp.pad(values, ((0, 0), (0, padding)))
+        ref[...] = values
+
+
+def ffn(normed, w_gate, w_up, grad):
+    tokens, count = grad.shape
+    rows, padded = (4 * GROUP, -(-count // 128) * 128)
+    return pl.pallas_call(
+        ffn_kernel,
+        grid=(tokens // rows,),
+        in_specs=[row_block(rows, normed.shape[1])]
+        + [whole(w_gate.shape)] * 2
+        + [row_block(rows, count)],
+        out_specs=[row_block(rows, padded)] * 3,
+        out_shape=[jax.ShapeDtypeStruct((tokens, padded), bf16)] * 3,
+        compiler_params=pltpu.CompilerParams(vmem_limit_bytes=VMEM),
+        cost_estimate=pl.CostEstimate(
+            flops=4 * normed.size * count, bytes_accessed=2 * 10**7, transcendentals=0
+        ),
+        name="ffn",
+    )(normed, w_gate, w_up, grad)
+
+
+def tied(*values):
+    return lax.optimization_barrier(values)
+
+
 def head_scattered(partial):
     width = partial.shape[1] // 2
     mine = partial[:, width:].astype(f32) + exchanged(partial[:, :width], "head", 1).astype(f32)
     width = width // 2
     return mine[:, width:] + exchanged(mine[:, :width].astype(bf16), "head", 2).astype(f32)
-
-
-def head_gathered(block):
-    place = lax.axis_index("head")
-    core, chip = (place % 2, place // 2)
-    across = exchanged(block, "head", 2)
-    beside = exchanged(block, "head", 1)
-    corner = exchanged(across, "head", 1)
-    low = jnp.where(core == 0, block, beside)
-    high = jnp.where(core == 0, beside, block)
-    far_low = jnp.where(core == 0, across, corner)
-    far_high = jnp.where(core == 0, corner, across)
-    near = jnp.concatenate([low, high], axis=1)
-    far = jnp.concatenate([far_low, far_high], axis=1)
-    return jnp.where(
-        chip == 0,
-        jnp.concatenate([near, far], axis=1),
-        jnp.concatenate([far, near], axis=1),
-    )
 
 
 def head_summed(values):
@@ -852,16 +1023,10 @@
     return values
 
 
-def own_half(rows, odd):
-    tokens, width = rows.shape
-    devices = lax.axis_size("seq")
-    parts = rows.reshape(tokens, devices // 2, 2, width // devices)
-    return lax.dynamic_index_in_dim(parts, odd, 2, False).reshape(tokens, width // 2)
-
-
-def halves_of(rows):
-    odd = lax.axis_index("seq") % 2
-    return own_half(rows, odd), own_half(rows, 1 - odd)
+def own_half(rows, odd, width):
+    tokens, total = rows.shape
+    parts = rows.reshape(tokens, total // (2 * width), 2, width)
+    return lax.dynamic_index_in_dim(parts, odd, 2, False).reshape(tokens, total // 2)
 
 
 def seq_scattered(mine):
@@ -872,26 +1037,69 @@
     ).astype(f32)
 
 
-def weight_grad(rows, cols):
-    own, other = rows
-    got = exchanged(dense(other.T, cols).astype(bf16), "seq", 1)
-    return seq_scattered(dense(own.T, cols) + got.astype(f32))
-
-
-def prefix(pair, direction):
-    pair = shifted(pair.astype(bf16), "seq", direction)
-    offset = pair[:, :, DK:].astype(f32)
-    distance = 1
+def line_step(send, step, planes, upward):
+    devices = 2 * planes
+    route = []
+    for i in range(devices):
+        plane = i // 2
+        if upward and plane < step and plane + 1 < planes:
+            route.append((i, i + 2))
+        if not upward and planes - 1 - plane < step and plane > 0:
+            route.append((i, i - 2))
+    return lax.ppermute(send, "seq", route)
+
+
+def line_scattered(kept):
+    planes = lax.axis_size("seq") // 2
+    if planes > 4:
+        return seq_scattered(kept)
+    plane = lax.axis_index("seq") // 2
+    rows = kept.shape[0] // planes
+
+    def chunk(at):
+        return lax.dynamic_slice_in_dim(kept, at * rows, rows, 0).astype(f32)
+
+    up, down = (None, None)
+    for step in range(1, planes):
+        to_up = chunk(jnp.minimum(plane + planes - step, planes - 1))
+        to_down = chunk(jnp.maximum(plane - planes + step, 0))
+        if up is not None:
+            to_up, to_down = (to_up + up.astype(f32), to_down + down.astype(f32))
+        up = line_step(to_up.astype(bf16), step, planes, True)
+        down = line_step(to_down.astype(bf16), step, planes, False)
+    return chunk(plane) + up.astype(f32) + down.astype(f32)
+
+
+def composed(later, before):
+    moved = jnp.einsum(
+        "hij,hjk->hik", later[:, :, :DK].astype(bf16), before, preferred_element_type=f32
+    )
+    linear = moved.shape[2] - DV
+    offset = later[:, :, DK:] + moved[:, :, linear:]
+    return jnp.concatenate([moved[:, :, :linear], offset], axis=2)
+
+
+def prefix(pair, got, direction):
+    odd = lax.axis_index("seq") % 2
+    front = odd == 1 if direction == 1 else odd == 0
+    wide = got.astype(f32)
+    low = pair.astype(bf16)
+    closed = composed(jnp.where(front, pair, wide), jnp.where(front, got, low))
+    distance = 2
+    before = shifted(closed.astype(bf16), "seq", direction * distance)
+    opened = before.astype(f32)
     while True:
-        last = distance * 2 >= lax.axis_size("seq") - 1
-        sent = pair[:, :, DK:] if last else pair
-        before = shifted(sent, "seq", direction * distance)
-        moved = jnp.einsum("hij,hjk->hik", pair[:, :, :DK], before, preferred_element_type=f32)
+        closed = composed(closed, before)
+        distance = distance * 2
+        last = distance * 2 >= lax.axis_size("seq")
+        sent = closed[:, :, DK:] if last else closed
+        before = shifted(sent.astype(bf16), "seq", direction * distance)
+        opened = composed(opened, before)
         if last:
-            return offset + moved
-        offset = offset + moved[:, :, DK:]
-        pair = jnp.concatenate([moved[:, :, :DK], offset], axis=2).astype(bf16)
-        distance = distance * 2
+            break
+    opened = opened[:, :, -DV:]
+    moved = composed(wide, opened.astype(bf16))[:, :, -DV:]
+    return jnp.where(front, moved, opened)
 
 
 def layout(lengths, positions):
@@ -956,62 +1164,62 @@
     split = lambda rows: [rows[:, a:b] for a, b in zip(edges[:-1], edges[1:])]
     tail_first = token_rows - (CONV - 1)
     rims = shifted(jnp.concatenate([pre[tail_first:] for pre in pres], 1), "seq", 1)
+    rims, grad_cols, normed_cols = tied(rims, grad_out, cols(normed))
+    got_grad_rows = head_gathered(partner_rows(grad_cols))
+    got_normed = head_gathered(partner_rows(normed_cols))
     rims = split(jnp.pad(rims, ((HALO - (CONV - 1), 0), (0, 0))))
-    alpha_pre = dense(normed, w_alpha)
-    beta_pre = dense(normed, w_beta)
-
-    def decays(alpha_pre, decay_log, decay_bias):
-        rate = jnp.exp(decay_log) * jax.nn.softplus(alpha_pre + decay_bias)
-        return -rate * valid_mask[:, None]
-
-    decay, decay_pull = jax.vjp(decays, alpha_pre, local_log, local_bias)
-    beta = jax.nn.sigmoid(beta_pre)
-    scal, grow, fade = scalars(decay, beta, valid_mask)
+    w_scal = jnp.concatenate([w_alpha, w_beta], axis=1)
+    scal = jnp.concatenate([dense(normed, w_scal), valid_mask[:, None]], axis=1)
+    rate = jnp.stack([jnp.exp(local_log), local_bias])
     convs = [conv_query, conv_key, conv_value]
     *made, linear, local, device_pair = delta_forward(
-        pres, rims, convs, scal, grow, fade, keep_flags
-    )
+        pres, rims, convs, scal, rate, keep_flags
+    )
+    grad_rows = head_gathered(grad_out)
+    device_pair, grad_rows = tied(device_pair, grad_rows)
     device_pair = device_pair.reshape(head_count, DK, WIDE)
-    entry = prefix(device_pair, 1).astype(bf16).reshape(head_count * DK, DV)
+    got_pair = exchanged(device_pair.astype(bf16), "seq", 1)
+    entry = prefix(device_pair, got_pair, 1).astype(bf16).reshape(head_count * DK, DV)
     gate_pre = dense(normed, w_gate)
+    d_inner = rows_dense(grad_rows, w_ffn_down)
+    entry, d_inner, gate_pre, got_grad_rows, got_normed = tied(
+        entry, d_inner, gate_pre, got_grad_rows, got_normed
+    )
     gated = gated_forward(linear, local, gate_pre, entry, out_gain)
     mixed = head_scattered(plain_dense(gated, w_out, place))
     middle = cols(hidden_in).astype(f32) + mixed
-    sent = head_gathered(middle.astype(bf16))
-    sent32 = sent.astype(f32)
-    ffn_scale = lax.rsqrt(jnp.mean(sent32 * sent32, axis=-1, keepdims=True) + epsilon_norm)
-    normed_ffn = (sent32 * ffn_scale * ffn_gain).astype(bf16)
-    ffn_gate_pre = dense(normed_ffn, w_ffn_gate)
-    ffn_up_pre = dense(normed_ffn, w_ffn_up)
-    sigmoid_gate = jax.nn.sigmoid(ffn_gate_pre)
-    silu_gate = ffn_gate_pre * sigmoid_gate
-    inner_act = (silu_gate * ffn_up_pre).astype(bf16)
+    sent, normed_ffn, ffn_scale = head_gathered(middle.astype(bf16), ffn_gain)
+    got_gated = exchanged(gated, "seq", 1)
+    d_inner, got_gated = tied(d_inner, got_gated)
+    inner_act, d_ffn_gate, d_ffn_up = ffn(normed_ffn, w_ffn_gate.T, w_ffn_up.T, d_inner)
     ffn_out = head_scattered(plain_dense(inner_act, w_ffn_down, place))
     hidden_out = (middle + ffn_out).astype(bf16)
-    grad_rows = head_gathered(grad_out)
-    d_inner = dense(grad_rows, w_ffn_down.T)
-    grad_w_ffn_down = weight_grad(halves_of(grad_rows), inner_act)
-    d_ffn_gate = (
-        d_inner * ffn_up_pre * sigmoid_gate * (1.0 + ffn_gate_pre * (1.0 - sigmoid_gate))
-    ).astype(bf16)
-    d_ffn_up = (d_inner * silu_gate).astype(bf16)
-    ffn_halves = halves_of(normed_ffn)
-    grad_w_ffn_gate = weight_grad(ffn_halves, d_ffn_gate)
-    grad_w_ffn_up = weight_grad(ffn_halves, d_ffn_up)
+    units = w_ffn_gate.shape[1]
+    got_ffn_cols = partner_rows(cols(normed_ffn))
+    inner_sent, got_ffn_cols = tied(inner_act, got_ffn_cols)
+    got_inner = exchanged(inner_sent, "seq", 1)
+    got_normed_ffn = head_gathered(got_ffn_cols)
     d_normed_ffn, grad_ffn_gain, ffn_dots = norm_dense(
-        [(d_ffn_gate, w_ffn_gate), (d_ffn_up, w_ffn_up)], sent, ffn_scale, ffn_gain, place
+        [(d_ffn_gate, w_ffn_gate.T), (d_ffn_up, w_ffn_up.T)], sent, ffn_scale, ffn_gain, place
     )
     ffn_dots = head_summed(ffn_dots[:, 0])[:, None] / sent.shape[1]
     d_sent_cols = ffn_scale * (
-        cols(ffn_gain) * head_scattered(d_normed_ffn) - cols(sent32) * ffn_scale * ffn_dots
+        cols(ffn_gain) * head_scattered(d_normed_ffn)
+        - cols(sent).astype(f32) * ffn_scale * ffn_dots
     )
     d_middle = grad_out.astype(f32) + d_sent_cols
     d_mixed = head_gathered(d_middle.astype(bf16))
     d_gated = dense(d_mixed, w_out.T)
+    got_mixed_cols = partner_rows(d_middle.astype(bf16))
+    d_gate_sent, got_inner, got_mixed_cols = tied(d_ffn_gate, got_inner, got_mixed_cols)
+    got_d_gate = exchanged(d_gate_sent, "seq", 1)
+    got_d_mixed = head_gathered(got_mixed_cols)
+    kept_down = pair_grad(grad_rows, got_grad_rows, inner_act, got_inner, True, units)
+    d_gated, kept_down, got_normed_ffn = tied(d_gated, kept_down, got_normed_ffn)
+    grad_w_ffn_down = seq_scattered(kept_down)
     d_delta, d_gate_pre, gain_part, entry_grad = gated_backward(
         linear, local, gate_pre, entry, out_gain, d_gated, valid_mask
     )
-    grad_w_out = weight_grad(halves_of(d_mixed), gated)
     back_pair = jnp.concatenate(
         [
             jnp.swapaxes(device_pair[:, :, :DK], 1, 2),
@@ -1019,27 +1227,37 @@
         ],
         axis=2,
     )
-    exit_grad = prefix(back_pair, -1).reshape(head_count * DK, DV)
+    kept_gate = pair_grad(normed_ffn, got_normed_ffn, d_ffn_gate, got_d_gate, True, units)
+    got_back = exchanged(back_pair.astype(bf16), "seq", 1)
+    d_ffn_up, d_gate_pre, got_back = tied(d_ffn_up, d_gate_pre, got_back)
+    got_d_up = exchanged(d_ffn_up, "seq", 1)
+    got_d_gate_pre = exchanged(d_gate_pre, "seq", 1)
+    kept_out = pair_grad(d_mixed, got_d_mixed, gated, got_gated, True)
+    exit_grad = prefix(back_pair, got_back, -1).reshape(head_count * DK, DV)
+    exit_grad, kept_gate, kept_out, grad_w_ffn_down, hidden_out = tied(
+        exit_grad, kept_gate, kept_out, grad_w_ffn_down, hidden_out
+    )
+    grad_w_ffn_gate = seq_scattered(kept_gate)
+    grad_w_out = seq_scattered(kept_out)
     results = delta_backward(
-        pres, rims, convs, scal, grow, fade, keep_flags, made, entry, exit_grad, d_delta
+        pres, rims, convs, scal, rate, keep_flags, made, entry, exit_grad, d_delta
     )
     d_pres, conv_parts, backs, tails = (results[i : i + 3] for i in range(0, 12, 3))
-    d_decay, d_beta = scalar_grads(*results[12:])
-    d_alpha, grad_log_local, grad_bias_local = decay_pull(d_decay)
-    d_alpha = d_alpha.astype(bf16)
-    d_beta_pre = (d_beta * beta * (1.0 - beta)).astype(bf16)
+    d_scal, d_rate = results[12:]
     backs = shifted(jnp.concatenate(backs, 1)[8 - (CONV - 1) :], "seq", -1)
     tails = split(jnp.concatenate(tails, 1) + jnp.pad(backs, ((8 - (CONV - 1), 0), (0, 0))))
     d_query_pre, d_key_pre, d_value_pre = [
         lax.dynamic_update_slice(d_pre, tail.astype(bf16), (token_rows - 8, 0))
         for d_pre, tail in zip(d_pres, tails)
     ]
-    normed_halves = halves_of(normed)
-    grad_w_gate = weight_grad(normed_halves, d_gate_pre)
-    grad_w_query = weight_grad(normed_halves, d_query_pre)
-    grad_w_key = weight_grad(normed_halves, d_key_pre)
-    grad_w_value = weight_grad(normed_halves, d_value_pre)
-    small = [dense(normed.T, d_alpha).reshape(devices, -1), dense(normed.T, d_beta_pre).reshape(devices, -1)]
+    d_query_pre, d_key_pre, d_value_pre, d_scal, got_d_up, got_d_gate_pre = tied(
+        d_query_pre, d_key_pre, d_value_pre, d_scal, got_d_up, got_d_gate_pre
+    )
+    kept_up = pair_grad(normed_ffn, got_normed_ffn, d_ffn_up, got_d_up, True, units)
+    kept_w_gate = pair_grad(normed, got_normed, d_gate_pre, got_d_gate_pre, False)
+    got_last = [exchanged(d_pre, "seq", 1) for d_pre in (d_query_pre, d_key_pre, d_value_pre)]
+    small = dense(normed.T, d_scal)
+    small = [part.reshape(devices, -1) for part in (small[:, :head_count], small[:, head_count:])]
     for part in conv_parts:
         part = jnp.sum(part.reshape(CONV, 8, -1), axis=1).reshape(CONV, devices, -1)
         small.append(jnp.swapaxes(part, 0, 1).reshape(devices, -1))
@@ -1062,24 +1280,34 @@
             (d_key_pre, w_key),
             (d_value_pre, w_value),
             (d_gate_pre, w_gate),
-            (d_alpha, w_alpha),
-            (d_beta_pre, w_beta),
+            (d_scal, w_scal),
         ],
         hidden_in,
         attn_scale,
         attn_gain,
         place,
     )
+    d_normed, kept_up, kept_w_gate, grad_w_ffn_gate, *got_last[:2] = tied(
+        d_normed, kept_up, kept_w_gate, grad_w_ffn_gate, *got_last[:2]
+    )
+    grad_w_ffn_up = seq_scattered(kept_up)
+    grad_w_gate = seq_scattered(kept_w_gate)
+    kept_last = [
+        pair_grad(normed, got_normed, d_pre, got, False)
+        for d_pre, got in zip((d_query_pre, d_key_pre, d_value_pre), got_last)
+    ]
+    d_normed = head_scattered(d_normed)
+    grad_w_query, grad_w_key, grad_w_value = [line_scattered(kept) for kept in kept_last]
     attn_dots = head_summed(attn_dots[:, 0])[:, None] / hidden_in.shape[1]
     grad_in = d_middle + attn_scale * (
-        cols(attn_gain) * head_scattered(d_normed)
+        cols(attn_gain) * d_normed
         - cols(hidden_in).astype(f32) * attn_scale * attn_dots
     )
     full_log = lax.dynamic_update_slice_in_dim(
-        jnp.zeros(decay_log.shape, f32), grad_log_local, head_first, 0
+        jnp.zeros(decay_log.shape, f32), d_rate[0], head_first, 0
     )
     full_bias = lax.dynamic_update_slice_in_dim(
-        jnp.zeros(decay_bias.shape, f32), grad_bias_local, head_first, 0
+        jnp.zeros(decay_bias.shape, f32), d_rate[1], head_first, 0
     )
     sums = all_summed(
         jnp.concatenate(
@@ -1103,11 +1331,11 @@
         sums[log_first:bias_first],
         sums[bias_first:],
         sums[:gain_first],
-        grad_w_out.T,
+        grad_w_out,
         rows_of(sums[gain_first:attn_first]),
-        grad_w_ffn_gate,
-        grad_w_ffn_up,
-        grad_w_ffn_down.T,
+        grad_w_ffn_gate.T,
+        grad_w_ffn_up.T,
+        grad_w_ffn_down,
     )
 
 

time: 951 us -> 804 us (0.85)
  waiting for transfers between devices: 386 us -> 237 us
  Pallas kernels: 140 us -> 241 us
  matrix products: 116 us -> 26.8 us
  local copies, waits for them, and re-layouts: 143 us -> 103 us
  starting transfers between devices: 67.7 us -> 103 us
    ppermute x35 -> x53, waiting for transfers between devices: 327 us -> 175 us  [exchanged(): return lax.ppermute(block, axis, route)]
    dot_general x28 -> x7, matrix products: 112 us -> 18 us  [dense(): return jnp.dot(left, right, preferred_element_type=jnp.float32)]
    pallas_call x2 -> x19, Pallas kernels: 30.1 us -> 122 us  [the longest x8 47.3 us: pair_grad(): pl.pallas_call(functools.partial(weight_grad_kernel, turned), grid_spec=p...]
    ppermute x0 -> x18, starting transfers between devices: none -> 53.8 us  [line_step(): return lax.ppermute(send, 'seq', route)]
    ppermute x0 -> x18, waiting for transfers between devices: none -> 40.9 us  [line_step(): return lax.ppermute(send, 'seq', route)]
    ppermute x10 -> x6, waiting for transfers between devices: 58.8 us -> 20 us  [shifted(): return lax.ppermute(block, axis, route)]
    concatenate x13 -> x2, local copies, waits for them, and re-layouts: 24.8 us -> 1.94 us  [the longest x1 1 us: shards(): w_scal = jnp.concatenate([w_alpha, w_beta], axis=1)]
    unnamed x325 -> x209, local copies, waits for them, and re-layouts: 77.8 us -> 60.4 us
  transfers between devices with their start and end apart: 54 -> 83, of which waited for: 27 -> 31; matrix products, arithmetic and copies ran while one was open for 22% -> 15% of each run, Pallas kernels for 8% -> 24%
where the time goes in v3:
time: 804 us; the launch traced here: 792 us
  Pallas kernels  241 us (30%)
  waiting for transfers between devices  237 us (29%)
  local copies, waits for them, and re-layouts  103 us (13%)
  starting transfers between devices  103 us (13%)
  other arithmetic  65.4 us (8%)
  matrix products  26.8 us (3%)
  between operations  16.2 us (2%)
    ppermute x53, waiting for transfers between devices, exchanged(): return lax.ppermute(block, axis, route)  175 us
    unnamed x209, local copies, waits for them, and re-layouts  60.4 us
    pallas_call x1, Pallas kernels, delta_backward(): pl.pallas_call(functools.partial(backward_kernel, heads, groups), grid=(g...  55.9 us
    ppermute x18, starting transfers between devices, line_step(): return lax.ppermute(send, 'seq', route)  53.8 us
    pallas_call x8, Pallas kernels, pair_grad(): pl.pallas_call(functools.partial(weight_grad_kernel, turned), grid_spec=p...  47.3 us
    pallas_call x1, Pallas kernels, delta_forward(): pl.pallas_call(functools.partial(forward_kernel, heads, groups), grid=(gr...  41.1 us
    ppermute x18, waiting for transfers between devices, line_step(): return lax.ppermute(send, 'seq', route)  40.9 us
    pallas_call x2, Pallas kernels, norm_dense(): pl.pallas_call(functools.partial(norm_dense_kernel, sides), grid_spec=plt...  35.9 us
  transfers between devices with their start and end apart: 83, of which 31 were waited for; matrix products, arithmetic and copies ran while one was open for 15% of the time, Pallas kernels for 24%

profile of v3, /device:TPU:0, one launch (start us, length us, event | category | flops | bytes accessed | tf_op | source)
XLA Modules:
  0.0 792.4 jit_solution(1325615202341097557)
XLA Ops:
  38.4 41.1 %delta_forward.1 = (bf16[768,512]{1,0:T(8,128)(2,1)}, bf16[768,512]{1,0:T(8,128)(2,1)}, bf16[768,1024]{1,0:T(8,128)(2,1)}, bf16[12,256,384]{2,1,0:T(8,128)(2,1)}...) custom-call(f32[12]{0:T(128)} %convert_subtract_fusion.keep_ref, ...), custom_call_target="tpu_custom_call" | custom-call | flops 1000000 | bytes 10000 | tf_op jit(solution)/shard_map/delta_forward/pallas_call | solution.py:289
  91.9 7.1 collective-permute-done.13.refs_2_
  120.3 5.5 rows_dense.1.grad_ref
  132.0 5.9 plain_dense.2
  144.1 17.8 %collective-permute-done.16 = bf16[768,512]{1,0:T(8,128)(2,1)S(1)} collective-permute-done((bf16[768,512]{1,0:T(8,128)(2,1)S(1)}, bf16[768,512]{1,0:T(8,128)(2,1)S(1)}, u32[]{:S(2)}, u32[]{:S(2)}) %collective-permute-start.16) | collective-permute-done | bytes 786464 | tf_op jit(solution)/shard_map/ppermute | solution.py:825
  164.6 17.9 %collective-permute-done.18.refs_2_ = bf16[768,512]{1,0:T(8,128)(2,1)S(1)} collective-permute-done((bf16[768,512]{1,0:T(8,128)(2,1)S(1)}, bf16[768,512]{1,0:T(8,128)(2,1)S(1)}, u32[]{:S(2)}, u32[]{:S(2)}) %collective-permute-start.18) | collective-permute-done | bytes 786464 | tf_op jit(solution)/shard_map/ppermute | solution.py:825
  190.6 17.3 %ffn.1 = (bf16[768,1408]{1,0:T(8,128)(2,1)}, bf16[768,1408]{1,0:T(8,128)(2,1)}, bf16[768,1408]{1,0:T(8,128)(2,1)}) custom-call(bf16[768,2048]{1,0:T(8,128)(2,1)} %copy-done.45, bf16[1376,2048]{1,0:T(8,128)(2,1)} %bitcast.103, bf16[1376,2048]{1,0:T(8,128)(2,1)} %bitcast.105, f32[768,1376]{1,0:T(8,128)} %copy-done.60), custom_call_target="tpu_custom_call" | custom-call | flops 8657043456 | bytes 20000000 | tf_op jit(solution)/shard_map/ffn/pallas_call | solution.py:982
  208.0 17.2 %norm_dense.2 = (bf16[768,2048]{1,0:T(8,128)(2,1)}, f32[1,2048]{1,0:T(1,128)}, f32[768,1]{1,0:T(8,128)}) custom-call(s32[1]{0:T(128)} %bitcast.place_ref, bf16[768,1408]{1,0:T(8,128)(2,1)} %get-tuple-element.128.refs_0_.cols_ref, bf16[768,1408]{1,0:T(8,128)(2,1)} %get-tuple-element.151.refs_1_.cols_ref, bf16[1376,2048]{1,0:T(8,128)(2,1)} %bitcast.104, ...), custom_call_target="tpu_custom_call" | custom-call | flops 8858370048 | bytes 20000000 | tf_op jit(solution)/shard_map/norm_dense/pallas_call | solution.py:779
  246.9 9.8 %collective-permute-done.24 = f32[768]{0:T(1024)S(1)} collective-permute-done((f32[768]{0:T(1024)S(1)}, f32[768]{0:T(1024)S(1)}, u32[]{:S(2)}, u32[]{:S(2)}) %collective-permute-start.24) | collective-permute-done | bytes 3104 | tf_op jit(solution)/shard_map/ppermute | solution.py:825
  262.9 25.4 %collective-permute-done.32.refs_2_ = bf16[768,256]{1,0:T(8,128)(2,1)S(1)} collective-permute-done((bf16[768,256]{1,0:T(8,128)(2,1)}, bf16[768,256]{1,0:T(8,128)(2,1)S(1)}, u32[]{:S(2)}, u32[]{:S(2)}) %collective-permute-start.32) | collective-permute-done | bytes 393248 | tf_op jit(solution)/shard_map/ppermute | solution.py:825
  293.8 7.2 collective-permute-done.30.refs_0_
  301.7 8.0 %weight_grad.8 = bf16[5504,256]{1,0:T(8,128)(2,1)S(1)} custom-call(s32[1]{0:T(128)} %bitcast.11.place_ref, bf16[768,2048]{1,0:T(8,128)(2,1)S(1)} %copy-done.18, bf16[768,1024]{1,0:T(8,128)(2,1)S(1)} %copy-done.38, bf16[768,1408]{1,0:T(8,128)(2,1)} %get-tuple-element.120.cols_ref.left_ref, bf16[768,1408]{1,0:T(8,128)(2,1)} %collective-permute-done.29.got_cols_ref), custom_call_target="tpu_custom_call" | custom-call | flops 4328521728 | bytes 10000000 | tf_op jit(solution)/shard_map/weight_grad/pallas_call | solution.py:860
  314.4 5.2 fusion.69.grad_ref
  323.9 9.2 %plain_dense.3 = bf16[768,2048]{1,0:T(8,128)(2,1)S(1)} custom-call(s32[1]{0:T(128)} %bitcast.place_ref, bf16[768,1408]{1,0:T(8,128)(2,1)} %get-tuple-element.120.cols_ref.left_ref, bf16[1376,2048]{1,0:T(8,128)(2,1)S(1)} %copy-done.50), custom_call_target="tpu_custom_call" | custom-call | flops 4429185024 | bytes 10000000 | tf_op jit(solution)/shard_map/plain_dense/pallas_call | solution.py:729
  349.2 5.1 gated_backward.1
  364.8 5.8 collective-permute-done.34
  375.8 6.5 collective-permute-done.42
  398.5 17.7 %collective-permute-done.37.got_cols_ref = bf16[768,1408]{1,0:T(8,128)(2,1)} collective-permute-done((bf16[768,1408]{1,0:T(8,128)(2,1)}, bf16[768,1408]{1,0:T(8,128)(2,1)}, u32[]{:S(2)}, u32[]{:S(2)}) %collective-permute-start.37) | collective-permute-done | bytes 2162720 | tf_op jit(solution)/shard_map/ppermute | solution.py:825
  419.7 7.4 weight_grad.9
  436.7 55.9 %delta_backward.1 = (bf16[768,512]{1,0:T(8,128)(2,1)}, bf16[768,512]{1,0:T(8,128)(2,1)}, bf16[768,1024]{1,0:T(8,128)(2,1)}, f32[32,512]{1,0:T(8,128)}, f32[32,51...) custom-call(f32[12]{0:T(128)} %convert_subtract_fusion.keep_ref, ...), custom_call_target="tpu_custom_call" | custom-call | flops 1000000 | bytes 10000 | tf_op jit(solution)/shard_map/delta_backward/pallas_call | solution.py:563
  497.7 20.0 %collective-permute-done.43 = f32[3,2048]{1,0:T(4,128)S(1)} collective-permute-done((f32[3,2048]{1,0:T(4,128)S(1)}, f32[3,2048]{1,0:T(4,128)S(1)}, u32[]{:S(2)}, u32[]{:S(2)}) %collective-permute-start.43) | collective-permute-done | bytes 24608 | tf_op jit(solution)/shard_map/ppermute | solution.py:820
  540.0 5.9 weight_grad.12
  552.2 7.4 weight_grad.11
  561.1 18.7 %norm_dense.3 = (bf16[768,2048]{1,0:T(8,128)(2,1)}, f32[1,2048]{1,0:T(1,128)}, f32[768,1]{1,0:T(8,128)}) custom-call(s32[1]{0:T(128)} %bitcast.place_ref, bf16[768,512]{1,0:T(8,128)(2,1)} %get-tuple-element.153.refs_0_.cols_ref, bf16[768,512]{1,0:T(8,128)(2,1)} %get-tuple-element.154.refs_1_.cols_ref, bf16[768,1024]{1,0:T(8,128)(2,1)} %fusion.52.refs_2_.cols_ref, ...), custom_call_target="tpu_custom_call" | custom-call | flops 9688842240 | bytes 20000000 | tf_op jit(solution)/shard_map/norm_dense/pallas_call | solution.py:779
  583.0 33.3 %collective-permute-done.69.got_cols_ref = bf16[768,1024]{1,0:T(8,128)(2,1)} collective-permute-done((bf16[768,1024]{1,0:T(8,128)(2,1)}, bf16[768,1024]{1,0:T(8,128)(2,1)}, u32[]{:S(2)}, u32[]{:S(2)}) %collective-permute-start.69) | collective-permute-done | bytes 1572896 | tf_op jit(solution)/shard_map/ppermute | solution.py:825
  619.1 5.9 weight_grad.15
  627.3 5.3 collective-permute-start.70
  667.0 15.3 %collective-permute-done.71 = bf16[256,1024]{1,0:T(8,128)(2,1)} collective-permute-done((bf16[256,1024]{1,0:T(8,128)(2,1)}, bf16[256,1024]{1,0:T(8,128)(2,1)}, u32[]{:S(2)}, u32[]{:S(2)}) %collective-permute-start.71) | collective-permute-done | bytes 524320 | tf_op jit(solution)/shard_map/ppermute | solution.py:1049
  689.1 12.7 %collective-permute-start.63 = (bf16[256,512]{1,0:T(8,128)(2,1)S(1)}, bf16[256,512]{1,0:T(8,128)(2,1)S(1)}, u32[]{:S(2)}, u32[]{:S(2)}) collective-permute-start(bf16[256,512]{1,0:T(8,128)(2,1)S(1)} %get-tuple-element.248), channel_id=1, source_target_pairs={{0,8},{4,12},{1,9},{5,13},{2,10},{6,14},{3,11},{7,15}} | collective-permute-start | bytes 786440 | tf_op jit(solution)/shard_map/ppermute | solution.py:1049
  708.2 5.1 collective-permute-done.63
  729.7 6.0 collective-permute-done.64
  743.2 6.0 collective-permute-done.58
  (523 shorter events, 341.8 us)
Async XLA Ops:
  7.2 425.1 %reduce-scatter.9.cloned.1.call-start = ((), (), s32[]{:S(2)}) async-start(), calls=%async_computation.6 | async-start | bytes 3522560 | tf_op jit(solution)/shard_map/reduce_scatter | solution.py:1035
  10.3 71.3 %collective-permute-start.1 = (bf16[768,512]{1,0:T(8,128)(2,1)}, bf16[768,512]{1,0:T(8,128)(2,1)}, u32[]{:S(2)}, u32[]{:S(2)}) collective-permute-start(bf16[768,512]{1,0:T(8,128)(2,1)} %refs_0_.1), channel_id=1, source_target_pairs={{0,1},{1,0},{2,3},{3,2},{4,5},{5,4},{6,7},{7,6},{8,9},{9,8},{10,11... | collective-permute-start | bytes 2359304 | tf_op jit(solution)/shard_map/ppermute | solution.py:825
  29.7 51.9 %collective-permute-start.3 = (bf16[768,512]{1,0:T(8,128)(2,1)}, bf16[768,512]{1,0:T(8,128)(2,1)}, u32[]{:S(2)}, u32[]{:S(2)}) collective-permute-start(bf16[768,512]{1,0:T(8,128)(2,1)} %collective-permute-done.2.refs_2_), channel_id=1, source_target_pairs={{0,1},{1,0},{2,3},{3,2},{4,5},{5,4},{6,7},{7,6},{8,9},{9,8},{10,11... | collective-permute-start | bytes 2359304 | tf_op jit(solution)/shard_map/ppermute | solution.py:825
  31.8 47.7 %collective-permute-start.7 = (bf16[768,256]{1,0:T(8,128)(2,1)}, bf16[768,256]{1,0:T(8,128)(2,1)}, u32[]{:S(2)}, u32[]{:S(2)}) collective-permute-start(bf16[768,256]{1,0:T(8,128)(2,1)} %constant_dynamic-slice_fusion.9), channel_id=1, source_target_pairs={{0,4},{4,0},{8,12},{12,8},{16,20},{20,16},{24,28},{28,24},{1,5},{5... | collective-permute-start | bytes 1179656 | tf_op jit(solution)/shard_map/ppermute | solution.py:825
  35.1 45.1 %collective-permute-start.11 = (bf16[768,256]{1,0:T(8,128)(2,1)}, bf16[768,256]{1,0:T(8,128)(2,1)}, u32[]{:S(2)}, u32[]{:S(2)}) collective-permute-start(bf16[768,256]{1,0:T(8,128)(2,1)} %constant_dynamic-slice_fusion.8), channel_id=1, source_target_pairs={{0,4},{4,0},{8,12},{12,8},{16,20},{20,16},{24,28},{28,24},{1,5},{5... | collective-permute-start | bytes 1179656 | tf_op jit(solution)/shard_map/ppermute | solution.py:825
  88.1 23.9 %collective-permute-start.12 = (bf16[768,256]{1,0:T(8,128)(2,1)}, bf16[768,256]{1,0:T(8,128)(2,1)S(1)}, u32[]{:S(2)}, u32[]{:S(2)}) collective-permute-start(bf16[768,256]{1,0:T(8,128)(2,1)} %collective-permute-done.11.refs_0_), channel_id=1, source_target_pairs={{0,1},{1,0},{2,3},{3,2},{4,5},{5,4},{6,7},{7,6},{8,9},{9,8},{10,11... | collective-permute-start | bytes 1179656 | tf_op jit(solution)/shard_map/ppermute | solution.py:825
  143.2 39.3 %collective-permute-start.20 = (bf16[768,1024]{1,0:T(8,128)(2,1)S(1)}, bf16[768,1024]{1,0:T(8,128)(2,1)S(1)}, u32[]{:S(2)}, u32[]{:S(2)}) collective-permute-start(bf16[768,1024]{1,0:T(8,128)(2,1)S(1)} %gated_forward.1.left_ref.cols_ref), channel_id=1, source_target_pairs={{0,4},{4,0},{8,12},{12,8},{16,20},{20,16},{24,28},{28,24},{1,5},{5... | collective-permute-start | bytes 4718600 | tf_op jit(solution)/shard_map/ppermute | solution.py:825
  240.8 53.0 %collective-permute-start.29 = (bf16[768,1408]{1,0:T(8,128)(2,1)}, bf16[768,1408]{1,0:T(8,128)(2,1)}, u32[]{:S(2)}, u32[]{:S(2)}) collective-permute-start(bf16[768,1408]{1,0:T(8,128)(2,1)} %get-tuple-element.120.cols_ref.left_ref), channel_id=1, source_target_pairs={{0,4},{4,0},{8,12},{12,8},{16,20},{20,16},{24,28},{28,24},{1,5},{5... | collective-permute-start | bytes 6488072 | tf_op jit(solution)/shard_map/ppermute | solution.py:825
  260.9 29.5 %collective-permute-start.26 = (bf16[768,512]{1,0:T(8,128)(2,1)}, bf16[768,512]{1,0:T(8,128)(2,1)}, u32[]{:S(2)}, u32[]{:S(2)}) collective-permute-start(bf16[768,512]{1,0:T(8,128)(2,1)} %get-tuple-element.240.refs_0_), channel_id=1, source_target_pairs={{0,2},{1,3},{2,0},{3,1},{4,6},{5,7},{6,4},{7,5},{8,10},{9,11},{10,... | collective-permute-start | bytes 2359304 | tf_op jit(solution)/shard_map/ppermute | solution.py:825
  261.7 26.6 %collective-permute-start.32 = (bf16[768,256]{1,0:T(8,128)(2,1)}, bf16[768,256]{1,0:T(8,128)(2,1)S(1)}, u32[]{:S(2)}, u32[]{:S(2)}) collective-permute-start(bf16[768,256]{1,0:T(8,128)(2,1)} %collective-permute-done.28.refs_0_), channel_id=1, source_target_pairs={{0,2},{1,3},{2,0},{3,1},{4,6},{5,7},{6,4},{7,5},{8,10},{9,11},{10,... | collective-permute-start | bytes 1179656 | tf_op jit(solution)/shard_map/ppermute | solution.py:825
  262.9 27.2 %collective-permute-start.31 = (bf16[768,256]{1,0:T(8,128)(2,1)}, bf16[768,256]{1,0:T(8,128)(2,1)S(1)}, u32[]{:S(2)}, u32[]{:S(2)}) collective-permute-start(bf16[768,256]{1,0:T(8,128)(2,1)} %collective-permute-done.28.refs_0_), channel_id=1, source_target_pairs={{0,1},{1,0},{2,3},{3,2},{4,5},{5,4},{6,7},{7,6},{8,9},{9,8},{10,11... | collective-permute-start | bytes 1179656 | tf_op jit(solution)/shard_map/ppermute | solution.py:825
  321.3 258.6 %reduce-scatter.11.cloned.1.call-start = ((), (), s32[]{:S(2)}) async-start(), calls=%async_computation.7 | async-start | bytes 3522560 | tf_op jit(solution)/shard_map/reduce_scatter | solution.py:1035
  336.1 24.3 %collective-permute-start.41 = (bf16[768,1024]{1,0:T(8,128)(2,1)}, bf16[768,1024]{1,0:T(8,128)(2,1)}, u32[]{:S(2)}, u32[]{:S(2)}) collective-permute-start(bf16[768,1024]{1,0:T(8,128)(2,1)} %slice.312), channel_id=1, source_target_pairs={{0,1},{1,0},{2,3},{3,2},{4,5},{5,4},{6,7},{7,6},{8,9},{9,8},{10,11... | collective-permute-start | bytes 4718600 | tf_op jit(solution)/shard_map/ppermute | solution.py:825
  359.2 57.0 %collective-permute-start.37 = (bf16[768,1408]{1,0:T(8,128)(2,1)}, bf16[768,1408]{1,0:T(8,128)(2,1)}, u32[]{:S(2)}, u32[]{:S(2)}) collective-permute-start(bf16[768,1408]{1,0:T(8,128)(2,1)} %get-tuple-element.128.refs_0_.cols_ref), channel_id=1, source_target_pairs={{0,4},{4,0},{8,12},{12,8},{16,20},{20,16},{24,28},{28,24},{1,5},{5... | collective-permute-start | bytes 6488072 | tf_op jit(solution)/shard_map/ppermute | solution.py:825
  397.2 31.6 %collective-permute-start.36 = (bf16[4,128,256]{2,1,0:T(8,128)(2,1)S(1)}, bf16[4,128,256]{2,1,0:T(8,128)(2,1)}, u32[]{:S(2)}, u32[]{:S(2)}) collective-permute-start(bf16[4,128,256]{2,1,0:T(8,128)(2,1)S(1)} %fusion.15), channel_id=1, source_target_pairs={{16,0},{20,4},{24,8},{28,12},{17,1},{21,5},{25,9},{29,13},{18,2},{... | collective-permute-start | bytes 786440 | tf_op jit(solution)/shard_map/ppermute | solution.py:820
  434.6 226.6 %reduce-scatter.19.cloned.1.call-start = ((), (), s32[]{:S(2)}) async-start(), calls=%async_computation.11 | async-start | bytes 30720
  434.6 85.8 %collective-permute-start.44 = (bf16[768,1408]{1,0:T(8,128)(2,1)}, bf16[768,1408]{1,0:T(8,128)(2,1)}, u32[]{:S(2)}, u32[]{:S(2)}) collective-permute-start(bf16[768,1408]{1,0:T(8,128)(2,1)} %get-tuple-element.151.refs_1_.cols_ref), channel_id=1, source_target_pairs={{0,4},{4,0},{8,12},{12,8},{16,20},{20,16},{24,28},{28,24},{1,5},{5... | collective-permute-start | bytes 6488072 | tf_op jit(solution)/shard_map/ppermute | solution.py:825
  435.6 84.8 %collective-permute-start.45 = (bf16[768,1024]{1,0:T(8,128)(2,1)}, bf16[768,1024]{1,0:T(8,128)(2,1)}, u32[]{:S(2)}, u32[]{:S(2)}) collective-permute-start(bf16[768,1024]{1,0:T(8,128)(2,1)} %copy-done.55), channel_id=1, source_target_pairs={{0,4},{4,0},{8,12},{12,8},{16,20},{20,16},{24,28},{28,24},{1,5},{5... | collective-permute-start | bytes 4718600 | tf_op jit(solution)/shard_map/ppermute | solution.py:825
  493.4 24.3 %collective-permute-start.43 = (f32[3,2048]{1,0:T(4,128)S(1)}, f32[3,2048]{1,0:T(4,128)S(1)}, u32[]{:S(2)}, u32[]{:S(2)}) collective-permute-start(f32[3,2048]{1,0:T(4,128)S(1)} %pad_maximum_fusion.6), channel_id=1, source_target_pairs={{4,0},{8,4},{12,8},{16,12},{20,16},{24,20},{28,24},{5,1},{9,5},{13... | collective-permute-start | bytes 73736 | tf_op jit(solution)/shard_map/ppermute | solution.py:820
  532.3 234.6 %reduce-scatter.15.cloned.1.call-start = ((), (), s32[]{:S(2)}) async-start(), calls=%async_computation.9 | async-start | bytes 2621440 | tf_op jit(solution)/shard_map/reduce_scatter | solution.py:1035
  532.9 247.8 %reduce-scatter.13.cloned.1.call-start = ((), (), s32[]{:S(2)}) async-start(), calls=%async_computation.8 | async-start | bytes 2621440 | tf_op jit(solution)/shard_map/reduce_scatter | solution.py:1035
  535.1 47.1 %collective-permute-start.46 = (bf16[768,512]{1,0:T(8,128)(2,1)}, bf16[768,512]{1,0:T(8,128)(2,1)}, u32[]{:S(2)}, u32[]{:S(2)}) collective-permute-start(bf16[768,512]{1,0:T(8,128)(2,1)} %get-tuple-element.153.refs_0_.cols_ref), channel_id=1, source_target_pairs={{0,4},{4,0},{8,12},{12,8},{16,20},{20,16},{24,28},{28,24},{1,5},{5... | collective-permute-start | bytes 2359304 | tf_op jit(solution)/shard_map/ppermute | solution.py:825
  535.1 47.1 %collective-permute-start.47 = (bf16[768,512]{1,0:T(8,128)(2,1)}, bf16[768,512]{1,0:T(8,128)(2,1)}, u32[]{:S(2)}, u32[]{:S(2)}) collective-permute-start(bf16[768,512]{1,0:T(8,128)(2,1)} %get-tuple-element.154.refs_1_.cols_ref), channel_id=1, source_target_pairs={{0,4},{4,0},{8,12},{12,8},{16,20},{20,16},{24,28},{28,24},{1,5},{5... | collective-permute-start | bytes 2359304 | tf_op jit(solution)/shard_map/ppermute | solution.py:825
  582.2 200.6 %reduce-scatter.17.cloned.1.call-start = ((), (), s32[]{:S(2)}) async-start(), calls=%async_computation.10 | async-start | bytes 3522560 | tf_op jit(solution)/shard_map/reduce_scatter | solution.py:1035
  582.3 34.0 %collective-permute-start.69 = (bf16[768,1024]{1,0:T(8,128)(2,1)}, bf16[768,1024]{1,0:T(8,128)(2,1)}, u32[]{:S(2)}, u32[]{:S(2)}) collective-permute-start(bf16[768,1024]{1,0:T(8,128)(2,1)} %fusion.52.refs_2_.cols_ref), channel_id=1, source_target_pairs={{0,4},{4,0},{8,12},{12,8},{16,20},{20,16},{24,28},{28,24},{1,5},{5... | collective-permute-start | bytes 4718600 | tf_op jit(solution)/shard_map/ppermute | solution.py:825
  627.3 27.0 %collective-permute-start.70 = (bf16[256,1024]{1,0:T(8,128)(2,1)}, bf16[256,1024]{1,0:T(8,128)(2,1)}, u32[]{:S(2)}, u32[]{:S(2)}) collective-permute-start(bf16[256,1024]{1,0:T(8,128)(2,1)} %get-tuple-element.244), channel_id=1, source_target_pairs={{0,8},{4,12},{1,9},{5,13},{2,10},{6,14},{3,11},{7,15}} | collective-permute-start | bytes 1572872 | tf_op jit(solution)/shard_map/ppermute | solution.py:1049
  656.5 25.8 %collective-permute-start.71 = (bf16[256,1024]{1,0:T(8,128)(2,1)}, bf16[256,1024]{1,0:T(8,128)(2,1)}, u32[]{:S(2)}, u32[]{:S(2)}) collective-permute-start(bf16[256,1024]{1,0:T(8,128)(2,1)} %add_convert_fusion.3), channel_id=1, source_target_pairs={{0,8},{4,12},{8,16},{12,20},{1,9},{5,13},{9,17},{13,21},{2,10},{6,... | collective-permute-start | bytes 1572872 | tf_op jit(solution)/shard_map/ppermute | solution.py:1049
  684.2 56.8 %collective-permute-start.74 = (bf16[256,1024]{1,0:T(8,128)(2,1)S(1)}, bf16[256,1024]{1,0:T(8,128)(2,1)S(1)}, u32[]{:S(2)}, u32[]{:S(2)}) collective-permute-start(bf16[256,1024]{1,0:T(8,128)(2,1)S(1)} %get-tuple-element.243), channel_id=1, source_target_pairs={{16,8},{20,12},{24,16},{28,20},{17,9},{21,13},{25,17},{29,21},{18,... | collective-permute-start | bytes 1572872 | tf_op jit(solution)/shard_map/ppermute | solution.py:1049
  689.1 24.2 %collective-permute-start.63 = (bf16[256,512]{1,0:T(8,128)(2,1)S(1)}, bf16[256,512]{1,0:T(8,128)(2,1)S(1)}, u32[]{:S(2)}, u32[]{:S(2)}) collective-permute-start(bf16[256,512]{1,0:T(8,128)(2,1)S(1)} %get-tuple-element.248), channel_id=1, source_target_pairs={{0,8},{4,12},{1,9},{5,13},{2,10},{6,14},{3,11},{7,15}} | collective-permute-start | bytes 786440 | tf_op jit(solution)/shard_map/ppermute | solution.py:1049
  701.8 27.2 %collective-permute-start.66 = (bf16[256,512]{1,0:T(8,128)(2,1)S(1)}, bf16[256,512]{1,0:T(8,128)(2,1)S(1)}, u32[]{:S(2)}, u32[]{:S(2)}) collective-permute-start(bf16[256,512]{1,0:T(8,128)(2,1)S(1)} %get-tuple-element.249), channel_id=1, source_target_pairs={{24,16},{28,20},{25,17},{29,21},{26,18},{30,22},{27,19},{31,23}} | collective-permute-start | bytes 786440 | tf_op jit(solution)/shard_map/ppermute | solution.py:1049
  708.1 47.8 %collective-permute-start.48 = (bf16[768,1024]{1,0:T(8,128)(2,1)S(1)}, bf16[768,1024]{1,0:T(8,128)(2,1)S(1)}, u32[]{:S(2)}, u32[]{:S(2)}) collective-permute-start(bf16[768,1024]{1,0:T(8,128)(2,1)S(1)} %slice.267), channel_id=1, source_target_pairs={{0,1},{1,0},{2,3},{3,2},{4,5},{5,4},{6,7},{7,6},{8,9},{9,8},{10,11... | collective-permute-start | bytes 4718600 | tf_op jit(solution)/shard_map/ppermute | solution.py:825
  724.5 38.5 %collective-permute-start.72 = (bf16[256,1024]{1,0:T(8,128)(2,1)S(1)}, bf16[256,1024]{1,0:T(8,128)(2,1)S(1)}, u32[]{:S(2)}, u32[]{:S(2)}) collective-permute-start(bf16[256,1024]{1,0:T(8,128)(2,1)S(1)} %get-tuple-element.242), channel_id=1, source_target_pairs={{0,8},{4,12},{8,16},{12,20},{16,24},{20,28},{1,9},{5,13},{9,17},{1... | collective-permute-start | bytes 1572872 | tf_op jit(solution)/shard_map/ppermute | solution.py:1049
  (152 other events, 1748.8 us)
Sparse Core Ops, SparseCore 0:
  321.4 57.2 reduce-scatter.8
  434.7 57.0 reduce-scatter.10
  532.5 20.5 reduce-scatter.18
  555.3 42.0 reduce-scatter.14
  599.5 49.0 reduce-scatter.12
  650.9 86.1 reduce-scatter.16

commit v4 on v3

--- a/solution.py
+++ b/solution.py
@@ -362,6 +362,7 @@
     value_tail_out,
     scal_out,
     rate_out,
+    got_out,
     carry,
     ext_query,
     ext_key,
@@ -369,10 +370,37 @@
     dy_query,
     dy_key,
     dy_value,
+    sending,
+    send_sem,
+    recv_sem,
 ):
     step = pl.program_id(0)
     group = groups - 1 - step
     keep = keep_ref[group]
+    seq, head = (lax.axis_index("seq"), lax.axis_index("head"))
+    partner = seq + 1 - 2 * (seq % 2)
+
+    def transfer(at, block):
+        return pltpu.make_async_remote_copy(
+            src_ref=sending.at[at % 2],
+            dst_ref=got_out.at[pl.ds(block * GROUP, GROUP), :],
+            send_sem=send_sem.at[at % 2],
+            recv_sem=recv_sem.at[block],
+            device_id=(partner, head),
+            device_id_type=pl.DeviceIdType.MESH,
+        )
+
+    @pl.when(step == 0)
+    def _():
+        barrier = pltpu.get_barrier_semaphore()
+        pl.semaphore_signal(
+            barrier, inc=1, device_id=(partner, head), device_id_type=pl.DeviceIdType.MESH
+        )
+        pl.semaphore_wait(barrier, 1)
+
+    @pl.when(step >= 2)
+    def _():
+        transfer(step, group + 2).wait_send()
 
     @pl.when(step == 0)
     def _():
@@ -512,6 +540,7 @@
     for kind, (section, out) in enumerate(zip(sections, outs)):
         now_ref, before_ref, rim_ref, conv_ref, ext_ref, dy_ref, width, cotangent = section
         pre_out, conv_out, back_out, tail_out = out
+        first_lane = kind * heads * DK
         fill(ext_ref, now_ref, before_ref, rim_ref, first, keep)
         dy_ref[8 + GROUP :, :] = dy_ref[8:16, :] * after_keep
         for h in range(heads):
@@ -540,6 +569,7 @@
             for tap in range(1, CONV):
                 d_pre = d_pre + dy_ref[pl.ds(8 + tap, GROUP), lanes] * conv_ref[tap : tap + 1, lanes]
             pre_out[:, lanes] = d_pre.astype(bf16)
+            sending[step % 2, :, pl.ds(first_lane + h * width, width)] = d_pre.astype(bf16)
 
             @pl.when(step == 0)
             def _():
@@ -551,6 +581,15 @@
                 for tap in range(2, CONV):
                     d_back = d_back + dy_ref[pl.ds(tap, 8), lanes] * conv_ref[tap : tap + 1, lanes]
                 back_out[:, lanes] = d_back * keep
+
+    transfer(step, group).start()
+
+    @pl.when(step == groups - 1)
+    def _():
+        transfer(step - 1, group + 1).wait_send()
+        transfer(step, group).wait_send()
+        for block in range(groups):
+            transfer(step, block).wait_recv()
 
 
 def delta_backward(pres, rims, convs, scal, rate, keep, made, entry, exit_grad, grad):
@@ -582,7 +621,8 @@
         + [whole((CONV * 8, w)) for w in widths]
         + [whole((8, w)) for w in widths]
         + [whole((8, w)) for w in widths]
-        + [token_block(columns, groups), whole((8, heads))],
+        + [token_block(columns, groups), whole((8, heads))]
+        + [pl.BlockSpec(memory_space=pl.ANY)],
         out_shape=[jax.ShapeDtypeStruct((tokens, w), bf16) for w in widths]
         + [jax.ShapeDtypeStruct((CONV * 8, w), f32) for w in widths]
         + [jax.ShapeDtypeStruct((8, w), f32) for w in widths]
@@ -590,11 +630,19 @@
         + [
             jax.ShapeDtypeStruct((tokens, columns), bf16),
             jax.ShapeDtypeStruct((8, heads), f32),
+            jax.ShapeDtypeStruct((tokens, sum(widths)), bf16),
         ],
         scratch_shapes=[pltpu.VMEM((heads * DK, DV), f32)]
         + [pltpu.VMEM((HALO + GROUP, w), f32) for w in widths]
-        + [pltpu.VMEM((16 + GROUP, w), f32) for w in widths],
-        compiler_params=pltpu.CompilerParams(vmem_limit_bytes=VMEM),
+        + [pltpu.VMEM((16 + GROUP, w), f32) for w in widths]
+        + [
+            pltpu.VMEM((2, GROUP, sum(widths)), bf16),
+            pltpu.SemaphoreType.DMA((2,)),
+            pltpu.SemaphoreType.DMA((groups,)),
+        ],
+        compiler_params=pltpu.CompilerParams(
+            vmem_limit_bytes=VMEM, collective_id=1, has_side_effects=True
+        ),
         cost_estimate=pl.CostEstimate(flops=10**6, bytes_accessed=10**4, transcendentals=0),
         name="delta_backward",
     )(keep, *pres, *pres, *rims, *convs, scal, rate, *made, entry, exit_grad, grad)
@@ -841,7 +889,7 @@
     out_ref[...] = total.astype(bf16)
 
 
-def pair_grad(rows, got_rows, cols, got_cols, turned, kept=None):
+def pair_grad(rows, got_rows, cols, got_cols, turned, kept=None, spot=0):
     odd = lax.axis_index("seq").astype(jnp.int32) % 2
     devices = lax.axis_size("seq")
     tokens, padded = cols.shape
@@ -849,6 +897,7 @@
     width = rows.shape[1] // devices
     if width % 128:
         part = jnp.concatenate([own_half(rows, odd, width), got_rows], axis=0)
+        got_cols = lax.slice_in_dim(got_cols, spot * padded, (spot + 1) * padded, axis=1)
         cols = jnp.concatenate([cols, got_cols], axis=0)[:, :count]
         if turned:
             part = part.reshape(2 * tokens, devices // 2, width)
@@ -866,15 +915,13 @@
                 pl.BlockSpec((tokens, width), lambda i, place: (0, 2 * i + place[0])),
                 pl.BlockSpec((tokens, width), lambda i, place: (0, i)),
                 still,
-                still,
+                pl.BlockSpec((tokens, padded), lambda i, place: (0, spot)),
             ],
             out_specs=pl.BlockSpec(block, lambda i, place: (i, 0)),
         ),
         out_shape=jax.ShapeDtypeStruct((devices // 2 * block[0], block[1]), bf16),
         compiler_params=pltpu.CompilerParams(vmem_limit_bytes=SMALL),
-        cost_estimate=pl.CostEstimate(
-            flops=2 * tokens * count * rows.shape[1], bytes_accessed=10**7, transcendentals=0
-        ),
+        cost_estimate=pl.CostEstimate(flops=10**6, bytes_accessed=10**4, transcendentals=0),
         name="weight_grad",
     )(odd[None], rows, got_rows, cols, got_cols)
 
@@ -1192,13 +1239,10 @@
     got_gated = exchanged(gated, "seq", 1)
     d_inner, got_gated = tied(d_inner, got_gated)
     inner_act, d_ffn_gate, d_ffn_up = ffn(normed_ffn, w_ffn_gate.T, w_ffn_up.T, d_inner)
-    ffn_out = head_scattered(plain_dense(inner_act, w_ffn_down, place))
-    hidden_out = (middle + ffn_out).astype(bf16)
     units = w_ffn_gate.shape[1]
     got_ffn_cols = partner_rows(cols(normed_ffn))
-    inner_sent, got_ffn_cols = tied(inner_act, got_ffn_cols)
+    inner_sent, d_ffn_gate, got_ffn_cols = tied(inner_act, d_ffn_gate, got_ffn_cols)
     got_inner = exchanged(inner_sent, "seq", 1)
-    got_normed_ffn = head_gathered(got_ffn_cols)
     d_normed_ffn, grad_ffn_gain, ffn_dots = norm_dense(
         [(d_ffn_gate, w_ffn_gate.T), (d_ffn_up, w_ffn_up.T)], sent, ffn_scale, ffn_gain, place
     )
@@ -1208,15 +1252,16 @@
         - cols(sent).astype(f32) * ffn_scale * ffn_dots
     )
     d_middle = grad_out.astype(f32) + d_sent_cols
-    d_mixed = head_gathered(d_middle.astype(bf16))
+    got_normed_ffn = head_gathered(got_ffn_cols)
+    middle_cols, got_normed_ffn = tied(d_middle.astype(bf16), got_normed_ffn)
+    d_mixed = head_gathered(middle_cols)
     d_gated = dense(d_mixed, w_out.T)
-    got_mixed_cols = partner_rows(d_middle.astype(bf16))
+    got_mixed_cols = partner_rows(middle_cols)
     d_gate_sent, got_inner, got_mixed_cols = tied(d_ffn_gate, got_inner, got_mixed_cols)
     got_d_gate = exchanged(d_gate_sent, "seq", 1)
-    got_d_mixed = head_gathered(got_mixed_cols)
     kept_down = pair_grad(grad_rows, got_grad_rows, inner_act, got_inner, True, units)
-    d_gated, kept_down, got_normed_ffn = tied(d_gated, kept_down, got_normed_ffn)
     grad_w_ffn_down = seq_scattered(kept_down)
+    d_gated, kept_down = tied(d_gated, kept_down)
     d_delta, d_gate_pre, gain_part, entry_grad = gated_backward(
         linear, local, gate_pre, entry, out_gain, d_gated, valid_mask
     )
@@ -1227,15 +1272,20 @@
         ],
         axis=2,
     )
+    back_pair, got_d_gate = tied(back_pair, got_d_gate)
+    got_back = exchanged(back_pair.astype(bf16), "seq", 1)
+    d_up_sent, got_mixed_cols, inner_late, got_back = tied(
+        d_ffn_up, got_mixed_cols, inner_act, got_back
+    )
+    got_d_up = exchanged(d_up_sent, "seq", 1)
     kept_gate = pair_grad(normed_ffn, got_normed_ffn, d_ffn_gate, got_d_gate, True, units)
-    got_back = exchanged(back_pair.astype(bf16), "seq", 1)
-    d_ffn_up, d_gate_pre, got_back = tied(d_ffn_up, d_gate_pre, got_back)
-    got_d_up = exchanged(d_ffn_up, "seq", 1)
-    got_d_gate_pre = exchanged(d_gate_pre, "seq", 1)
+    got_d_mixed = head_gathered(got_mixed_cols)
     kept_out = pair_grad(d_mixed, got_d_mixed, gated, got_gated, True)
+    ffn_out = head_scattered(plain_dense(inner_late, w_ffn_down, place))
+    hidden_out = (middle + ffn_out).astype(bf16)
     exit_grad = prefix(back_pair, got_back, -1).reshape(head_count * DK, DV)
-    exit_grad, kept_gate, kept_out, grad_w_ffn_down, hidden_out = tied(
-        exit_grad, kept_gate, kept_out, grad_w_ffn_down, hidden_out
+    exit_grad, kept_gate, kept_out, grad_w_ffn_down, hidden_out, got_d_up = tied(
+        exit_grad, kept_gate, kept_out, grad_w_ffn_down, hidden_out, got_d_up
     )
     grad_w_ffn_gate = seq_scattered(kept_gate)
     grad_w_out = seq_scattered(kept_out)
@@ -1243,19 +1293,35 @@
         pres, rims, convs, scal, rate, keep_flags, made, entry, exit_grad, d_delta
     )
     d_pres, conv_parts, backs, tails = (results[i : i + 3] for i in range(0, 12, 3))
-    d_scal, d_rate = results[12:]
-    backs = shifted(jnp.concatenate(backs, 1)[8 - (CONV - 1) :], "seq", -1)
-    tails = split(jnp.concatenate(tails, 1) + jnp.pad(backs, ((8 - (CONV - 1), 0), (0, 0))))
+    d_scal, d_rate, got_all = results[12:]
+    backs = jnp.concatenate(backs, 1)[8 - (CONV - 1) :]
+    tails = jnp.concatenate(tails, 1)
+    backs, tails, gate_sent, d_up_late = tied(backs, tails, d_gate_pre, d_ffn_up)
+    got_d_gate_pre = exchanged(gate_sent, "seq", 1)
+    kept_up = pair_grad(normed_ffn, got_normed_ffn, d_up_late, got_d_up, True, units)
+    grad_w_ffn_up = seq_scattered(kept_up)
+    crossing = [(i, (i - 1) ^ 1) for i in range(1, devices)]
+    got_tails = exchanged(tails, "seq", 1)
+    more = jnp.pad(lax.ppermute(backs, "seq", crossing), ((8 - (CONV - 1), 0), (0, 0)))
+    backs = jnp.pad(shifted(backs, "seq", -1), ((8 - (CONV - 1), 0), (0, 0)))
+    got_tails, more, backs, kept_up = tied(got_tails, more, backs, kept_up)
+    got_all = lax.dynamic_update_slice(
+        got_all, (got_tails + more).astype(bf16), (token_rows - 8, 0)
+    )
     d_query_pre, d_key_pre, d_value_pre = [
         lax.dynamic_update_slice(d_pre, tail.astype(bf16), (token_rows - 8, 0))
-        for d_pre, tail in zip(d_pres, tails)
+        for d_pre, tail in zip(d_pres, split(tails + backs))
     ]
-    d_query_pre, d_key_pre, d_value_pre, d_scal, got_d_up, got_d_gate_pre = tied(
-        d_query_pre, d_key_pre, d_value_pre, d_scal, got_d_up, got_d_gate_pre
-    )
-    kept_up = pair_grad(normed_ffn, got_normed_ffn, d_ffn_up, got_d_up, True, units)
+    kept_value = pair_grad(normed, got_normed, d_value_pre, got_all, False, None, 1)
+    kept_query = pair_grad(normed, got_normed, d_query_pre, got_all, False, None, 0)
+    kept_key = pair_grad(normed, got_normed, d_key_pre, got_all, False, None, 1)
+    query_key = jnp.concatenate([kept_query, kept_key], axis=1)
+    d_scal, kept_value, query_key, got_d_gate_pre, grad_w_ffn_gate = tied(
+        d_scal, kept_value, query_key, got_d_gate_pre, grad_w_ffn_gate
+    )
     kept_w_gate = pair_grad(normed, got_normed, d_gate_pre, got_d_gate_pre, False)
-    got_last = [exchanged(d_pre, "seq", 1) for d_pre in (d_query_pre, d_key_pre, d_value_pre)]
+    grad_w_gate = seq_scattered(kept_w_gate)
+    d_scal, kept_w_gate = tied(d_scal, kept_w_gate)
     small = dense(normed.T, d_scal)
     small = [part.reshape(devices, -1) for part in (small[:, :head_count], small[:, head_count:])]
     for part in conv_parts:
@@ -1287,17 +1353,10 @@
         attn_gain,
         place,
     )
-    d_normed, kept_up, kept_w_gate, grad_w_ffn_gate, *got_last[:2] = tied(
-        d_normed, kept_up, kept_w_gate, grad_w_ffn_gate, *got_last[:2]
-    )
-    grad_w_ffn_up = seq_scattered(kept_up)
-    grad_w_gate = seq_scattered(kept_w_gate)
-    kept_last = [
-        pair_grad(normed, got_normed, d_pre, got, False)
-        for d_pre, got in zip((d_query_pre, d_key_pre, d_value_pre), got_last)
-    ]
+    query_key = line_scattered(query_key)
+    grad_w_query, grad_w_key = (query_key[:, : widths[0]], query_key[:, widths[0] :])
+    grad_w_value = line_scattered(kept_value)
     d_normed = head_scattered(d_normed)
-    grad_w_query, grad_w_key, grad_w_value = [line_scattered(kept) for kept in kept_last]
     attn_dots = head_summed(attn_dots[:, 0])[:, None] / hidden_in.shape[1]
     grad_in = d_middle + attn_scale * (
         cols(attn_gain) * d_normed

time: 804 us -> 740 us (0.920)
  waiting for transfers between devices: 237 us -> 194 us
  Pallas kernels: 241 us -> 268 us
  local copies, waits for them, and re-layouts: 103 us -> 80.4 us
  starting transfers between devices: 103 us -> 91.5 us
  other arithmetic: 65.4 us -> 55.8 us
    ppermute x53 -> x51, waiting for transfers between devices: 175 us -> 132 us  [exchanged(): return lax.ppermute(block, axis, route)]
    unnamed x209 -> x205, local copies, waits for them, and re-layouts: 60.4 us -> 39.6 us
    pallas_call x1, Pallas kernels: 55.9 us -> 76.5 us  [delta_backward(): pl.pallas_call(functools.partial(backward_kernel, heads, groups), grid=(g...]
    ppermute x18 -> x12, starting transfers between devices: 53.8 us -> 33.3 us  [line_step(): return lax.ppermute(send, 'seq', route)]
    ppermute x18 -> x12, waiting for transfers between devices: 40.9 us -> 49.8 us  [line_step(): return lax.ppermute(send, 'seq', route)]
    ppermute x53 -> x51, starting transfers between devices: 32.3 us -> 40.8 us  [exchanged(): return lax.ppermute(block, axis, route)]
  transfers between devices with their start and end apart: 83 -> 76, of which waited for: 31 -> 26; matrix products, arithmetic and copies ran while one was open for 15% -> 16% of each run, Pallas kernels for 24% -> 32%
where the time goes in v4:
time: 740 us; the launch traced here: 730 us
  Pallas kernels  268 us (36%)
  waiting for transfers between devices  194 us (26%)
  starting transfers between devices  91.5 us (12%)
  local copies, waits for them, and re-layouts  80.4 us (11%)
  other arithmetic  55.8 us (8%)
  matrix products  23.3 us (3%)
  between operations  16.4 us (2%)
    ppermute x51, waiting for transfers between devices, exchanged(): return lax.ppermute(block, axis, route)  132 us
    pallas_call x1, Pallas kernels, delta_backward(): pl.pallas_call(functools.partial(backward_kernel, heads, groups), grid=(g...  76.5 us
    ppermute x12, waiting for transfers between devices, line_step(): return lax.ppermute(send, 'seq', route)  49.8 us
    pallas_call x8, Pallas kernels, pair_grad(): pl.pallas_call(functools.partial(weight_grad_kernel, turned), grid_spec=p...  47.7 us
    pallas_call x1, Pallas kernels, delta_forward(): pl.pallas_call(functools.partial(forward_kernel, heads, groups), grid=(gr...  41.1 us
    ppermute x51, starting transfers between devices, exchanged(): return lax.ppermute(block, axis, route)  40.8 us
    unnamed x205, local copies, waits for them, and re-layouts  39.6 us
    pallas_call x2, Pallas kernels, norm_dense(): pl.pallas_call(functools.partial(norm_dense_kernel, sides), grid_spec=plt...  35.7 us
  transfers between devices with their start and end apart: 76, of which 26 were waited for; matrix products, arithmetic and copies ran while one was open for 16% of the time, Pallas kernels for 32%

profile of v4, /device:TPU:0, one launch (start us, length us, event | category | flops | bytes accessed | tf_op | source)
XLA Modules:
  0.0 729.5 jit_solution(12533175742922129049)
XLA Ops:
  38.4 41.1 %delta_forward.1 = (bf16[768,512]{1,0:T(8,128)(2,1)}, bf16[768,512]{1,0:T(8,128)(2,1)}, bf16[768,1024]{1,0:T(8,128)(2,1)}, bf16[12,256,384]{2,1,0:T(8,128)(2,1)}...) custom-call(f32[12]{0:T(128)} %convert_subtract_fusion.keep_ref, ...), custom_call_target="tpu_custom_call" | custom-call | flops 1000000 | bytes 10000 | tf_op jit(solution)/shard_map/delta_forward/pallas_call | solution.py:289
  91.9 7.1 collective-permute-done.13.refs_2_
  120.2 5.5 rows_dense.1.grad_ref
  133.3 7.2 plain_dense.2
  146.8 17.8 %collective-permute-done.16 = bf16[768,512]{1,0:T(8,128)(2,1)S(1)} collective-permute-done((bf16[768,512]{1,0:T(8,128)(2,1)S(1)}, bf16[768,512]{1,0:T(8,128)(2,1)S(1)}, u32[]{:S(2)}, u32[]{:S(2)}) %collective-permute-start.16) | collective-permute-done | bytes 786464 | tf_op jit(solution)/shard_map/ppermute | solution.py:873
  168.1 18.3 %collective-permute-done.18.refs_2_ = bf16[768,512]{1,0:T(8,128)(2,1)} collective-permute-done((bf16[768,512]{1,0:T(8,128)(2,1)}, bf16[768,512]{1,0:T(8,128)(2,1)}, u32[]{:S(2)}, u32[]{:S(2)}) %collective-permute-start.18) | collective-permute-done | bytes 786464 | tf_op jit(solution)/shard_map/ppermute | solution.py:873
  197.1 17.3 %ffn.1 = (bf16[768,1408]{1,0:T(8,128)(2,1)}, bf16[768,1408]{1,0:T(8,128)(2,1)}, bf16[768,1408]{1,0:T(8,128)(2,1)}) custom-call(bf16[768,2048]{1,0:T(8,128)(2,1)} %copy-done.8, bf16[1376,2048]{1,0:T(8,128)(2,1)} %bitcast.104, bf16[1376,2048]{1,0:T(8,128)(2,1)} %bitcast.106, f32[768,1376]{1,0:T(8,128)} %copy-done.53), custom_call_target="tpu_custom_call" | custom-call | flops 8657043456 | bytes 20000000 | tf_op jit(solution)/shard_map/ffn/pallas_call | solution.py:1029
  214.4 16.9 %norm_dense.2 = (bf16[768,2048]{1,0:T(8,128)(2,1)}, f32[1,2048]{1,0:T(1,128)}, f32[768,1]{1,0:T(8,128)}) custom-call(s32[1]{0:T(128)} %bitcast.place_ref, bf16[768,1408]{1,0:T(8,128)(2,1)} %get-tuple-element.135.refs_0_.cols_ref, bf16[768,1408]{1,0:T(8,128)(2,1)} %get-tuple-element.163.refs_1_.cols_ref, bf16[1376,2048]{1,0:T(8,128)(2,1)} %bitcast.105, ...), custom_call_target="tpu_custom_call" | custom-call | flops 8858370048 | bytes 20000000 | tf_op jit(solution)/shard_map/norm_dense/pallas_call | solution.py:827
  240.8 5.9 collective-permute-done.28.refs_2_
  252.0 10.8 %collective-permute-done.26 = f32[768]{0:T(1024)S(1)} collective-permute-done((f32[768]{0:T(1024)S(1)}, f32[768]{0:T(1024)S(1)}, u32[]{:S(2)}, u32[]{:S(2)}) %collective-permute-start.26) | collective-permute-done | bytes 3104 | tf_op jit(solution)/shard_map/ppermute | solution.py:873
  272.9 10.4 %collective-permute-done.22.got_cols_ref = bf16[768,1408]{1,0:T(8,128)(2,1)} collective-permute-done((bf16[768,1408]{1,0:T(8,128)(2,1)}, bf16[768,1408]{1,0:T(8,128)(2,1)}, u32[]{:S(2)}, u32[]{:S(2)}) %collective-permute-start.22) | collective-permute-done | bytes 2162720 | tf_op jit(solution)/shard_map/ppermute | solution.py:873
  283.3 7.9 %collective-permute-done.30.refs_0_ = bf16[768,256]{1,0:T(8,128)(2,1)S(1)} collective-permute-done((bf16[768,256]{1,0:T(8,128)(2,1)S(1)}, bf16[768,256]{1,0:T(8,128)(2,1)S(1)}, u32[]{:S(2)}, u32[]{:S(2)}) %collective-permute-start.30) | collective-permute-done | bytes 393248 | tf_op jit(solution)/shard_map/ppermute | solution.py:873
  292.9 8.0 %weight_grad.8 = bf16[5504,256]{1,0:T(8,128)(2,1)S(1)} custom-call(s32[1]{0:T(128)} %bitcast.12.place_ref, bf16[768,2048]{1,0:T(8,128)(2,1)S(1)} %copy-done.20, bf16[768,1024]{1,0:T(8,128)(2,1)S(1)} %copy-done.29, bf16[768,1408]{1,0:T(8,128)(2,1)} %get-tuple-element.142.cols_ref.left_ref, bf16[768,1408]{1,0:T(8,128)(2,1)} %collective-permute-done.22.got_cols_ref), custom_call_target="tpu_custom_call" | custom-call | flops 1000000 | bytes 10000 | tf_op jit(solution)/shard_map/weight_grad/pallas_call | solution.py:909
  315.9 5.3 gated_backward.1
  322.5 17.6 %collective-permute-done.34.got_cols_ref = bf16[768,1408]{1,0:T(8,128)(2,1)} collective-permute-done((bf16[768,1408]{1,0:T(8,128)(2,1)}, bf16[768,1408]{1,0:T(8,128)(2,1)}, u32[]{:S(2)}, u32[]{:S(2)}) %collective-permute-start.34) | collective-permute-done | bytes 2162720 | tf_op jit(solution)/shard_map/ppermute | solution.py:873
  341.4 8.5 %collective-permute-done.35 = bf16[4,128,384]{2,1,0:T(8,128)(2,1)S(1)} collective-permute-done((bf16[4,128,384]{2,1,0:T(8,128)(2,1)S(1)}, bf16[4,128,384]{2,1,0:T(8,128)(2,1)S(1)}, u32[]{:S(2)}, u32[]{:S(2)}) %collective-permute-start.35) | collective-permute-done | bytes 393248 | tf_op jit(solution)/shard_map/ppermute | solution.py:873
  350.0 9.3 %plain_dense.3 = bf16[768,2048]{1,0:T(8,128)(2,1)S(1)} custom-call(s32[1]{0:T(128)} %bitcast.place_ref, bf16[768,1408]{1,0:T(8,128)(2,1)} %get-tuple-element.142.cols_ref.left_ref, bf16[1376,2048]{1,0:T(8,128)(2,1)S(1)} %bitcast.87), custom_call_target="tpu_custom_call" | custom-call | flops 4429185024 | bytes 10000000 | tf_op jit(solution)/shard_map/plain_dense/pallas_call | solution.py:777
  371.8 7.5 %collective-permute-done.36 = bf16[4,128,384]{2,1,0:T(8,128)(2,1)S(1)} collective-permute-done((bf16[4,128,384]{2,1,0:T(8,128)(2,1)S(1)}, bf16[4,128,384]{2,1,0:T(8,128)(2,1)S(1)}, u32[]{:S(2)}, u32[]{:S(2)}) %collective-permute-start.36) | collective-permute-done | bytes 393248 | tf_op jit(solution)/shard_map/ppermute | solution.py:868
  381.6 8.2 %weight_grad.9 = bf16[5504,256]{1,0:T(8,128)(2,1)S(1)} custom-call(s32[1]{0:T(128)} %bitcast.12.place_ref, bf16[768,2048]{1,0:T(8,128)(2,1)S(1)} %copy-done.9, bf16[768,1024]{1,0:T(8,128)(2,1)S(1)} %copy-done.12, bf16[768,1408]{1,0:T(8,128)(2,1)} %get-tuple-element.135.refs_0_.cols_ref, bf16[768,1408]{1,0:T(8,128)(2,1)} %collective-permute-done.34.got_cols_ref), custom_call_target="tpu_custom_call" | custom-call | flops 1000000 | bytes 10000 | tf_op jit(solution)/shard_map/weight_grad/pallas_call | solution.py:909
  402.6 6.6 weight_grad.10
  417.6 76.5 %delta_backward.1 = (bf16[768,512]{1,0:T(8,128)(2,1)}, bf16[768,512]{1,0:T(8,128)(2,1)}, bf16[768,1024]{1,0:T(8,128)(2,1)}, f32[32,512]{1,0:T(8,128)}, f32[32,51...) custom-call(f32[12]{0:T(128)} %convert_subtract_fusion.keep_ref, ...), custom_call_target="tpu_custom_call" | custom-call | flops 1000000 | bytes 10000 | tf_op jit(solution)/shard_map/delta_backward/pallas_call | solution.py:602
  499.6 8.0 %weight_grad.11 = bf16[5504,256]{1,0:T(8,128)(2,1)S(1)} custom-call(s32[1]{0:T(128)} %bitcast.12.place_ref, bf16[768,2048]{1,0:T(8,128)(2,1)S(1)} %copy-done.10, bf16[768,1024]{1,0:T(8,128)(2,1)S(1)} %copy-done.13, bf16[768,1408]{1,0:T(8,128)(2,1)} %get-tuple-element.163.refs_1_.cols_ref, bf16[768,1408]{1,0:T(8,128)(2,1)} %collective-permute-done.43.got_cols_ref), custom_call_target="tpu_custom_call" | custom-call | flops 1000000 | bytes 10000 | tf_op jit(solution)/shard_map/weight_grad/pallas_call | solution.py:909
  547.1 7.1 collective-permute-done.47.got_cols_ref
  555.7 5.9 weight_grad.15
  567.1 18.8 %norm_dense.3 = (bf16[768,2048]{1,0:T(8,128)(2,1)}, f32[1,2048]{1,0:T(1,128)}, f32[768,1]{1,0:T(8,128)}) custom-call(s32[1]{0:T(128)} %bitcast.place_ref, bf16[768,512]{1,0:T(8,128)(2,1)} %get-tuple-element.269.cols_ref.refs_0_, bf16[768,512]{1,0:T(8,128)(2,1)} %get-tuple-element.268.cols_ref.refs_1_, bf16[768,1024]{1,0:T(8,128)(2,1)} %copy-done.42, ...), custom_call_target="tpu_custom_call" | custom-call | flops 9688842240 | bytes 20000000 | tf_op jit(solution)/shard_map/norm_dense/pallas_call | solution.py:827
  608.5 7.4 %collective-permute-done.55 = f32[4384]{0:T(1024)S(1)} collective-permute-done((f32[4384]{0:T(1024)S(1)}, f32[4384]{0:T(1024)S(1)}, u32[]{:S(2)}, u32[]{:S(2)}) %collective-permute-start.55) | collective-permute-done | bytes 17568 | tf_op jit(solution)/shard_map/ppermute | solution.py:873
  615.9 6.3 collective-permute-start.56
  635.4 14.1 %collective-permute-done.58 = bf16[256,1024]{1,0:T(8,128)(2,1)} collective-permute-done((bf16[256,1024]{1,0:T(8,128)(2,1)}, bf16[256,1024]{1,0:T(8,128)(2,1)}, u32[]{:S(2)}, u32[]{:S(2)}) %collective-permute-start.58) | collective-permute-done | bytes 524320 | tf_op jit(solution)/shard_map/ppermute | solution.py:1096
  652.3 18.7 %collective-permute-done.64 = bf16[256,1024]{1,0:T(8,128)(2,1)} collective-permute-done((bf16[256,1024]{1,0:T(8,128)(2,1)S(1)}, bf16[256,1024]{1,0:T(8,128)(2,1)}, u32[]{:S(2)}, u32[]{:S(2)}) %collective-permute-start.64) | collective-permute-done | bytes 524320 | tf_op jit(solution)/shard_map/ppermute | solution.py:1096
  675.9 10.2 %collective-permute-start.65 = (bf16[256,1024]{1,0:T(8,128)(2,1)S(1)}, bf16[256,1024]{1,0:T(8,128)(2,1)S(1)}, u32[]{:S(2)}, u32[]{:S(2)}) collective-permute-start(bf16[256,1024]{1,0:T(8,128)(2,1)S(1)} %get-tuple-element.256), channel_id=1, source_target_pairs={{0,8},{4,12},{8,16},{12,20},{16,24},{20,28},{1,9},{5,13},{9,17},{1... | collective-permute-start | bytes 1572872 | tf_op jit(solution)/shard_map/ppermute | solution.py:1096
  697.9 8.9 %collective-permute-done.59 = bf16[256,1024]{1,0:T(8,128)(2,1)S(1)} collective-permute-done((bf16[256,1024]{1,0:T(8,128)(2,1)S(1)}, bf16[256,1024]{1,0:T(8,128)(2,1)S(1)}, u32[]{:S(2)}, u32[]{:S(2)}) %collective-permute-start.59) | collective-permute-done | bytes 524320 | tf_op jit(solution)/shard_map/ppermute | solution.py:1096
  709.4 6.7 collective-permute-done.68
  (509 shorter events, 287.4 us)
Async XLA Ops:
  7.2 407.3 %reduce-scatter.9.cloned.1.call-start = ((), (), s32[]{:S(2)}) async-start(), calls=%async_computation.6 | async-start | bytes 3522560 | tf_op jit(solution)/shard_map/reduce_scatter | solution.py:1082
  7.3 22.5 %collective-permute-start.2 = (bf16[768,512]{1,0:T(8,128)(2,1)}, bf16[768,512]{1,0:T(8,128)(2,1)}, u32[]{:S(2)}, u32[]{:S(2)}) collective-permute-start(bf16[768,512]{1,0:T(8,128)(2,1)} %refs_0_.1), channel_id=1, source_target_pairs={{0,2},{1,3},{2,0},{3,1},{4,6},{5,7},{6,4},{7,5},{8,10},{9,11},{10,... | collective-permute-start | bytes 2359304 | tf_op jit(solution)/shard_map/ppermute | solution.py:873
  10.3 71.3 %collective-permute-start.1 = (bf16[768,512]{1,0:T(8,128)(2,1)}, bf16[768,512]{1,0:T(8,128)(2,1)}, u32[]{:S(2)}, u32[]{:S(2)}) collective-permute-start(bf16[768,512]{1,0:T(8,128)(2,1)} %refs_0_.1), channel_id=1, source_target_pairs={{0,1},{1,0},{2,3},{3,2},{4,5},{5,4},{6,7},{7,6},{8,9},{9,8},{10,11... | collective-permute-start | bytes 2359304 | tf_op jit(solution)/shard_map/ppermute | solution.py:873
  29.7 51.8 %collective-permute-start.3 = (bf16[768,512]{1,0:T(8,128)(2,1)}, bf16[768,512]{1,0:T(8,128)(2,1)}, u32[]{:S(2)}, u32[]{:S(2)}) collective-permute-start(bf16[768,512]{1,0:T(8,128)(2,1)} %collective-permute-done.2.refs_2_), channel_id=1, source_target_pairs={{0,1},{1,0},{2,3},{3,2},{4,5},{5,4},{6,7},{7,6},{8,9},{9,8},{10,11... | collective-permute-start | bytes 2359304 | tf_op jit(solution)/shard_map/ppermute | solution.py:873
  31.8 47.7 %collective-permute-start.7 = (bf16[768,256]{1,0:T(8,128)(2,1)}, bf16[768,256]{1,0:T(8,128)(2,1)}, u32[]{:S(2)}, u32[]{:S(2)}) collective-permute-start(bf16[768,256]{1,0:T(8,128)(2,1)} %constant_dynamic-slice_fusion.7), channel_id=1, source_target_pairs={{0,4},{4,0},{8,12},{12,8},{16,20},{20,16},{24,28},{28,24},{1,5},{5... | collective-permute-start | bytes 1179656 | tf_op jit(solution)/shard_map/ppermute | solution.py:873
  35.0 45.1 %collective-permute-start.11 = (bf16[768,256]{1,0:T(8,128)(2,1)}, bf16[768,256]{1,0:T(8,128)(2,1)}, u32[]{:S(2)}, u32[]{:S(2)}) collective-permute-start(bf16[768,256]{1,0:T(8,128)(2,1)} %constant_dynamic-slice_fusion.6), channel_id=1, source_target_pairs={{0,4},{4,0},{8,12},{12,8},{16,20},{20,16},{24,28},{28,24},{1,5},{5... | collective-permute-start | bytes 1179656 | tf_op jit(solution)/shard_map/ppermute | solution.py:873
  88.1 23.8 %collective-permute-start.12 = (bf16[768,256]{1,0:T(8,128)(2,1)}, bf16[768,256]{1,0:T(8,128)(2,1)S(1)}, u32[]{:S(2)}, u32[]{:S(2)}) collective-permute-start(bf16[768,256]{1,0:T(8,128)(2,1)} %collective-permute-done.11.refs_0_), channel_id=1, source_target_pairs={{0,1},{1,0},{2,3},{3,2},{4,5},{5,4},{6,7},{7,6},{8,9},{9,8},{10,11... | collective-permute-start | bytes 1179656 | tf_op jit(solution)/shard_map/ppermute | solution.py:873
  145.8 40.6 %collective-permute-start.20 = (bf16[768,1024]{1,0:T(8,128)(2,1)}, bf16[768,1024]{1,0:T(8,128)(2,1)}, u32[]{:S(2)}, u32[]{:S(2)}) collective-permute-start(bf16[768,1024]{1,0:T(8,128)(2,1)} %gated_forward.1.left_ref.cols_ref), channel_id=1, source_target_pairs={{0,4},{4,0},{8,12},{12,8},{16,20},{20,16},{24,28},{28,24},{1,5},{5... | collective-permute-start | bytes 4718600 | tf_op jit(solution)/shard_map/ppermute | solution.py:873
  233.0 50.2 %collective-permute-start.22 = (bf16[768,1408]{1,0:T(8,128)(2,1)}, bf16[768,1408]{1,0:T(8,128)(2,1)}, u32[]{:S(2)}, u32[]{:S(2)}) collective-permute-start(bf16[768,1408]{1,0:T(8,128)(2,1)} %get-tuple-element.142.cols_ref.left_ref), channel_id=1, source_target_pairs={{0,4},{4,0},{8,12},{12,8},{16,20},{20,16},{24,28},{28,24},{1,5},{5... | collective-permute-start | bytes 6488072 | tf_op jit(solution)/shard_map/ppermute | solution.py:873
  239.8 25.7 %collective-permute-start.24 = (bf16[768,512]{1,0:T(8,128)(2,1)}, bf16[768,512]{1,0:T(8,128)(2,1)}, u32[]{:S(2)}, u32[]{:S(2)}) collective-permute-start(bf16[768,512]{1,0:T(8,128)(2,1)} %slice.458), channel_id=1, source_target_pairs={{0,2},{1,3},{2,0},{3,1},{4,6},{5,7},{6,4},{7,5},{8,10},{9,11},{10,... | collective-permute-start | bytes 2359304 | tf_op jit(solution)/shard_map/ppermute | solution.py:873
  270.0 22.4 %collective-permute-start.32 = (bf16[768,512]{1,0:T(8,128)(2,1)}, bf16[768,512]{1,0:T(8,128)(2,1)}, u32[]{:S(2)}, u32[]{:S(2)}) collective-permute-start(bf16[768,512]{1,0:T(8,128)(2,1)} %get-tuple-element.129.refs_0_), channel_id=1, source_target_pairs={{0,2},{1,3},{2,0},{3,1},{4,6},{5,7},{6,4},{7,5},{8,10},{9,11},{10,... | collective-permute-start | bytes 2359304 | tf_op jit(solution)/shard_map/ppermute | solution.py:873
  291.1 48.9 %collective-permute-start.34 = (bf16[768,1408]{1,0:T(8,128)(2,1)}, bf16[768,1408]{1,0:T(8,128)(2,1)}, u32[]{:S(2)}, u32[]{:S(2)}) collective-permute-start(bf16[768,1408]{1,0:T(8,128)(2,1)} %get-tuple-element.135.refs_0_.cols_ref), channel_id=1, source_target_pairs={{0,4},{4,0},{8,12},{12,8},{16,20},{20,16},{24,28},{28,24},{1,5},{5... | collective-permute-start | bytes 6488072 | tf_op jit(solution)/shard_map/ppermute | solution.py:873
  302.6 240.0 %reduce-scatter.15.cloned.1.call-start = ((), (), s32[]{:S(2)}) async-start(), calls=%async_computation.9 | async-start | bytes 2621440 | tf_op jit(solution)/shard_map/reduce_scatter | solution.py:1082
  365.0 51.7 %collective-permute-start.43 = (bf16[768,1408]{1,0:T(8,128)(2,1)}, bf16[768,1408]{1,0:T(8,128)(2,1)}, u32[]{:S(2)}, u32[]{:S(2)}) collective-permute-start(bf16[768,1408]{1,0:T(8,128)(2,1)} %get-tuple-element.163.refs_1_.cols_ref), channel_id=1, source_target_pairs={{0,4},{4,0},{8,12},{12,8},{16,20},{20,16},{24,28},{28,24},{1,5},{5... | collective-permute-start | bytes 6488072 | tf_op jit(solution)/shard_map/ppermute | solution.py:873
  366.5 26.0 %collective-permute-start.39 = (bf16[768,256]{1,0:T(8,128)(2,1)S(1)}, bf16[768,256]{1,0:T(8,128)(2,1)}, u32[]{:S(2)}, u32[]{:S(2)}) collective-permute-start(bf16[768,256]{1,0:T(8,128)(2,1)S(1)} %copy-done.47), channel_id=1, source_target_pairs={{0,2},{1,3},{2,0},{3,1},{4,6},{5,7},{6,4},{7,5},{8,10},{9,11},{10,... | collective-permute-start | bytes 1179656 | tf_op jit(solution)/shard_map/ppermute | solution.py:873
  370.8 39.7 %collective-permute-start.42 = (bf16[768,512]{1,0:T(8,128)(2,1)}, bf16[768,512]{1,0:T(8,128)(2,1)}, u32[]{:S(2)}, u32[]{:S(2)}) collective-permute-start(bf16[768,512]{1,0:T(8,128)(2,1)} %slice.457), channel_id=1, source_target_pairs={{0,2},{1,3},{2,0},{3,1},{4,6},{5,7},{6,4},{7,5},{8,10},{9,11},{10,... | collective-permute-start | bytes 2359304 | tf_op jit(solution)/shard_map/ppermute | solution.py:873
  416.8 127.9 %reduce-scatter.11.cloned.1.call-start = ((), (), s32[]{:S(2)}) async-start(), calls=%async_computation.7 | async-start | bytes 3522560 | tf_op jit(solution)/shard_map/reduce_scatter | solution.py:1082
  417.5 186.9 %reduce-scatter.17.cloned.1.call-start = ((), (), s32[]{:S(2)}) async-start(), calls=%async_computation.10 | async-start | bytes 3522560 | tf_op jit(solution)/shard_map/reduce_scatter | solution.py:1082
  509.3 120.5 %reduce-scatter.19.cloned.1.call-start = ((), (), s32[]{:S(2)}) async-start(), calls=%async_computation.11 | async-start | bytes 30720
  518.0 36.3 %collective-permute-start.47 = (bf16[768,1024]{1,0:T(8,128)(2,1)}, bf16[768,1024]{1,0:T(8,128)(2,1)}, u32[]{:S(2)}, u32[]{:S(2)}) collective-permute-start(bf16[768,1024]{1,0:T(8,128)(2,1)} %copy-done.38), channel_id=1, source_target_pairs={{0,4},{4,0},{8,12},{12,8},{16,20},{20,16},{24,28},{28,24},{1,5},{5... | collective-permute-start | bytes 4718600 | tf_op jit(solution)/shard_map/ppermute | solution.py:873
  565.9 29.4 %collective-permute-start.69 = (bf16[4,24,128]{2,1,0:T(8,128)(2,1)S(1)}, bf16[4,24,128]{2,1,0:T(8,128)(2,1)S(1)}, u32[]{:S(2)}, u32[]{:S(2)}) collective-permute-start(bf16[4,24,128]{2,1,0:T(8,128)(2,1)S(1)} %dynamic-slice_bitcast_fusion), channel_id=1, source_target_pairs={{0,4},{4,0},{8,12},{12,8},{16,20},{20,16},{24,28},{28,24},{1,5},{5... | collective-permute-start | bytes 73736 | tf_op jit(solution)/shard_map/ppermute | solution.py:873
  587.8 38.7 %collective-permute-start.63 = (bf16[256,1024]{1,0:T(8,128)(2,1)}, bf16[256,1024]{1,0:T(8,128)(2,1)S(1)}, u32[]{:S(2)}, u32[]{:S(2)}) collective-permute-start(bf16[256,1024]{1,0:T(8,128)(2,1)} %get-tuple-element.258), channel_id=1, source_target_pairs={{0,8},{4,12},{1,9},{5,13},{2,10},{6,14},{3,11},{7,15}} | collective-permute-start | bytes 1572872 | tf_op jit(solution)/shard_map/ppermute | solution.py:1096
  591.8 60.5 %collective-permute-start.66 = (bf16[256,1024]{1,0:T(8,128)(2,1)}, bf16[256,1024]{1,0:T(8,128)(2,1)}, u32[]{:S(2)}, u32[]{:S(2)}) collective-permute-start(bf16[256,1024]{1,0:T(8,128)(2,1)} %get-tuple-element.259), channel_id=1, source_target_pairs={{24,16},{28,20},{25,17},{29,21},{26,18},{30,22},{27,19},{31,23}} | collective-permute-start | bytes 1572872 | tf_op jit(solution)/shard_map/ppermute | solution.py:1096
  595.9 124.2 %reduce-scatter.13.cloned.1.call-start = ((), (), s32[]{:S(2)}) async-start(), calls=%async_computation.8 | async-start | bytes 2621440 | tf_op jit(solution)/shard_map/reduce_scatter | solution.py:1082
  598.2 24.0 %collective-permute-start.57 = (bf16[256,1024]{1,0:T(8,128)(2,1)}, bf16[256,1024]{1,0:T(8,128)(2,1)S(1)}, u32[]{:S(2)}, u32[]{:S(2)}) collective-permute-start(bf16[256,1024]{1,0:T(8,128)(2,1)} %get-tuple-element.262), channel_id=1, source_target_pairs={{0,8},{4,12},{1,9},{5,13},{2,10},{6,14},{3,11},{7,15}} | collective-permute-start | bytes 1572872 | tf_op jit(solution)/shard_map/ppermute | solution.py:1096
  607.0 28.4 %collective-permute-start.60 = (bf16[256,1024]{1,0:T(8,128)(2,1)}, bf16[256,1024]{1,0:T(8,128)(2,1)}, u32[]{:S(2)}, u32[]{:S(2)}) collective-permute-start(bf16[256,1024]{1,0:T(8,128)(2,1)} %get-tuple-element.263), channel_id=1, source_target_pairs={{24,16},{28,20},{25,17},{29,21},{26,18},{30,22},{27,19},{31,23}} | collective-permute-start | bytes 1572872 | tf_op jit(solution)/shard_map/ppermute | solution.py:1096
  624.2 25.3 %collective-permute-start.58 = (bf16[256,1024]{1,0:T(8,128)(2,1)}, bf16[256,1024]{1,0:T(8,128)(2,1)}, u32[]{:S(2)}, u32[]{:S(2)}) collective-permute-start(bf16[256,1024]{1,0:T(8,128)(2,1)} %add_convert_fusion.7), channel_id=1, source_target_pairs={{0,8},{4,12},{8,16},{12,20},{1,9},{5,13},{9,17},{13,21},{2,10},{6,... | collective-permute-start | bytes 1572872 | tf_op jit(solution)/shard_map/ppermute | solution.py:1096
  626.7 44.3 %collective-permute-start.64 = (bf16[256,1024]{1,0:T(8,128)(2,1)S(1)}, bf16[256,1024]{1,0:T(8,128)(2,1)}, u32[]{:S(2)}, u32[]{:S(2)}) collective-permute-start(bf16[256,1024]{1,0:T(8,128)(2,1)S(1)} %add_convert_fusion.3), channel_id=1, source_target_pairs={{0,8},{4,12},{8,16},{12,20},{1,9},{5,13},{9,17},{13,21},{2,10},{6,... | collective-permute-start | bytes 1572872 | tf_op jit(solution)/shard_map/ppermute | solution.py:1096
  630.4 63.8 %collective-permute-start.48 = (bf16[768,1024]{1,0:T(8,128)(2,1)}, bf16[768,1024]{1,0:T(8,128)(2,1)}, u32[]{:S(2)}, u32[]{:S(2)}) collective-permute-start(bf16[768,1024]{1,0:T(8,128)(2,1)} %slice.273), channel_id=1, source_target_pairs={{0,1},{1,0},{2,3},{3,2},{4,5},{5,4},{6,7},{7,6},{8,9},{9,8},{10,11... | collective-permute-start | bytes 4718600 | tf_op jit(solution)/shard_map/ppermute | solution.py:873
  651.5 39.7 %collective-permute-start.61 = (bf16[256,1024]{1,0:T(8,128)(2,1)S(1)}, bf16[256,1024]{1,0:T(8,128)(2,1)S(1)}, u32[]{:S(2)}, u32[]{:S(2)}) collective-permute-start(bf16[256,1024]{1,0:T(8,128)(2,1)S(1)} %get-tuple-element.261), channel_id=1, source_target_pairs={{16,8},{20,12},{24,16},{28,20},{17,9},{21,13},{25,17},{29,21},{18,... | collective-permute-start | bytes 1572872 | tf_op jit(solution)/shard_map/ppermute | solution.py:1096
  675.9 33.6 %collective-permute-start.65 = (bf16[256,1024]{1,0:T(8,128)(2,1)S(1)}, bf16[256,1024]{1,0:T(8,128)(2,1)S(1)}, u32[]{:S(2)}, u32[]{:S(2)}) collective-permute-start(bf16[256,1024]{1,0:T(8,128)(2,1)S(1)} %get-tuple-element.256), channel_id=1, source_target_pairs={{0,8},{4,12},{8,16},{12,20},{16,24},{20,28},{1,9},{5,13},{9,17},{1... | collective-permute-start | bytes 1572872 | tf_op jit(solution)/shard_map/ppermute | solution.py:1096
  692.9 23.3 %collective-permute-start.68 = (bf16[256,1024]{1,0:T(8,128)(2,1)S(1)}, bf16[256,1024]{1,0:T(8,128)(2,1)S(1)}, u32[]{:S(2)}, u32[]{:S(2)}) collective-permute-start(bf16[256,1024]{1,0:T(8,128)(2,1)S(1)} %add_convert_fusion), channel_id=1, source_target_pairs={{8,0},{12,4},{16,8},{20,12},{24,16},{28,20},{9,1},{13,5},{17,9},{2... | collective-permute-start | bytes 1572872 | tf_op jit(solution)/shard_map/ppermute | solution.py:1096
  (143 other events, 1603.0 us)
Sparse Core Ops, SparseCore 0:
  302.7 57.2 reduce-scatter.8
  416.9 43.8 reduce-scatter.14
  463.2 54.3 reduce-scatter.10
  519.9 54.9 reduce-scatter.16
  596.0 17.5 reduce-scatter.18
  615.8 61.8 reduce-scatter.12

commit v5 on v4

--- a/solution.py
+++ b/solution.py
@@ -324,6 +324,7 @@
 def backward_kernel(
     heads,
     groups,
+    devices,
     keep_ref,
     query_pre,
     key_pre,
@@ -354,14 +355,12 @@
     query_conv_out,
     key_conv_out,
     value_conv_out,
-    query_back_out,
-    key_back_out,
-    value_back_out,
-    query_tail_out,
-    key_tail_out,
-    value_tail_out,
     scal_out,
     rate_out,
+    tail_out,
+    own_back_out,
+    other_back_out,
+    got_tail_out,
     got_out,
     carry,
     ext_query,
@@ -373,6 +372,12 @@
     sending,
     send_sem,
     recv_sem,
+    back_send,
+    tail_got,
+    own_got,
+    other_got,
+    rim_send_sem,
+    rim_recv_sem,
 ):
     step = pl.program_id(0)
     group = groups - 1 - step
@@ -390,13 +395,42 @@
             device_id_type=pl.DeviceIdType.MESH,
         )
 
+    def rim_transfer(kind, source, target, to):
+        return pltpu.make_async_remote_copy(
+            src_ref=source,
+            dst_ref=target,
+            send_sem=rim_send_sem.at[kind],
+            recv_sem=rim_recv_sem.at[kind],
+            device_id=(to, head),
+            device_id_type=pl.DeviceIdType.MESH,
+        )
+
+    tail_transfer = rim_transfer(0, tail_out, tail_got, partner)
+    own_transfer = rim_transfer(1, back_send, own_got, seq - 1)
+    other_transfer = rim_transfer(2, back_send, other_got, seq - 2)
+    even = seq % 2 == 0
+
     @pl.when(step == 0)
     def _():
         barrier = pltpu.get_barrier_semaphore()
-        pl.semaphore_signal(
-            barrier, inc=1, device_id=(partner, head), device_id_type=pl.DeviceIdType.MESH
-        )
-        pl.semaphore_wait(barrier, 1)
+        mesh = pl.DeviceIdType.MESH
+        pl.semaphore_signal(barrier, inc=1, device_id=(partner, head), device_id_type=mesh)
+
+        @pl.when(even & (seq + 2 < devices))
+        def _():
+            pl.semaphore_signal(barrier, inc=1, device_id=(seq + 2, head), device_id_type=mesh)
+
+        @pl.when((seq % 2 == 1) & (seq + 1 < devices))
+        def _():
+            pl.semaphore_signal(barrier, inc=1, device_id=(seq + 1, head), device_id_type=mesh)
+
+        @pl.when(even & (seq >= 2))
+        def _():
+            pl.semaphore_wait(barrier, 3)
+
+        @pl.when((seq % 2 == 1) | (seq < 2))
+        def _():
+            pl.semaphore_wait(barrier, 1)
 
     @pl.when(step >= 2)
     def _():
@@ -533,13 +567,13 @@
         (value_pre, value_before, value_rim, conv_value, ext_value, dy_value, DV, d_value),
     )
     outs = (
-        (query_out, query_conv_out, query_back_out, query_tail_out),
-        (key_out, key_conv_out, key_back_out, key_tail_out),
-        (value_out, value_conv_out, value_back_out, value_tail_out),
+        (query_out, query_conv_out),
+        (key_out, key_conv_out),
+        (value_out, value_conv_out),
     )
     for kind, (section, out) in enumerate(zip(sections, outs)):
         now_ref, before_ref, rim_ref, conv_ref, ext_ref, dy_ref, width, cotangent = section
-        pre_out, conv_out, back_out, tail_out = out
+        pre_out, conv_out = out
         first_lane = kind * heads * DK
         fill(ext_ref, now_ref, before_ref, rim_ref, first, keep)
         dy_ref[8 + GROUP :, :] = dy_ref[8:16, :] * after_keep
@@ -573,19 +607,65 @@
 
             @pl.when(step == 0)
             def _():
-                tail_out[:, lanes] = d_pre[GROUP - 8 :]
+                tail_out[:, pl.ds(first_lane + h * width, width)] = d_pre[GROUP - 8 :]
 
             @pl.when(first)
             def _():
                 d_back = dy_ref[pl.ds(1, 8), lanes] * conv_ref[1:2, lanes]
                 for tap in range(2, CONV):
                     d_back = d_back + dy_ref[pl.ds(tap, 8), lanes] * conv_ref[tap : tap + 1, lanes]
-                back_out[:, lanes] = d_back * keep
+                back_send[:, pl.ds(first_lane + h * width, width)] = d_back * keep
 
     transfer(step, group).start()
+
+    @pl.when(step == 0)
+    def _():
+        tail_transfer.start()
 
     @pl.when(step == groups - 1)
     def _():
+        @pl.when(seq >= 1)
+        def _():
+            own_transfer.start()
+
+        @pl.when(even & (seq >= 2))
+        def _():
+            other_transfer.start()
+
+        tail_transfer.wait_send()
+        tail_transfer.wait_recv()
+        got_tail_out[...] = tail_got[...]
+
+        @pl.when(seq >= 1)
+        def _():
+            own_transfer.wait_send()
+
+        @pl.when(even & (seq >= 2))
+        def _():
+            other_transfer.wait_send()
+
+        @pl.when(seq + 1 < devices)
+        def _():
+            own_transfer.wait_recv()
+            own_back_out[...] = own_got[...]
+
+        @pl.when(seq + 1 >= devices)
+        def _():
+            own_back_out[...] = jnp.zeros_like(own_back_out)
+
+        @pl.when(even & (seq + 2 < devices))
+        def _():
+            other_transfer.wait_recv()
+            other_back_out[...] = other_got[...]
+
+        @pl.when(even & (seq + 2 >= devices))
+        def _():
+            other_back_out[...] = jnp.zeros_like(other_back_out)
+
+        @pl.when(seq % 2 == 1)
+        def _():
+            other_back_out[...] = back_send[...]
+
         transfer(step - 1, group + 1).wait_send()
         transfer(step, group).wait_send()
         for block in range(groups):
@@ -600,7 +680,7 @@
     turn = lambda *shape: pl.BlockSpec(shape, lambda g: (groups - 1 - g, 0, 0))
     columns = 2 * heads
     return pl.pallas_call(
-        functools.partial(backward_kernel, heads, groups),
+        functools.partial(backward_kernel, heads, groups, lax.axis_size("seq")),
         grid=(groups,),
         in_specs=[smem]
         + [token_block(w, groups) for w in widths]
@@ -619,17 +699,16 @@
         ],
         out_specs=[token_block(w, groups) for w in widths]
         + [whole((CONV * 8, w)) for w in widths]
-        + [whole((8, w)) for w in widths]
-        + [whole((8, w)) for w in widths]
         + [token_block(columns, groups), whole((8, heads))]
+        + [pl.BlockSpec(memory_space=pltpu.VMEM)]
+        + [whole((8, sum(widths)))] * 3
         + [pl.BlockSpec(memory_space=pl.ANY)],
         out_shape=[jax.ShapeDtypeStruct((tokens, w), bf16) for w in widths]
         + [jax.ShapeDtypeStruct((CONV * 8, w), f32) for w in widths]
-        + [jax.ShapeDtypeStruct((8, w), f32) for w in widths]
-        + [jax.ShapeDtypeStruct((8, w), f32) for w in widths]
         + [
             jax.ShapeDtypeStruct((tokens, columns), bf16),
             jax.ShapeDtypeStruct((8, heads), f32),
+            *[jax.ShapeDtypeStruct((8, sum(widths)), f32)] * 4,
             jax.ShapeDtypeStruct((tokens, sum(widths)), bf16),
         ],
         scratch_shapes=[pltpu.VMEM((heads * DK, DV), f32)]
@@ -639,6 +718,9 @@
             pltpu.VMEM((2, GROUP, sum(widths)), bf16),
             pltpu.SemaphoreType.DMA((2,)),
             pltpu.SemaphoreType.DMA((groups,)),
+            *[pltpu.VMEM((8, sum(widths)), f32)] * 4,
+            pltpu.SemaphoreType.DMA((3,)),
+            pltpu.SemaphoreType.DMA((3,)),
         ],
         compiler_params=pltpu.CompilerParams(
             vmem_limit_bytes=VMEM, collective_id=1, has_side_effects=True
@@ -926,6 +1008,198 @@
     )(odd[None], rows, got_rows, cols, got_cols)
 
 
+def triple_grad_kernel(
+    place_ref, rows_ref, got_rows_ref, first_ref, second_ref, third_ref, got_ref, out_ref
+):
+    rows, got_rows = (rows_ref[...], got_rows_ref[...])
+    start = 0
+    for ref in (first_ref, second_ref, third_ref):
+        spot = pl.ds(start, ref.shape[1])
+        total = contract(rows, ref[...], 0, 0) + contract(got_rows, got_ref[:, spot], 0, 0)
+        out_ref[:, spot] = total.astype(bf16)
+        start += ref.shape[1]
+
+
+def triple_grad(rows, got_rows, parts, got_all):
+    odd = lax.axis_index("seq").astype(jnp.int32) % 2
+    devices = lax.axis_size("seq")
+    tokens, total = got_all.shape
+    width = rows.shape[1] // devices
+    if width % 128:
+        part = jnp.concatenate([own_half(rows, odd, width), got_rows], axis=0)
+        cols = jnp.concatenate([jnp.concatenate(parts, axis=1), got_all], axis=0)
+        return dense(part.T, cols).astype(bf16)
+    still = lambda cols: pl.BlockSpec((tokens, cols), lambda i, place: (0, 0))
+    return pl.pallas_call(
+        triple_grad_kernel,
+        grid_spec=pltpu.PrefetchScalarGridSpec(
+            num_scalar_prefetch=1,
+            grid=(devices // 2,),
+            in_specs=[
+                pl.BlockSpec((tokens, width), lambda i, place: (0, 2 * i + place[0])),
+                pl.BlockSpec((tokens, width), lambda i, place: (0, i)),
+                *[still(part.shape[1]) for part in parts],
+                still(total),
+            ],
+            out_specs=pl.BlockSpec((width, total), lambda i, place: (i, 0)),
+        ),
+        out_shape=jax.ShapeDtypeStruct((devices // 2 * width, total), bf16),
+        compiler_params=pltpu.CompilerParams(vmem_limit_bytes=SMALL),
+        cost_estimate=pl.CostEstimate(flops=10**6, bytes_accessed=10**4, transcendentals=0),
+        name="triple_grad",
+    )(odd[None], rows, got_rows, *parts, got_all)
+
+
+def line_kernel(
+    planes,
+    kept_ref,
+    across_ref,
+    out_ref,
+    across_out,
+    up_send,
+    up_got,
+    down_send,
+    down_got,
+    send_sem,
+    recv_sem,
+    across_sem,
+):
+    seq, head = (lax.axis_index("seq"), lax.axis_index("head"))
+    plane = seq // 2
+    mesh = pl.DeviceIdType.MESH
+    lower, upper = (plane > 0, plane < planes - 1)
+    beside = head + 2 - 4 * (head // 2)
+    barrier = pltpu.get_barrier_semaphore()
+    pl.semaphore_signal(barrier, inc=1, device_id=(seq, beside), device_id_type=mesh)
+
+    @pl.when(lower)
+    def _():
+        pl.semaphore_signal(barrier, inc=1, device_id=(seq - 2, head), device_id_type=mesh)
+
+    @pl.when(upper)
+    def _():
+        pl.semaphore_signal(barrier, inc=1, device_id=(seq + 2, head), device_id_type=mesh)
+
+    @pl.when(lower & upper)
+    def _():
+        pl.semaphore_wait(barrier, 3)
+
+    @pl.when((plane == 0) | (plane == planes - 1))
+    def _():
+        pl.semaphore_wait(barrier, 2)
+
+    crossing = pltpu.make_async_remote_copy(
+        src_ref=across_ref,
+        dst_ref=across_out,
+        send_sem=across_sem.at[0],
+        recv_sem=across_sem.at[1],
+        device_id=(seq, beside),
+        device_id_type=mesh,
+    )
+    crossing.start()
+    ways = ((up_send, up_got, 2, 0), (down_send, down_got, -2, 1))
+
+    def transfer(way, step):
+        send, got, hop, side = ways[way]
+        return pltpu.make_async_remote_copy(
+            src_ref=send.at[step - 1],
+            dst_ref=got.at[step - 1],
+            send_sem=send_sem.at[side, step - 1],
+            recv_sem=recv_sem.at[side, step - 1],
+            device_id=(seq + hop, head),
+            device_id_type=mesh,
+        )
+
+    rows = out_ref.shape[0]
+    slab = 2 * HALO
+
+    def each(body):
+        def run(i, carry):
+            body(pl.ds(pl.multiple_of(i * slab, slab), slab))
+            return carry
+
+        lax.fori_loop(0, rows // slab, run, 0)
+
+    for step in range(1, planes):
+        for way in range(2):
+            send, got, hop, side = ways[way]
+            rank = plane if way == 0 else planes - 1 - plane
+            at = plane + planes - step if way == 0 else plane - planes + step
+
+            @pl.when((rank < step) & (rank == 0))
+            def _(send=send, at=at, way=way, step=step):
+                def body(span):
+                    send[step - 1, span, :] = kept_ref[at, span, :]
+
+                each(body)
+                transfer(way, step).start()
+
+            if step > 1:
+
+                @pl.when((rank < step) & (rank > 0) & (rank < planes - 1))
+                def _(send=send, got=got, at=at, way=way, step=step):
+                    transfer(way, step - 1).wait_recv()
+
+                    def body(span):
+                        total = kept_ref[at, span, :].astype(f32)
+                        total = total + got[step - 2, span, :].astype(f32)
+                        send[step - 1, span, :] = total.astype(bf16)
+
+                    each(body)
+                    transfer(way, step).start()
+
+    def own(span):
+        out_ref[span, :] = kept_ref[plane, span, :].astype(f32)
+
+    each(own)
+    for way in range(2):
+        got = ways[way][1]
+
+        @pl.when(lower if way == 0 else upper)
+        def _(got=got, way=way):
+            transfer(way, planes - 1).wait_recv()
+
+            def body(span):
+                out_ref[span, :] += got[planes - 2, span, :].astype(f32)
+
+            each(body)
+
+    for step in range(1, planes):
+        for way in range(2):
+            rank = plane if way == 0 else planes - 1 - plane
+
+            @pl.when((rank < step) & (rank < planes - 1))
+            def _(way=way, step=step):
+                transfer(way, step).wait_send()
+
+    crossing.wait()
+
+
+def line_summed(kept, across):
+    planes = lax.axis_size("seq") // 2
+    rows, cols = (kept.shape[0] // planes, kept.shape[1])
+    if planes > 4 or rows % (2 * HALO):
+        return seq_scattered(kept), exchanged(across, "head", 2)
+    slots = pltpu.VMEM((planes - 1, rows, cols), bf16)
+    return pl.pallas_call(
+        functools.partial(line_kernel, planes),
+        in_specs=[pl.BlockSpec(memory_space=pltpu.VMEM)] * 2,
+        out_specs=[pl.BlockSpec(memory_space=pltpu.VMEM)] * 2,
+        out_shape=[
+            jax.ShapeDtypeStruct((rows, cols), f32),
+            jax.ShapeDtypeStruct(across.shape, bf16),
+        ],
+        scratch_shapes=[slots] * 4
+        + [pltpu.SemaphoreType.DMA((2, planes - 1))] * 2
+        + [pltpu.SemaphoreType.DMA((2,))],
+        compiler_params=pltpu.CompilerParams(
+            vmem_limit_bytes=VMEM, collective_id=2, has_side_effects=True
+        ),
+        cost_estimate=pl.CostEstimate(flops=9 * 10**10, bytes_accessed=10**7, transcendentals=0),
+        name="line_sum",
+    )(kept.reshape(planes, rows, cols), across)
+
+
 def partner_rows(block):
     width = block.shape[1] * 4 // lax.axis_size("seq")
     odd = lax.axis_index("seq") % 2
@@ -1061,15 +1335,6 @@
     return values
 
 
-def all_summed(values):
-    values = head_summed(values)
-    bit = 1
-    while bit < lax.axis_size("seq"):
-        values = values + exchanged(values, "seq", bit)
-        bit = bit * 2
-    return values
-
-
 def own_half(rows, odd, width):
     tokens, total = rows.shape
     parts = rows.reshape(tokens, total // (2 * width), 2, width)
@@ -1082,39 +1347,6 @@
     return lax.psum_scatter(
         mine.astype(bf16), "seq", scatter_dimension=0, axis_index_groups=groups, tiled=True
     ).astype(f32)
-
-
-def line_step(send, step, planes, upward):
-    devices = 2 * planes
-    route = []
-    for i in range(devices):
-        plane = i // 2
-        if upward and plane < step and plane + 1 < planes:
-            route.append((i, i + 2))
-        if not upward and planes - 1 - plane < step and plane > 0:
-            route.append((i, i - 2))
-    return lax.ppermute(send, "seq", route)
-
-
-def line_scattered(kept):
-    planes = lax.axis_size("seq") // 2
-    if planes > 4:
-        return seq_scattered(kept)
-    plane = lax.axis_index("seq") // 2
-    rows = kept.shape[0] // planes
-
-    def chunk(at):
-        return lax.dynamic_slice_in_dim(kept, at * rows, rows, 0).astype(f32)
-
-    up, down = (None, None)
-    for step in range(1, planes):
-        to_up = chunk(jnp.minimum(plane + planes - step, planes - 1))
-        to_down = chunk(jnp.maximum(plane - planes + step, 0))
-        if up is not None:
-            to_up, to_down = (to_up + up.astype(f32), to_down + down.astype(f32))
-        up = line_step(to_up.astype(bf16), step, planes, True)
-        down = line_step(to_down.astype(bf16), step, planes, False)
-    return chunk(plane) + up.astype(f32) + down.astype(f32)
 
 
 def composed(later, before):
@@ -1292,54 +1524,34 @@
     results = delta_backward(
         pres, rims, convs, scal, rate, keep_flags, made, entry, exit_grad, d_delta
     )
-    d_pres, conv_parts, backs, tails = (results[i : i + 3] for i in range(0, 12, 3))
-    d_scal, d_rate, got_all = results[12:]
-    backs = jnp.concatenate(backs, 1)[8 - (CONV - 1) :]
-    tails = jnp.concatenate(tails, 1)
-    backs, tails, gate_sent, d_up_late = tied(backs, tails, d_gate_pre, d_ffn_up)
-    got_d_gate_pre = exchanged(gate_sent, "seq", 1)
+    d_pres, conv_parts = (results[:3], results[3:6])
+    d_scal, d_rate, tails, own_back, other_back, got_tails, got_all = results[6:]
+    d_scal, gate_sent, d_up_late = tied(d_scal, d_gate_pre, d_ffn_up)
+    gate_middle = gate_sent.shape[1] // 2
+    got_gate_low = exchanged(gate_sent[:, :gate_middle], "seq", 1)
+    got_gate_high = exchanged(gate_sent[:, gate_middle:], "seq", 1)
     kept_up = pair_grad(normed_ffn, got_normed_ffn, d_up_late, got_d_up, True, units)
     grad_w_ffn_up = seq_scattered(kept_up)
-    crossing = [(i, (i - 1) ^ 1) for i in range(1, devices)]
-    got_tails = exchanged(tails, "seq", 1)
-    more = jnp.pad(lax.ppermute(backs, "seq", crossing), ((8 - (CONV - 1), 0), (0, 0)))
-    backs = jnp.pad(shifted(backs, "seq", -1), ((8 - (CONV - 1), 0), (0, 0)))
-    got_tails, more, backs, kept_up = tied(got_tails, more, backs, kept_up)
     got_all = lax.dynamic_update_slice(
-        got_all, (got_tails + more).astype(bf16), (token_rows - 8, 0)
+        got_all, (got_tails + other_back).astype(bf16), (token_rows - 8, 0)
     )
     d_query_pre, d_key_pre, d_value_pre = [
         lax.dynamic_update_slice(d_pre, tail.astype(bf16), (token_rows - 8, 0))
-        for d_pre, tail in zip(d_pres, split(tails + backs))
+        for d_pre, tail in zip(d_pres, split(tails + own_back))
     ]
-    kept_value = pair_grad(normed, got_normed, d_value_pre, got_all, False, None, 1)
-    kept_query = pair_grad(normed, got_normed, d_query_pre, got_all, False, None, 0)
-    kept_key = pair_grad(normed, got_normed, d_key_pre, got_all, False, None, 1)
-    query_key = jnp.concatenate([kept_query, kept_key], axis=1)
-    d_scal, kept_value, query_key, got_d_gate_pre, grad_w_ffn_gate = tied(
-        d_scal, kept_value, query_key, got_d_gate_pre, grad_w_ffn_gate
-    )
-    kept_w_gate = pair_grad(normed, got_normed, d_gate_pre, got_d_gate_pre, False)
-    grad_w_gate = seq_scattered(kept_w_gate)
-    d_scal, kept_w_gate = tied(d_scal, kept_w_gate)
-    small = dense(normed.T, d_scal)
-    small = [part.reshape(devices, -1) for part in (small[:, :head_count], small[:, head_count:])]
-    for part in conv_parts:
-        part = jnp.sum(part.reshape(CONV, 8, -1), axis=1).reshape(CONV, devices, -1)
-        small.append(jnp.swapaxes(part, 0, 1).reshape(devices, -1))
-    small = jnp.concatenate(small, axis=1)
-    small_width = small.shape[1]
-    odd = lax.axis_index("seq") % 2
-    small = small.astype(bf16).reshape(devices // 2, 2, small_width // 128, 128)
-    got = exchanged(lax.dynamic_index_in_dim(small, 1 - odd, 1, False), "seq", 1)
-    small = lax.dynamic_index_in_dim(small, odd, 1, False).astype(f32) + got.astype(f32)
-    small = seq_scattered(small.reshape(devices * small_width // 256, 128)).reshape(small_width)
-    small_pieces = []
-    for rows, width in [(normed.shape[1] // devices, head_count)] * 2 + [
-        (CONV, width // devices) for width in widths
-    ]:
-        small_pieces.append(small[: rows * width].reshape(rows, width))
-        small = small[rows * width :]
+    kept_last = triple_grad(
+        normed, got_normed, [d_query_pre, d_key_pre, d_value_pre], got_all
+    )
+    d_scal, kept_last, grad_w_ffn_gate, kept_up, got_gate_low = tied(
+        d_scal, kept_last, grad_w_ffn_gate, kept_up, got_gate_low
+    )
+    gain_count = out_gain.shape[0]
+    full_log, full_bias = [
+        lax.dynamic_update_slice_in_dim(
+            jnp.zeros(decay_log.shape, f32), d_rate[i], head_first, 0
+        )
+        for i in range(2)
+    ]
     d_normed, grad_attn_gain, attn_dots = norm_dense(
         [
             (d_query_pre, w_query),
@@ -1353,45 +1565,91 @@
         attn_gain,
         place,
     )
-    query_key = line_scattered(query_key)
-    grad_w_query, grad_w_key = (query_key[:, : widths[0]], query_key[:, widths[0] :])
-    grad_w_value = line_scattered(kept_value)
-    d_normed = head_scattered(d_normed)
-    attn_dots = head_summed(attn_dots[:, 0])[:, None] / hidden_in.shape[1]
+    d_normed, got_gate_high = tied(d_normed, got_gate_high)
+    got_d_gate_pre = jnp.concatenate([got_gate_low, got_gate_high], axis=1)
+    kept_w_gate = pair_grad(normed, got_normed, d_gate_pre, got_d_gate_pre, False)
+    grad_w_gate = seq_scattered(kept_w_gate)
+    attn_dots, kept_w_gate = tied(attn_dots, kept_w_gate)
+    wide = d_normed.shape[1] // 2
+    mine = d_normed[:, wide:].astype(f32) + exchanged(d_normed[:, :wide], "head", 1).astype(f32)
+    across = mine[:, : wide // 2].astype(bf16)
+    model = attn_gain.shape[0]
+    packed_sums = head_summed(
+        jnp.concatenate(
+            [
+                attn_dots[:, 0],
+                grad_attn_gain[0],
+                grad_ffn_gain[0],
+                jnp.sum(gain_part, 0),
+                full_log,
+                full_bias,
+            ]
+        )
+    )
+    packed_sums, across = tied(packed_sums, across)
+    attn_dots = packed_sums[:token_rows, None] / hidden_in.shape[1]
+    small = dense(d_scal.T, normed)
+    small = [jnp.swapaxes(small.reshape(2 * head_count, devices, -1), 0, 1).reshape(devices, -1)]
+    for part in conv_parts:
+        part = jnp.sum(part.reshape(CONV, 8, -1), axis=1).reshape(CONV, devices, -1)
+        small.append(jnp.swapaxes(part, 0, 1).reshape(devices, -1))
+    sums = packed_sums[token_rows + 2 * model :]
+    for first in (token_rows, token_rows + model):
+        small.append(packed_sums[first : first + model].reshape(devices, -1))
+    small.append(jnp.broadcast_to(sums, (devices, sums.shape[0])))
+    small = jnp.concatenate(small, axis=1)
+    small = jnp.pad(small, ((0, 0), (0, -small.shape[1] % 2048)))
+    small_width = small.shape[1]
+    odd = lax.axis_index("seq") % 2
+    small = small.reshape(devices // 2, 2, small_width // 128, 128)
+    got = exchanged(lax.dynamic_index_in_dim(small, 1 - odd, 1, False), "seq", 1)
+    small = lax.dynamic_index_in_dim(small, odd, 1, False) + got
+    small = small.reshape(devices * small_width // 256, 128)
+    small_sum = lax.psum_scatter(
+        small,
+        "seq",
+        scatter_dimension=0,
+        axis_index_groups=[list(range(first, devices, 2)) for first in range(2)],
+        tiled=True,
+    )
+    kept_last, across, small, grad_w_out, kept_w_gate = tied(
+        kept_last, across, small, grad_w_out, kept_w_gate
+    )
+    last_grads, across = line_summed(kept_last, across)
+    grad_w_query, grad_w_key, grad_w_value = split(last_grads)
+    small = small_sum.reshape(small_width)
+    small_pieces = []
+    for rows, width in [(head_count, model // devices)] * 2 + [
+        (CONV, width // devices) for width in widths
+    ]:
+        piece = small[: rows * width].reshape(rows, width)
+        small_pieces.append(piece.T if len(small_pieces) < 2 else piece)
+        small = small[rows * width :]
+    grad_attn_rows, grad_ffn_rows = (
+        small[: model // devices],
+        small[model // devices : 2 * (model // devices)],
+    )
+    sums = small[2 * (model // devices) :]
     grad_in = d_middle + attn_scale * (
-        cols(attn_gain) * d_normed
+        cols(attn_gain) * (mine[:, wide // 2 :] + across.astype(f32))
         - cols(hidden_in).astype(f32) * attn_scale * attn_dots
     )
-    full_log = lax.dynamic_update_slice_in_dim(
-        jnp.zeros(decay_log.shape, f32), d_rate[0], head_first, 0
-    )
-    full_bias = lax.dynamic_update_slice_in_dim(
-        jnp.zeros(decay_bias.shape, f32), d_rate[1], head_first, 0
-    )
-    sums = all_summed(
-        jnp.concatenate(
-            [jnp.sum(gain_part, 0), grad_ffn_gain[0], grad_attn_gain[0], full_log, full_bias]
-        )
-    )
-    gain_first = out_gain.shape[0]
-    attn_first = gain_first + ffn_gain.shape[0]
-    log_first = attn_first + attn_gain.shape[0]
+    log_first = gain_count
     bias_first = log_first + decay_log.shape[0]
-    rows_of = lambda whole: half(whole, 0, lax.axis_index("seq"), devices)
     return (
         hidden_out,
         grad_in,
-        rows_of(sums[attn_first:log_first]),
+        grad_attn_rows,
         grad_w_query,
         grad_w_key,
         grad_w_value,
         grad_w_gate,
         *small_pieces,
         sums[log_first:bias_first],
-        sums[bias_first:],
-        sums[:gain_first],
+        sums[bias_first : bias_first + decay_bias.shape[0]],
+        sums[:gain_count],
         grad_w_out,
-        rows_of(sums[gain_first:attn_first]),
+        grad_ffn_rows,
         grad_w_ffn_gate.T,
         grad_w_ffn_up.T,
         grad_w_ffn_down,

time: 740 us -> 737 us (level)
  Pallas kernels: 268 us -> 374 us
  waiting for transfers between devices: 194 us -> 133 us
  starting transfers between devices: 91.5 us -> 46.5 us
  other arithmetic: 55.8 us -> 45.6 us
  local copies, waits for them, and re-layouts: 80.4 us -> 88.3 us
    pallas_call x1 -> x3, Pallas kernels: 76.5 us -> 195 us  [the longest x1 105 us: line_summed(): pl.pallas_call(functools.partial(line_kernel, planes), in_specs=[pl.Block...]
    ppermute x13 -> x0, waiting for transfers between devices: 49.8 us -> none  [the longest x12 49.8 us: line_step(): return lax.ppermute(send, 'seq', route)]
    ppermute x13 -> x0, starting transfers between devices: 34.6 us -> none  [the longest x12 33.3 us: line_step(): return lax.ppermute(send, 'seq', route)]
    pallas_call x8 -> x5, Pallas kernels: 47.7 us -> 35.6 us  [pair_grad(): pl.pallas_call(functools.partial(weight_grad_kernel, turned), grid_spec=p...]
    ppermute x51 -> x45, waiting for transfers between devices: 132 us -> 121 us  [exchanged(): return lax.ppermute(block, axis, route)]
    ppermute x51 -> x45, starting transfers between devices: 40.8 us -> 31.4 us  [exchanged(): return lax.ppermute(block, axis, route)]
    unnamed x205 -> x203, local copies, waits for them, and re-layouts: 39.6 us -> 43.3 us
    ppermute x6 -> x5, starting transfers between devices: 15.9 us -> 14.8 us  [shifted(): return lax.ppermute(block, axis, route)]
  transfers between devices with their start and end apart: 76 -> 56, of which waited for: 26 -> 18; matrix products, arithmetic and copies ran while one was open for 16% -> 15% of each run, Pallas kernels for 32% -> 47%
where the time goes in v5:
time: 737 us; the launch traced here: 727 us
  Pallas kernels  374 us (51%)
  waiting for transfers between devices  133 us (18%)
  local copies, waits for them, and re-layouts  88.3 us (12%)
  starting transfers between devices  46.5 us (6%)
  other arithmetic  45.6 us (6%)
  matrix products  23.1 us (3%)
  between operations  16.1 us (2%)
    ppermute x45, waiting for transfers between devices, exchanged(): return lax.ppermute(block, axis, route)  121 us
    pallas_call x1, Pallas kernels, line_summed(): pl.pallas_call(functools.partial(line_kernel, planes), in_specs=[pl.Block...  105 us
    pallas_call x1, Pallas kernels, delta_backward(): pl.pallas_call(functools.partial(backward_kernel, heads, groups, lax.axis...  81.4 us
    unnamed x203, local copies, waits for them, and re-layouts  43.3 us
    pallas_call x1, Pallas kernels, delta_forward(): pl.pallas_call(functools.partial(forward_kernel, heads, groups), grid=(gr...  41.1 us
    pallas_call x5, Pallas kernels, pair_grad(): pl.pallas_call(functools.partial(weight_grad_kernel, turned), grid_spec=p...  35.6 us
    pallas_call x2, Pallas kernels, norm_dense(): pl.pallas_call(functools.partial(norm_dense_kernel, sides), grid_spec=plt...  35.6 us
    ppermute x45, starting transfers between devices, exchanged(): return lax.ppermute(block, axis, route)  31.4 us
  transfers between devices with their start and end apart: 56, of which 18 were waited for; matrix products, arithmetic and copies ran while one was open for 15% of the time, Pallas kernels for 47%

profile of v5, /device:TPU:0, one launch (start us, length us, event | category | flops | bytes accessed | tf_op | source)
XLA Modules:
  0.0 726.8 jit_solution(12513530098707787446)
XLA Ops:
  38.4 41.1 %delta_forward.1 = (bf16[768,512]{1,0:T(8,128)(2,1)}, bf16[768,512]{1,0:T(8,128)(2,1)}, bf16[768,1024]{1,0:T(8,128)(2,1)}, bf16[12,256,384]{2,1,0:T(8,128)(2,1)}...) custom-call(f32[12]{0:T(128)} %convert_subtract_fusion.keep_ref, ...), custom_call_target="tpu_custom_call" | custom-call | flops 1000000 | bytes 10000 | tf_op jit(solution)/shard_map/delta_forward/pallas_call | solution.py:289
  91.9 7.1 collective-permute-done.13.refs_2_
  100.7 4.2 collective-permute-start.5
  115.7 4.6 collective-permute-start.6
  120.4 5.5 rows_dense.1.grad_ref
  133.6 7.2 plain_dense.2
  147.1 17.7 %collective-permute-done.16 = bf16[768,512]{1,0:T(8,128)(2,1)S(1)} collective-permute-done((bf16[768,512]{1,0:T(8,128)(2,1)S(1)}, bf16[768,512]{1,0:T(8,128)(2,1)S(1)}, u32[]{:S(2)}, u32[]{:S(2)}) %collective-permute-start.16) | collective-permute-done | bytes 786464 | tf_op jit(solution)/shard_map/ppermute | solution.py:955
  168.3 18.3 %collective-permute-done.18.refs_2_ = bf16[768,512]{1,0:T(8,128)(2,1)} collective-permute-done((bf16[768,512]{1,0:T(8,128)(2,1)}, bf16[768,512]{1,0:T(8,128)(2,1)}, u32[]{:S(2)}, u32[]{:S(2)}) %collective-permute-start.18) | collective-permute-done | bytes 786464 | tf_op jit(solution)/shard_map/ppermute | solution.py:955
  197.2 17.3 %ffn.1 = (bf16[768,1408]{1,0:T(8,128)(2,1)}, bf16[768,1408]{1,0:T(8,128)(2,1)}, bf16[768,1408]{1,0:T(8,128)(2,1)}) custom-call(bf16[768,2048]{1,0:T(8,128)(2,1)} %copy-done, bf16[1376,2048]{1,0:T(8,128)(2,1)} %bitcast.125, bf16[1376,2048]{1,0:T(8,128)(2,1)} %bitcast.127, f32[768,1376]{1,0:T(8,128)} %copy-done.49), custom_call_target="tpu_custom_call" | custom-call | flops 8657043456 | bytes 20000000 | tf_op jit(solution)/shard_map/ffn/pallas_call | solution.py:1303
  214.5 16.8 %norm_dense.2 = (bf16[768,2048]{1,0:T(8,128)(2,1)}, f32[1,2048]{1,0:T(1,128)}, f32[768,1]{1,0:T(8,128)}) custom-call(s32[1]{0:T(128)} %bitcast.place_ref, bf16[768,1408]{1,0:T(8,128)(2,1)} %get-tuple-element.137.refs_0_.cols_ref, bf16[768,1408]{1,0:T(8,128)(2,1)} %get-tuple-element.168.refs_1_.cols_ref, bf16[1376,2048]{1,0:T(8,128)(2,1)} %bitcast.126, ...), custom_call_target="tpu_custom_call" | custom-call | flops 8858370048 | bytes 20000000 | tf_op jit(solution)/shard_map/norm_dense/pallas_call | solution.py:909
  241.0 5.8 collective-permute-done.28.refs_2_
  252.1 10.8 %collective-permute-done.26 = f32[768]{0:T(1024)S(1)} collective-permute-done((f32[768]{0:T(1024)S(1)}, f32[768]{0:T(1024)S(1)}, u32[]{:S(2)}, u32[]{:S(2)}) %collective-permute-start.26) | collective-permute-done | bytes 3104 | tf_op jit(solution)/shard_map/ppermute | solution.py:955
  265.5 4.5 fusion.56
  272.9 10.4 %collective-permute-done.22.got_cols_ref = bf16[768,1408]{1,0:T(8,128)(2,1)} collective-permute-done((bf16[768,1408]{1,0:T(8,128)(2,1)}, bf16[768,1408]{1,0:T(8,128)(2,1)}, u32[]{:S(2)}, u32[]{:S(2)}) %collective-permute-start.22) | collective-permute-done | bytes 2162720 | tf_op jit(solution)/shard_map/ppermute | solution.py:955
  283.2 7.9 %collective-permute-done.30.refs_0_ = bf16[768,256]{1,0:T(8,128)(2,1)S(1)} collective-permute-done((bf16[768,256]{1,0:T(8,128)(2,1)S(1)}, bf16[768,256]{1,0:T(8,128)(2,1)S(1)}, u32[]{:S(2)}, u32[]{:S(2)}) %collective-permute-start.30) | collective-permute-done | bytes 393248 | tf_op jit(solution)/shard_map/ppermute | solution.py:955
  293.1 8.0 %weight_grad.5 = bf16[5504,256]{1,0:T(8,128)(2,1)S(1)} custom-call(s32[1]{0:T(128)} %bitcast.12.place_ref, bf16[768,2048]{1,0:T(8,128)(2,1)S(1)} %copy-done.15, bf16[768,1024]{1,0:T(8,128)(2,1)S(1)} %copy-done.25, bf16[768,1408]{1,0:T(8,128)(2,1)} %get-tuple-element.144.cols_ref.left_ref, bf16[768,1408]{1,0:T(8,128)(2,1)} %collective-permute-done.22.got_cols_ref), custom_call_target="tpu_custom_call" | custom-call | flops 1000000 | bytes 10000 | tf_op jit(solution)/shard_map/weight_grad/pallas_call | solution.py:991
  316.1 5.3 gated_backward.1
  322.7 17.3 %collective-permute-done.34.got_cols_ref = bf16[768,1408]{1,0:T(8,128)(2,1)} collective-permute-done((bf16[768,1408]{1,0:T(8,128)(2,1)}, bf16[768,1408]{1,0:T(8,128)(2,1)}, u32[]{:S(2)}, u32[]{:S(2)}) %collective-permute-start.34) | collective-permute-done | bytes 2162720 | tf_op jit(solution)/shard_map/ppermute | solution.py:955
  341.6 8.4 %collective-permute-done.35 = bf16[4,128,384]{2,1,0:T(8,128)(2,1)S(1)} collective-permute-done((bf16[4,128,384]{2,1,0:T(8,128)(2,1)S(1)}, bf16[4,128,384]{2,1,0:T(8,128)(2,1)S(1)}, u32[]{:S(2)}, u32[]{:S(2)}) %collective-permute-start.35) | collective-permute-done | bytes 393248 | tf_op jit(solution)/shard_map/ppermute | solution.py:955
  349.9 9.3 %plain_dense.3 = bf16[768,2048]{1,0:T(8,128)(2,1)S(1)} custom-call(s32[1]{0:T(128)} %bitcast.place_ref, bf16[768,1408]{1,0:T(8,128)(2,1)} %get-tuple-element.144.cols_ref.left_ref, bf16[1376,2048]{1,0:T(8,128)(2,1)S(1)} %bitcast.105), custom_call_target="tpu_custom_call" | custom-call | flops 4429185024 | bytes 10000000 | tf_op jit(solution)/shard_map/plain_dense/pallas_call | solution.py:859
  372.2 7.2 collective-permute-done.36
  381.6 8.3 %weight_grad.6 = bf16[5504,256]{1,0:T(8,128)(2,1)S(1)} custom-call(s32[1]{0:T(128)} %bitcast.12.place_ref, bf16[768,2048]{1,0:T(8,128)(2,1)S(1)} %copy-done.1, bf16[768,1024]{1,0:T(8,128)(2,1)S(1)} %copy-done.7, bf16[768,1408]{1,0:T(8,128)(2,1)} %get-tuple-element.137.refs_0_.cols_ref, bf16[768,1408]{1,0:T(8,128)(2,1)} %collective-permute-done.34.got_cols_ref), custom_call_target="tpu_custom_call" | custom-call | flops 1000000 | bytes 10000 | tf_op jit(solution)/shard_map/weight_grad/pallas_call | solution.py:991
  393.1 4.0 collective-permute-done.37
  402.4 6.6 weight_grad.7
  410.3 4.0 fusion.9
  420.0 81.4 %delta_backward.1 = (bf16[768,512]{1,0:T(8,128)(2,1)}, bf16[768,512]{1,0:T(8,128)(2,1)}, bf16[768,1024]{1,0:T(8,128)(2,1)}, f32[32,512]{1,0:T(8,128)}, f32[32,51...) custom-call(f32[12]{0:T(128)} %convert_subtract_fusion.keep_ref, ...), custom_call_target="tpu_custom_call" | custom-call | flops 1000000 | bytes 10000 | tf_op jit(solution)/shard_map/delta_backward/pallas_call | solution.py:682
  509.8 7.4 %weight_grad.8 = bf16[5504,256]{1,0:T(8,128)(2,1)S(1)} custom-call(s32[1]{0:T(128)} %bitcast.12.place_ref, bf16[768,2048]{1,0:T(8,128)(2,1)S(1)} %copy-done.2, bf16[768,1024]{1,0:T(8,128)(2,1)S(1)} %copy-done.8, bf16[768,1408]{1,0:T(8,128)(2,1)S(1)} %copy-done.35, bf16[768,1408]{1,0:T(8,128)(2,1)} %collective-permute-done.43.got_cols_ref), custom_call_target="tpu_custom_call" | custom-call | flops 1000000 | bytes 10000 | tf_op jit(solution)/shard_map/weight_grad/pallas_call | solution.py:991
  531.7 8.0 %triple_grad.1 = bf16[1024,2048]{1,0:T(8,128)(2,1)S(1)} custom-call(s32[1]{0:T(128)} %bitcast.12.place_ref, bf16[768,2048]{1,0:T(8,128)(2,1)S(1)} %fusion.2.rows_ref, bf16[768,1024]{1,0:T(8,128)(2,1)S(1)} %copy-done.4, bf16[768,512]{1,0:T(8,128)(2,1)S(1)} %copy-done.39, bf16[768,512]{1,0:T(8,128)(2,1)S(1)} %copy-done.40, bf16[768,1024]{1,0:T(8,128)(2,1)S(1)} %copy-done.38, ...), custom_call_target="tpu_custom_call" | custom-call | flops 1000000 | bytes 10000 | tf_op jit(solution)/shard_map/triple_grad/pallas_call | solution.py:1033
  544.2 18.8 %norm_dense.3 = (bf16[768,2048]{1,0:T(8,128)(2,1)}, f32[1,2048]{1,0:T(1,128)}, f32[768,1]{1,0:T(8,128)}) custom-call(s32[1]{0:T(128)} %bitcast.place_ref, bf16[768,512]{1,0:T(8,128)(2,1)} %get-tuple-element.205.first_ref.refs_0_, bf16[768,512]{1,0:T(8,128)(2,1)} %get-tuple-element.204.second_ref.refs_1_, ...), custom_call_target="tpu_custom_call" | custom-call | flops 9688842240 | bytes 20000000 | tf_op jit(solution)/shard_map/norm_dense/pallas_call | solution.py:909
  571.1 5.3 weight_grad.9
  587.8 4.2 collective-permute-done.49
  598.0 105.5 %line_sum.1 = (f32[256,2048]{1,0:T(8,128)}, bf16[768,512]{1,0:T(8,128)(2,1)}) custom-call(bf16[4,256,2048]{2,1,0:T(8,128)(2,1)} %bitcast.96, bf16[768,512]{1,0:T(8,128)(2,1)} %slice.500.across_ref), custom_call_target="tpu_custom_call" | custom-call | flops 89999998976 | bytes 10000000 | tf_op jit(solution)/shard_map/line_sum/pallas_call | solution.py:1184
  (445 shorter events, 222.7 us)
Async XLA Ops:
  7.2 407.1 %reduce-scatter.7.cloned.1.call-start = ((), (), s32[]{:S(2)}) async-start(), calls=%async_computation.6 | async-start | bytes 3522560 | tf_op jit(solution)/shard_map/reduce_scatter | solution.py:1347
  7.3 22.5 %collective-permute-start.2 = (bf16[768,512]{1,0:T(8,128)(2,1)}, bf16[768,512]{1,0:T(8,128)(2,1)}, u32[]{:S(2)}, u32[]{:S(2)}) collective-permute-start(bf16[768,512]{1,0:T(8,128)(2,1)} %refs_0_.1), channel_id=1, source_target_pairs={{0,2},{1,3},{2,0},{3,1},{4,6},{5,7},{6,4},{7,5},{8,10},{9,11},{10,... | collective-permute-start | bytes 2359304 | tf_op jit(solution)/shard_map/ppermute | solution.py:955
  10.3 71.3 %collective-permute-start.1 = (bf16[768,512]{1,0:T(8,128)(2,1)}, bf16[768,512]{1,0:T(8,128)(2,1)}, u32[]{:S(2)}, u32[]{:S(2)}) collective-permute-start(bf16[768,512]{1,0:T(8,128)(2,1)} %refs_0_.1), channel_id=1, source_target_pairs={{0,1},{1,0},{2,3},{3,2},{4,5},{5,4},{6,7},{7,6},{8,9},{9,8},{10,11... | collective-permute-start | bytes 2359304 | tf_op jit(solution)/shard_map/ppermute | solution.py:955
  29.7 51.8 %collective-permute-start.3 = (bf16[768,512]{1,0:T(8,128)(2,1)}, bf16[768,512]{1,0:T(8,128)(2,1)}, u32[]{:S(2)}, u32[]{:S(2)}) collective-permute-start(bf16[768,512]{1,0:T(8,128)(2,1)} %collective-permute-done.2.refs_2_), channel_id=1, source_target_pairs={{0,1},{1,0},{2,3},{3,2},{4,5},{5,4},{6,7},{7,6},{8,9},{9,8},{10,11... | collective-permute-start | bytes 2359304 | tf_op jit(solution)/shard_map/ppermute | solution.py:955
  31.8 47.7 %collective-permute-start.7 = (bf16[768,256]{1,0:T(8,128)(2,1)}, bf16[768,256]{1,0:T(8,128)(2,1)}, u32[]{:S(2)}, u32[]{:S(2)}) collective-permute-start(bf16[768,256]{1,0:T(8,128)(2,1)} %constant_dynamic-slice_fusion.3), channel_id=1, source_target_pairs={{0,4},{4,0},{8,12},{12,8},{16,20},{20,16},{24,28},{28,24},{1,5},{5... | collective-permute-start | bytes 1179656 | tf_op jit(solution)/shard_map/ppermute | solution.py:955
  35.1 45.1 %collective-permute-start.11 = (bf16[768,256]{1,0:T(8,128)(2,1)}, bf16[768,256]{1,0:T(8,128)(2,1)}, u32[]{:S(2)}, u32[]{:S(2)}) collective-permute-start(bf16[768,256]{1,0:T(8,128)(2,1)} %constant_dynamic-slice_fusion.2), channel_id=1, source_target_pairs={{0,4},{4,0},{8,12},{12,8},{16,20},{20,16},{24,28},{28,24},{1,5},{5... | collective-permute-start | bytes 1179656 | tf_op jit(solution)/shard_map/ppermute | solution.py:955
  80.2 18.8 %collective-permute-start.13 = (bf16[768,256]{1,0:T(8,128)(2,1)}, bf16[768,256]{1,0:T(8,128)(2,1)}, u32[]{:S(2)}, u32[]{:S(2)}) collective-permute-start(bf16[768,256]{1,0:T(8,128)(2,1)} %collective-permute-done.11.refs_0_), channel_id=1, source_target_pairs={{0,2},{1,3},{2,0},{3,1},{4,6},{5,7},{6,4},{7,5},{8,10},{9,11},{10,... | collective-permute-start | bytes 1179656 | tf_op jit(solution)/shard_map/ppermute | solution.py:955
  88.1 20.3 %collective-permute-start.8 = (bf16[768,256]{1,0:T(8,128)(2,1)}, bf16[768,256]{1,0:T(8,128)(2,1)S(1)}, u32[]{:S(2)}, u32[]{:S(2)}) collective-permute-start(bf16[768,256]{1,0:T(8,128)(2,1)} %collective-permute-done.7.refs_0_), channel_id=1, source_target_pairs={{0,1},{1,0},{2,3},{3,2},{4,5},{5,4},{6,7},{7,6},{8,9},{9,8},{10,11... | collective-permute-start | bytes 1179656 | tf_op jit(solution)/shard_map/ppermute | solution.py:955
  88.1 23.9 %collective-permute-start.12 = (bf16[768,256]{1,0:T(8,128)(2,1)}, bf16[768,256]{1,0:T(8,128)(2,1)S(1)}, u32[]{:S(2)}, u32[]{:S(2)}) collective-permute-start(bf16[768,256]{1,0:T(8,128)(2,1)} %collective-permute-done.11.refs_0_), channel_id=1, source_target_pairs={{0,1},{1,0},{2,3},{3,2},{4,5},{5,4},{6,7},{7,6},{8,9},{9,8},{10,11... | collective-permute-start | bytes 1179656 | tf_op jit(solution)/shard_map/ppermute | solution.py:955
  145.2 19.6 %collective-permute-start.16 = (bf16[768,512]{1,0:T(8,128)(2,1)S(1)}, bf16[768,512]{1,0:T(8,128)(2,1)S(1)}, u32[]{:S(2)}, u32[]{:S(2)}) collective-permute-start(bf16[768,512]{1,0:T(8,128)(2,1)S(1)} %slice.503), channel_id=1, source_target_pairs={{0,2},{1,3},{2,0},{3,1},{4,6},{5,7},{6,4},{7,5},{8,10},{9,11},{10,... | collective-permute-start | bytes 2359304 | tf_op jit(solution)/shard_map/ppermute | solution.py:955
  146.1 40.6 %collective-permute-start.20 = (bf16[768,1024]{1,0:T(8,128)(2,1)}, bf16[768,1024]{1,0:T(8,128)(2,1)}, u32[]{:S(2)}, u32[]{:S(2)}) collective-permute-start(bf16[768,1024]{1,0:T(8,128)(2,1)} %gated_forward.1.left_ref.cols_ref), channel_id=1, source_target_pairs={{0,4},{4,0},{8,12},{12,8},{16,20},{20,16},{24,28},{28,24},{1,5},{5... | collective-permute-start | bytes 4718600 | tf_op jit(solution)/shard_map/ppermute | solution.py:955
  167.5 19.2 %collective-permute-start.18 = (bf16[768,512]{1,0:T(8,128)(2,1)}, bf16[768,512]{1,0:T(8,128)(2,1)}, u32[]{:S(2)}, u32[]{:S(2)}) collective-permute-start(bf16[768,512]{1,0:T(8,128)(2,1)} %fusion.19.refs_0_), channel_id=1, source_target_pairs={{0,2},{1,3},{2,0},{3,1},{4,6},{5,7},{6,4},{7,5},{8,10},{9,11},{10,... | collective-permute-start | bytes 2359304 | tf_op jit(solution)/shard_map/ppermute | solution.py:955
  168.3 18.3 %collective-permute-start.17 = (bf16[768,512]{1,0:T(8,128)(2,1)}, bf16[768,512]{1,0:T(8,128)(2,1)}, u32[]{:S(2)}, u32[]{:S(2)}) collective-permute-start(bf16[768,512]{1,0:T(8,128)(2,1)} %fusion.19.refs_0_), channel_id=1, source_target_pairs={{0,1},{1,0},{2,3},{3,2},{4,5},{5,4},{6,7},{7,6},{8,9},{9,8},{10,11... | collective-permute-start | bytes 2359304 | tf_op jit(solution)/shard_map/ppermute | solution.py:955
  196.5 17.9 %collective-permute-start.21 = (bf16[768,256]{1,0:T(8,128)(2,1)S(1)}, bf16[768,256]{1,0:T(8,128)(2,1)}, u32[]{:S(2)}, u32[]{:S(2)}) collective-permute-start(bf16[768,256]{1,0:T(8,128)(2,1)S(1)} %constant_dynamic-slice_fusion.1), channel_id=1, source_target_pairs={{0,4},{4,0},{8,12},{12,8},{16,20},{20,16},{24,28},{28,24},{1,5},{5... | collective-permute-start | bytes 1179656 | tf_op jit(solution)/shard_map/ppermute | solution.py:955
  233.0 50.2 %collective-permute-start.22 = (bf16[768,1408]{1,0:T(8,128)(2,1)}, bf16[768,1408]{1,0:T(8,128)(2,1)}, u32[]{:S(2)}, u32[]{:S(2)}) collective-permute-start(bf16[768,1408]{1,0:T(8,128)(2,1)} %get-tuple-element.144.cols_ref.left_ref), channel_id=1, source_target_pairs={{0,4},{4,0},{8,12},{12,8},{16,20},{20,16},{24,28},{28,24},{1,5},{5... | collective-permute-start | bytes 6488072 | tf_op jit(solution)/shard_map/ppermute | solution.py:955
  239.7 25.7 %collective-permute-start.24 = (bf16[768,512]{1,0:T(8,128)(2,1)}, bf16[768,512]{1,0:T(8,128)(2,1)}, u32[]{:S(2)}, u32[]{:S(2)}) collective-permute-start(bf16[768,512]{1,0:T(8,128)(2,1)} %slice.502), channel_id=1, source_target_pairs={{0,2},{1,3},{2,0},{3,1},{4,6},{5,7},{6,4},{7,5},{8,10},{9,11},{10,... | collective-permute-start | bytes 2359304 | tf_op jit(solution)/shard_map/ppermute | solution.py:955
  241.0 21.9 %collective-permute-start.27 = (bf16[768,256]{1,0:T(8,128)(2,1)}, bf16[768,256]{1,0:T(8,128)(2,1)}, u32[]{:S(2)}, u32[]{:S(2)}) collective-permute-start(bf16[768,256]{1,0:T(8,128)(2,1)} %collective-permute-done.21.refs_0_), channel_id=1, source_target_pairs={{0,1},{1,0},{2,3},{3,2},{4,5},{5,4},{6,7},{7,6},{8,9},{9,8},{10,11... | collective-permute-start | bytes 1179656 | tf_op jit(solution)/shard_map/ppermute | solution.py:955
  269.9 22.6 %collective-permute-start.32 = (bf16[768,512]{1,0:T(8,128)(2,1)}, bf16[768,512]{1,0:T(8,128)(2,1)}, u32[]{:S(2)}, u32[]{:S(2)}) collective-permute-start(bf16[768,512]{1,0:T(8,128)(2,1)} %get-tuple-element.131.refs_0_), channel_id=1, source_target_pairs={{0,2},{1,3},{2,0},{3,1},{4,6},{5,7},{6,4},{7,5},{8,10},{9,11},{10,... | collective-permute-start | bytes 2359304 | tf_op jit(solution)/shard_map/ppermute | solution.py:955
  271.8 19.3 %collective-permute-start.30 = (bf16[768,256]{1,0:T(8,128)(2,1)S(1)}, bf16[768,256]{1,0:T(8,128)(2,1)S(1)}, u32[]{:S(2)}, u32[]{:S(2)}) collective-permute-start(bf16[768,256]{1,0:T(8,128)(2,1)S(1)} %constant_dynamic-slice_fusion), channel_id=1, source_target_pairs={{0,4},{4,0},{8,12},{12,8},{16,20},{20,16},{24,28},{28,24},{1,5},{5... | collective-permute-start | bytes 1179656 | tf_op jit(solution)/shard_map/ppermute | solution.py:955
  291.1 48.9 %collective-permute-start.34 = (bf16[768,1408]{1,0:T(8,128)(2,1)}, bf16[768,1408]{1,0:T(8,128)(2,1)}, u32[]{:S(2)}, u32[]{:S(2)}) collective-permute-start(bf16[768,1408]{1,0:T(8,128)(2,1)} %get-tuple-element.137.refs_0_.cols_ref), channel_id=1, source_target_pairs={{0,4},{4,0},{8,12},{12,8},{16,20},{20,16},{24,28},{28,24},{1,5},{5... | collective-permute-start | bytes 6488072 | tf_op jit(solution)/shard_map/ppermute | solution.py:955
  302.7 239.1 %reduce-scatter.9.cloned.1.call-start = ((), (), s32[]{:S(2)}) async-start(), calls=%async_computation.7 | async-start | bytes 3522560 | tf_op jit(solution)/shard_map/reduce_scatter | solution.py:1347
  364.2 52.5 %collective-permute-start.43 = (bf16[768,1408]{1,0:T(8,128)(2,1)}, bf16[768,1408]{1,0:T(8,128)(2,1)}, u32[]{:S(2)}, u32[]{:S(2)}) collective-permute-start(bf16[768,1408]{1,0:T(8,128)(2,1)} %get-tuple-element.168.refs_1_.cols_ref), channel_id=1, source_target_pairs={{0,4},{4,0},{8,12},{12,8},{16,20},{20,16},{24,28},{28,24},{1,5},{5... | collective-permute-start | bytes 6488072 | tf_op jit(solution)/shard_map/ppermute | solution.py:955
  366.9 25.7 %collective-permute-start.39 = (bf16[768,256]{1,0:T(8,128)(2,1)S(1)}, bf16[768,256]{1,0:T(8,128)(2,1)}, u32[]{:S(2)}, u32[]{:S(2)}) collective-permute-start(bf16[768,256]{1,0:T(8,128)(2,1)S(1)} %copy-done.43), channel_id=1, source_target_pairs={{0,2},{1,3},{2,0},{3,1},{4,6},{5,7},{6,4},{7,5},{8,10},{9,11},{10,... | collective-permute-start | bytes 1179656 | tf_op jit(solution)/shard_map/ppermute | solution.py:955
  371.0 39.3 %collective-permute-start.42 = (bf16[768,512]{1,0:T(8,128)(2,1)}, bf16[768,512]{1,0:T(8,128)(2,1)}, u32[]{:S(2)}, u32[]{:S(2)}) collective-permute-start(bf16[768,512]{1,0:T(8,128)(2,1)} %slice.501), channel_id=1, source_target_pairs={{0,2},{1,3},{2,0},{3,1},{4,6},{5,7},{6,4},{7,5},{8,10},{9,11},{10,... | collective-permute-start | bytes 2359304 | tf_op jit(solution)/shard_map/ppermute | solution.py:955
  380.3 16.8 %collective-permute-start.37 = (bf16[4,128,256]{2,1,0:T(8,128)(2,1)}, bf16[4,128,256]{2,1,0:T(8,128)(2,1)}, u32[]{:S(2)}, u32[]{:S(2)}) collective-permute-start(bf16[4,128,256]{2,1,0:T(8,128)(2,1)} %fusion.15), channel_id=1, source_target_pairs={{16,0},{20,4},{24,8},{28,12},{17,1},{21,5},{25,9},{29,13},{18,2},{... | collective-permute-start | bytes 786440 | tf_op jit(solution)/shard_map/ppermute | solution.py:950
  416.7 176.9 %reduce-scatter.11.cloned.1.call-start = ((), (), s32[]{:S(2)}) async-start(), calls=%async_computation.8 | async-start | bytes 2621440 | tf_op jit(solution)/shard_map/reduce_scatter | solution.py:1347
  417.4 178.3 %reduce-scatter.17.cloned.1.call-start = ((), (), s32[]{:S(2)}) async-start(), calls=%async_computation.11 | async-start | bytes 3522560 | tf_op jit(solution)/shard_map/reduce_scatter | solution.py:1347
  504.0 40.1 %collective-permute-start.44 = (bf16[768,512]{1,0:T(8,128)(2,1)}, bf16[768,512]{1,0:T(8,128)(2,1)}, u32[]{:S(2)}, u32[]{:S(2)}) collective-permute-start(bf16[768,512]{1,0:T(8,128)(2,1)} %get-tuple-element.203), channel_id=1, source_target_pairs={{0,4},{4,0},{8,12},{12,8},{16,20},{20,16},{24,28},{28,24},{1,5},{5... | collective-permute-start | bytes 2359304 | tf_op jit(solution)/shard_map/ppermute | solution.py:955
  518.8 192.2 %reduce-scatter.13.cloned.1.call-start = ((), (), s32[]{:S(2)}) async-start(), calls=%async_computation.9 | async-start | bytes 81920 | tf_op jit(solution)/shard_map/reduce_scatter | solution.py:1608
  520.4 42.6 %collective-permute-start.45 = (bf16[768,512]{1,0:T(8,128)(2,1)}, bf16[768,512]{1,0:T(8,128)(2,1)}, u32[]{:S(2)}, u32[]{:S(2)}) collective-permute-start(bf16[768,512]{1,0:T(8,128)(2,1)} %get-tuple-element.202), channel_id=1, source_target_pairs={{0,4},{4,0},{8,12},{12,8},{16,20},{20,16},{24,28},{28,24},{1,5},{5... | collective-permute-start | bytes 2359304 | tf_op jit(solution)/shard_map/ppermute | solution.py:955
  565.7 18.4 %collective-permute-start.46 = (bf16[768,1024]{1,0:T(8,128)(2,1)}, bf16[768,1024]{1,0:T(8,128)(2,1)}, u32[]{:S(2)}, u32[]{:S(2)}) collective-permute-start(bf16[768,1024]{1,0:T(8,128)(2,1)} %slice.309), channel_id=1, source_target_pairs={{0,1},{1,0},{2,3},{3,2},{4,5},{5,4},{6,7},{7,6},{8,9},{9,8},{10,11... | collective-permute-start | bytes 4718600 | tf_op jit(solution)/shard_map/ppermute | solution.py:955
  592.7 124.7 %reduce-scatter.15.cloned.1.call-start = ((), (), s32[]{:S(2)}) async-start(), calls=%async_computation.10 | async-start | bytes 2621440 | tf_op jit(solution)/shard_map/reduce_scatter | solution.py:1347
  (121 other events, 1564.6 us)
Sparse Core Ops, SparseCore 0:
  302.9 56.8 reduce-scatter.6
  416.8 54.4 reduce-scatter.8
  473.6 46.3 reduce-scatter.10
  522.3 53.5 reduce-scatter.16
  592.9 16.6 reduce-scatter.12
  611.8 74.0 reduce-scatter.14

commit v6 on v5

--- a/solution.py
+++ b/solution.py
@@ -1099,10 +1099,10 @@
     crossing.start()
     ways = ((up_send, up_got, 2, 0), (down_send, down_got, -2, 1))
 
-    def transfer(way, step):
+    def transfer(way, step, source=None):
         send, got, hop, side = ways[way]
         return pltpu.make_async_remote_copy(
-            src_ref=send.at[step - 1],
+            src_ref=send.at[step - 1] if source is None else source,
             dst_ref=got.at[step - 1],
             send_sem=send_sem.at[side, step - 1],
             recv_sem=recv_sem.at[side, step - 1],
@@ -1127,12 +1127,8 @@
             at = plane + planes - step if way == 0 else plane - planes + step
 
             @pl.when((rank < step) & (rank == 0))
-            def _(send=send, at=at, way=way, step=step):
-                def body(span):
-                    send[step - 1, span, :] = kept_ref[at, span, :]
-
-                each(body)
-                transfer(way, step).start()
+            def _(at=at, way=way, step=step):
+                transfer(way, step, kept_ref.at[at]).start()
 
             if step > 1:
 

time: 737 us -> 737 us (level)
  no operation moved by 1% of the time
where the time goes in v6:
time: 737 us; the launch traced here: 727 us
  Pallas kernels  374 us (51%)
  waiting for transfers between devices  133 us (18%)
  local copies, waits for them, and re-layouts  88.3 us (12%)
  starting transfers between devices  46.5 us (6%)
  other arithmetic  45.6 us (6%)
  matrix products  23.1 us (3%)
  between operations  16.1 us (2%)
    ppermute x45, waiting for transfers between devices, exchanged(): return lax.ppermute(block, axis, route)  121 us
    pallas_call x1, Pallas kernels, line_summed(): pl.pallas_call(functools.partial(line_kernel, planes), in_specs=[pl.Block...  105 us
    pallas_call x1, Pallas kernels, delta_backward(): pl.pallas_call(functools.partial(backward_kernel, heads, groups, lax.axis...  81.4 us
    unnamed x203, local copies, waits for them, and re-layouts  43.3 us
    pallas_call x1, Pallas kernels, delta_forward(): pl.pallas_call(functools.partial(forward_kernel, heads, groups), grid=(gr...  41.1 us
    pallas_call x5, Pallas kernels, pair_grad(): pl.pallas_call(functools.partial(weight_grad_kernel, turned), grid_spec=p...  35.6 us
    pallas_call x2, Pallas kernels, norm_dense(): pl.pallas_call(functools.partial(norm_dense_kernel, sides), grid_spec=plt...  35.6 us
    ppermute x45, starting transfers between devices, exchanged(): return lax.ppermute(block, axis, route)  31.4 us
  transfers between devices with their start and end apart: 56, of which 18 were waited for; matrix products, arithmetic and copies ran while one was open for 15% of the time, Pallas kernels for 47%

profile of v6, /device:TPU:0, one launch (start us, length us, event | category | flops | bytes accessed | tf_op | source)
XLA Modules:
  0.0 726.8 jit_solution(13399409718846988554)
XLA Ops:
  38.4 41.1 %delta_forward.1 = (bf16[768,512]{1,0:T(8,128)(2,1)}, bf16[768,512]{1,0:T(8,128)(2,1)}, bf16[768,1024]{1,0:T(8,128)(2,1)}, bf16[12,256,384]{2,1,0:T(8,128)(2,1)}...) custom-call(f32[12]{0:T(128)} %convert_subtract_fusion.keep_ref, ...), custom_call_target="tpu_custom_call" | custom-call | flops 1000000 | bytes 10000 | tf_op jit(solution)/shard_map/delta_forward/pallas_call | solution.py:289
  91.9 7.1 collective-permute-done.13.refs_2_
  100.7 4.2 collective-permute-start.5
  115.7 4.6 collective-permute-start.6
  120.4 5.5 rows_dense.1.grad_ref
  133.6 7.2 plain_dense.2
  147.1 17.7 %collective-permute-done.16 = bf16[768,512]{1,0:T(8,128)(2,1)S(1)} collective-permute-done((bf16[768,512]{1,0:T(8,128)(2,1)S(1)}, bf16[768,512]{1,0:T(8,128)(2,1)S(1)}, u32[]{:S(2)}, u32[]{:S(2)}) %collective-permute-start.16) | collective-permute-done | bytes 786464 | tf_op jit(solution)/shard_map/ppermute | solution.py:955
  168.3 18.3 %collective-permute-done.18.refs_2_ = bf16[768,512]{1,0:T(8,128)(2,1)} collective-permute-done((bf16[768,512]{1,0:T(8,128)(2,1)}, bf16[768,512]{1,0:T(8,128)(2,1)}, u32[]{:S(2)}, u32[]{:S(2)}) %collective-permute-start.18) | collective-permute-done | bytes 786464 | tf_op jit(solution)/shard_map/ppermute | solution.py:955
  197.2 17.3 %ffn.1 = (bf16[768,1408]{1,0:T(8,128)(2,1)}, bf16[768,1408]{1,0:T(8,128)(2,1)}, bf16[768,1408]{1,0:T(8,128)(2,1)}) custom-call(bf16[768,2048]{1,0:T(8,128)(2,1)} %copy-done, bf16[1376,2048]{1,0:T(8,128)(2,1)} %bitcast.125, bf16[1376,2048]{1,0:T(8,128)(2,1)} %bitcast.127, f32[768,1376]{1,0:T(8,128)} %copy-done.49), custom_call_target="tpu_custom_call" | custom-call | flops 8657043456 | bytes 20000000 | tf_op jit(solution)/shard_map/ffn/pallas_call | solution.py:1299
  214.5 16.8 %norm_dense.2 = (bf16[768,2048]{1,0:T(8,128)(2,1)}, f32[1,2048]{1,0:T(1,128)}, f32[768,1]{1,0:T(8,128)}) custom-call(s32[1]{0:T(128)} %bitcast.place_ref, bf16[768,1408]{1,0:T(8,128)(2,1)} %get-tuple-element.137.refs_0_.cols_ref, bf16[768,1408]{1,0:T(8,128)(2,1)} %get-tuple-element.168.refs_1_.cols_ref, bf16[1376,2048]{1,0:T(8,128)(2,1)} %bitcast.126, ...), custom_call_target="tpu_custom_call" | custom-call | flops 8858370048 | bytes 20000000 | tf_op jit(solution)/shard_map/norm_dense/pallas_call | solution.py:909
  241.0 5.8 collective-permute-done.28.refs_2_
  252.1 10.8 %collective-permute-done.26 = f32[768]{0:T(1024)S(1)} collective-permute-done((f32[768]{0:T(1024)S(1)}, f32[768]{0:T(1024)S(1)}, u32[]{:S(2)}, u32[]{:S(2)}) %collective-permute-start.26) | collective-permute-done | bytes 3104 | tf_op jit(solution)/shard_map/ppermute | solution.py:955
  265.5 4.5 fusion.56
  272.9 10.4 %collective-permute-done.22.got_cols_ref = bf16[768,1408]{1,0:T(8,128)(2,1)} collective-permute-done((bf16[768,1408]{1,0:T(8,128)(2,1)}, bf16[768,1408]{1,0:T(8,128)(2,1)}, u32[]{:S(2)}, u32[]{:S(2)}) %collective-permute-start.22) | collective-permute-done | bytes 2162720 | tf_op jit(solution)/shard_map/ppermute | solution.py:955
  283.2 7.9 %collective-permute-done.30.refs_0_ = bf16[768,256]{1,0:T(8,128)(2,1)S(1)} collective-permute-done((bf16[768,256]{1,0:T(8,128)(2,1)S(1)}, bf16[768,256]{1,0:T(8,128)(2,1)S(1)}, u32[]{:S(2)}, u32[]{:S(2)}) %collective-permute-start.30) | collective-permute-done | bytes 393248 | tf_op jit(solution)/shard_map/ppermute | solution.py:955
  293.1 8.0 %weight_grad.5 = bf16[5504,256]{1,0:T(8,128)(2,1)S(1)} custom-call(s32[1]{0:T(128)} %bitcast.12.place_ref, bf16[768,2048]{1,0:T(8,128)(2,1)S(1)} %copy-done.15, bf16[768,1024]{1,0:T(8,128)(2,1)S(1)} %copy-done.25, bf16[768,1408]{1,0:T(8,128)(2,1)} %get-tuple-element.144.cols_ref.left_ref, bf16[768,1408]{1,0:T(8,128)(2,1)} %collective-permute-done.22.got_cols_ref), custom_call_target="tpu_custom_call" | custom-call | flops 1000000 | bytes 10000 | tf_op jit(solution)/shard_map/weight_grad/pallas_call | solution.py:991
  316.1 5.3 gated_backward.1
  322.7 17.3 %collective-permute-done.34.got_cols_ref = bf16[768,1408]{1,0:T(8,128)(2,1)} collective-permute-done((bf16[768,1408]{1,0:T(8,128)(2,1)}, bf16[768,1408]{1,0:T(8,128)(2,1)}, u32[]{:S(2)}, u32[]{:S(2)}) %collective-permute-start.34) | collective-permute-done | bytes 2162720 | tf_op jit(solution)/shard_map/ppermute | solution.py:955
  341.6 8.4 %collective-permute-done.35 = bf16[4,128,384]{2,1,0:T(8,128)(2,1)S(1)} collective-permute-done((bf16[4,128,384]{2,1,0:T(8,128)(2,1)S(1)}, bf16[4,128,384]{2,1,0:T(8,128)(2,1)S(1)}, u32[]{:S(2)}, u32[]{:S(2)}) %collective-permute-start.35) | collective-permute-done | bytes 393248 | tf_op jit(solution)/shard_map/ppermute | solution.py:955
  349.9 9.3 %plain_dense.3 = bf16[768,2048]{1,0:T(8,128)(2,1)S(1)} custom-call(s32[1]{0:T(128)} %bitcast.place_ref, bf16[768,1408]{1,0:T(8,128)(2,1)} %get-tuple-element.144.cols_ref.left_ref, bf16[1376,2048]{1,0:T(8,128)(2,1)S(1)} %bitcast.105), custom_call_target="tpu_custom_call" | custom-call | flops 4429185024 | bytes 10000000 | tf_op jit(solution)/shard_map/plain_dense/pallas_call | solution.py:859
  372.2 7.2 collective-permute-done.36
  381.6 8.3 %weight_grad.6 = bf16[5504,256]{1,0:T(8,128)(2,1)S(1)} custom-call(s32[1]{0:T(128)} %bitcast.12.place_ref, bf16[768,2048]{1,0:T(8,128)(2,1)S(1)} %copy-done.1, bf16[768,1024]{1,0:T(8,128)(2,1)S(1)} %copy-done.7, bf16[768,1408]{1,0:T(8,128)(2,1)} %get-tuple-element.137.refs_0_.cols_ref, bf16[768,1408]{1,0:T(8,128)(2,1)} %collective-permute-done.34.got_cols_ref), custom_call_target="tpu_custom_call" | custom-call | flops 1000000 | bytes 10000 | tf_op jit(solution)/shard_map/weight_grad/pallas_call | solution.py:991
  393.1 4.0 collective-permute-done.37
  402.4 6.6 weight_grad.7
  410.3 4.0 fusion.9
  420.0 81.4 %delta_backward.1 = (bf16[768,512]{1,0:T(8,128)(2,1)}, bf16[768,512]{1,0:T(8,128)(2,1)}, bf16[768,1024]{1,0:T(8,128)(2,1)}, f32[32,512]{1,0:T(8,128)}, f32[32,51...) custom-call(f32[12]{0:T(128)} %convert_subtract_fusion.keep_ref, ...), custom_call_target="tpu_custom_call" | custom-call | flops 1000000 | bytes 10000 | tf_op jit(solution)/shard_map/delta_backward/pallas_call | solution.py:682
  509.8 7.4 %weight_grad.8 = bf16[5504,256]{1,0:T(8,128)(2,1)S(1)} custom-call(s32[1]{0:T(128)} %bitcast.12.place_ref, bf16[768,2048]{1,0:T(8,128)(2,1)S(1)} %copy-done.2, bf16[768,1024]{1,0:T(8,128)(2,1)S(1)} %copy-done.8, bf16[768,1408]{1,0:T(8,128)(2,1)S(1)} %copy-done.35, bf16[768,1408]{1,0:T(8,128)(2,1)} %collective-permute-done.43.got_cols_ref), custom_call_target="tpu_custom_call" | custom-call | flops 1000000 | bytes 10000 | tf_op jit(solution)/shard_map/weight_grad/pallas_call | solution.py:991
  531.7 8.0 %triple_grad.1 = bf16[1024,2048]{1,0:T(8,128)(2,1)S(1)} custom-call(s32[1]{0:T(128)} %bitcast.12.place_ref, bf16[768,2048]{1,0:T(8,128)(2,1)S(1)} %fusion.2.rows_ref, bf16[768,1024]{1,0:T(8,128)(2,1)S(1)} %copy-done.4, bf16[768,512]{1,0:T(8,128)(2,1)S(1)} %copy-done.39, bf16[768,512]{1,0:T(8,128)(2,1)S(1)} %copy-done.40, bf16[768,1024]{1,0:T(8,128)(2,1)S(1)} %copy-done.38, ...), custom_call_target="tpu_custom_call" | custom-call | flops 1000000 | bytes 10000 | tf_op jit(solution)/shard_map/triple_grad/pallas_call | solution.py:1033
  544.2 18.8 %norm_dense.3 = (bf16[768,2048]{1,0:T(8,128)(2,1)}, f32[1,2048]{1,0:T(1,128)}, f32[768,1]{1,0:T(8,128)}) custom-call(s32[1]{0:T(128)} %bitcast.place_ref, bf16[768,512]{1,0:T(8,128)(2,1)} %get-tuple-element.205.first_ref.refs_0_, bf16[768,512]{1,0:T(8,128)(2,1)} %get-tuple-element.204.second_ref.refs_1_, ...), custom_call_target="tpu_custom_call" | custom-call | flops 9688842240 | bytes 20000000 | tf_op jit(solution)/shard_map/norm_dense/pallas_call | solution.py:909
  571.1 5.3 weight_grad.9
  587.8 4.2 collective-permute-done.49
  598.0 105.4 %line_sum.1 = (f32[256,2048]{1,0:T(8,128)}, bf16[768,512]{1,0:T(8,128)(2,1)}) custom-call(bf16[4,256,2048]{2,1,0:T(8,128)(2,1)} %bitcast.96, bf16[768,512]{1,0:T(8,128)(2,1)} %slice.500.across_ref), custom_call_target="tpu_custom_call" | custom-call | flops 89999998976 | bytes 10000000 | tf_op jit(solution)/shard_map/line_sum/pallas_call | solution.py:1180
  (445 shorter events, 222.7 us)
Async XLA Ops:
  7.2 407.1 %reduce-scatter.7.cloned.1.call-start = ((), (), s32[]{:S(2)}) async-start(), calls=%async_computation.6 | async-start | bytes 3522560 | tf_op jit(solution)/shard_map/reduce_scatter | solution.py:1343
  7.3 22.5 %collective-permute-start.2 = (bf16[768,512]{1,0:T(8,128)(2,1)}, bf16[768,512]{1,0:T(8,128)(2,1)}, u32[]{:S(2)}, u32[]{:S(2)}) collective-permute-start(bf16[768,512]{1,0:T(8,128)(2,1)} %refs_0_.1), channel_id=1, source_target_pairs={{0,2},{1,3},{2,0},{3,1},{4,6},{5,7},{6,4},{7,5},{8,10},{9,11},{10,... | collective-permute-start | bytes 2359304 | tf_op jit(solution)/shard_map/ppermute | solution.py:955
  10.3 71.3 %collective-permute-start.1 = (bf16[768,512]{1,0:T(8,128)(2,1)}, bf16[768,512]{1,0:T(8,128)(2,1)}, u32[]{:S(2)}, u32[]{:S(2)}) collective-permute-start(bf16[768,512]{1,0:T(8,128)(2,1)} %refs_0_.1), channel_id=1, source_target_pairs={{0,1},{1,0},{2,3},{3,2},{4,5},{5,4},{6,7},{7,6},{8,9},{9,8},{10,11... | collective-permute-start | bytes 2359304 | tf_op jit(solution)/shard_map/ppermute | solution.py:955
  29.7 51.8 %collective-permute-start.3 = (bf16[768,512]{1,0:T(8,128)(2,1)}, bf16[768,512]{1,0:T(8,128)(2,1)}, u32[]{:S(2)}, u32[]{:S(2)}) collective-permute-start(bf16[768,512]{1,0:T(8,128)(2,1)} %collective-permute-done.2.refs_2_), channel_id=1, source_target_pairs={{0,1},{1,0},{2,3},{3,2},{4,5},{5,4},{6,7},{7,6},{8,9},{9,8},{10,11... | collective-permute-start | bytes 2359304 | tf_op jit(solution)/shard_map/ppermute | solution.py:955
  31.8 47.7 %collective-permute-start.7 = (bf16[768,256]{1,0:T(8,128)(2,1)}, bf16[768,256]{1,0:T(8,128)(2,1)}, u32[]{:S(2)}, u32[]{:S(2)}) collective-permute-start(bf16[768,256]{1,0:T(8,128)(2,1)} %constant_dynamic-slice_fusion.3), channel_id=1, source_target_pairs={{0,4},{4,0},{8,12},{12,8},{16,20},{20,16},{24,28},{28,24},{1,5},{5... | collective-permute-start | bytes 1179656 | tf_op jit(solution)/shard_map/ppermute | solution.py:955
  35.1 45.1 %collective-permute-start.11 = (bf16[768,256]{1,0:T(8,128)(2,1)}, bf16[768,256]{1,0:T(8,128)(2,1)}, u32[]{:S(2)}, u32[]{:S(2)}) collective-permute-start(bf16[768,256]{1,0:T(8,128)(2,1)} %constant_dynamic-slice_fusion.2), channel_id=1, source_target_pairs={{0,4},{4,0},{8,12},{12,8},{16,20},{20,16},{24,28},{28,24},{1,5},{5... | collective-permute-start | bytes 1179656 | tf_op jit(solution)/shard_map/ppermute | solution.py:955
  80.2 18.8 %collective-permute-start.13 = (bf16[768,256]{1,0:T(8,128)(2,1)}, bf16[768,256]{1,0:T(8,128)(2,1)}, u32[]{:S(2)}, u32[]{:S(2)}) collective-permute-start(bf16[768,256]{1,0:T(8,128)(2,1)} %collective-permute-done.11.refs_0_), channel_id=1, source_target_pairs={{0,2},{1,3},{2,0},{3,1},{4,6},{5,7},{6,4},{7,5},{8,10},{9,11},{10,... | collective-permute-start | bytes 1179656 | tf_op jit(solution)/shard_map/ppermute | solution.py:955
  88.1 20.3 %collective-permute-start.8 = (bf16[768,256]{1,0:T(8,128)(2,1)}, bf16[768,256]{1,0:T(8,128)(2,1)S(1)}, u32[]{:S(2)}, u32[]{:S(2)}) collective-permute-start(bf16[768,256]{1,0:T(8,128)(2,1)} %collective-permute-done.7.refs_0_), channel_id=1, source_target_pairs={{0,1},{1,0},{2,3},{3,2},{4,5},{5,4},{6,7},{7,6},{8,9},{9,8},{10,11... | collective-permute-start | bytes 1179656 | tf_op jit(solution)/shard_map/ppermute | solution.py:955
  88.1 23.9 %collective-permute-start.12 = (bf16[768,256]{1,0:T(8,128)(2,1)}, bf16[768,256]{1,0:T(8,128)(2,1)S(1)}, u32[]{:S(2)}, u32[]{:S(2)}) collective-permute-start(bf16[768,256]{1,0:T(8,128)(2,1)} %collective-permute-done.11.refs_0_), channel_id=1, source_target_pairs={{0,1},{1,0},{2,3},{3,2},{4,5},{5,4},{6,7},{7,6},{8,9},{9,8},{10,11... | collective-permute-start | bytes 1179656 | tf_op jit(solution)/shard_map/ppermute | solution.py:955
  145.2 19.6 %collective-permute-start.16 = (bf16[768,512]{1,0:T(8,128)(2,1)S(1)}, bf16[768,512]{1,0:T(8,128)(2,1)S(1)}, u32[]{:S(2)}, u32[]{:S(2)}) collective-permute-start(bf16[768,512]{1,0:T(8,128)(2,1)S(1)} %slice.503), channel_id=1, source_target_pairs={{0,2},{1,3},{2,0},{3,1},{4,6},{5,7},{6,4},{7,5},{8,10},{9,11},{10,... | collective-permute-start | bytes 2359304 | tf_op jit(solution)/shard_map/ppermute | solution.py:955
  146.1 40.6 %collective-permute-start.20 = (bf16[768,1024]{1,0:T(8,128)(2,1)}, bf16[768,1024]{1,0:T(8,128)(2,1)}, u32[]{:S(2)}, u32[]{:S(2)}) collective-permute-start(bf16[768,1024]{1,0:T(8,128)(2,1)} %gated_forward.1.left_ref.cols_ref), channel_id=1, source_target_pairs={{0,4},{4,0},{8,12},{12,8},{16,20},{20,16},{24,28},{28,24},{1,5},{5... | collective-permute-start | bytes 4718600 | tf_op jit(solution)/shard_map/ppermute | solution.py:955
  167.5 19.2 %collective-permute-start.18 = (bf16[768,512]{1,0:T(8,128)(2,1)}, bf16[768,512]{1,0:T(8,128)(2,1)}, u32[]{:S(2)}, u32[]{:S(2)}) collective-permute-start(bf16[768,512]{1,0:T(8,128)(2,1)} %fusion.19.refs_0_), channel_id=1, source_target_pairs={{0,2},{1,3},{2,0},{3,1},{4,6},{5,7},{6,4},{7,5},{8,10},{9,11},{10,... | collective-permute-start | bytes 2359304 | tf_op jit(solution)/shard_map/ppermute | solution.py:955
  168.3 18.3 %collective-permute-start.17 = (bf16[768,512]{1,0:T(8,128)(2,1)}, bf16[768,512]{1,0:T(8,128)(2,1)}, u32[]{:S(2)}, u32[]{:S(2)}) collective-permute-start(bf16[768,512]{1,0:T(8,128)(2,1)} %fusion.19.refs_0_), channel_id=1, source_target_pairs={{0,1},{1,0},{2,3},{3,2},{4,5},{5,4},{6,7},{7,6},{8,9},{9,8},{10,11... | collective-permute-start | bytes 2359304 | tf_op jit(solution)/shard_map/ppermute | solution.py:955
  196.5 17.9 %collective-permute-start.21 = (bf16[768,256]{1,0:T(8,128)(2,1)S(1)}, bf16[768,256]{1,0:T(8,128)(2,1)}, u32[]{:S(2)}, u32[]{:S(2)}) collective-permute-start(bf16[768,256]{1,0:T(8,128)(2,1)S(1)} %constant_dynamic-slice_fusion.1), channel_id=1, source_target_pairs={{0,4},{4,0},{8,12},{12,8},{16,20},{20,16},{24,28},{28,24},{1,5},{5... | collective-permute-start | bytes 1179656 | tf_op jit(solution)/shard_map/ppermute | solution.py:955
  233.0 50.2 %collective-permute-start.22 = (bf16[768,1408]{1,0:T(8,128)(2,1)}, bf16[768,1408]{1,0:T(8,128)(2,1)}, u32[]{:S(2)}, u32[]{:S(2)}) collective-permute-start(bf16[768,1408]{1,0:T(8,128)(2,1)} %get-tuple-element.144.cols_ref.left_ref), channel_id=1, source_target_pairs={{0,4},{4,0},{8,12},{12,8},{16,20},{20,16},{24,28},{28,24},{1,5},{5... | collective-permute-start | bytes 6488072 | tf_op jit(solution)/shard_map/ppermute | solution.py:955
  239.7 25.7 %collective-permute-start.24 = (bf16[768,512]{1,0:T(8,128)(2,1)}, bf16[768,512]{1,0:T(8,128)(2,1)}, u32[]{:S(2)}, u32[]{:S(2)}) collective-permute-start(bf16[768,512]{1,0:T(8,128)(2,1)} %slice.502), channel_id=1, source_target_pairs={{0,2},{1,3},{2,0},{3,1},{4,6},{5,7},{6,4},{7,5},{8,10},{9,11},{10,... | collective-permute-start | bytes 2359304 | tf_op jit(solution)/shard_map/ppermute | solution.py:955
  241.0 21.9 %collective-permute-start.27 = (bf16[768,256]{1,0:T(8,128)(2,1)}, bf16[768,256]{1,0:T(8,128)(2,1)}, u32[]{:S(2)}, u32[]{:S(2)}) collective-permute-start(bf16[768,256]{1,0:T(8,128)(2,1)} %collective-permute-done.21.refs_0_), channel_id=1, source_target_pairs={{0,1},{1,0},{2,3},{3,2},{4,5},{5,4},{6,7},{7,6},{8,9},{9,8},{10,11... | collective-permute-start | bytes 1179656 | tf_op jit(solution)/shard_map/ppermute | solution.py:955
  269.9 22.6 %collective-permute-start.32 = (bf16[768,512]{1,0:T(8,128)(2,1)}, bf16[768,512]{1,0:T(8,128)(2,1)}, u32[]{:S(2)}, u32[]{:S(2)}) collective-permute-start(bf16[768,512]{1,0:T(8,128)(2,1)} %get-tuple-element.131.refs_0_), channel_id=1, source_target_pairs={{0,2},{1,3},{2,0},{3,1},{4,6},{5,7},{6,4},{7,5},{8,10},{9,11},{10,... | collective-permute-start | bytes 2359304 | tf_op jit(solution)/shard_map/ppermute | solution.py:955
  271.8 19.3 %collective-permute-start.30 = (bf16[768,256]{1,0:T(8,128)(2,1)S(1)}, bf16[768,256]{1,0:T(8,128)(2,1)S(1)}, u32[]{:S(2)}, u32[]{:S(2)}) collective-permute-start(bf16[768,256]{1,0:T(8,128)(2,1)S(1)} %constant_dynamic-slice_fusion), channel_id=1, source_target_pairs={{0,4},{4,0},{8,12},{12,8},{16,20},{20,16},{24,28},{28,24},{1,5},{5... | collective-permute-start | bytes 1179656 | tf_op jit(solution)/shard_map/ppermute | solution.py:955
  291.1 48.9 %collective-permute-start.34 = (bf16[768,1408]{1,0:T(8,128)(2,1)}, bf16[768,1408]{1,0:T(8,128)(2,1)}, u32[]{:S(2)}, u32[]{:S(2)}) collective-permute-start(bf16[768,1408]{1,0:T(8,128)(2,1)} %get-tuple-element.137.refs_0_.cols_ref), channel_id=1, source_target_pairs={{0,4},{4,0},{8,12},{12,8},{16,20},{20,16},{24,28},{28,24},{1,5},{5... | collective-permute-start | bytes 6488072 | tf_op jit(solution)/shard_map/ppermute | solution.py:955
  302.7 239.1 %reduce-scatter.9.cloned.1.call-start = ((), (), s32[]{:S(2)}) async-start(), calls=%async_computation.7 | async-start | bytes 3522560 | tf_op jit(solution)/shard_map/reduce_scatter | solution.py:1343
  364.2 52.5 %collective-permute-start.43 = (bf16[768,1408]{1,0:T(8,128)(2,1)}, bf16[768,1408]{1,0:T(8,128)(2,1)}, u32[]{:S(2)}, u32[]{:S(2)}) collective-permute-start(bf16[768,1408]{1,0:T(8,128)(2,1)} %get-tuple-element.168.refs_1_.cols_ref), channel_id=1, source_target_pairs={{0,4},{4,0},{8,12},{12,8},{16,20},{20,16},{24,28},{28,24},{1,5},{5... | collective-permute-start | bytes 6488072 | tf_op jit(solution)/shard_map/ppermute | solution.py:955
  366.9 25.7 %collective-permute-start.39 = (bf16[768,256]{1,0:T(8,128)(2,1)S(1)}, bf16[768,256]{1,0:T(8,128)(2,1)}, u32[]{:S(2)}, u32[]{:S(2)}) collective-permute-start(bf16[768,256]{1,0:T(8,128)(2,1)S(1)} %copy-done.43), channel_id=1, source_target_pairs={{0,2},{1,3},{2,0},{3,1},{4,6},{5,7},{6,4},{7,5},{8,10},{9,11},{10,... | collective-permute-start | bytes 1179656 | tf_op jit(solution)/shard_map/ppermute | solution.py:955
  371.0 39.3 %collective-permute-start.42 = (bf16[768,512]{1,0:T(8,128)(2,1)}, bf16[768,512]{1,0:T(8,128)(2,1)}, u32[]{:S(2)}, u32[]{:S(2)}) collective-permute-start(bf16[768,512]{1,0:T(8,128)(2,1)} %slice.501), channel_id=1, source_target_pairs={{0,2},{1,3},{2,0},{3,1},{4,6},{5,7},{6,4},{7,5},{8,10},{9,11},{10,... | collective-permute-start | bytes 2359304 | tf_op jit(solution)/shard_map/ppermute | solution.py:955
  380.3 16.8 %collective-permute-start.37 = (bf16[4,128,256]{2,1,0:T(8,128)(2,1)}, bf16[4,128,256]{2,1,0:T(8,128)(2,1)}, u32[]{:S(2)}, u32[]{:S(2)}) collective-permute-start(bf16[4,128,256]{2,1,0:T(8,128)(2,1)} %fusion.15), channel_id=1, source_target_pairs={{16,0},{20,4},{24,8},{28,12},{17,1},{21,5},{25,9},{29,13},{18,2},{... | collective-permute-start | bytes 786440 | tf_op jit(solution)/shard_map/ppermute | solution.py:950
  416.7 176.9 %reduce-scatter.11.cloned.1.call-start = ((), (), s32[]{:S(2)}) async-start(), calls=%async_computation.8 | async-start | bytes 2621440 | tf_op jit(solution)/shard_map/reduce_scatter | solution.py:1343
  417.4 178.3 %reduce-scatter.17.cloned.1.call-start = ((), (), s32[]{:S(2)}) async-start(), calls=%async_computation.11 | async-start | bytes 3522560 | tf_op jit(solution)/shard_map/reduce_scatter | solution.py:1343
  504.0 40.1 %collective-permute-start.44 = (bf16[768,512]{1,0:T(8,128)(2,1)}, bf16[768,512]{1,0:T(8,128)(2,1)}, u32[]{:S(2)}, u32[]{:S(2)}) collective-permute-start(bf16[768,512]{1,0:T(8,128)(2,1)} %get-tuple-element.203), channel_id=1, source_target_pairs={{0,4},{4,0},{8,12},{12,8},{16,20},{20,16},{24,28},{28,24},{1,5},{5... | collective-permute-start | bytes 2359304 | tf_op jit(solution)/shard_map/ppermute | solution.py:955
  518.8 192.1 %reduce-scatter.13.cloned.1.call-start = ((), (), s32[]{:S(2)}) async-start(), calls=%async_computation.9 | async-start | bytes 81920 | tf_op jit(solution)/shard_map/reduce_scatter | solution.py:1604
  520.4 42.6 %collective-permute-start.45 = (bf16[768,512]{1,0:T(8,128)(2,1)}, bf16[768,512]{1,0:T(8,128)(2,1)}, u32[]{:S(2)}, u32[]{:S(2)}) collective-permute-start(bf16[768,512]{1,0:T(8,128)(2,1)} %get-tuple-element.202), channel_id=1, source_target_pairs={{0,4},{4,0},{8,12},{12,8},{16,20},{20,16},{24,28},{28,24},{1,5},{5... | collective-permute-start | bytes 2359304 | tf_op jit(solution)/shard_map/ppermute | solution.py:955
  565.7 18.4 %collective-permute-start.46 = (bf16[768,1024]{1,0:T(8,128)(2,1)}, bf16[768,1024]{1,0:T(8,128)(2,1)}, u32[]{:S(2)}, u32[]{:S(2)}) collective-permute-start(bf16[768,1024]{1,0:T(8,128)(2,1)} %slice.309), channel_id=1, source_target_pairs={{0,1},{1,0},{2,3},{3,2},{4,5},{5,4},{6,7},{7,6},{8,9},{9,8},{10,11... | collective-permute-start | bytes 4718600 | tf_op jit(solution)/shard_map/ppermute | solution.py:955
  592.7 124.6 %reduce-scatter.15.cloned.1.call-start = ((), (), s32[]{:S(2)}) async-start(), calls=%async_computation.10 | async-start | bytes 2621440 | tf_op jit(solution)/shard_map/reduce_scatter | solution.py:1343
  (121 other events, 1564.6 us)
Sparse Core Ops, SparseCore 0:
  302.9 56.8 reduce-scatter.6
  416.8 54.4 reduce-scatter.8
  473.6 46.3 reduce-scatter.10
  522.3 53.5 reduce-scatter.16
  592.9 16.5 reduce-scatter.12
  611.7 74.0 reduce-scatter.14
